TPU v7x, 32 devices: a whole 2x2x4 slice. The times are simulated.
32 devices in a mesh: space: 8 (over y, x, core), tm: 4 (over z).
Axes of the slice: x: 2, y: 2, z: 4, core: 2. Of those that a mesh axis runs over, the one named last changes fastest.
Arguments:
- velocity: bfloat16 [4288, 3, 16384], P('tm', None, 'space'), may hold values from -6 to 6
- rotor_mask: int32 [16384], P('space'), may hold values 0 or 1
- rotor_angle: float32 [4288], P('tm'), may hold values from -3.140625 to 3.140625
- block_starts: int32 [32], replicated, may hold values from 0 to 4031, as said below
- frequencies: int32 [8], replicated, may hold values from 1 to 127, as said below
Outputs:
- spectra: float32 [8, 2, 32, 3, 16384], P('tm', None, None, None, 'space')
- factors: float32 [8, 64, 64], P('tm')
Inputs may be any that keep to these rules, and one draw needn't show every extreme that they name: `block_starts`: block b starts at b * 128 plus an offset of 0 to 63 samples; the last block's offset is 63. `frequencies`: distinct; 1 and 127 are always among them.
All inputs are finite; a program needn't handle non-finite values. No bound on the sum of `rotor_mask` on one device may be relied on, other than what follows from the above.
Results may differ from a plain program's by a relative error of at most 0.0033.
Values may be sent and summed in bfloat16 or wider, within the bound.
No kernel may reach another device: no remote copies, remote signals or barrier semaphores. Data moves between devices by JAX's collectives and lax.ppermute only.
A program may use at most 128 MiB of HBM per device.

v0:
```python
import math

import jax
import jax.numpy as jnp
from jax import lax
from jax.sharding import PartitionSpec as P

COMPS = 3
NFFT = 256


TWO_PI = 2.0 * math.pi


def to_stator(samples, angles, rotor_mask):
    along_x = samples[:, 0, :].astype(jnp.float32)
    along_y = samples[:, 1, :].astype(jnp.float32)
    cosine = jnp.cos(angles)[:, None]
    sine = jnp.sin(angles)[:, None]
    turning = (rotor_mask == 1)[None, :]
    new_x = jnp.where(turning, cosine * along_x - sine * along_y, along_x)
    new_y = jnp.where(turning, sine * along_x + cosine * along_y, along_y)
    third = samples[:, 2, :].astype(jnp.float32)
    return jnp.stack([new_x, new_y, third], axis=1).astype(jnp.bfloat16)


def window_rows(frequencies, block_starts, sample_ids, length):
    offsets = sample_ids[None, :] - block_starts[:, None]
    inside = (offsets >= 0) & (offsets < length)
    clipped = jnp.clip(offsets, 0, length - 1)
    phases = frequencies[:, None, None] * clipped[None, :, :] % length
    turns = phases.astype(jnp.float32) * (TWO_PI / length)
    taper = (0.5 - 0.5 * jnp.cos(clipped.astype(jnp.float32) * (TWO_PI / length))) * (
        8.0 / (3.0 * length)
    ) ** 0.5
    real_part = jnp.where(inside[None], taper[None] * jnp.cos(turns), 0.0)
    imag_part = jnp.where(inside[None], -(taper[None] * jnp.sin(turns)), 0.0)
    return jnp.stack([real_part, imag_part], axis=1).astype(jnp.bfloat16)


def upper_factor(gram):
    return jnp.swapaxes(jnp.linalg.cholesky(gram), 1, 2)


def factor_gram(factor):
    return jnp.einsum("fkc,fkd->fcd", factor, factor, precision=lax.Precision.HIGHEST)


def per_device(velocity, rotor_mask, rotor_angle, block_starts, frequencies):
    rotated = to_stator(velocity, rotor_angle, rotor_mask)
    span = rotated.shape[0]
    points = rotated.shape[2]
    blocks_total = block_starts.shape[0]
    freq_total = frequencies.shape[0]
    time_groups = lax.axis_size("tm")
    sample_ids = lax.axis_index("tm") * span + jnp.arange(span, dtype=jnp.int32)
    flat_samples = rotated.reshape(span, COMPS * points)
    basis_rows = window_rows(frequencies, block_starts, sample_ids, NFFT).reshape(
        lax.axis_size("tm") * (freq_total // time_groups) * 2 * blocks_total, span
    )
    product = jnp.dot(basis_rows, flat_samples, preferred_element_type=jnp.float32)
    owned = lax.psum_scatter(
        product.reshape(
            lax.axis_size("tm") * (freq_total // time_groups), 2, blocks_total, COMPS, points
        ),
        "tm",
        scatter_dimension=0,
        tiled=True,
    )
    owned_count = owned.shape[0]
    flat_rows = owned.reshape(owned_count, 2 * blocks_total, COMPS * points)
    gram_local = jnp.einsum(
        "fcr,fdr->fcd", flat_rows, flat_rows, precision=lax.Precision.HIGHEST
    ) / (COMPS * points * lax.axis_size("space"))
    local_factor = upper_factor(gram_local)
    stacked = lax.all_gather(local_factor, "space", axis=1, tiled=True)
    factor = upper_factor(factor_gram(stacked))
    return (owned, factor)


def solution(mesh):
    in_specs = (P("tm", None, "space"), P("space"), P("tm"), P(), P())
    out_specs = (P("tm", None, None, None, "space"), P("tm", None, None))
    return jax.shard_map(
        per_device, mesh=mesh, in_specs=in_specs, out_specs=out_specs, check_vma=False
    )
```

profile of v0, /device:TPU:0, one launch (start us, length us, event | category | flops | bytes accessed | tf_op | source)
XLA Modules:
  0.0 305.7 jit_solution(18112905594533068989)
XLA Ops:
  7.2 0.0 reduce-scatter.2.cloned.1.call-start
  7.2 0.8 subtract_clamp_fusion
  8.0 1.3 subtract_multiply_fusion
  9.2 0.8 fusion.16
  10.0 0.7 fusion.20
  10.7 0.7 broadcast_compare_fusion
  11.5 0.0 copy-start
  11.5 0.0 slice-start
  11.5 6.5 %fusion.6 = (bf16[1072,1,2048]{2,0,1:T(8,128)(2,1)S(1)}, bf16[1072,1,2048]{2,0,1:T(8,128)(2,1)S(1)}) fusion(f32[1072]{0:T(1024)S(1)} %get-tuple-element.16, f32[1072]{0:T(1024)S(1)} %get-tuple-element.15, pred[2048]{0:T(1024)(128)(4,1)S(1)} %broadcast_compare_fusion, bf16[1072,3,2048]{2,0,1:T(8,128)(2,1)} %param.6), kind=kLoop, calls=%fused_computation.13 | loop fusion | flops 26345472 | bytes 17574272 | tf_op jit(solution)/shard_map/convert
  18.0 0.0 copy-done
  18.0 5.1 %select_convert_fusion.1 = (bf16[8,1,32,1072]{3,2,1,0:T(8,128)(2,1)S(1)}, bf16[8,1,32,1072]{3,2,1,0:T(8,128)(2,1)S(1)}) fusion(s32[32,1072]{1,0:T(8,128)S(1)} %subtract_clamp_fusion, s32[8]{0:T(128)S(1)} %copy-done, f32[32,1072]{1,0:T(8,128)S(1)} %subtract_multiply_fusion, pred[32,1072]{1,0:T(8,128)(4,1)S(1)} %fusion.16), kind=kLoop, calls=%fused_computation.28 | loop fusion | flops 5763072 | bytes 1406496 | tf_op jit(solution)/shard_map/convert.3
  23.1 0.0 slice-done
  23.1 11.2 %fusion = f32[8,2,32,3,2048]{4,2,3,1,0:T(8,128)} fusion(bf16[1072,1,2048]{2,0,1:T(8,128)(2,1)S(1)} %slice-done, bf16[1072,1,2048]{2,0,1:T(8,128)(2,1)S(1)} %get-tuple-element.12, bf16[1072,1,2048]{2,0,1:T(8,128)(2,1)S(1)} %get-tuple-element.11, bf16[8,1,32,1072]{3,2,1,0:T(8,128)(2,1)S(1)} %get-tuple-element.14, ...), kind=kOutput, calls=%fused_computation.1 | convolution fusion | flops 6786154496 | bytes 26853376 | tf_op jit(solution)/shard_map/dot_general | solution.py:61
  34.3 0.0 reduce-scatter.2.cloned.1.call-update
  34.4 214.7 %reduce-scatter.2.cloned.1.call-done = f32[2,2,32,3,2048]{4,2,3,1,0:T(8,128)} async-done(((f32[8,2,32,3,2048]{4,2,3,1,0:T(8,128)}), f32[2,2,32,3,2048]{4,2,3,1,0:T(8,128)}) %reduce-scatter.2.cloned.1.call-update) | async-done | bytes 3145744 | tf_op jit(solution)/shard_map/reduce_scatter | solution.py:62
  249.1 6.0 %copy.32 = f32[2,2,32,3,2048]{4,3,2,1,0:T(4,128)} copy(f32[2,2,32,3,2048]{4,2,3,1,0:T(8,128)} %reduce-scatter.2.cloned.1.call-done) | data formatting | bytes 6291456 | tf_op jit(solution)/shard_map/reduce_scatter | solution.py:62
  255.0 5.1 %reshape.199 = f32[2,64,6144]{2,1,0:T(8,128)S(1)} reshape(f32[2,2,32,3,2048]{4,3,2,1,0:T(4,128)} %copy.32) | data formatting | bytes 6291456 | tf_op jit(solution)/shard_map/reshape | solution.py:71
  260.2 2.9 convolution_multiply_fusion
  263.1 0.1 copy.34
  263.2 11.7 %custom-call.4 = f32[2,64,64]{2,1,0:T(8,128)S(1)} custom-call(f32[2,64,64]{2,1,0:T(8,128)S(1)} %fusion.18), custom_call_target="Cholesky" | custom-call | tf_op jit(solution)/shard_map/jit(cholesky)/cholesky | solution.py:42
  275.0 0.1 compare_reduce_fusion.1
  275.1 0.1 select_bitcast_fusion.1
  275.2 0.1 copy.35
  275.3 9.8 %all_gather.3 = f32[2,512,64]{2,0,1:T(2,128)S(1)} all-gather(f32[2,64,64]{2,0,1:T(2,128)S(1)} %copy.35), channel_id=1, replica_groups=mesh['space'=8,'tm'=4] {'space'}, dimensions={1}, use_global_device_ids=true | all-gather | bytes 294912 | tf_op jit(solution)/shard_map/all_gather | solution.py:76
  285.0 1.0 fusion.14
  286.1 0.1 copy.38
  286.2 11.7 %custom-call.5 = f32[2,64,64]{2,1,0:T(8,128)S(1)} custom-call(f32[2,64,64]{2,1,0:T(8,128)S(1)} %fusion.17), custom_call_target="Cholesky" | custom-call | tf_op jit(solution)/shard_map/jit(cholesky)/cholesky | solution.py:42
  298.0 0.1 compare_reduce_fusion
  298.1 0.1 select_bitcast_fusion
  298.2 0.7 copy.39
  (7 shorter events, 0.1 us)
Async XLA Ops:
  7.2 241.9 %reduce-scatter.2.cloned.1.call-start = ((), (), s32[]{:S(2)}) async-start(), calls=%async_computation.1 | async-start | bytes 15728640 | tf_op jit(solution)/shard_map/reduce_scatter | solution.py:62
  11.5 6.5 %copy-start = (s32[8]{0:T(128)S(1)}, s32[8]{0:T(128)}, u32[]{:S(2)}) copy-start(s32[8]{0:T(128)} %param.10) | copy-start | bytes 100
  11.5 11.6 %slice-start = ((bf16[1072,3,2048]{2,0,1:T(8,128)(2,1)}), bf16[1072,1,2048]{2,0,1:T(8,128)(2,1)S(1)}, s32[]{:S(2)}) async-start(bf16[1072,3,2048]{2,0,1:T(8,128)(2,1)} %param.6), calls=%async_computation.2 | async-start | bytes 8781824 | tf_op jit(solution)/shard_map/slice | solution.py:23
Sparse Core Ops, SparseCore 0:
  34.5 214.5 reduce-scatter.1
where the time goes:
time: 306 us
  waiting for transfers between devices  215 us (70%)
  other arithmetic  39.1 us (13%)
  matrix products  15.1 us (5%)
  between operations  14.2 us (5%)
  local copies, waits for them, and re-layouts  12.8 us (4%)
  blocking collectives  9.78 us (3%)
    reduce_scatter x1, waiting for transfers between devices, per_device(): lax.psum_scatter(product.reshape(lax.axis_size('tm') * (freq_total // tim...  215 us
    another operation x7, other arithmetic, upper_factor(): return jnp.swapaxes(jnp.linalg.cholesky(gram), 1, 2)  23.8 us
    another operation x2, other arithmetic  11.6 us
    dot_general x1, matrix products, per_device(): jnp.dot(basis_rows, flat_samples, preferred_element_type=jnp.float32)  11.2 us
    all_gather x1, blocking collectives, per_device(): stacked = lax.all_gather(local_factor, 'space', axis=1, tiled=True)  9.78 us
  transfers between devices with their start and end apart: 1, of which 1 were waited for; matrix products, arithmetic and copies ran while one was open for 0% of the time, Pallas kernels for 0%

commit v1 on v0

v1 whole, which is shorter than its diff:
```python
import functools
import math

import jax
import jax.numpy as jnp
from jax import lax
from jax.experimental import pallas as pl
from jax.experimental.pallas import tpu as pltpu
from jax.sharding import PartitionSpec as P

COMPS = 3
NFFT = 256
JIT = 64
HOP = 128
LANES = 128
TILE = 256
SCALE = (8.0 / (3.0 * NFFT)) ** 0.5
HIGHEST = lax.Precision.HIGHEST


def first_block(shard, span):
    return jnp.maximum((shard * span - (NFFT + JIT - 1) + HOP) // HOP, 0)


def slot_count(shards, span, blocks, rows_per_slot):
    most = 0
    for s in range(shards):
        lo = max((s * span - (NFFT + JIT - 1) + HOP) // HOP, 0)
        hi = min((span * (s + 1) - 1) // HOP, blocks - 1)
        most = max(most, hi - lo + 1)
    step = 16 // math.gcd(16, rows_per_slot)
    return -(-most // step) * step


def half_turn_sine(x):
    z = x * x
    c = [math.pi ** (2 * i + 1) * (-1) ** i / math.factorial(2 * i + 1) for i in range(7)]
    acc = jnp.full_like(z, c[-1])
    for term in c[-2::-1]:
        acc = acc * z + term
    return acc * x


def build_rows(n, owned, slots, span, blocks, me, starts_ref, freqs_ref, a_ref):
    group = owned * 2
    rid = lax.broadcasted_iota(jnp.int32, (n * group, 1), 0)
    k_of, j_of, r_of = rid // group, (rid // 2) % owned, rid % 2
    f_of = lax.rem(me + k_of, n) * owned + j_of
    freq = jnp.zeros((n * group, 1), jnp.float32)
    for f in range(n * owned):
        freq = jnp.where(f_of == f, freqs_ref[f].astype(jnp.float32), freq)
    step = freq * (1.0 / NFFT)
    quarter = r_of.astype(jnp.float32) * 0.25
    lo = first_block(me, span)
    sample = lax.broadcasted_iota(jnp.int32, (1, span), 1) + me * span
    pieces = [[] for _ in range(n)]
    for s in range(slots):
        b = lo + s
        start = starts_ref[jnp.minimum(b, blocks - 1)]
        ni = sample - start
        inside = (ni >= 0) & (ni < NFFT) & (b < blocks)
        nf = ni.astype(jnp.float32)
        w = half_turn_sine(jnp.minimum(nf, NFFT - nf) * (1.0 / NFFT))
        w = jnp.where(inside, w * w * SCALE, 0.0)
        nf = jnp.where(inside, nf, 0.0)
        turns = nf * step + quarter
        turns = turns - jnp.floor(turns + 0.5)
        h = half_turn_sine(turns)
        rows = w * (1.0 - 2.0 * h * h)
        for k in range(n):
            pieces[k].append(rows[k * group:(k + 1) * group])
    for k in range(n):
        a_ref[k] = jnp.concatenate(pieces[k], axis=0).astype(jnp.bfloat16)


def spread_column(row, span, out_ref):
    for at in range(0, span, LANES):
        width = min(LANES, span - at)
        part = row[:, at:at + width]
        if width < LANES:
            part = jnp.concatenate([part, jnp.zeros((1, LANES - width), jnp.float32)], axis=1)
        turned = jnp.transpose(jnp.broadcast_to(part, (LANES, LANES)))
        out_ref[at:at + width, :] = turned[:width]


def dft_body(n, owned, slots, span, blocks, first, *refs):
    if first:
        pos_ref, starts_ref, freqs_ref, angle_ref, mask_ref, vel_ref = refs[:6]
        outs = refs[6:6 + n]
        a_ref, cos_ref, sin_ref = refs[6 + n:9 + n]
        rot_ref = refs[9 + n]

        @pl.when(pl.program_id(0) == 0)
        def _():
            build_rows(n, owned, slots, span, blocks, pos_ref[0], starts_ref, freqs_ref, a_ref)
            spread_column(jnp.cos(angle_ref[...]), span, cos_ref)
            spread_column(jnp.sin(angle_ref[...]), span, sin_ref)
    else:
        mask_ref, vel_ref, a_ref, cos_ref, sin_ref = refs[:5]
        outs = refs[5:5 + n]
        rot_ref = refs[5 + n]
    width = vel_ref.shape[2]
    turning = mask_ref[...] == 1
    for at in range(0, span, 16):
        rows = min(16, span - at)
        here = pl.ds(at, rows)
        cosine = jnp.concatenate([cos_ref[here, :]] * (width // LANES), axis=1)
        sine = jnp.concatenate([sin_ref[here, :]] * (width // LANES), axis=1)
        x = vel_ref[0, here, :].astype(jnp.float32)
        y = vel_ref[1, here, :].astype(jnp.float32)
        rot_ref[0, here, :] = jnp.where(turning, cosine * x - sine * y, x).astype(jnp.bfloat16)
        rot_ref[1, here, :] = jnp.where(turning, sine * x + cosine * y, y).astype(jnp.bfloat16)
    rows = a_ref.shape[1]
    a = a_ref[...].reshape(n * rows, span)
    for c in range(COMPS):
        samples = rot_ref[c] if c < 2 else vel_ref[2]
        sums = jnp.dot(a, samples, preferred_element_type=jnp.float32).astype(jnp.bfloat16)
        for k in range(n):
            outs[k][c * rows:(c + 1) * rows, :] = sums[k * rows:(k + 1) * rows]


def dft_call(n, owned, slots, blocks, first, offset, points, position, starts, freqs, angles, mask, velocity, shared):
    span = velocity.shape[1]
    rows = slots * owned * 2
    shift = offset // TILE
    whole = lambda shape: pl.BlockSpec(shape, lambda i: (0,) * len(shape))
    smem = pl.BlockSpec(memory_space=pltpu.SMEM)
    data_specs = [
        pl.BlockSpec((1, TILE), lambda i: (0, i + shift)),
        pl.BlockSpec((COMPS, span, TILE), lambda i: (0, 0, i + shift)),
    ]
    shared_types = [
        jax.ShapeDtypeStruct((n, rows, span), jnp.bfloat16),
        jax.ShapeDtypeStruct((span, LANES), jnp.float32),
        jax.ShapeDtypeStruct((span, LANES), jnp.float32),
    ]
    shared_specs = [whole(t.shape) for t in shared_types]
    out_types = [jax.ShapeDtypeStruct((COMPS * rows, points), jnp.bfloat16)] * n
    out_specs = [pl.BlockSpec((COMPS * rows, TILE), lambda i: (0, i))] * n
    if first:
        args = (position, starts, freqs, angles, mask, velocity)
        in_specs = [smem] * 3 + [whole((1, span))] + data_specs
        out_types = out_types + shared_types
        out_specs = out_specs + shared_specs
    else:
        args = (mask, velocity) + tuple(shared)
        in_specs = data_specs + shared_specs
    out = pl.pallas_call(
        functools.partial(dft_body, n, owned, slots, span, blocks, first),
        grid=(points // TILE,),
        out_shape=out_types,
        in_specs=in_specs,
        out_specs=out_specs,
        scratch_shapes=[pltpu.VMEM((2, span, TILE), jnp.bfloat16)],
        compiler_params=pltpu.CompilerParams(vmem_limit_bytes=40 * 2**20),
        cost_estimate=pl.CostEstimate(
            flops=2 * n * rows * span * COMPS * points,
            bytes_accessed=2 * COMPS * span * points,
            transcendentals=0,
        ),
        name="rotate_dft",
    )(*args)
    return out[:n], out[n:] if first else shared


def selection(n, owned, slots, span, blocks, me):
    rows = slots * owned * 2
    shape = (owned * 2 * blocks, n * rows)
    out = lax.broadcasted_iota(jnp.int32, shape, 0)
    col = lax.broadcasted_iota(jnp.int32, shape, 1)
    k_of = jnp.zeros(shape, jnp.int32)
    lo = jnp.broadcast_to(first_block(me, span), shape)
    for k in range(1, n):
        past = col >= k * rows
        k_of = jnp.where(past, k, k_of)
        lo = jnp.where(past, first_block(lax.rem(me + n - k, n), span), lo)
    rem = col - k_of * rows
    slot = rem // (owned * 2)
    same = (out // blocks == rem % (owned * 2)) & (out % blocks == lo + slot)
    return jnp.where(same, 1.0, 0.0)


def assemble_body(n, owned, slots, span, blocks, total, has_sum, last, *refs):
    pos_ref = refs[0]
    parts = refs[1:1 + n]
    rest = refs[1 + n:]
    if has_sum:
        sum_in, rest = rest[0], rest[2:]
    spectra_ref, gram_ref, sel_ref, acc_ref = rest
    step = pl.program_id(0)
    rows = slots * owned * 2

    @pl.when(step == 0)
    def _():
        sel_ref[...] = selection(n, owned, slots, span, blocks, pos_ref[0]).astype(jnp.bfloat16)
        acc_ref[...] = sum_in[...] if has_sum else jnp.zeros_like(acc_ref)

    for c in range(COMPS):
        stack = jnp.concatenate([p[c * rows:(c + 1) * rows, :] for p in parts], axis=0)
        full = jnp.dot(sel_ref[...], stack, preferred_element_type=jnp.float32)
        for j in range(owned):
            for r in range(2):
                at = (j * 2 + r) * blocks
                spectra_ref[j, r, c] = full[at:at + blocks]
        acc_ref[...] += lax.dot_general(
            stack, stack, (((1,), (1,)), ((), ())), preferred_element_type=jnp.float32
        )

    @pl.when(step == pl.num_programs(0) - 1)
    def _():
        if not last:
            gram_ref[...] = acc_ref[...]
        else:
            sel = sel_ref[...].astype(jnp.float32)
            half = jnp.dot(sel, acc_ref[...], precision=HIGHEST, preferred_element_type=jnp.float32)
            order = 2 * blocks
            gram = lax.dot_general(
                half, sel, (((1,), (1,)), ((), ())), precision=HIGHEST, preferred_element_type=jnp.float32
            ) * (1.0 / total)
            gram_ref[...] = jnp.concatenate(
                [gram[j * order:(j + 1) * order, j * order:(j + 1) * order] for j in range(owned)], axis=1
            )


def assemble_call(n, owned, slots, span, blocks, total, offset, points, all_points, position, parts, spectra, gram, last):
    rows = slots * owned * 2
    tile = min(points, 512)
    shift = offset // tile
    order = 2 * blocks
    has_sum = gram is not None
    whole = lambda shape: pl.BlockSpec(shape, lambda i: (0,) * len(shape))
    gram_shape = (order, owned * order) if last else (n * rows, n * rows)
    args = [position] + list(parts)
    in_specs = [pl.BlockSpec(memory_space=pltpu.SMEM)] + [pl.BlockSpec((COMPS * rows, tile), lambda i: (0, i))] * n
    aliases = {}
    if has_sum:
        args += [gram, spectra]
        in_specs += [whole((n * rows, n * rows)), pl.BlockSpec(memory_space=pl.ANY)]
        aliases = {len(args) - 1: 0}
    return pl.pallas_call(
        functools.partial(assemble_body, n, owned, slots, span, blocks, total, has_sum, last),
        grid=(points // tile,),
        out_shape=[
            jax.ShapeDtypeStruct((owned, 2, COMPS, blocks, all_points), jnp.float32),
            jax.ShapeDtypeStruct(gram_shape, jnp.float32),
        ],
        in_specs=in_specs,
        out_specs=[
            pl.BlockSpec((owned, 2, COMPS, blocks, tile), lambda i: (0, 0, 0, 0, i + shift)),
            whole(gram_shape),
        ],
        scratch_shapes=[
            pltpu.VMEM((owned * order, n * rows), jnp.bfloat16),
            pltpu.VMEM((n * rows, n * rows), jnp.float32),
        ],
        input_output_aliases=aliases,
        compiler_params=pltpu.CompilerParams(vmem_limit_bytes=40 * 2**20),
        cost_estimate=pl.CostEstimate(
            flops=4 * (n * rows) ** 2 * COMPS * points,
            bytes_accessed=4 * owned * order * COMPS * points,
            transcendentals=0,
        ),
        name="assemble",
    )(*args)


def factor_body(owned, order, count, *refs):
    parts = refs[:count]
    out_ref, row_ref = refs[count:]
    s = parts[0][...]
    for p in parts[1:]:
        s = s + p[...]
    lane = lax.broadcasted_iota(jnp.int32, (1, owned * order), 1)
    for k in range(order):
        base = k // 8 * 8
        s = s[base - (k - 1) // 8 * 8:] if k else s
        column = jnp.broadcast_to(s[:, k:k + 1], s.shape)
        for j in range(1, owned):
            column = jnp.where(lane >= j * order, s[:, j * order + k:j * order + k + 1], column)
        at = k - base
        pivot = column[at:at + 1]
        inverse_root = lax.rsqrt(pivot)
        row = s[at:at + 1] * inverse_root
        row_ref[k:k + 1, :] = jnp.where(lane % order >= k, row, 0.0)
        s = s - column * (row * inverse_root)
    for j in range(owned):
        out_ref[j] = row_ref[:, j * order:(j + 1) * order]


def factor_call(owned, order, parts):
    return pl.pallas_call(
        functools.partial(factor_body, owned, order, len(parts)),
        out_shape=jax.ShapeDtypeStruct((owned, order, order), jnp.float32),
        scratch_shapes=[pltpu.VMEM((order, owned * order), jnp.float32)],
        name="factor",
    )(*parts)


def chunks_of(points):
    tile = 512
    return [(at, tile) for at in range(0, points, tile)]


def per_device(velocity, rotor_mask, rotor_angle, block_starts, frequencies):
    span, _, points = velocity.shape
    n = lax.axis_size("tm")
    groups = lax.axis_size("space")
    blocks = block_starts.shape[0]
    owned = frequencies.shape[0] // n
    order = 2 * blocks
    slots = slot_count(n, span, blocks, owned * 2)
    position = lax.axis_index("tm").astype(jnp.int32).reshape(1)
    samples = velocity.transpose(1, 0, 2)
    mask = rotor_mask.reshape(1, points)
    angles = rotor_angle.reshape(1, span)

    pieces = []
    shared = None
    for at, count in chunks_of(points):
        sums, shared = dft_call(
            n, owned, slots, blocks, shared is None, at, count,
            position, block_starts, frequencies, angles, mask, samples, shared,
        )
        moved = [sums[0]] + [
            lax.ppermute(sums[k], "tm", [(i, (i + k) % n) for i in range(n)]) for k in range(1, n)
        ]
        pieces.append((at, count, moved))

    spectra, gram = None, None
    total = COMPS * points * groups
    for at, count, moved in pieces:
        last = at + count == points
        spectra, gram = assemble_call(
            n, owned, slots, span, blocks, total, at, count, points, position, moved, spectra, gram, last
        )
    if groups <= 8:
        grams = [gram] + [
            lax.ppermute(gram, "space", [(i, (i + k) % groups) for i in range(groups)]) for k in range(1, groups)
        ]
    else:
        grams = [lax.psum(gram, "space")]
    factors = factor_call(owned, order, grams)
    return spectra.transpose(0, 1, 3, 2, 4), factors


def solution(mesh):
    in_specs = (P("tm", None, "space"), P("space"), P("tm"), P(), P())
    out_specs = (P("tm", None, None, None, "space"), P("tm", None, None))
    return jax.shard_map(
        per_device, mesh=mesh, in_specs=in_specs, out_specs=out_specs, check_vma=False
    )
```

time: 306 us -> 82.8 us (0.27)
  waiting for transfers between devices: 215 us -> 14 us
  other arithmetic: 39.1 us -> 0 us
  starting transfers between devices: 0.04 us -> 36.6 us
  Pallas kernels: 0 us -> 27.1 us
  matrix products: 15.1 us -> 0 us
  between operations: 14.2 us -> 0.78 us
  blocking collectives: 9.78 us -> 0 us
  local copies, waits for them, and re-layouts: 12.8 us -> 3.33 us
    reduce_scatter x1 -> x0, waiting for transfers between devices: 215 us -> none  [per_device(): lax.psum_scatter(product.reshape(lax.axis_size('tm') * (freq_total // tim...]
    ppermute x0 -> x19, starting transfers between devices: none -> 36.6 us  [the longest x12 29.7 us: per_device(): lax.ppermute(sums[k], 'tm', [(i, (i + k) % n) for i in range(n)])]
    another operation x9 -> x0, other arithmetic: 35.4 us -> none  [the longest x7 23.8 us: upper_factor(): return jnp.swapaxes(jnp.linalg.cholesky(gram), 1, 2)]
    pallas_call x0 -> x9, Pallas kernels: none -> 27.1 us  [the longest x4 14.5 us: dft_call(): pl.pallas_call(functools.partial(dft_body, n, owned, slots, span, blocks,...]
    dot_general x3 -> x0, matrix products: 15.1 us -> none  [the longest x1 11.2 us: per_device(): jnp.dot(basis_rows, flat_samples, preferred_element_type=jnp.float32)]
    ppermute x0 -> x19, waiting for transfers between devices: none -> 14 us  [the longest x12 9.85 us: per_device(): lax.ppermute(sums[k], 'tm', [(i, (i + k) % n) for i in range(n)])]
    all_gather x1 -> x0, blocking collectives: 9.78 us -> none  [per_device(): stacked = lax.all_gather(local_factor, 'space', axis=1, tiled=True)]
    reduce_scatter x1 -> x0, local copies, waits for them, and re-layouts: 5.97 us -> none  [per_device(): lax.psum_scatter(product.reshape(lax.axis_size('tm') * (freq_total // tim...]
  transfers between devices with their start and end apart: 1 -> 19, of which waited for: 1 -> 6; matrix products, arithmetic and copies ran while one was open for 0% -> 0% of each run, Pallas kernels for 0% -> 17%
where the time goes in v1:
time: 82.8 us; the launch traced here: 81.8 us
  starting transfers between devices  36.6 us (44%)
  Pallas kernels  27.1 us (33%)
  waiting for transfers between devices  14 us (17%)
  local copies, waits for them, and re-layouts  3.33 us (4%)
    ppermute x12, starting transfers between devices, per_device(): lax.ppermute(sums[k], 'tm', [(i, (i + k) % n) for i in range(n)])  29.7 us
    pallas_call x4, Pallas kernels, dft_call(): pl.pallas_call(functools.partial(dft_body, n, owned, slots, span, blocks,...  14.5 us
    ppermute x12, waiting for transfers between devices, per_device(): lax.ppermute(sums[k], 'tm', [(i, (i + k) % n) for i in range(n)])  9.85 us
    pallas_call x1, Pallas kernels, factor_call(): pl.pallas_call(functools.partial(factor_body, owned, order, len(parts)),...  7.09 us
    ppermute x7, starting transfers between devices, per_device(): lax.ppermute(gram, 'space', [(i, (i + k) % groups) for i in range(groups)])  6.87 us
    pallas_call x4, Pallas kernels, assemble_call(): pl.pallas_call(functools.partial(assemble_body, n, owned, slots, span, bl...  5.47 us
    ppermute x7, waiting for transfers between devices, per_device(): lax.ppermute(gram, 'space', [(i, (i + k) % groups) for i in range(groups)])  4.2 us
    unnamed x22, local copies, waits for them, and re-layouts  2.63 us
  transfers between devices with their start and end apart: 19, of which 6 were waited for; matrix products, arithmetic and copies ran while one was open for 0% of the time, Pallas kernels for 17%

profile of v1, /device:TPU:0, one launch (start us, length us, event | category | flops | bytes accessed | tf_op | source)
XLA Modules:
  0.0 81.8 jit_solution(7652558204290270348)
XLA Ops:
  0.6 0.7 reshape.15.refs_3_
  1.3 0.7 copy-done
  2.0 0.7 copy-done.2
  2.7 0.7 copy-done.3
  3.3 4.8 %rotate_dft.4 = (bf16[144,512]{1,0:T(8,128)(2,1)S(1)}, bf16[144,512]{1,0:T(8,128)(2,1)S(1)}, bf16[144,512]{1,0:T(8,128)(2,1)S(1)}, bf16[144,512]{1,0:T(8,128)(2,...) custom-call(s32[1]{0:T(128)} %bitcast.refs_0_, s32[32]{0:T(128)S(1)} %copy-done.2, ...), custom_call_target="tpu_custom_call" | custom-call | flops 632291328 | bytes 3293184 | tf_op jit(solution)/shard_map/rotate_dft/pallas_call | solution.py:148
  8.2 3.1 %collective-permute-start.9 = (bf16[144,512]{1,0:T(8,128)(2,1)S(1)}, bf16[144,512]{1,0:T(8,128)(2,1)S(1)}, u32[]{:S(2)}, u32[]{:S(2)}) collective-permute-start(bf16[144,512]{1,0:T(8,128)(2,1)S(1)} %get-tuple-element.45), channel_id=1, source_target_pairs={{0,1},{1,2},{2,3},{3,0},{4,5},{5,6},{6,7},{7,4},{8,9},{9,10},{10,1... | collective-permute-start | bytes 442376 | tf_op jit(solution)/shard_map/ppermute | solution.py:325
  11.2 2.6 %collective-permute-start.10 = (bf16[144,512]{1,0:T(8,128)(2,1)S(1)}, bf16[144,512]{1,0:T(8,128)(2,1)S(1)}, u32[]{:S(2)}, u32[]{:S(2)}) collective-permute-start(bf16[144,512]{1,0:T(8,128)(2,1)S(1)} %get-tuple-element.46), channel_id=1, source_target_pairs={{0,2},{1,3},{2,0},{3,1},{4,6},{5,7},{6,4},{7,5},{8,10},{9,11},{10,... | collective-permute-start | bytes 442376 | tf_op jit(solution)/shard_map/ppermute | solution.py:325
  13.8 1.3 %collective-permute-start.11 = (bf16[144,512]{1,0:T(8,128)(2,1)S(1)}, bf16[144,512]{1,0:T(8,128)(2,1)S(1)}, u32[]{:S(2)}, u32[]{:S(2)}) collective-permute-start(bf16[144,512]{1,0:T(8,128)(2,1)S(1)} %get-tuple-element.47), channel_id=1, source_target_pairs={{0,3},{1,0},{2,1},{3,2},{4,7},{5,4},{6,5},{7,6},{8,11},{9,8},{10,9... | collective-permute-start | bytes 442376 | tf_op jit(solution)/shard_map/ppermute | solution.py:325
  15.2 3.2 %rotate_dft.7 = (bf16[144,512]{1,0:T(8,128)(2,1)S(1)}, bf16[144,512]{1,0:T(8,128)(2,1)S(1)}, bf16[144,512]{1,0:T(8,128)(2,1)S(1)}, bf16[144,512]{1,0:T(8,128)(2,1)S(1)}) custom-call(s32[1,2048]{1,0:T(1,128)S(1)} %bitcast.5, bf16[3,1072,2048]{2,1,0:T(8,128)(2,1)} %bitcast.9, bf16[4,48,1072]{2,1,0:T(8,128)(2,1)S(1)} %get-tuple-element.29.refs_2_, ...), custom_call_target="tpu_custom_call" | custom-call | flops 632291328 | bytes 3293184 | tf_op jit(solution)/shard_map/rotate_dft/pallas_call | solution.py:148
  18.4 0.7 collective-permute-start.6
  19.5 3.2 %rotate_dft.6 = (bf16[144,512]{1,0:T(8,128)(2,1)S(1)}, bf16[144,512]{1,0:T(8,128)(2,1)S(1)}, bf16[144,512]{1,0:T(8,128)(2,1)S(1)}, bf16[144,512]{1,0:T(8,128)(2,1)S(1)}) custom-call(s32[1,2048]{1,0:T(1,128)S(1)} %bitcast.6, bf16[3,1072,2048]{2,1,0:T(8,128)(2,1)} %bitcast.10, bf16[4,48,1072]{2,1,0:T(8,128)(2,1)S(1)} %get-tuple-element.29.refs_2_, ...), custom_call_target="tpu_custom_call" | custom-call | flops 632291328 | bytes 3293184 | tf_op jit(solution)/shard_map/rotate_dft/pallas_call | solution.py:148
  22.7 2.9 %collective-permute-start.8 = (bf16[144,512]{1,0:T(8,128)(2,1)S(1)}, bf16[144,512]{1,0:T(8,128)(2,1)S(1)}, u32[]{:S(2)}, u32[]{:S(2)}) collective-permute-start(bf16[144,512]{1,0:T(8,128)(2,1)S(1)} %get-tuple-element.43), channel_id=1, source_target_pairs={{0,3},{1,0},{2,1},{3,2},{4,7},{5,4},{6,5},{7,6},{8,11},{9,8},{10,9... | collective-permute-start | bytes 442376 | tf_op jit(solution)/shard_map/ppermute | solution.py:325
  25.6 7.2 %collective-permute-start.3 = (bf16[144,512]{1,0:T(8,128)(2,1)S(1)}, bf16[144,512]{1,0:T(8,128)(2,1)S(1)}, u32[]{:S(2)}, u32[]{:S(2)}) collective-permute-start(bf16[144,512]{1,0:T(8,128)(2,1)S(1)} %get-tuple-element.37), channel_id=1, source_target_pairs={{0,1},{1,2},{2,3},{3,0},{4,5},{5,6},{6,7},{7,4},{8,9},{9,10},{10,1... | collective-permute-start | bytes 442376 | tf_op jit(solution)/shard_map/ppermute | solution.py:325
  32.8 3.5 %collective-permute-start.4 = (bf16[144,512]{1,0:T(8,128)(2,1)S(1)}, bf16[144,512]{1,0:T(8,128)(2,1)S(1)}, u32[]{:S(2)}, u32[]{:S(2)}) collective-permute-start(bf16[144,512]{1,0:T(8,128)(2,1)S(1)} %get-tuple-element.38), channel_id=1, source_target_pairs={{0,2},{1,3},{2,0},{3,1},{4,6},{5,7},{6,4},{7,5},{8,10},{9,11},{10,... | collective-permute-start | bytes 442376 | tf_op jit(solution)/shard_map/ppermute | solution.py:325
  36.8 3.2 %rotate_dft.5 = (bf16[144,512]{1,0:T(8,128)(2,1)S(1)}, bf16[144,512]{1,0:T(8,128)(2,1)S(1)}, bf16[144,512]{1,0:T(8,128)(2,1)S(1)}, bf16[144,512]{1,0:T(8,128)(2,1)S(1)}) custom-call(s32[1,2048]{1,0:T(1,128)S(1)} %bitcast.7, bf16[3,1072,2048]{2,1,0:T(8,128)(2,1)} %bitcast.11, bf16[4,48,1072]{2,1,0:T(8,128)(2,1)S(1)} %get-tuple-element.29.refs_2_, ...), custom_call_target="tpu_custom_call" | custom-call | flops 632291328 | bytes 3293184 | tf_op jit(solution)/shard_map/rotate_dft/pallas_call | solution.py:148
  40.0 1.4 %collective-permute-done.7.refs_3_ = bf16[144,512]{1,0:T(8,128)(2,1)S(1)} collective-permute-done((bf16[144,512]{1,0:T(8,128)(2,1)S(1)}, bf16[144,512]{1,0:T(8,128)(2,1)S(1)}, u32[]{:S(2)}, u32[]{:S(2)}) %collective-permute-start.7) | collective-permute-done | bytes 147488 | tf_op jit(solution)/shard_map/ppermute | solution.py:325
  41.4 4.2 %collective-permute-start = (bf16[144,512]{1,0:T(8,128)(2,1)S(1)}, bf16[144,512]{1,0:T(8,128)(2,1)S(1)}, u32[]{:S(2)}, u32[]{:S(2)}) collective-permute-start(bf16[144,512]{1,0:T(8,128)(2,1)S(1)} %get-tuple-element.33), channel_id=1, source_target_pairs={{0,1},{1,2},{2,3},{3,0},{4,5},{5,6},{6,7},{7,4},{8,9},{9,10},{10,1... | collective-permute-start | bytes 442376 | tf_op jit(solution)/shard_map/ppermute | solution.py:325
  45.6 3.4 %collective-permute-start.1 = (bf16[144,512]{1,0:T(8,128)(2,1)S(1)}, bf16[144,512]{1,0:T(8,128)(2,1)S(1)}, u32[]{:S(2)}, u32[]{:S(2)}) collective-permute-start(bf16[144,512]{1,0:T(8,128)(2,1)S(1)} %get-tuple-element.34), channel_id=1, source_target_pairs={{0,2},{1,3},{2,0},{3,1},{4,6},{5,7},{6,4},{7,5},{8,10},{9,11},{10,... | collective-permute-start | bytes 442376 | tf_op jit(solution)/shard_map/ppermute | solution.py:325
  49.0 1.4 %assemble.4 = (f32[2,2,3,32,2048]{4,3,2,1,0:T(8,128)}, f32[192,192]{1,0:T(8,128)S(1)}) custom-call(s32[1]{0:T(128)} %bitcast.refs_0_, bf16[144,512]{1,0:T(8,128)(2,1)S(1)} %get-tuple-element.44.refs_1_, bf16[144,512]{1,0:T(8,128)(2,1)S(1)} %collective-permute-done.9.refs_2_, bf16[144,512]{1,0:T(8,128)(2,1)S(1)} %collective-permute-done.10.refs_3_, ...), custom_call_target="tpu_custom_call" | custom-call | flops 226492416 | bytes 786432 | tf_op jit(solution)/shard_map/assemble/pallas_call | solution.py:240
  50.4 1.4 %assemble.5 = (f32[2,2,3,32,2048]{4,3,2,1,0:T(8,128)}, f32[192,192]{1,0:T(8,128)S(1)}) custom-call(s32[1]{0:T(128)} %bitcast.refs_0_, bf16[144,512]{1,0:T(8,128)(2,1)S(1)} %get-tuple-element.40.refs_1_, bf16[144,512]{1,0:T(8,128)(2,1)S(1)} %collective-permute-done.6.refs_2_, ...), custom_call_target="tpu_custom_call", output_to_operand_aliasing={{0}: (6, {})} | custom-call | flops 226492416 | bytes 786432 | tf_op jit(solution)/shard_map/assemble/pallas_call | solution.py:240
  51.7 2.4 %collective-permute-done.4.refs_3_ = bf16[144,512]{1,0:T(8,128)(2,1)S(1)} collective-permute-done((bf16[144,512]{1,0:T(8,128)(2,1)S(1)}, bf16[144,512]{1,0:T(8,128)(2,1)S(1)}, u32[]{:S(2)}, u32[]{:S(2)}) %collective-permute-start.4) | collective-permute-done | bytes 147488 | tf_op jit(solution)/shard_map/ppermute | solution.py:325
  54.1 1.4 %assemble.6 = (f32[2,2,3,32,2048]{4,3,2,1,0:T(8,128)}, f32[192,192]{1,0:T(8,128)S(1)}) custom-call(s32[1]{0:T(128)} %bitcast.refs_0_, bf16[144,512]{1,0:T(8,128)(2,1)S(1)} %get-tuple-element.36.refs_1_, bf16[144,512]{1,0:T(8,128)(2,1)S(1)} %collective-permute-done.3.refs_2_, ...), custom_call_target="tpu_custom_call", output_to_operand_aliasing={{0}: (6, {})} | custom-call | flops 226492416 | bytes 786432 | tf_op jit(solution)/shard_map/assemble/pallas_call | solution.py:240
  55.4 6.1 %collective-permute-done.1.refs_3_ = bf16[144,512]{1,0:T(8,128)(2,1)S(1)} collective-permute-done((bf16[144,512]{1,0:T(8,128)(2,1)S(1)}, bf16[144,512]{1,0:T(8,128)(2,1)S(1)}, u32[]{:S(2)}, u32[]{:S(2)}) %collective-permute-start.1) | collective-permute-done | bytes 147488 | tf_op jit(solution)/shard_map/ppermute | solution.py:325
  61.5 1.4 %assemble.7 = (f32[2,2,3,32,2048]{4,3,2,1,0:T(8,128)}, f32[64,128]{1,0:T(8,128)S(1)}) custom-call(s32[1]{0:T(128)} %bitcast.refs_0_, bf16[144,512]{1,0:T(8,128)(2,1)S(1)} %get-tuple-element.32.refs_1_, bf16[144,512]{1,0:T(8,128)(2,1)S(1)} %collective-permute-done.refs_2_, ...), custom_call_target="tpu_custom_call", output_to_operand_aliasing={{0}: (6, {})} | custom-call | flops 226492416 | bytes 786432 | tf_op jit(solution)/shard_map/assemble/pallas_call | solution.py:240
  62.9 2.0 %collective-permute-start.18 = (f32[64,128]{1,0:T(8,128)S(1)}, f32[64,128]{1,0:T(8,128)S(1)}, u32[]{:S(2)}, u32[]{:S(2)}) collective-permute-start(f32[64,128]{1,0:T(8,128)S(1)} %get-tuple-element.55.refs_0_), channel_id=1, source_target_pairs={{0,28},{4,0},{8,4},{12,8},{16,12},{20,16},{24,20},{28,24},{1,29},{... | collective-permute-start | bytes 98312 | tf_op jit(solution)/shard_map/ppermute | solution.py:338
  65.7 1.5 %collective-permute-start.15 = (f32[64,128]{1,0:T(8,128)S(1)}, f32[64,128]{1,0:T(8,128)S(1)}, u32[]{:S(2)}, u32[]{:S(2)}) collective-permute-start(f32[64,128]{1,0:T(8,128)S(1)} %get-tuple-element.55.refs_0_), channel_id=1, source_target_pairs={{0,16},{4,20},{8,24},{12,28},{16,0},{20,4},{24,8},{28,12},{1,17},{... | collective-permute-start | bytes 98312 | tf_op jit(solution)/shard_map/ppermute | solution.py:338
  67.4 2.4 %collective-permute-start.13 = (f32[64,128]{1,0:T(8,128)S(1)}, f32[64,128]{1,0:T(8,128)S(1)}, u32[]{:S(2)}, u32[]{:S(2)}) collective-permute-start(f32[64,128]{1,0:T(8,128)S(1)} %get-tuple-element.55.refs_0_), channel_id=1, source_target_pairs={{0,8},{4,12},{8,16},{12,20},{16,24},{20,28},{24,0},{28,4},{1,9},{5... | collective-permute-start | bytes 98312 | tf_op jit(solution)/shard_map/ppermute | solution.py:338
  69.8 0.7 collective-permute-done.14.refs_3_
  70.6 2.4 %collective-permute-done.13.refs_2_ = f32[64,128]{1,0:T(8,128)S(1)} collective-permute-done((f32[64,128]{1,0:T(8,128)S(1)}, f32[64,128]{1,0:T(8,128)S(1)}, u32[]{:S(2)}, u32[]{:S(2)}) %collective-permute-start.13) | collective-permute-done | bytes 32800 | tf_op jit(solution)/shard_map/ppermute | solution.py:338
  73.0 1.1 %collective-permute-done.12.refs_1_ = f32[64,128]{1,0:T(8,128)S(1)} collective-permute-done((f32[64,128]{1,0:T(8,128)S(1)}, f32[64,128]{1,0:T(8,128)S(1)}, u32[]{:S(2)}, u32[]{:S(2)}) %collective-permute-start.12) | collective-permute-done | bytes 32800 | tf_op jit(solution)/shard_map/ppermute | solution.py:338
  74.1 0.6 copy-done.10
  74.7 7.1 %factor.1 = f32[2,64,64]{2,1,0:T(8,128)} custom-call(f32[64,128]{1,0:T(8,128)} %copy-done.1, f32[64,128]{1,0:T(8,128)} %copy-done.10, f32[64,128]{1,0:T(8,128)} %copy-done.9, f32[64,128]{1,0:T(8,128)} %copy-done.8, f32[64,128]{1,0:T(8,128)} %copy-done.7, f32[64,128]{1,0:T(8,128)} %copy-done.6, f32[64,128]{1,0:T(8,128)} %copy-done.5, f32[64,128]{1,0:T(8,128)} %copy-done.4), custom_call_target="tpu_custom_call" | custom-call | tf_op jit(solution)/shard_map/factor/pallas_call | solution.py:291
  (38 shorter events, 1.9 us)
Async XLA Ops:
  1.3 0.7 copy-start
  2.0 0.7 copy-start.2
  2.7 0.7 copy-start.3
  8.2 14.6 %collective-permute-start.9 = (bf16[144,512]{1,0:T(8,128)(2,1)S(1)}, bf16[144,512]{1,0:T(8,128)(2,1)S(1)}, u32[]{:S(2)}, u32[]{:S(2)}) collective-permute-start(bf16[144,512]{1,0:T(8,128)(2,1)S(1)} %get-tuple-element.45), channel_id=1, source_target_pairs={{0,1},{1,2},{2,3},{3,0},{4,5},{5,6},{6,7},{7,4},{8,9},{9,10},{10,1... | collective-permute-start | bytes 442376 | tf_op jit(solution)/shard_map/ppermute | solution.py:325
  11.2 14.4 %collective-permute-start.10 = (bf16[144,512]{1,0:T(8,128)(2,1)S(1)}, bf16[144,512]{1,0:T(8,128)(2,1)S(1)}, u32[]{:S(2)}, u32[]{:S(2)}) collective-permute-start(bf16[144,512]{1,0:T(8,128)(2,1)S(1)} %get-tuple-element.46), channel_id=1, source_target_pairs={{0,2},{1,3},{2,0},{3,1},{4,6},{5,7},{6,4},{7,5},{8,10},{9,11},{10,... | collective-permute-start | bytes 442376 | tf_op jit(solution)/shard_map/ppermute | solution.py:325
  13.8 18.9 %collective-permute-start.11 = (bf16[144,512]{1,0:T(8,128)(2,1)S(1)}, bf16[144,512]{1,0:T(8,128)(2,1)S(1)}, u32[]{:S(2)}, u32[]{:S(2)}) collective-permute-start(bf16[144,512]{1,0:T(8,128)(2,1)S(1)} %get-tuple-element.47), channel_id=1, source_target_pairs={{0,3},{1,0},{2,1},{3,2},{4,7},{5,4},{6,5},{7,6},{8,11},{9,8},{10,9... | collective-permute-start | bytes 442376 | tf_op jit(solution)/shard_map/ppermute | solution.py:325
  18.4 17.9 %collective-permute-start.6 = (bf16[144,512]{1,0:T(8,128)(2,1)S(1)}, bf16[144,512]{1,0:T(8,128)(2,1)S(1)}, u32[]{:S(2)}, u32[]{:S(2)}) collective-permute-start(bf16[144,512]{1,0:T(8,128)(2,1)S(1)} %get-tuple-element.41), channel_id=1, source_target_pairs={{0,1},{1,2},{2,3},{3,0},{4,5},{5,6},{6,7},{7,4},{8,9},{9,10},{10,1... | collective-permute-start | bytes 442376 | tf_op jit(solution)/shard_map/ppermute | solution.py:325
  19.2 22.3 %collective-permute-start.7 = (bf16[144,512]{1,0:T(8,128)(2,1)S(1)}, bf16[144,512]{1,0:T(8,128)(2,1)S(1)}, u32[]{:S(2)}, u32[]{:S(2)}) collective-permute-start(bf16[144,512]{1,0:T(8,128)(2,1)S(1)} %get-tuple-element.42), channel_id=1, source_target_pairs={{0,2},{1,3},{2,0},{3,1},{4,6},{5,7},{6,4},{7,5},{8,10},{9,11},{10,... | collective-permute-start | bytes 442376 | tf_op jit(solution)/shard_map/ppermute | solution.py:325
  22.7 22.9 %collective-permute-start.8 = (bf16[144,512]{1,0:T(8,128)(2,1)S(1)}, bf16[144,512]{1,0:T(8,128)(2,1)S(1)}, u32[]{:S(2)}, u32[]{:S(2)}) collective-permute-start(bf16[144,512]{1,0:T(8,128)(2,1)S(1)} %get-tuple-element.43), channel_id=1, source_target_pairs={{0,3},{1,0},{2,1},{3,2},{4,7},{5,4},{6,5},{7,6},{8,11},{9,8},{10,9... | collective-permute-start | bytes 442376 | tf_op jit(solution)/shard_map/ppermute | solution.py:325
  25.6 23.4 %collective-permute-start.3 = (bf16[144,512]{1,0:T(8,128)(2,1)S(1)}, bf16[144,512]{1,0:T(8,128)(2,1)S(1)}, u32[]{:S(2)}, u32[]{:S(2)}) collective-permute-start(bf16[144,512]{1,0:T(8,128)(2,1)S(1)} %get-tuple-element.37), channel_id=1, source_target_pairs={{0,1},{1,2},{2,3},{3,0},{4,5},{5,6},{6,7},{7,4},{8,9},{9,10},{10,1... | collective-permute-start | bytes 442376 | tf_op jit(solution)/shard_map/ppermute | solution.py:325
  32.8 21.3 %collective-permute-start.4 = (bf16[144,512]{1,0:T(8,128)(2,1)S(1)}, bf16[144,512]{1,0:T(8,128)(2,1)S(1)}, u32[]{:S(2)}, u32[]{:S(2)}) collective-permute-start(bf16[144,512]{1,0:T(8,128)(2,1)S(1)} %get-tuple-element.38), channel_id=1, source_target_pairs={{0,2},{1,3},{2,0},{3,1},{4,6},{5,7},{6,4},{7,5},{8,10},{9,11},{10,... | collective-permute-start | bytes 442376 | tf_op jit(solution)/shard_map/ppermute | solution.py:325
  36.3 17.8 %collective-permute-start.5 = (bf16[144,512]{1,0:T(8,128)(2,1)S(1)}, bf16[144,512]{1,0:T(8,128)(2,1)S(1)}, u32[]{:S(2)}, u32[]{:S(2)}) collective-permute-start(bf16[144,512]{1,0:T(8,128)(2,1)S(1)} %get-tuple-element.39), channel_id=1, source_target_pairs={{0,3},{1,0},{2,1},{3,2},{4,7},{5,4},{6,5},{7,6},{8,11},{9,8},{10,9... | collective-permute-start | bytes 442376 | tf_op jit(solution)/shard_map/ppermute | solution.py:325
  41.4 14.0 %collective-permute-start = (bf16[144,512]{1,0:T(8,128)(2,1)S(1)}, bf16[144,512]{1,0:T(8,128)(2,1)S(1)}, u32[]{:S(2)}, u32[]{:S(2)}) collective-permute-start(bf16[144,512]{1,0:T(8,128)(2,1)S(1)} %get-tuple-element.33), channel_id=1, source_target_pairs={{0,1},{1,2},{2,3},{3,0},{4,5},{5,6},{6,7},{7,4},{8,9},{9,10},{10,1... | collective-permute-start | bytes 442376 | tf_op jit(solution)/shard_map/ppermute | solution.py:325
  45.6 15.9 %collective-permute-start.1 = (bf16[144,512]{1,0:T(8,128)(2,1)S(1)}, bf16[144,512]{1,0:T(8,128)(2,1)S(1)}, u32[]{:S(2)}, u32[]{:S(2)}) collective-permute-start(bf16[144,512]{1,0:T(8,128)(2,1)S(1)} %get-tuple-element.34), channel_id=1, source_target_pairs={{0,2},{1,3},{2,0},{3,1},{4,6},{5,7},{6,4},{7,5},{8,10},{9,11},{10,... | collective-permute-start | bytes 442376 | tf_op jit(solution)/shard_map/ppermute | solution.py:325
  49.0 12.5 %collective-permute-start.2 = (bf16[144,512]{1,0:T(8,128)(2,1)S(1)}, bf16[144,512]{1,0:T(8,128)(2,1)S(1)}, u32[]{:S(2)}, u32[]{:S(2)}) collective-permute-start(bf16[144,512]{1,0:T(8,128)(2,1)S(1)} %get-tuple-element.35), channel_id=1, source_target_pairs={{0,3},{1,0},{2,1},{3,2},{4,7},{5,4},{6,5},{7,6},{8,11},{9,8},{10,9... | collective-permute-start | bytes 442376 | tf_op jit(solution)/shard_map/ppermute | solution.py:325
  62.9 11.1 %copy-start.1 = (f32[64,128]{1,0:T(8,128)}, f32[64,128]{1,0:T(8,128)S(1)}, u32[]{:S(2)}) copy-start(f32[64,128]{1,0:T(8,128)S(1)} %get-tuple-element.55.refs_0_) | copy-start | bytes 98308
  62.9 4.5 %collective-permute-start.18 = (f32[64,128]{1,0:T(8,128)S(1)}, f32[64,128]{1,0:T(8,128)S(1)}, u32[]{:S(2)}, u32[]{:S(2)}) collective-permute-start(f32[64,128]{1,0:T(8,128)S(1)} %get-tuple-element.55.refs_0_), channel_id=1, source_target_pairs={{0,28},{4,0},{8,4},{12,8},{16,12},{20,16},{24,20},{28,24},{1,29},{... | collective-permute-start | bytes 98312 | tf_op jit(solution)/shard_map/ppermute | solution.py:338
  64.9 4.9 %collective-permute-start.17 = (f32[64,128]{1,0:T(8,128)S(1)}, f32[64,128]{1,0:T(8,128)S(1)}, u32[]{:S(2)}, u32[]{:S(2)}) collective-permute-start(f32[64,128]{1,0:T(8,128)S(1)} %get-tuple-element.55.refs_0_), channel_id=1, source_target_pairs={{0,24},{4,28},{8,0},{12,4},{16,8},{20,12},{24,16},{28,20},{1,25},{... | collective-permute-start | bytes 98312 | tf_op jit(solution)/shard_map/ppermute | solution.py:338
  65.4 4.4 %collective-permute-start.16 = (f32[64,128]{1,0:T(8,128)S(1)}, f32[64,128]{1,0:T(8,128)S(1)}, u32[]{:S(2)}, u32[]{:S(2)}) collective-permute-start(f32[64,128]{1,0:T(8,128)S(1)} %get-tuple-element.55.refs_0_), channel_id=1, source_target_pairs={{0,20},{4,24},{8,28},{12,0},{16,4},{20,8},{24,12},{28,16},{1,21},{... | collective-permute-start | bytes 98312 | tf_op jit(solution)/shard_map/ppermute | solution.py:338
  65.7 4.1 %collective-permute-start.15 = (f32[64,128]{1,0:T(8,128)S(1)}, f32[64,128]{1,0:T(8,128)S(1)}, u32[]{:S(2)}, u32[]{:S(2)}) collective-permute-start(f32[64,128]{1,0:T(8,128)S(1)} %get-tuple-element.55.refs_0_), channel_id=1, source_target_pairs={{0,16},{4,20},{8,24},{12,28},{16,0},{20,4},{24,8},{28,12},{1,17},{... | collective-permute-start | bytes 98312 | tf_op jit(solution)/shard_map/ppermute | solution.py:338
  67.2 3.3 %collective-permute-start.14 = (f32[64,128]{1,0:T(8,128)S(1)}, f32[64,128]{1,0:T(8,128)S(1)}, u32[]{:S(2)}, u32[]{:S(2)}) collective-permute-start(f32[64,128]{1,0:T(8,128)S(1)} %get-tuple-element.55.refs_0_), channel_id=1, source_target_pairs={{0,12},{4,16},{8,20},{12,24},{16,28},{20,0},{24,4},{28,8},{1,13},{... | collective-permute-start | bytes 98312 | tf_op jit(solution)/shard_map/ppermute | solution.py:338
  67.4 6.6 %copy-start.4 = (f32[64,128]{1,0:T(8,128)}, f32[64,128]{1,0:T(8,128)S(1)}, u32[]{:S(2)}) copy-start(f32[64,128]{1,0:T(8,128)S(1)} %collective-permute-done.18.refs_7_) | copy-start | bytes 98308
  67.4 5.6 %collective-permute-start.13 = (f32[64,128]{1,0:T(8,128)S(1)}, f32[64,128]{1,0:T(8,128)S(1)}, u32[]{:S(2)}, u32[]{:S(2)}) collective-permute-start(f32[64,128]{1,0:T(8,128)S(1)} %get-tuple-element.55.refs_0_), channel_id=1, source_target_pairs={{0,8},{4,12},{8,16},{12,20},{16,24},{20,28},{24,0},{28,4},{1,9},{5... | collective-permute-start | bytes 98312 | tf_op jit(solution)/shard_map/ppermute | solution.py:338
  69.8 4.2 %copy-start.5 = (f32[64,128]{1,0:T(8,128)}, f32[64,128]{1,0:T(8,128)S(1)}, u32[]{:S(2)}) copy-start(f32[64,128]{1,0:T(8,128)S(1)} %collective-permute-done.17.refs_6_) | copy-start | bytes 98308
  69.8 4.2 %collective-permute-start.12 = (f32[64,128]{1,0:T(8,128)S(1)}, f32[64,128]{1,0:T(8,128)S(1)}, u32[]{:S(2)}, u32[]{:S(2)}) collective-permute-start(f32[64,128]{1,0:T(8,128)S(1)} %get-tuple-element.55.refs_0_), channel_id=1, source_target_pairs={{0,4},{4,8},{8,12},{12,16},{16,20},{20,24},{24,28},{28,0},{1,5},{5... | collective-permute-start | bytes 98312 | tf_op jit(solution)/shard_map/ppermute | solution.py:338
  69.8 4.2 %copy-start.6 = (f32[64,128]{1,0:T(8,128)}, f32[64,128]{1,0:T(8,128)S(1)}, u32[]{:S(2)}) copy-start(f32[64,128]{1,0:T(8,128)S(1)} %collective-permute-done.16.refs_5_) | copy-start | bytes 98308
  69.8 4.2 %copy-start.7 = (f32[64,128]{1,0:T(8,128)}, f32[64,128]{1,0:T(8,128)S(1)}, u32[]{:S(2)}) copy-start(f32[64,128]{1,0:T(8,128)S(1)} %collective-permute-done.15.refs_4_) | copy-start | bytes 98308
  70.6 3.5 %copy-start.8 = (f32[64,128]{1,0:T(8,128)}, f32[64,128]{1,0:T(8,128)S(1)}, u32[]{:S(2)}) copy-start(f32[64,128]{1,0:T(8,128)S(1)} %collective-permute-done.14.refs_3_) | copy-start | bytes 98308
  73.0 1.1 %copy-start.9 = (f32[64,128]{1,0:T(8,128)}, f32[64,128]{1,0:T(8,128)S(1)}, u32[]{:S(2)}) copy-start(f32[64,128]{1,0:T(8,128)S(1)} %collective-permute-done.13.refs_2_) | copy-start | bytes 98308
  74.1 0.6 copy-start.10

commit v2 on v1

--- a/solution.py
+++ b/solution.py
@@ -14,6 +14,7 @@
 HOP = 128
 LANES = 128
 TILE = 256
+PIVOT = 4
 SCALE = (8.0 / (3.0 * NFFT)) ** 0.5
 HIGHEST = lax.Precision.HIGHEST
 
@@ -93,8 +94,8 @@
         @pl.when(pl.program_id(0) == 0)
         def _():
             build_rows(n, owned, slots, span, blocks, pos_ref[0], starts_ref, freqs_ref, a_ref)
-            spread_column(jnp.cos(angle_ref[...]), span, cos_ref)
-            spread_column(jnp.sin(angle_ref[...]), span, sin_ref)
+            spread_column(jnp.cos(angle_ref[...].reshape(1, span)), span, cos_ref)
+            spread_column(jnp.sin(angle_ref[...].reshape(1, span)), span, sin_ref)
     else:
         mask_ref, vel_ref, a_ref, cos_ref, sin_ref = refs[:5]
         outs = refs[5:5 + n]
@@ -139,7 +140,7 @@
     out_specs = [pl.BlockSpec((COMPS * rows, TILE), lambda i: (0, i))] * n
     if first:
         args = (position, starts, freqs, angles, mask, velocity)
-        in_specs = [smem] * 3 + [whole((1, span))] + data_specs
+        in_specs = [smem] * 3 + [whole((span,))] + data_specs
         out_types = out_types + shared_types
         out_specs = out_specs + shared_specs
     else:
@@ -152,7 +153,7 @@
         in_specs=in_specs,
         out_specs=out_specs,
         scratch_shapes=[pltpu.VMEM((2, span, TILE), jnp.bfloat16)],
-        compiler_params=pltpu.CompilerParams(vmem_limit_bytes=40 * 2**20),
+        compiler_params=pltpu.CompilerParams(vmem_limit_bytes=(60 if first else 40) * 2**20),
         cost_estimate=pl.CostEstimate(
             flops=2 * n * rows * span * COMPS * points,
             bytes_accessed=2 * COMPS * span * points,
@@ -217,19 +218,21 @@
             gram = lax.dot_general(
                 half, sel, (((1,), (1,)), ((), ())), precision=HIGHEST, preferred_element_type=jnp.float32
             ) * (1.0 / total)
-            gram_ref[...] = jnp.concatenate(
+            gram = jnp.concatenate(
                 [gram[j * order:(j + 1) * order, j * order:(j + 1) * order] for j in range(owned)], axis=1
             )
-
-
-def assemble_call(n, owned, slots, span, blocks, total, offset, points, all_points, position, parts, spectra, gram, last):
+            for at in range(0, gram_ref.shape[0], order):
+                gram_ref[at:at + order, :] = gram
+
+
+def assemble_call(n, owned, slots, span, blocks, total, offset, points, all_points, position, parts, spectra, gram, last, copies):
     rows = slots * owned * 2
     tile = min(points, 512)
     shift = offset // tile
     order = 2 * blocks
     has_sum = gram is not None
     whole = lambda shape: pl.BlockSpec(shape, lambda i: (0,) * len(shape))
-    gram_shape = (order, owned * order) if last else (n * rows, n * rows)
+    gram_shape = (copies * order, owned * order) if last else (n * rows, n * rows)
     args = [position] + list(parts)
     in_specs = [pl.BlockSpec(memory_space=pltpu.SMEM)] + [pl.BlockSpec((COMPS * rows, tile), lambda i: (0, i))] * n
     aliases = {}
@@ -268,21 +271,30 @@
     parts = refs[:count]
     out_ref, row_ref = refs[count:]
     s = parts[0][...]
-    for p in parts[1:]:
-        s = s + p[...]
+    if len(s.shape) == 3:
+        s = sum(s[i] for i in range(s.shape[0]))
     lane = lax.broadcasted_iota(jnp.int32, (1, owned * order), 1)
-    for k in range(order):
+    for k in range(0, order, PIVOT):
         base = k // 8 * 8
-        s = s[base - (k - 1) // 8 * 8:] if k else s
-        column = jnp.broadcast_to(s[:, k:k + 1], s.shape)
-        for j in range(1, owned):
-            column = jnp.where(lane >= j * order, s[:, j * order + k:j * order + k + 1], column)
+        s = s[base - max(k - PIVOT, 0) // 8 * 8:]
+        columns = []
+        for i in range(k, k + PIVOT):
+            column = jnp.broadcast_to(s[:, i:i + 1], s.shape)
+            for j in range(1, owned):
+                column = jnp.where(lane >= j * order, s[:, j * order + i:j * order + i + 1], column)
+            columns.append(column)
         at = k - base
-        pivot = column[at:at + 1]
-        inverse_root = lax.rsqrt(pivot)
-        row = s[at:at + 1] * inverse_root
-        row_ref[k:k + 1, :] = jnp.where(lane % order >= k, row, 0.0)
-        s = s - column * (row * inverse_root)
+        rows = [s[at + i:at + i + 1] for i in range(PIVOT)]
+        for i in range(PIVOT):
+            inverse_root = lax.rsqrt(columns[i][at + i:at + i + 1])
+            columns[i] = columns[i] * inverse_root
+            rows[i] = rows[i] * inverse_root
+            for j in range(i + 1, PIVOT):
+                weight = columns[i][at + j:at + j + 1]
+                columns[j] = columns[j] - columns[i] * weight
+                rows[j] = rows[j] - rows[i] * weight
+            row_ref[k + i:k + i + 1, :] = jnp.where(lane % order >= k + i, rows[i], 0.0)
+            s = s - columns[i] * rows[i]
     for j in range(owned):
         out_ref[j] = row_ref[:, j * order:(j + 1) * order]
 
@@ -312,7 +324,7 @@
     position = lax.axis_index("tm").astype(jnp.int32).reshape(1)
     samples = velocity.transpose(1, 0, 2)
     mask = rotor_mask.reshape(1, points)
-    angles = rotor_angle.reshape(1, span)
+    angles = rotor_angle
 
     pieces = []
     shared = None
@@ -331,15 +343,13 @@
     for at, count, moved in pieces:
         last = at + count == points
         spectra, gram = assemble_call(
-            n, owned, slots, span, blocks, total, at, count, points, position, moved, spectra, gram, last
+            n, owned, slots, span, blocks, total, at, count, points, position, moved, spectra, gram, last, groups if groups <= 8 else 1
         )
     if groups <= 8:
-        grams = [gram] + [
-            lax.ppermute(gram, "space", [(i, (i + k) % groups) for i in range(groups)]) for k in range(1, groups)
-        ]
+        gram = lax.all_to_all(gram, "space", 0, 0, tiled=True).reshape(groups, order, owned * order)
     else:
-        grams = [lax.psum(gram, "space")]
-    factors = factor_call(owned, order, grams)
+        gram = lax.psum(gram, "space")
+    factors = factor_call(owned, order, [gram])
     return spectra.transpose(0, 1, 3, 2, 4), factors
 
 

time: 82.8 us -> 76.4 us (0.923)
  starting transfers between devices: 36.6 us -> 25.8 us
  blocking collectives: 0 us -> 10.5 us
  Pallas kernels: 27.1 us -> 24.2 us
  waiting for transfers between devices: 14 us -> 11.1 us
    all_to_all x0 -> x1, blocking collectives: none -> 10.5 us  [per_device(): lax.all_to_all(gram, 'space', 0, 0, tiled=True)]
    ppermute x7 -> x0, starting transfers between devices: 6.87 us -> none  [per_device(): lax.ppermute(gram, 'space', [(i, (i + k) % groups) for i in range(groups)])]
    ppermute x7 -> x0, waiting for transfers between devices: 4.2 us -> none  [per_device(): lax.ppermute(gram, 'space', [(i, (i + k) % groups) for i in range(groups)])]
    ppermute x12, starting transfers between devices: 29.7 us -> 25.8 us  [per_device(): lax.ppermute(sums[k], 'tm', [(i, (i + k) % n) for i in range(n)])]
    pallas_call x1, Pallas kernels: 7.09 us -> 3.91 us  [factor_call(): pl.pallas_call(functools.partial(factor_body, owned, order, len(parts)),...]
    ppermute x12, waiting for transfers between devices: 9.85 us -> 11.1 us  [per_device(): lax.ppermute(sums[k], 'tm', [(i, (i + k) % n) for i in range(n)])]
    unnamed x22 -> x10, local copies, waits for them, and re-layouts: 2.63 us -> 3.12 us
  transfers between devices with their start and end apart: 19 -> 12, of which waited for: 6 -> 3; matrix products, arithmetic and copies ran while one was open for 0% -> 0% of each run, Pallas kernels for 17% -> 18%
where the time goes in v2:
time: 76.4 us; the launch traced here: 75.5 us
  starting transfers between devices  25.8 us (34%)
  Pallas kernels  24.2 us (32%)
  waiting for transfers between devices  11.1 us (15%)
  blocking collectives  10.5 us (14%)
  local copies, waits for them, and re-layouts  3.12 us (4%)
    ppermute x12, starting transfers between devices, per_device(): lax.ppermute(sums[k], 'tm', [(i, (i + k) % n) for i in range(n)])  25.8 us
    pallas_call x4, Pallas kernels, dft_call(): pl.pallas_call(functools.partial(dft_body, n, owned, slots, span, blocks,...  14.8 us
    ppermute x12, waiting for transfers between devices, per_device(): lax.ppermute(sums[k], 'tm', [(i, (i + k) % n) for i in range(n)])  11.1 us
    all_to_all x1, blocking collectives, per_device(): lax.all_to_all(gram, 'space', 0, 0, tiled=True)  10.5 us
    pallas_call x4, Pallas kernels, assemble_call(): pl.pallas_call(functools.partial(assemble_body, n, owned, slots, span, bl...  5.46 us
    pallas_call x1, Pallas kernels, factor_call(): pl.pallas_call(functools.partial(factor_body, owned, order, len(parts)),...  3.91 us
    unnamed x10, local copies, waits for them, and re-layouts  3.12 us
  transfers between devices with their start and end apart: 12, of which 3 were waited for; matrix products, arithmetic and copies ran while one was open for 0% of the time, Pallas kernels for 18%

profile of v2, /device:TPU:0, one launch (start us, length us, event | category | flops | bytes accessed | tf_op | source)
XLA Modules:
  0.0 75.5 jit_solution(93131901764888536)
XLA Ops:
  0.6 5.4 %rotate_dft.4 = (bf16[144,512]{1,0:T(8,128)(2,1)}, bf16[144,512]{1,0:T(8,128)(2,1)}, bf16[144,512]{1,0:T(8,128)(2,1)}, bf16[144,512]{1,0:T(8,128)(2,1)}, bf16[4,...) custom-call(s32[1]{0:T(128)} %bitcast.refs_0_, s32[32]{0:T(128)} %refs_1_.1, s32[8]{0:T(128)} %refs_2_.1, ...), custom_call_target="tpu_custom_call" | custom-call | flops 632291328 | bytes 3293184 | tf_op jit(solution)/shard_map/rotate_dft/pallas_call | solution.py:149
  6.1 3.1 %collective-permute-start.9 = (bf16[144,512]{1,0:T(8,128)(2,1)}, bf16[144,512]{1,0:T(8,128)(2,1)S(1)}, u32[]{:S(2)}, u32[]{:S(2)}) collective-permute-start(bf16[144,512]{1,0:T(8,128)(2,1)} %get-tuple-element.45), channel_id=1, source_target_pairs={{0,1},{1,2},{2,3},{3,0},{4,5},{5,6},{6,7},{7,4},{8,9},{9,10},{10,1... | collective-permute-start | bytes 442376 | tf_op jit(solution)/shard_map/ppermute | solution.py:337
  9.1 2.6 %collective-permute-start.10 = (bf16[144,512]{1,0:T(8,128)(2,1)}, bf16[144,512]{1,0:T(8,128)(2,1)S(1)}, u32[]{:S(2)}, u32[]{:S(2)}) collective-permute-start(bf16[144,512]{1,0:T(8,128)(2,1)} %get-tuple-element.46), channel_id=1, source_target_pairs={{0,2},{1,3},{2,0},{3,1},{4,6},{5,7},{6,4},{7,5},{8,10},{9,11},{10,... | collective-permute-start | bytes 442376 | tf_op jit(solution)/shard_map/ppermute | solution.py:337
  11.7 1.3 %collective-permute-start.11 = (bf16[144,512]{1,0:T(8,128)(2,1)}, bf16[144,512]{1,0:T(8,128)(2,1)S(1)}, u32[]{:S(2)}, u32[]{:S(2)}) collective-permute-start(bf16[144,512]{1,0:T(8,128)(2,1)} %get-tuple-element.47), channel_id=1, source_target_pairs={{0,3},{1,0},{2,1},{3,2},{4,7},{5,4},{6,5},{7,6},{8,11},{9,8},{10,9... | collective-permute-start | bytes 442376 | tf_op jit(solution)/shard_map/ppermute | solution.py:337
  13.1 1.0 %copy-done = f32[1072,128]{1,0:T(8,128)S(1)} copy-done((f32[1072,128]{1,0:T(8,128)S(1)}, f32[1072,128]{1,0:T(8,128)}, u32[]{:S(2)}) %copy-start) | copy-done | bytes 548888
  14.1 1.0 %copy-done.1 = f32[1072,128]{1,0:T(8,128)S(1)} copy-done((f32[1072,128]{1,0:T(8,128)S(1)}, f32[1072,128]{1,0:T(8,128)}, u32[]{:S(2)}) %copy-start.1) | copy-done | bytes 548888
  15.2 1.0 %copy-done.2 = bf16[4,48,1072]{2,1,0:T(8,128)(2,1)S(1)} copy-done((bf16[4,48,1072]{2,1,0:T(8,128)(2,1)S(1)}, bf16[4,48,1072]{2,1,0:T(8,128)(2,1)}, u32[]{:S(2)}) %copy-start.2) | copy-done | bytes 411672
  16.2 3.1 %rotate_dft.7 = (bf16[144,512]{1,0:T(8,128)(2,1)S(1)}, bf16[144,512]{1,0:T(8,128)(2,1)S(1)}, bf16[144,512]{1,0:T(8,128)(2,1)S(1)}, bf16[144,512]{1,0:T(8,128)(2,1)S(1)}) custom-call(s32[1,2048]{1,0:T(1,128)S(1)} %bitcast.7, bf16[3,1072,2048]{2,1,0:T(8,128)(2,1)} %bitcast.11, bf16[4,48,1072]{2,1,0:T(8,128)(2,1)S(1)} %copy-done.2, f32[1072,128]{1,0:T(8,128)S(1)} %copy-done, ...), custom_call_target="tpu_custom_call" | custom-call | flops 632291328 | bytes 3293184 | tf_op jit(solution)/shard_map/rotate_dft/pallas_call | solution.py:149
  19.3 0.7 collective-permute-start.6
  20.1 0.3 collective-permute-start.7
  20.4 3.1 %rotate_dft.6 = (bf16[144,512]{1,0:T(8,128)(2,1)S(1)}, bf16[144,512]{1,0:T(8,128)(2,1)S(1)}, bf16[144,512]{1,0:T(8,128)(2,1)S(1)}, bf16[144,512]{1,0:T(8,128)(2,1)S(1)}) custom-call(s32[1,2048]{1,0:T(1,128)S(1)} %bitcast.8, bf16[3,1072,2048]{2,1,0:T(8,128)(2,1)} %bitcast.12, bf16[4,48,1072]{2,1,0:T(8,128)(2,1)S(1)} %copy-done.2, f32[1072,128]{1,0:T(8,128)S(1)} %copy-done, ...), custom_call_target="tpu_custom_call" | custom-call | flops 632291328 | bytes 3293184 | tf_op jit(solution)/shard_map/rotate_dft/pallas_call | solution.py:149
  23.5 2.9 %collective-permute-start.8 = (bf16[144,512]{1,0:T(8,128)(2,1)S(1)}, bf16[144,512]{1,0:T(8,128)(2,1)S(1)}, u32[]{:S(2)}, u32[]{:S(2)}) collective-permute-start(bf16[144,512]{1,0:T(8,128)(2,1)S(1)} %get-tuple-element.43), channel_id=1, source_target_pairs={{0,3},{1,0},{2,1},{3,2},{4,7},{5,4},{6,5},{7,6},{8,11},{9,8},{10,9... | collective-permute-start | bytes 442376 | tf_op jit(solution)/shard_map/ppermute | solution.py:337
  26.4 0.0 collective-permute-done.10.refs_3_
  26.4 3.2 %collective-permute-start.3 = (bf16[144,512]{1,0:T(8,128)(2,1)S(1)}, bf16[144,512]{1,0:T(8,128)(2,1)S(1)}, u32[]{:S(2)}, u32[]{:S(2)}) collective-permute-start(bf16[144,512]{1,0:T(8,128)(2,1)S(1)} %get-tuple-element.37), channel_id=1, source_target_pairs={{0,1},{1,2},{2,3},{3,0},{4,5},{5,6},{6,7},{7,4},{8,9},{9,10},{10,1... | collective-permute-start | bytes 442376 | tf_op jit(solution)/shard_map/ppermute | solution.py:337
  29.6 3.8 %collective-permute-start.4 = (bf16[144,512]{1,0:T(8,128)(2,1)S(1)}, bf16[144,512]{1,0:T(8,128)(2,1)S(1)}, u32[]{:S(2)}, u32[]{:S(2)}) collective-permute-start(bf16[144,512]{1,0:T(8,128)(2,1)S(1)} %get-tuple-element.38), channel_id=1, source_target_pairs={{0,2},{1,3},{2,0},{3,1},{4,6},{5,7},{6,4},{7,5},{8,10},{9,11},{10,... | collective-permute-start | bytes 442376 | tf_op jit(solution)/shard_map/ppermute | solution.py:337
  33.3 1.5 %collective-permute-start.5 = (bf16[144,512]{1,0:T(8,128)(2,1)S(1)}, bf16[144,512]{1,0:T(8,128)(2,1)S(1)}, u32[]{:S(2)}, u32[]{:S(2)}) collective-permute-start(bf16[144,512]{1,0:T(8,128)(2,1)S(1)} %get-tuple-element.39), channel_id=1, source_target_pairs={{0,3},{1,0},{2,1},{3,2},{4,7},{5,4},{6,5},{7,6},{8,11},{9,8},{10,9... | collective-permute-start | bytes 442376 | tf_op jit(solution)/shard_map/ppermute | solution.py:337
  34.9 3.1 %rotate_dft.5 = (bf16[144,512]{1,0:T(8,128)(2,1)S(1)}, bf16[144,512]{1,0:T(8,128)(2,1)S(1)}, bf16[144,512]{1,0:T(8,128)(2,1)S(1)}, bf16[144,512]{1,0:T(8,128)(2,1)S(1)}) custom-call(s32[1,2048]{1,0:T(1,128)S(1)} %bitcast.9, bf16[3,1072,2048]{2,1,0:T(8,128)(2,1)} %bitcast.13, bf16[4,48,1072]{2,1,0:T(8,128)(2,1)S(1)} %copy-done.2, f32[1072,128]{1,0:T(8,128)S(1)} %copy-done, ...), custom_call_target="tpu_custom_call" | custom-call | flops 632291328 | bytes 3293184 | tf_op jit(solution)/shard_map/rotate_dft/pallas_call | solution.py:149
  38.0 2.6 %collective-permute-done.7.refs_3_ = bf16[144,512]{1,0:T(8,128)(2,1)S(1)} collective-permute-done((bf16[144,512]{1,0:T(8,128)(2,1)S(1)}, bf16[144,512]{1,0:T(8,128)(2,1)S(1)}, u32[]{:S(2)}, u32[]{:S(2)}) %collective-permute-start.7) | collective-permute-done | bytes 147488 | tf_op jit(solution)/shard_map/ppermute | solution.py:337
  40.7 3.1 %collective-permute-start = (bf16[144,512]{1,0:T(8,128)(2,1)S(1)}, bf16[144,512]{1,0:T(8,128)(2,1)S(1)}, u32[]{:S(2)}, u32[]{:S(2)}) collective-permute-start(bf16[144,512]{1,0:T(8,128)(2,1)S(1)} %get-tuple-element.33), channel_id=1, source_target_pairs={{0,1},{1,2},{2,3},{3,0},{4,5},{5,6},{6,7},{7,4},{8,9},{9,10},{10,1... | collective-permute-start | bytes 442376 | tf_op jit(solution)/shard_map/ppermute | solution.py:337
  43.7 0.0 collective-permute-done.8.refs_4_
  43.7 3.4 %collective-permute-start.1 = (bf16[144,512]{1,0:T(8,128)(2,1)S(1)}, bf16[144,512]{1,0:T(8,128)(2,1)S(1)}, u32[]{:S(2)}, u32[]{:S(2)}) collective-permute-start(bf16[144,512]{1,0:T(8,128)(2,1)S(1)} %get-tuple-element.34), channel_id=1, source_target_pairs={{0,2},{1,3},{2,0},{3,1},{4,6},{5,7},{6,4},{7,5},{8,10},{9,11},{10,... | collective-permute-start | bytes 442376 | tf_op jit(solution)/shard_map/ppermute | solution.py:337
  47.1 0.0 collective-permute-done.3.refs_2_
  47.1 0.0 collective-permute-start.2
  47.1 1.4 %assemble.4 = (f32[2,2,3,32,2048]{4,3,2,1,0:T(8,128)}, f32[192,192]{1,0:T(8,128)S(1)}) custom-call(s32[1]{0:T(128)} %bitcast.refs_0_, bf16[144,512]{1,0:T(8,128)(2,1)S(1)} %copy-done.4, bf16[144,512]{1,0:T(8,128)(2,1)S(1)} %collective-permute-done.9.refs_2_, bf16[144,512]{1,0:T(8,128)(2,1)S(1)} %collective-permute-done.10.refs_3_, ...), custom_call_target="tpu_custom_call" | custom-call | flops 226492416 | bytes 786432 | tf_op jit(solution)/shard_map/assemble/pallas_call | solution.py:243
  48.5 1.3 %assemble.5 = (f32[2,2,3,32,2048]{4,3,2,1,0:T(8,128)}, f32[192,192]{1,0:T(8,128)S(1)}) custom-call(s32[1]{0:T(128)} %bitcast.refs_0_, bf16[144,512]{1,0:T(8,128)(2,1)S(1)} %get-tuple-element.40.refs_1_, bf16[144,512]{1,0:T(8,128)(2,1)S(1)} %collective-permute-done.6.refs_2_, ...), custom_call_target="tpu_custom_call", output_to_operand_aliasing={{0}: (6, {})} | custom-call | flops 226492416 | bytes 786432 | tf_op jit(solution)/shard_map/assemble/pallas_call | solution.py:243
  49.8 2.4 %collective-permute-done.4.refs_3_ = bf16[144,512]{1,0:T(8,128)(2,1)S(1)} collective-permute-done((bf16[144,512]{1,0:T(8,128)(2,1)S(1)}, bf16[144,512]{1,0:T(8,128)(2,1)S(1)}, u32[]{:S(2)}, u32[]{:S(2)}) %collective-permute-start.4) | collective-permute-done | bytes 147488 | tf_op jit(solution)/shard_map/ppermute | solution.py:337
  52.2 0.0 collective-permute-done.5.refs_4_
  52.2 1.4 %assemble.6 = (f32[2,2,3,32,2048]{4,3,2,1,0:T(8,128)}, f32[192,192]{1,0:T(8,128)S(1)}) custom-call(s32[1]{0:T(128)} %bitcast.refs_0_, bf16[144,512]{1,0:T(8,128)(2,1)S(1)} %get-tuple-element.36.refs_1_, bf16[144,512]{1,0:T(8,128)(2,1)S(1)} %collective-permute-done.3.refs_2_, ...), custom_call_target="tpu_custom_call", output_to_operand_aliasing={{0}: (6, {})} | custom-call | flops 226492416 | bytes 786432 | tf_op jit(solution)/shard_map/assemble/pallas_call | solution.py:243
  53.6 6.0 %collective-permute-done.1.refs_3_ = bf16[144,512]{1,0:T(8,128)(2,1)S(1)} collective-permute-done((bf16[144,512]{1,0:T(8,128)(2,1)S(1)}, bf16[144,512]{1,0:T(8,128)(2,1)S(1)}, u32[]{:S(2)}, u32[]{:S(2)}) %collective-permute-start.1) | collective-permute-done | bytes 147488 | tf_op jit(solution)/shard_map/ppermute | solution.py:337
  59.6 1.4 %assemble.7 = (f32[2,2,3,32,2048]{4,3,2,1,0:T(8,128)}, f32[512,128]{1,0:T(8,128)S(1)}) custom-call(s32[1]{0:T(128)} %bitcast.refs_0_, bf16[144,512]{1,0:T(8,128)(2,1)S(1)} %get-tuple-element.32.refs_1_, bf16[144,512]{1,0:T(8,128)(2,1)S(1)} %collective-permute-done.refs_2_, ...), custom_call_target="tpu_custom_call", output_to_operand_aliasing={{0}: (6, {})} | custom-call | flops 226492416 | bytes 786432 | tf_op jit(solution)/shard_map/assemble/pallas_call | solution.py:243
  61.0 10.5 %all_to_all.9.refs_0_ = f32[8,64,128]{2,1,0:T(8,128)} all-to-all(f32[8,64,128]{2,1,0:T(8,128)S(1)} %bitcast.5), channel_id=1, replica_groups=mesh['space'=8,'tm'=4] {'space'}, dimensions={0} | all-to-all | bytes 524288 | tf_op jit(solution)/shard_map/all_to_all | solution.py:349
  71.6 3.9 %factor.1 = f32[2,64,64]{2,1,0:T(8,128)} custom-call(f32[8,64,128]{2,1,0:T(8,128)} %all_to_all.9.refs_0_), custom_call_target="tpu_custom_call" | custom-call | tf_op jit(solution)/shard_map/factor/pallas_call | solution.py:303
  (12 shorter events, 0.0 us)
Async XLA Ops:
  0.6 12.5 %copy-start.3 = (s32[2048]{0:T(1024)S(1)}, s32[2048]{0:T(1024)}, u32[]{:S(2)}) copy-start(s32[2048]{0:T(1024)} %param.6) | copy-start | bytes 24580
  6.1 17.4 %collective-permute-start.9 = (bf16[144,512]{1,0:T(8,128)(2,1)}, bf16[144,512]{1,0:T(8,128)(2,1)S(1)}, u32[]{:S(2)}, u32[]{:S(2)}) collective-permute-start(bf16[144,512]{1,0:T(8,128)(2,1)} %get-tuple-element.45), channel_id=1, source_target_pairs={{0,1},{1,2},{2,3},{3,0},{4,5},{5,6},{6,7},{7,4},{8,9},{9,10},{10,1... | collective-permute-start | bytes 442376 | tf_op jit(solution)/shard_map/ppermute | solution.py:337
  9.1 17.3 %collective-permute-start.10 = (bf16[144,512]{1,0:T(8,128)(2,1)}, bf16[144,512]{1,0:T(8,128)(2,1)S(1)}, u32[]{:S(2)}, u32[]{:S(2)}) collective-permute-start(bf16[144,512]{1,0:T(8,128)(2,1)} %get-tuple-element.46), channel_id=1, source_target_pairs={{0,2},{1,3},{2,0},{3,1},{4,6},{5,7},{6,4},{7,5},{8,10},{9,11},{10,... | collective-permute-start | bytes 442376 | tf_op jit(solution)/shard_map/ppermute | solution.py:337
  11.7 17.8 %collective-permute-start.11 = (bf16[144,512]{1,0:T(8,128)(2,1)}, bf16[144,512]{1,0:T(8,128)(2,1)S(1)}, u32[]{:S(2)}, u32[]{:S(2)}) collective-permute-start(bf16[144,512]{1,0:T(8,128)(2,1)} %get-tuple-element.47), channel_id=1, source_target_pairs={{0,3},{1,0},{2,1},{3,2},{4,7},{5,4},{6,5},{7,6},{8,11},{9,8},{10,9... | collective-permute-start | bytes 442376 | tf_op jit(solution)/shard_map/ppermute | solution.py:337
  13.1 1.1 %copy-start = (f32[1072,128]{1,0:T(8,128)S(1)}, f32[1072,128]{1,0:T(8,128)}, u32[]{:S(2)}) copy-start(f32[1072,128]{1,0:T(8,128)} %get-tuple-element.30.refs_3_) | copy-start | bytes 1646596
  14.1 1.1 %copy-start.1 = (f32[1072,128]{1,0:T(8,128)S(1)}, f32[1072,128]{1,0:T(8,128)}, u32[]{:S(2)}) copy-start(f32[1072,128]{1,0:T(8,128)} %get-tuple-element.31.refs_4_) | copy-start | bytes 1646596
  15.2 1.0 %copy-start.2 = (bf16[4,48,1072]{2,1,0:T(8,128)(2,1)S(1)}, bf16[4,48,1072]{2,1,0:T(8,128)(2,1)}, u32[]{:S(2)}) copy-start(bf16[4,48,1072]{2,1,0:T(8,128)(2,1)} %get-tuple-element.29.refs_2_) | copy-start | bytes 1234948
  19.3 14.0 %collective-permute-start.6 = (bf16[144,512]{1,0:T(8,128)(2,1)S(1)}, bf16[144,512]{1,0:T(8,128)(2,1)S(1)}, u32[]{:S(2)}, u32[]{:S(2)}) collective-permute-start(bf16[144,512]{1,0:T(8,128)(2,1)S(1)} %get-tuple-element.41), channel_id=1, source_target_pairs={{0,1},{1,2},{2,3},{3,0},{4,5},{5,6},{6,7},{7,4},{8,9},{9,10},{10,1... | collective-permute-start | bytes 442376 | tf_op jit(solution)/shard_map/ppermute | solution.py:337
  20.1 20.6 %collective-permute-start.7 = (bf16[144,512]{1,0:T(8,128)(2,1)S(1)}, bf16[144,512]{1,0:T(8,128)(2,1)S(1)}, u32[]{:S(2)}, u32[]{:S(2)}) collective-permute-start(bf16[144,512]{1,0:T(8,128)(2,1)S(1)} %get-tuple-element.42), channel_id=1, source_target_pairs={{0,2},{1,3},{2,0},{3,1},{4,6},{5,7},{6,4},{7,5},{8,10},{9,11},{10,... | collective-permute-start | bytes 442376 | tf_op jit(solution)/shard_map/ppermute | solution.py:337
  23.5 20.2 %collective-permute-start.8 = (bf16[144,512]{1,0:T(8,128)(2,1)S(1)}, bf16[144,512]{1,0:T(8,128)(2,1)S(1)}, u32[]{:S(2)}, u32[]{:S(2)}) collective-permute-start(bf16[144,512]{1,0:T(8,128)(2,1)S(1)} %get-tuple-element.43), channel_id=1, source_target_pairs={{0,3},{1,0},{2,1},{3,2},{4,7},{5,4},{6,5},{7,6},{8,11},{9,8},{10,9... | collective-permute-start | bytes 442376 | tf_op jit(solution)/shard_map/ppermute | solution.py:337
  26.4 20.7 %collective-permute-start.3 = (bf16[144,512]{1,0:T(8,128)(2,1)S(1)}, bf16[144,512]{1,0:T(8,128)(2,1)S(1)}, u32[]{:S(2)}, u32[]{:S(2)}) collective-permute-start(bf16[144,512]{1,0:T(8,128)(2,1)S(1)} %get-tuple-element.37), channel_id=1, source_target_pairs={{0,1},{1,2},{2,3},{3,0},{4,5},{5,6},{6,7},{7,4},{8,9},{9,10},{10,1... | collective-permute-start | bytes 442376 | tf_op jit(solution)/shard_map/ppermute | solution.py:337
  29.6 22.7 %collective-permute-start.4 = (bf16[144,512]{1,0:T(8,128)(2,1)S(1)}, bf16[144,512]{1,0:T(8,128)(2,1)S(1)}, u32[]{:S(2)}, u32[]{:S(2)}) collective-permute-start(bf16[144,512]{1,0:T(8,128)(2,1)S(1)} %get-tuple-element.38), channel_id=1, source_target_pairs={{0,2},{1,3},{2,0},{3,1},{4,6},{5,7},{6,4},{7,5},{8,10},{9,11},{10,... | collective-permute-start | bytes 442376 | tf_op jit(solution)/shard_map/ppermute | solution.py:337
  33.3 13.8 %copy-start.4 = (bf16[144,512]{1,0:T(8,128)(2,1)S(1)}, bf16[144,512]{1,0:T(8,128)(2,1)}, u32[]{:S(2)}) copy-start(bf16[144,512]{1,0:T(8,128)(2,1)} %get-tuple-element.44.refs_1_) | copy-start | bytes 442372
  33.3 18.9 %collective-permute-start.5 = (bf16[144,512]{1,0:T(8,128)(2,1)S(1)}, bf16[144,512]{1,0:T(8,128)(2,1)S(1)}, u32[]{:S(2)}, u32[]{:S(2)}) collective-permute-start(bf16[144,512]{1,0:T(8,128)(2,1)S(1)} %get-tuple-element.39), channel_id=1, source_target_pairs={{0,3},{1,0},{2,1},{3,2},{4,7},{5,4},{6,5},{7,6},{8,11},{9,8},{10,9... | collective-permute-start | bytes 442376 | tf_op jit(solution)/shard_map/ppermute | solution.py:337
  40.7 12.9 %collective-permute-start = (bf16[144,512]{1,0:T(8,128)(2,1)S(1)}, bf16[144,512]{1,0:T(8,128)(2,1)S(1)}, u32[]{:S(2)}, u32[]{:S(2)}) collective-permute-start(bf16[144,512]{1,0:T(8,128)(2,1)S(1)} %get-tuple-element.33), channel_id=1, source_target_pairs={{0,1},{1,2},{2,3},{3,0},{4,5},{5,6},{6,7},{7,4},{8,9},{9,10},{10,1... | collective-permute-start | bytes 442376 | tf_op jit(solution)/shard_map/ppermute | solution.py:337
  43.7 15.9 %collective-permute-start.1 = (bf16[144,512]{1,0:T(8,128)(2,1)S(1)}, bf16[144,512]{1,0:T(8,128)(2,1)S(1)}, u32[]{:S(2)}, u32[]{:S(2)}) collective-permute-start(bf16[144,512]{1,0:T(8,128)(2,1)S(1)} %get-tuple-element.34), channel_id=1, source_target_pairs={{0,2},{1,3},{2,0},{3,1},{4,6},{5,7},{6,4},{7,5},{8,10},{9,11},{10,... | collective-permute-start | bytes 442376 | tf_op jit(solution)/shard_map/ppermute | solution.py:337
  47.1 12.5 %collective-permute-start.2 = (bf16[144,512]{1,0:T(8,128)(2,1)S(1)}, bf16[144,512]{1,0:T(8,128)(2,1)S(1)}, u32[]{:S(2)}, u32[]{:S(2)}) collective-permute-start(bf16[144,512]{1,0:T(8,128)(2,1)S(1)} %get-tuple-element.35), channel_id=1, source_target_pairs={{0,3},{1,0},{2,1},{3,2},{4,7},{5,4},{6,5},{7,6},{8,11},{9,8},{10,9... | collective-permute-start | bytes 442376 | tf_op jit(solution)/shard_map/ppermute | solution.py:337

commit v3 on v2

--- a/solution.py
+++ b/solution.py
@@ -17,6 +17,7 @@
 PIVOT = 4
 SCALE = (8.0 / (3.0 * NFFT)) ** 0.5
 HIGHEST = lax.Precision.HIGHEST
+SHORT = pl.CostEstimate(flops=1000, bytes_accessed=1000, transcendentals=0)
 
 
 def first_block(shard, span):
@@ -153,7 +154,7 @@
         in_specs=in_specs,
         out_specs=out_specs,
         scratch_shapes=[pltpu.VMEM((2, span, TILE), jnp.bfloat16)],
-        compiler_params=pltpu.CompilerParams(vmem_limit_bytes=(60 if first else 40) * 2**20),
+        compiler_params=pltpu.CompilerParams(vmem_limit_bytes=40 * 2**20),
         cost_estimate=pl.CostEstimate(
             flops=2 * n * rows * span * COMPS * points,
             bytes_accessed=2 * COMPS * span * points,
@@ -218,21 +219,19 @@
             gram = lax.dot_general(
                 half, sel, (((1,), (1,)), ((), ())), precision=HIGHEST, preferred_element_type=jnp.float32
             ) * (1.0 / total)
-            gram = jnp.concatenate(
+            gram_ref[...] = jnp.concatenate(
                 [gram[j * order:(j + 1) * order, j * order:(j + 1) * order] for j in range(owned)], axis=1
             )
-            for at in range(0, gram_ref.shape[0], order):
-                gram_ref[at:at + order, :] = gram
-
-
-def assemble_call(n, owned, slots, span, blocks, total, offset, points, all_points, position, parts, spectra, gram, last, copies):
+
+
+def assemble_call(n, owned, slots, span, blocks, total, offset, points, all_points, position, parts, spectra, gram, last):
     rows = slots * owned * 2
     tile = min(points, 512)
     shift = offset // tile
     order = 2 * blocks
     has_sum = gram is not None
     whole = lambda shape: pl.BlockSpec(shape, lambda i: (0,) * len(shape))
-    gram_shape = (copies * order, owned * order) if last else (n * rows, n * rows)
+    gram_shape = (order, owned * order) if last else (n * rows, n * rows)
     args = [position] + list(parts)
     in_specs = [pl.BlockSpec(memory_space=pltpu.SMEM)] + [pl.BlockSpec((COMPS * rows, tile), lambda i: (0, i))] * n
     aliases = {}
@@ -270,9 +269,10 @@
 def factor_body(owned, order, count, *refs):
     parts = refs[:count]
     out_ref, row_ref = refs[count:]
-    s = parts[0][...]
-    if len(s.shape) == 3:
-        s = sum(s[i] for i in range(s.shape[0]))
+    s = [p[...] for p in parts]
+    while len(s) > 1:
+        s = [a + b for a, b in zip(s[::2], s[1::2])]
+    s = s[0]
     lane = lax.broadcasted_iota(jnp.int32, (1, owned * order), 1)
     for k in range(0, order, PIVOT):
         base = k // 8 * 8
@@ -308,9 +308,374 @@
     )(*parts)
 
 
+LINE_LO = [0, 6, 15, 23]
+LINE_HI = [8, 16, 25, 31]
+WIDE = 12
+FAR = 9
+SHARED = 2
+
+
+def pick(values, me):
+    out = jnp.int32(values[0])
+    for i in range(1, len(values)):
+        out = jnp.where(me == i, jnp.int32(values[i]), out)
+    return out
+
+
+def far_block(shard, slot):
+    return pick([0, 8, 23, 31], shard) + pick([1, 1, -1, -1], shard) * slot
+
+
+def cosine_of(turns):
+    s = half_turn_sine(turns - jnp.floor(turns + 0.5))
+    return 1.0 - 2.0 * s * s
+
+
+def build_line(span, blocks, me, starts_ref, freqs_ref, direct_ref, a_ref, rows_ref):
+    lo = pick(LINE_LO, me)
+    starts = [starts_ref[jnp.minimum(lo + s, blocks - 1)] for s in range(WIDE)]
+
+    def by_slot(shape, axis):
+        at = lax.broadcasted_iota(jnp.int32, shape, axis)
+        out = jnp.full(shape, starts[0], jnp.int32)
+        for s in range(1, WIDE):
+            out = jnp.where(at == s, starts[s], out)
+        return out
+
+    rid = lax.broadcasted_iota(jnp.int32, (16, 1), 0)
+    f_of = ((rid // 4) ^ me) * 2 + (rid // 2) % 2
+    freq = jnp.zeros((16, 1), jnp.float32)
+    for f in range(8):
+        freq = jnp.where(f_of == f, freqs_ref[f].astype(jnp.float32), freq)
+    step = freq * (1.0 / NFFT)
+    quarter = (rid % 2).astype(jnp.float32) * 0.25
+
+    sample = lax.broadcasted_iota(jnp.int32, (1, span), 1) + me * span
+    turns = sample.astype(jnp.float32) * step
+    turns = turns - jnp.floor(turns) + quarter
+    cos_t, sin_t = cosine_of(turns), cosine_of(turns - 0.25)
+    begin = by_slot((1, LANES), 1).astype(jnp.float32) * step
+    begin = begin - jnp.floor(begin)
+    cos_b, sin_b = cosine_of(begin), cosine_of(begin - 0.25)
+
+    slot = lax.broadcasted_iota(jnp.int32, (16, 1), 0)
+    ni = sample - by_slot((16, 1), 0)
+    nf = ni.astype(jnp.float32)
+    w = half_turn_sine(jnp.minimum(nf, NFFT - nf) * (1.0 / NFFT))
+    w = jnp.where((ni >= 0) & (ni < NFFT) & (slot + lo < blocks), w * w * SCALE, 0.0)
+
+    own, near, direct2, direct3 = [], [], [], []
+    for s in range(WIDE):
+        rows = (cos_t * cos_b[:, s:s + 1] + sin_t * sin_b[:, s:s + 1]) * w[s:s + 1]
+        rows_ref[s] = rows[8:]
+        own.append(rows[:4])
+        near.append(rows[4:8])
+        direct2.append(rows[8:12])
+        direct3.append(rows[12:])
+    direct_ref[...] = jnp.concatenate(own + near + direct2 + direct3, axis=0).astype(jnp.bfloat16)
+    far = [rows_ref[far_block(me, s) - lo] for s in range(FAR)]
+    inner = ((me == 1) | (me == 2)).astype(jnp.float32)
+    shared = [rows_ref[pick([0, s, 10 - s, 0], me)] * inner for s in range(SHARED)]
+    pieces = own + near
+    pieces += [r[4:] for r in shared] + [r[:4] for r in shared]
+    pieces += [r[:4] for r in far[:-1]] + [r[4:] for r in far[:-1]]
+    pieces += [far[-1], jnp.zeros((8, span), jnp.float32)]
+    a_ref[...] = jnp.concatenate(pieces, axis=0).astype(jnp.bfloat16)
+
+
+def line_dft_body(span, blocks, first, *refs):
+    if first:
+        pos_ref, starts_ref, freqs_ref, angle_ref, mask_ref, vel_ref = refs[:6]
+        out_refs = refs[6:10]
+        shared_refs = refs[10:13]
+        rot_ref, a_ref, rows_ref = refs[13:]
+        _, cos_ref, sin_ref = shared_refs
+
+        @pl.when(pl.program_id(0) == 0)
+        def _():
+            build_line(span, blocks, pos_ref[0], starts_ref, freqs_ref, a_ref, shared_refs[0], rows_ref)
+            spread_column(jnp.cos(angle_ref[...].reshape(1, span)), span, cos_ref)
+            spread_column(jnp.sin(angle_ref[...].reshape(1, span)), span, sin_ref)
+    else:
+        mask_ref, vel_ref, a_ref, cos_ref, sin_ref = refs[:5]
+        own_ref, near_ref, shared_ref, far2_ref, far3_ref, rot_ref = refs[6:]
+    width = vel_ref.shape[2]
+    turning = mask_ref[...] == 1
+    for at in range(0, span, 16):
+        rows = min(16, span - at)
+        here = pl.ds(at, rows)
+        cosine = jnp.concatenate([cos_ref[here, :]] * (width // LANES), axis=1)
+        sine = jnp.concatenate([sin_ref[here, :]] * (width // LANES), axis=1)
+        x = vel_ref[0, here, :].astype(jnp.float32)
+        y = vel_ref[1, here, :].astype(jnp.float32)
+        rot_ref[0, here, :] = jnp.where(turning, cosine * x - sine * y, x).astype(jnp.bfloat16)
+        rot_ref[1, here, :] = jnp.where(turning, sine * x + cosine * y, y).astype(jnp.bfloat16)
+    tails = []
+    for c in range(COMPS):
+        samples = rot_ref[c] if c < 2 else vel_ref[2]
+        sums = jnp.dot(a_ref[...], samples, preferred_element_type=jnp.float32)
+        if first:
+            for k, ref in enumerate(out_refs):
+                ref[48 * c:48 * c + 48, :] = sums[48 * k:48 * k + 48].astype(jnp.bfloat16)
+            continue
+        own_ref[48 * c:48 * c + 48, :] = sums[:48].astype(jnp.bfloat16)
+        near_ref[48 * c:48 * c + 48, :] = sums[48:96].astype(jnp.bfloat16)
+        shared_ref[16 * c:16 * c + 16, :] = sums[96:112].astype(jnp.bfloat16)
+        far2_ref[32 * c:32 * c + 32, :] = sums[112:144].astype(jnp.bfloat16)
+        far3_ref[32 * c:32 * c + 32, :] = sums[144:176].astype(jnp.bfloat16)
+        tails.append(sums[176:184])
+    if not first:
+        none = jnp.zeros((4, width), jnp.float32)
+        far2_ref[96:112, :] = jnp.concatenate([t[:4] for t in tails] + [none], axis=0).astype(jnp.bfloat16)
+        far3_ref[96:112, :] = jnp.concatenate([t[4:] for t in tails] + [none], axis=0).astype(jnp.bfloat16)
+
+
+def line_dft(blocks, offset, points, position, starts, freqs, angles, mask, velocity, shared, after):
+    first = shared is None
+    span = velocity.shape[1]
+    shift = offset // TILE
+    whole = lambda shape: pl.BlockSpec(shape, lambda i: (0,) * len(shape))
+    smem = pl.BlockSpec(memory_space=pltpu.SMEM)
+    data_specs = [
+        pl.BlockSpec((1, TILE), lambda i: (0, i + shift)),
+        pl.BlockSpec((COMPS, span, TILE), lambda i: (0, 0, i + shift)),
+    ]
+    shared_types = [
+        jax.ShapeDtypeStruct((192, span), jnp.bfloat16),
+        jax.ShapeDtypeStruct((span, LANES), jnp.float32),
+        jax.ShapeDtypeStruct((span, LANES), jnp.float32),
+    ]
+    shared_specs = [whole(t.shape) for t in shared_types]
+    heights = [144] * 4 if first else [144, 144, 48, 112, 112]
+    out_types = [jax.ShapeDtypeStruct((h, points), jnp.bfloat16) for h in heights]
+    out_specs = [pl.BlockSpec((h, TILE), lambda i: (0, i)) for h in heights]
+    scratch = [pltpu.VMEM((2, span, TILE), jnp.bfloat16)]
+    if first:
+        args = (position, starts, freqs, angles, mask, velocity)
+        in_specs = [smem] * 3 + [whole((span,))] + data_specs
+        out_types = out_types + shared_types
+        out_specs = out_specs + shared_specs
+        scratch += [pltpu.VMEM((192, span), jnp.bfloat16), pltpu.VMEM((WIDE, 8, span), jnp.float32)]
+    else:
+        args = (mask, velocity) + tuple(shared) + (after,)
+        in_specs = data_specs + shared_specs + [pl.BlockSpec(memory_space=pl.ANY)]
+    out = pl.pallas_call(
+        functools.partial(line_dft_body, span, blocks, first),
+        grid=(points // TILE,),
+        out_shape=out_types,
+        in_specs=in_specs,
+        out_specs=out_specs,
+        scratch_shapes=scratch,
+        compiler_params=pltpu.CompilerParams(vmem_limit_bytes=(60 if first else 40) * 2**20),
+        cost_estimate=SHORT,
+        name="rotate_dft",
+    )(*args)
+    return (out[:4], out[4:]) if first else (out, shared)
+
+
+def combine_body(far2_ref, far3_ref, shared_ref, near_ref, out2_ref, out3_ref, near_out_ref):
+    for c in range(COMPS):
+        here = slice(32 * c, 32 * c + 32)
+        add = shared_ref[16 * c:16 * c + 16, :].astype(jnp.float32)
+        none = jnp.zeros((24, add.shape[1]), jnp.float32)
+        for src, dst, part in ((far2_ref, out2_ref, add[:8]), (far3_ref, out3_ref, add[8:])):
+            dst[here, :] = (src[here, :].astype(jnp.float32) + jnp.concatenate([none, part], axis=0)).astype(jnp.bfloat16)
+    near_out_ref[...] = near_ref[...]
+    out2_ref[96:112, :] = far2_ref[96:112, :]
+    out3_ref[96:112, :] = far3_ref[96:112, :]
+
+
+def combine(far2, far3, shared, near):
+    return pl.pallas_call(
+        combine_body,
+        out_shape=[jax.ShapeDtypeStruct(x.shape, x.dtype) for x in (far2, far3, near)],
+        compiler_params=pltpu.CompilerParams(vmem_limit_bytes=40 * 2**20),
+        cost_estimate=pl.CostEstimate(flops=far2.size, bytes_accessed=8 * far2.size, transcendentals=0),
+        name="add_shared",
+    )(far2, far3, shared, near)
+
+
+def line_selection(blocks, me, direct, sel_ref):
+    shape = (4 * blocks, 192)
+    out = lax.broadcasted_iota(jnp.int32, shape, 0)
+    col = lax.broadcasted_iota(jnp.int32, shape, 1)
+    two, three = me ^ 2, me ^ 3
+    block = jnp.where(col < 48, pick(LINE_LO, me) + col // 4, pick(LINE_LO, me ^ 1) + (col - 48) // 4)
+    if direct:
+        block = jnp.where(col >= 96, pick(LINE_LO, two) + (col - 96) // 4, block)
+        block = jnp.where(col >= 144, pick(LINE_LO, three) + (col - 144) // 4, block)
+    else:
+        block = jnp.where(col >= 96, far_block(two, (col - 96) // 4), block)
+        block = jnp.where(col >= 128, far_block(three, (col - 128) // 4), block)
+        block = jnp.where(col >= 160, far_block(two, FAR - 1), block)
+        block = jnp.where(col >= 176, far_block(three, FAR - 1), block)
+    same = (out // blocks == col % 4) & (out % blocks == block)
+    for c in range(COMPS):
+        mine = same if direct else same & ((col < 160) | ((col % 16) // 4 == c))
+        sel_ref[c] = jnp.where(mine, 1.0, 0.0).astype(jnp.bfloat16)
+
+
+def line_assemble_body(blocks, total, has_sum, last, direct, *refs):
+    pos_ref, own_ref, near_ref, far2_ref, far3_ref = refs[:5]
+    rest = refs[5:]
+    if has_sum:
+        sum_in, rest = rest[0], rest[2:]
+    spectra_ref, gram_ref, sel_ref, acc_ref = rest
+    step = pl.program_id(0)
+    me = pos_ref[0]
+
+    @pl.when(step == 0)
+    def _():
+        line_selection(blocks, me, direct, sel_ref)
+        acc_ref[...] = sum_in[...] if has_sum else jnp.zeros_like(acc_ref)
+
+    for c in range(COMPS):
+        wide = slice(48 * c, 48 * c + 48)
+        parts = [own_ref[wide, :], near_ref[wide, :]]
+        if direct:
+            parts += [far2_ref[wide, :], far3_ref[wide, :]]
+        else:
+            here = slice(32 * c, 32 * c + 32)
+            parts += [far2_ref[here, :], far3_ref[here, :], far2_ref[96:112, :], far3_ref[96:112, :]]
+        stack = jnp.concatenate(parts, axis=0)
+        full = jnp.dot(sel_ref[c], stack, preferred_element_type=jnp.float32)
+        for jr in range(4):
+            spectra_ref[jr // 2, jr % 2, c] = full[jr * blocks:(jr + 1) * blocks]
+        high = full.astype(jnp.bfloat16)
+        low = (full - high.astype(jnp.float32)).astype(jnp.bfloat16)
+        pair = jnp.concatenate([high, low], axis=0)
+        acc_ref[...] += lax.dot_general(
+            pair, pair, (((1,), (1,)), ((), ())), preferred_element_type=jnp.float32
+        )
+
+    @pl.when(step == pl.num_programs(0) - 1)
+    def _():
+        if not last:
+            gram_ref[...] = acc_ref[...]
+        else:
+            n = 4 * blocks
+            order = 2 * blocks
+            acc = acc_ref[...]
+            gram = (acc[:n, :n] + (acc[:n, n:] + acc[n:, :n])) * (1.0 / total)
+            gram_ref[...] = jnp.concatenate([gram[:order, :order], gram[order:, order:]], axis=1)
+
+
+def line_assemble(blocks, total, offset, points, all_points, position, own, near, fars, spectra, gram, last):
+    shift = offset // TILE
+    order = 2 * blocks
+    has_sum = gram is not None
+    whole = lambda shape: pl.BlockSpec(shape, lambda i: (0,) * len(shape))
+    gram_shape = (order, 2 * order) if last else (4 * order, 4 * order)
+    args = [position, own, near] + list(fars)
+    in_specs = [pl.BlockSpec(memory_space=pltpu.SMEM)]
+    in_specs += [pl.BlockSpec((a.shape[0], TILE), lambda i: (0, i)) for a in args[1:]]
+    aliases = {}
+    if has_sum:
+        args += [gram, spectra]
+        in_specs += [whole((4 * order, 4 * order)), pl.BlockSpec(memory_space=pl.ANY)]
+        aliases = {len(args) - 1: 0}
+    return pl.pallas_call(
+        functools.partial(line_assemble_body, blocks, total, has_sum, last, fars[0].shape[0] == 144),
+        grid=(points // TILE,),
+        out_shape=[
+            jax.ShapeDtypeStruct((2, 2, COMPS, blocks, all_points), jnp.float32),
+            jax.ShapeDtypeStruct(gram_shape, jnp.float32),
+        ],
+        in_specs=in_specs,
+        out_specs=[
+            pl.BlockSpec((2, 2, COMPS, blocks, TILE), lambda i: (0, 0, 0, 0, i + shift)),
+            whole(gram_shape),
+        ],
+        scratch_shapes=[
+            pltpu.VMEM((COMPS, 4 * blocks, 192), jnp.bfloat16),
+            pltpu.VMEM((4 * order, 4 * order), jnp.float32),
+        ],
+        input_output_aliases=aliases,
+        compiler_params=pltpu.CompilerParams(vmem_limit_bytes=40 * 2**20),
+        cost_estimate=SHORT,
+        name="assemble",
+    )(*args)
+
+
+def line_chunks(points):
+    cuts = [0, points // 4, points * 5 // 8, points]
+    return [(a, b - a) for a, b in zip(cuts[:-1], cuts[1:])]
+
+
+def line_spectra(samples, mask, angles, block_starts, frequencies, position, total):
+    points = samples.shape[2]
+    blocks = block_starts.shape[0]
+    move = lambda x, pairs: lax.ppermute(x, "tm", pairs)
+    across = lambda x, k: move(x, [(i, i ^ k) for i in range(4)])
+    chunks = line_chunks(points)
+    spectra, gram, shared, sent = None, None, None, []
+
+    def assemble():
+        at, count, own, near, fars = sent.pop(0)
+        return line_assemble(
+            blocks, total, at, count, points, position, own, near, fars, spectra, gram, at + count == points
+        )
+
+    for i, (at, count) in enumerate(chunks):
+        if i >= 2:
+            spectra, gram = assemble()
+        after = gram if i >= 2 else mask
+        sums, shared = line_dft(
+            blocks, at, count, position, block_starts, frequencies, angles, mask, samples, shared, after
+        )
+        if i == 0:
+            own, near, far2, far3 = sums
+        else:
+            own, near, part, far2, far3 = sums
+            far2, far3, near = combine(far2, far3, move(part, [(1, 0), (2, 3)]), near)
+        sent.append((at, count, own, across(near, 1), [across(far2, 2), across(far3, 3)]))
+    while sent:
+        spectra, gram = assemble()
+    return spectra, gram
+
+
+def fits_line(n, span, blocks, owned):
+    if n != 4 or owned != 2:
+        return False
+    lo = [max((s * span - (NFFT + JIT - 1) + HOP) // HOP, 0) for s in range(n)]
+    hi = [min((span * (s + 1) - 1) // HOP, blocks - 1) for s in range(n)]
+    return lo == LINE_LO and hi == LINE_HI and blocks == 32
+
+
+def sum_over_space(gram, groups):
+    if groups != 8:
+        return [lax.psum(gram, "space")]
+    swap = lambda x, k: lax.ppermute(x, "space", [(i, i ^ k) for i in range(groups)])
+    gram = gram + swap(gram, 1)
+    return [gram] + [swap(gram, k) for k in (2, 4, 6)]
+
+
 def chunks_of(points):
     tile = 512
     return [(at, tile) for at in range(0, points, tile)]
+
+
+def ring_spectra(n, owned, slots, blocks, total, position, block_starts, frequencies, angles, mask, samples):
+    span, points = samples.shape[1:]
+    pieces = []
+    shared = None
+    for at, count in chunks_of(points):
+        sums, shared = dft_call(
+            n, owned, slots, blocks, shared is None, at, count,
+            position, block_starts, frequencies, angles, mask, samples, shared,
+        )
+        moved = [sums[0]] + [
+            lax.ppermute(sums[k], "tm", [(i, (i + k) % n) for i in range(n)]) for k in range(1, n)
+        ]
+        pieces.append((at, count, moved))
+
+    spectra, gram = None, None
+    for at, count, moved in pieces:
+        last = at + count == points
+        spectra, gram = assemble_call(
+            n, owned, slots, span, blocks, total, at, count, points, position, moved, spectra, gram, last
+        )
+    return spectra, gram
 
 
 def per_device(velocity, rotor_mask, rotor_angle, block_starts, frequencies):
@@ -326,30 +691,14 @@
     mask = rotor_mask.reshape(1, points)
     angles = rotor_angle
 
-    pieces = []
-    shared = None
-    for at, count in chunks_of(points):
-        sums, shared = dft_call(
-            n, owned, slots, blocks, shared is None, at, count,
-            position, block_starts, frequencies, angles, mask, samples, shared,
+    total = COMPS * points * groups
+    if fits_line(n, span, blocks, owned):
+        spectra, gram = line_spectra(samples, mask, angles, block_starts, frequencies, position, total)
+    else:
+        spectra, gram = ring_spectra(
+            n, owned, slots, blocks, total, position, block_starts, frequencies, angles, mask, samples
         )
-        moved = [sums[0]] + [
-            lax.ppermute(sums[k], "tm", [(i, (i + k) % n) for i in range(n)]) for k in range(1, n)
-        ]
-        pieces.append((at, count, moved))
-
-    spectra, gram = None, None
-    total = COMPS * points * groups
-    for at, count, moved in pieces:
-        last = at + count == points
-        spectra, gram = assemble_call(
-            n, owned, slots, span, blocks, total, at, count, points, position, moved, spectra, gram, last, groups if groups <= 8 else 1
-        )
-    if groups <= 8:
-        gram = lax.all_to_all(gram, "space", 0, 0, tiled=True).reshape(groups, order, owned * order)
-    else:
-        gram = lax.psum(gram, "space")
-    factors = factor_call(owned, order, [gram])
+    factors = factor_call(owned, order, sum_over_space(gram, groups))
     return spectra.transpose(0, 1, 3, 2, 4), factors
 
 

time: 76.4 us -> 77.5 us (1.014)
  waiting for transfers between devices: 11.1 us -> 25.6 us
  blocking collectives: 10.5 us -> 0 us
  starting transfers between devices: 25.8 us -> 22 us
  Pallas kernels: 24.2 us -> 25 us
    ppermute x12 -> x15, waiting for transfers between devices: 11.1 us -> 25.6 us  [the longest x11 20.1 us: line_spectra(): move = lambda x, pairs: lax.ppermute(x, 'tm', pairs)]
    all_to_all x1 -> x0, blocking collectives: 10.5 us -> none  [per_device(): lax.all_to_all(gram, 'space', 0, 0, tiled=True)]
    ppermute x12 -> x15, starting transfers between devices: 25.8 us -> 22 us  [the longest x11 18.4 us: line_spectra(): move = lambda x, pairs: lax.ppermute(x, 'tm', pairs)]
    pallas_call x8, Pallas kernels: 20.2 us -> 21.2 us  [the longest x3 14 us: line_dft(): pl.pallas_call(functools.partial(line_dft_body, span, blocks, first), gri...]
    unnamed x10 -> x24, local copies, waits for them, and re-layouts: 3.12 us -> 3.74 us
  transfers between devices with their start and end apart: 12 -> 15, of which waited for: 3 -> 8; matrix products, arithmetic and copies ran while one was open for 0% -> 0% of each run, Pallas kernels for 18% -> 18%
where the time goes in v3:
time: 77.5 us; the launch traced here: 77 us
  waiting for transfers between devices  25.6 us (33%)
  Pallas kernels  25 us (32%)
  starting transfers between devices  22 us (28%)
  local copies, waits for them, and re-layouts  3.74 us (5%)
    ppermute x11, waiting for transfers between devices, line_spectra(): move = lambda x, pairs: lax.ppermute(x, 'tm', pairs)  20.1 us
    ppermute x11, starting transfers between devices, line_spectra(): move = lambda x, pairs: lax.ppermute(x, 'tm', pairs)  18.4 us
    pallas_call x3, Pallas kernels, line_dft(): pl.pallas_call(functools.partial(line_dft_body, span, blocks, first), gri...  14 us
    pallas_call x3, Pallas kernels, line_assemble(): pl.pallas_call(functools.partial(line_assemble_body, blocks, total, has_s...  7.1 us
    ppermute x4, waiting for transfers between devices, sum_over_space(): lax.ppermute(x, 'space', [(i, i ^ k) for i in range(groups)])  5.54 us
    pallas_call x1, Pallas kernels, factor_call(): pl.pallas_call(functools.partial(factor_body, owned, order, len(parts)),...  3.76 us
    unnamed x24, local copies, waits for them, and re-layouts  3.74 us
    ppermute x4, starting transfers between devices, sum_over_space(): lax.ppermute(x, 'space', [(i, i ^ k) for i in range(groups)])  3.56 us
  transfers between devices with their start and end apart: 15, of which 8 were waited for; matrix products, arithmetic and copies ran while one was open for 0% of the time, Pallas kernels for 18%

profile of v3, /device:TPU:0, one launch (start us, length us, event | category | flops | bytes accessed | tf_op | source)
XLA Modules:
  0.0 77.0 jit_solution(11098395821985123052)
XLA Ops:
  0.6 4.8 %rotate_dft.3 = (bf16[144,512]{1,0:T(8,128)(2,1)}, bf16[144,512]{1,0:T(8,128)(2,1)}, bf16[144,512]{1,0:T(8,128)(2,1)}, bf16[144,512]{1,0:T(8,128)(2,1)}, bf16[19...) custom-call(s32[1]{0:T(128)} %bitcast.refs_0_, s32[32]{0:T(128)} %refs_1_.1, s32[8]{0:T(128)} %refs_2_.1, ...), custom_call_target="tpu_custom_call" | custom-call | flops 1000 | bytes 1000 | tf_op jit(solution)/shard_map/rotate_dft/pallas_call | solution.py:462
  5.4 3.1 %collective-permute-start = (bf16[144,512]{1,0:T(8,128)(2,1)}, bf16[144,512]{1,0:T(8,128)(2,1)S(1)}, u32[]{:S(2)}, u32[]{:S(2)}) collective-permute-start(bf16[144,512]{1,0:T(8,128)(2,1)} %get-tuple-element.35), channel_id=1, source_target_pairs={{0,1},{1,0},{2,3},{3,2},{4,5},{5,4},{6,7},{7,6},{8,9},{9,8},{10,11... | collective-permute-start | bytes 442376 | tf_op jit(solution)/shard_map/ppermute | solution.py:608
  8.5 2.6 %collective-permute-start.1 = (bf16[144,512]{1,0:T(8,128)(2,1)}, bf16[144,512]{1,0:T(8,128)(2,1)S(1)}, u32[]{:S(2)}, u32[]{:S(2)}) collective-permute-start(bf16[144,512]{1,0:T(8,128)(2,1)} %get-tuple-element.36), channel_id=1, source_target_pairs={{0,2},{1,3},{2,0},{3,1},{4,6},{5,7},{6,4},{7,5},{8,10},{9,11},{10,... | collective-permute-start | bytes 442376 | tf_op jit(solution)/shard_map/ppermute | solution.py:608
  11.1 1.0 %copy-done = f32[1072,128]{1,0:T(8,128)S(1)} copy-done((f32[1072,128]{1,0:T(8,128)S(1)}, f32[1072,128]{1,0:T(8,128)}, u32[]{:S(2)}) %copy-start) | copy-done | bytes 548888
  12.1 1.0 %copy-done.2 = f32[1072,128]{1,0:T(8,128)S(1)} copy-done((f32[1072,128]{1,0:T(8,128)S(1)}, f32[1072,128]{1,0:T(8,128)}, u32[]{:S(2)}) %copy-start.2) | copy-done | bytes 548888
  13.2 1.0 %copy-done.4 = bf16[192,1072]{1,0:T(8,128)(2,1)S(1)} copy-done((bf16[192,1072]{1,0:T(8,128)(2,1)S(1)}, bf16[192,1072]{1,0:T(8,128)(2,1)}, u32[]{:S(2)}) %copy-start.4) | copy-done | bytes 411672
  14.2 4.7 %rotate_dft.5 = (bf16[144,768]{1,0:T(8,128)(2,1)S(1)}, bf16[144,768]{1,0:T(8,128)(2,1)S(1)}, bf16[48,768]{1,0:T(8,128)(2,1)S(1)}, bf16[112,768]{1,0:T(8,128)(2,1)S(1)}, bf16[112,768]{1,0:T(8,128)(2,1)S(1)}) custom-call(s32[1,2048]{1,0:T(1,128)S(1)} %bitcast.5, bf16[3,1072,2048]{2,1,0:T(8,128)(2,1)} %bitcast.9, bf16[192,1072]{1,0:T(8,128)(2,1)S(1)} %copy-done.4, ...), custom_call_target="tpu_custom_call" | custom-call | flops 1000 | bytes 1000 | tf_op jit(solution)/shard_map/rotate_dft/pallas_call | solution.py:462
  18.9 1.3 %collective-permute-start.7 = (bf16[48,768]{1,0:T(8,128)(2,1)S(1)}, bf16[48,768]{1,0:T(8,128)(2,1)S(1)}, u32[]{:S(2)}, u32[]{:S(2)}) collective-permute-start(bf16[48,768]{1,0:T(8,128)(2,1)S(1)} %get-tuple-element.50), channel_id=1, source_target_pairs={{1,0},{2,3},{5,4},{6,7},{9,8},{10,11},{13,12},{14,15},{17,16},{18,... | collective-permute-start | bytes 221192 | tf_op jit(solution)/shard_map/ppermute | solution.py:608
  20.2 4.9 %collective-permute-done.7.shared_ref = bf16[48,768]{1,0:T(8,128)(2,1)S(1)} collective-permute-done((bf16[48,768]{1,0:T(8,128)(2,1)S(1)}, bf16[48,768]{1,0:T(8,128)(2,1)S(1)}, u32[]{:S(2)}, u32[]{:S(2)}) %collective-permute-start.7) | collective-permute-done | bytes 73760 | tf_op jit(solution)/shard_map/ppermute | solution.py:608
  25.2 2.1 %collective-permute-start.9 = (bf16[112,768]{1,0:T(8,128)(2,1)S(1)}, bf16[112,768]{1,0:T(8,128)(2,1)S(1)}, u32[]{:S(2)}, u32[]{:S(2)}) collective-permute-start(bf16[112,768]{1,0:T(8,128)(2,1)S(1)} %get-tuple-element.53), channel_id=1, source_target_pairs={{0,2},{1,3},{2,0},{3,1},{4,6},{5,7},{6,4},{7,5},{8,10},{9,11},{10,... | collective-permute-start | bytes 516104 | tf_op jit(solution)/shard_map/ppermute | solution.py:608
  27.3 1.9 %assemble.3 = (f32[2,2,3,32,2048]{4,3,2,1,0:T(8,128)}, f32[256,256]{1,0:T(8,128)S(1)}) custom-call(s32[1]{0:T(128)} %bitcast.refs_0_, bf16[144,512]{1,0:T(8,128)(2,1)S(1)} %copy-done.6, bf16[144,512]{1,0:T(8,128)(2,1)S(1)} %collective-permute-done.refs_2_, bf16[144,512]{1,0:T(8,128)(2,1)S(1)} %collective-permute-done.1.refs_3_, ...), custom_call_target="tpu_custom_call" | custom-call | flops 1000 | bytes 1000 | tf_op jit(solution)/shard_map/assemble/pallas_call | solution.py:577
  29.2 4.5 %rotate_dft.4 = (bf16[144,768]{1,0:T(8,128)(2,1)S(1)}, bf16[144,768]{1,0:T(8,128)(2,1)S(1)}, bf16[48,768]{1,0:T(8,128)(2,1)S(1)}, bf16[112,768]{1,0:T(8,128)(2,1)S(1)}, bf16[112,768]{1,0:T(8,128)(2,1)S(1)}) custom-call(s32[1,2048]{1,0:T(1,128)S(1)} %bitcast.7, bf16[3,1072,2048]{2,1,0:T(8,128)(2,1)} %bitcast.10, bf16[192,1072]{1,0:T(8,128)(2,1)S(1)} %copy-done.5, ...), custom_call_target="tpu_custom_call" | custom-call | flops 1000 | bytes 1000 | tf_op jit(solution)/shard_map/rotate_dft/pallas_call | solution.py:462
  33.7 1.3 %collective-permute-start.3 = (bf16[48,768]{1,0:T(8,128)(2,1)S(1)}, bf16[48,768]{1,0:T(8,128)(2,1)S(1)}, u32[]{:S(2)}, u32[]{:S(2)}) collective-permute-start(bf16[48,768]{1,0:T(8,128)(2,1)S(1)} %get-tuple-element.42), channel_id=1, source_target_pairs={{1,0},{2,3},{5,4},{6,7},{9,8},{10,11},{13,12},{14,15},{17,16},{18,... | collective-permute-start | bytes 221192 | tf_op jit(solution)/shard_map/ppermute | solution.py:608
  35.0 2.7 %collective-permute-start.8 = (bf16[144,768]{1,0:T(8,128)(2,1)S(1)}, bf16[144,768]{1,0:T(8,128)(2,1)S(1)}, u32[]{:S(2)}, u32[]{:S(2)}) collective-permute-start(bf16[144,768]{1,0:T(8,128)(2,1)S(1)} %get-tuple-element.52), channel_id=1, source_target_pairs={{0,1},{1,0},{2,3},{3,2},{4,5},{5,4},{6,7},{7,6},{8,9},{9,8},{10,11... | collective-permute-start | bytes 663560 | tf_op jit(solution)/shard_map/ppermute | solution.py:608
  37.7 2.9 %collective-permute-done.3.shared_ref = bf16[48,768]{1,0:T(8,128)(2,1)S(1)} collective-permute-done((bf16[48,768]{1,0:T(8,128)(2,1)S(1)}, bf16[48,768]{1,0:T(8,128)(2,1)S(1)}, u32[]{:S(2)}, u32[]{:S(2)}) %collective-permute-start.3) | collective-permute-done | bytes 73760 | tf_op jit(solution)/shard_map/ppermute | solution.py:608
  40.7 0.1 collective-permute-start.4
  40.8 1.9 %collective-permute-start.10 = (bf16[112,768]{1,0:T(8,128)(2,1)S(1)}, bf16[112,768]{1,0:T(8,128)(2,1)S(1)}, u32[]{:S(2)}, u32[]{:S(2)}) collective-permute-start(bf16[112,768]{1,0:T(8,128)(2,1)S(1)} %get-tuple-element.54), channel_id=1, source_target_pairs={{0,3},{1,2},{2,1},{3,0},{4,7},{5,6},{6,5},{7,4},{8,11},{9,10},{10,... | collective-permute-start | bytes 516104 | tf_op jit(solution)/shard_map/ppermute | solution.py:608
  42.7 1.6 %collective-permute-start.5 = (bf16[112,768]{1,0:T(8,128)(2,1)S(1)}, bf16[112,768]{1,0:T(8,128)(2,1)S(1)}, u32[]{:S(2)}, u32[]{:S(2)}) collective-permute-start(bf16[112,768]{1,0:T(8,128)(2,1)S(1)} %get-tuple-element.45), channel_id=1, source_target_pairs={{0,2},{1,3},{2,0},{3,1},{4,6},{5,7},{6,4},{7,5},{8,10},{9,11},{10,... | collective-permute-start | bytes 516104 | tf_op jit(solution)/shard_map/ppermute | solution.py:608
  44.3 1.8 %collective-permute-start.6 = (bf16[112,768]{1,0:T(8,128)(2,1)S(1)}, bf16[112,768]{1,0:T(8,128)(2,1)S(1)}, u32[]{:S(2)}, u32[]{:S(2)}) collective-permute-start(bf16[112,768]{1,0:T(8,128)(2,1)S(1)} %get-tuple-element.46), channel_id=1, source_target_pairs={{0,3},{1,2},{2,1},{3,0},{4,7},{5,6},{6,5},{7,4},{8,11},{9,10},{10,... | collective-permute-start | bytes 516104 | tf_op jit(solution)/shard_map/ppermute | solution.py:608
  46.1 8.4 %collective-permute-done.10.refs_4_ = bf16[112,768]{1,0:T(8,128)(2,1)S(1)} collective-permute-done((bf16[112,768]{1,0:T(8,128)(2,1)S(1)}, bf16[112,768]{1,0:T(8,128)(2,1)S(1)}, u32[]{:S(2)}, u32[]{:S(2)}) %collective-permute-start.10) | collective-permute-done | bytes 172064 | tf_op jit(solution)/shard_map/ppermute | solution.py:608
  54.5 2.6 %assemble.4 = (f32[2,2,3,32,2048]{4,3,2,1,0:T(8,128)}, f32[256,256]{1,0:T(8,128)S(1)}) custom-call(s32[1]{0:T(128)} %bitcast.refs_0_, bf16[144,768]{1,0:T(8,128)(2,1)S(1)} %get-tuple-element.47.refs_1_, bf16[144,768]{1,0:T(8,128)(2,1)S(1)} %collective-permute-done.8.refs_2_, ...), custom_call_target="tpu_custom_call", output_to_operand_aliasing={{0}: (6, {})} | custom-call | flops 1000 | bytes 1000 | tf_op jit(solution)/shard_map/assemble/pallas_call | solution.py:577
  57.1 3.8 %collective-permute-done.5.refs_3_ = bf16[112,768]{1,0:T(8,128)(2,1)S(1)} collective-permute-done((bf16[112,768]{1,0:T(8,128)(2,1)S(1)}, bf16[112,768]{1,0:T(8,128)(2,1)S(1)}, u32[]{:S(2)}, u32[]{:S(2)}) %collective-permute-start.5) | collective-permute-done | bytes 172064 | tf_op jit(solution)/shard_map/ppermute | solution.py:608
  60.9 2.6 %assemble.5 = (f32[2,2,3,32,2048]{4,3,2,1,0:T(8,128)}, f32[64,128]{1,0:T(8,128)S(1)}) custom-call(s32[1]{0:T(128)} %bitcast.refs_0_, bf16[144,768]{1,0:T(8,128)(2,1)S(1)} %get-tuple-element.39.refs_1_, bf16[144,768]{1,0:T(8,128)(2,1)S(1)} %collective-permute-done.4.refs_2_, ...), custom_call_target="tpu_custom_call", output_to_operand_aliasing={{0}: (6, {})} | custom-call | flops 1000 | bytes 1000 | tf_op jit(solution)/shard_map/assemble/pallas_call | solution.py:577
  63.5 1.2 %collective-permute-done.11 = f32[64,128]{1,0:T(8,128)S(1)} collective-permute-done((f32[64,128]{1,0:T(8,128)S(1)}, f32[64,128]{1,0:T(8,128)S(1)}, u32[]{:S(2)}, u32[]{:S(2)}) %collective-permute-start.11) | collective-permute-done | bytes 32800 | tf_op jit(solution)/shard_map/ppermute | solution.py:648
  64.8 1.6 %collective-permute-start.12 = (f32[64,128]{1,0:T(8,128)S(1)}, f32[64,128]{1,0:T(8,128)S(1)}, u32[]{:S(2)}, u32[]{:S(2)}) collective-permute-start(f32[64,128]{1,0:T(8,128)S(1)} %add.3.refs_0_), channel_id=1, source_target_pairs={{0,8},{4,12},{8,0},{12,4},{16,24},{20,28},{24,16},{28,20},{1,9},{5... | collective-permute-start | bytes 98312 | tf_op jit(solution)/shard_map/ppermute | solution.py:648
  66.3 1.5 %collective-permute-start.13 = (f32[64,128]{1,0:T(8,128)S(1)}, f32[64,128]{1,0:T(8,128)S(1)}, u32[]{:S(2)}, u32[]{:S(2)}) collective-permute-start(f32[64,128]{1,0:T(8,128)S(1)} %add.3.refs_0_), channel_id=1, source_target_pairs={{0,16},{4,20},{8,24},{12,28},{16,0},{20,4},{24,8},{28,12},{1,17},{... | collective-permute-start | bytes 98312 | tf_op jit(solution)/shard_map/ppermute | solution.py:648
  67.8 0.5 collective-permute-start.14
  68.3 0.4 collective-permute-done.12.refs_1_
  68.7 1.5 %collective-permute-done.13.refs_2_ = f32[64,128]{1,0:T(8,128)S(1)} collective-permute-done((f32[64,128]{1,0:T(8,128)S(1)}, f32[64,128]{1,0:T(8,128)S(1)}, u32[]{:S(2)}, u32[]{:S(2)}) %collective-permute-start.13) | collective-permute-done | bytes 32800 | tf_op jit(solution)/shard_map/ppermute | solution.py:648
  70.2 2.4 %collective-permute-done.14.refs_3_ = f32[64,128]{1,0:T(8,128)S(1)} collective-permute-done((f32[64,128]{1,0:T(8,128)S(1)}, f32[64,128]{1,0:T(8,128)S(1)}, u32[]{:S(2)}, u32[]{:S(2)}) %collective-permute-start.14) | collective-permute-done | bytes 32800 | tf_op jit(solution)/shard_map/ppermute | solution.py:648
  72.7 0.6 copy-done.11
  73.3 3.8 %factor.1 = f32[2,64,64]{2,1,0:T(8,128)} custom-call(f32[64,128]{1,0:T(8,128)} %copy-done.8, f32[64,128]{1,0:T(8,128)} %copy-done.9, f32[64,128]{1,0:T(8,128)} %copy-done.10, f32[64,128]{1,0:T(8,128)} %copy-done.11), custom_call_target="tpu_custom_call" | custom-call | tf_op jit(solution)/shard_map/factor/pallas_call | solution.py:303
  (32 shorter events, 0.2 us)
Async XLA Ops:
  0.6 10.5 %copy-start.7 = (s32[2048]{0:T(1024)S(1)}, s32[2048]{0:T(1024)}, u32[]{:S(2)}) copy-start(s32[2048]{0:T(1024)} %param.6) | copy-start | bytes 24580
  5.4 21.9 %collective-permute-start = (bf16[144,512]{1,0:T(8,128)(2,1)}, bf16[144,512]{1,0:T(8,128)(2,1)S(1)}, u32[]{:S(2)}, u32[]{:S(2)}) collective-permute-start(bf16[144,512]{1,0:T(8,128)(2,1)} %get-tuple-element.35), channel_id=1, source_target_pairs={{0,1},{1,0},{2,3},{3,2},{4,5},{5,4},{6,7},{7,6},{8,9},{9,8},{10,11... | collective-permute-start | bytes 442376 | tf_op jit(solution)/shard_map/ppermute | solution.py:608
  8.5 18.8 %collective-permute-start.1 = (bf16[144,512]{1,0:T(8,128)(2,1)}, bf16[144,512]{1,0:T(8,128)(2,1)S(1)}, u32[]{:S(2)}, u32[]{:S(2)}) collective-permute-start(bf16[144,512]{1,0:T(8,128)(2,1)} %get-tuple-element.36), channel_id=1, source_target_pairs={{0,2},{1,3},{2,0},{3,1},{4,6},{5,7},{6,4},{7,5},{8,10},{9,11},{10,... | collective-permute-start | bytes 442376 | tf_op jit(solution)/shard_map/ppermute | solution.py:608
  11.1 16.2 %collective-permute-start.2 = (bf16[144,512]{1,0:T(8,128)(2,1)}, bf16[144,512]{1,0:T(8,128)(2,1)S(1)}, u32[]{:S(2)}, u32[]{:S(2)}) collective-permute-start(bf16[144,512]{1,0:T(8,128)(2,1)} %get-tuple-element.37), channel_id=1, source_target_pairs={{0,3},{1,2},{2,1},{3,0},{4,7},{5,6},{6,5},{7,4},{8,11},{9,10},{10,... | collective-permute-start | bytes 442376 | tf_op jit(solution)/shard_map/ppermute | solution.py:608
  11.1 1.1 %copy-start = (f32[1072,128]{1,0:T(8,128)S(1)}, f32[1072,128]{1,0:T(8,128)}, u32[]{:S(2)}) copy-start(f32[1072,128]{1,0:T(8,128)} %get-tuple-element.32.refs_3_) | copy-start | bytes 1646596
  12.1 1.1 %copy-start.2 = (f32[1072,128]{1,0:T(8,128)S(1)}, f32[1072,128]{1,0:T(8,128)}, u32[]{:S(2)}) copy-start(f32[1072,128]{1,0:T(8,128)} %get-tuple-element.33.refs_4_) | copy-start | bytes 1646596
  13.2 1.0 %copy-start.4 = (bf16[192,1072]{1,0:T(8,128)(2,1)S(1)}, bf16[192,1072]{1,0:T(8,128)(2,1)}, u32[]{:S(2)}) copy-start(bf16[192,1072]{1,0:T(8,128)(2,1)} %get-tuple-element.31.refs_2_) | copy-start | bytes 1234948
  14.2 13.1 %copy-start.6 = (bf16[144,512]{1,0:T(8,128)(2,1)S(1)}, bf16[144,512]{1,0:T(8,128)(2,1)}, u32[]{:S(2)}) copy-start(bf16[144,512]{1,0:T(8,128)(2,1)} %get-tuple-element.34.refs_1_) | copy-start | bytes 442372
  14.2 15.0 %copy-start.1 = (f32[1072,128]{1,0:T(8,128)S(1)}, f32[1072,128]{1,0:T(8,128)}, u32[]{:S(2)}) copy-start(f32[1072,128]{1,0:T(8,128)} %get-tuple-element.32.refs_3_) | copy-start | bytes 1646596
  14.2 15.0 %copy-start.3 = (f32[1072,128]{1,0:T(8,128)S(1)}, f32[1072,128]{1,0:T(8,128)}, u32[]{:S(2)}) copy-start(f32[1072,128]{1,0:T(8,128)} %get-tuple-element.33.refs_4_) | copy-start | bytes 1646596
  14.2 15.0 %copy-start.5 = (bf16[192,1072]{1,0:T(8,128)(2,1)S(1)}, bf16[192,1072]{1,0:T(8,128)(2,1)}, u32[]{:S(2)}) copy-start(bf16[192,1072]{1,0:T(8,128)(2,1)} %get-tuple-element.31.refs_2_) | copy-start | bytes 1234948
  18.9 6.2 %collective-permute-start.7 = (bf16[48,768]{1,0:T(8,128)(2,1)S(1)}, bf16[48,768]{1,0:T(8,128)(2,1)S(1)}, u32[]{:S(2)}, u32[]{:S(2)}) collective-permute-start(bf16[48,768]{1,0:T(8,128)(2,1)S(1)} %get-tuple-element.50), channel_id=1, source_target_pairs={{1,0},{2,3},{5,4},{6,7},{9,8},{10,11},{13,12},{14,15},{17,16},{18,... | collective-permute-start | bytes 221192 | tf_op jit(solution)/shard_map/ppermute | solution.py:608
  25.2 19.0 %collective-permute-start.9 = (bf16[112,768]{1,0:T(8,128)(2,1)S(1)}, bf16[112,768]{1,0:T(8,128)(2,1)S(1)}, u32[]{:S(2)}, u32[]{:S(2)}) collective-permute-start(bf16[112,768]{1,0:T(8,128)(2,1)S(1)} %get-tuple-element.53), channel_id=1, source_target_pairs={{0,2},{1,3},{2,0},{3,1},{4,6},{5,7},{6,4},{7,5},{8,10},{9,11},{10,... | collective-permute-start | bytes 516104 | tf_op jit(solution)/shard_map/ppermute | solution.py:608
  33.7 6.9 %collective-permute-start.3 = (bf16[48,768]{1,0:T(8,128)(2,1)S(1)}, bf16[48,768]{1,0:T(8,128)(2,1)S(1)}, u32[]{:S(2)}, u32[]{:S(2)}) collective-permute-start(bf16[48,768]{1,0:T(8,128)(2,1)S(1)} %get-tuple-element.42), channel_id=1, source_target_pairs={{1,0},{2,3},{5,4},{6,7},{9,8},{10,11},{13,12},{14,15},{17,16},{18,... | collective-permute-start | bytes 221192 | tf_op jit(solution)/shard_map/ppermute | solution.py:608
  35.0 19.4 %collective-permute-start.8 = (bf16[144,768]{1,0:T(8,128)(2,1)S(1)}, bf16[144,768]{1,0:T(8,128)(2,1)S(1)}, u32[]{:S(2)}, u32[]{:S(2)}) collective-permute-start(bf16[144,768]{1,0:T(8,128)(2,1)S(1)} %get-tuple-element.52), channel_id=1, source_target_pairs={{0,1},{1,0},{2,3},{3,2},{4,5},{5,4},{6,7},{7,6},{8,9},{9,8},{10,11... | collective-permute-start | bytes 663560 | tf_op jit(solution)/shard_map/ppermute | solution.py:608
  40.7 20.2 %collective-permute-start.4 = (bf16[144,768]{1,0:T(8,128)(2,1)S(1)}, bf16[144,768]{1,0:T(8,128)(2,1)S(1)}, u32[]{:S(2)}, u32[]{:S(2)}) collective-permute-start(bf16[144,768]{1,0:T(8,128)(2,1)S(1)} %get-tuple-element.44), channel_id=1, source_target_pairs={{0,1},{1,0},{2,3},{3,2},{4,5},{5,4},{6,7},{7,6},{8,9},{9,8},{10,11... | collective-permute-start | bytes 663560 | tf_op jit(solution)/shard_map/ppermute | solution.py:608
  40.8 13.7 %collective-permute-start.10 = (bf16[112,768]{1,0:T(8,128)(2,1)S(1)}, bf16[112,768]{1,0:T(8,128)(2,1)S(1)}, u32[]{:S(2)}, u32[]{:S(2)}) collective-permute-start(bf16[112,768]{1,0:T(8,128)(2,1)S(1)} %get-tuple-element.54), channel_id=1, source_target_pairs={{0,3},{1,2},{2,1},{3,0},{4,7},{5,6},{6,5},{7,4},{8,11},{9,10},{10,... | collective-permute-start | bytes 516104 | tf_op jit(solution)/shard_map/ppermute | solution.py:608
  42.7 18.2 %collective-permute-start.5 = (bf16[112,768]{1,0:T(8,128)(2,1)S(1)}, bf16[112,768]{1,0:T(8,128)(2,1)S(1)}, u32[]{:S(2)}, u32[]{:S(2)}) collective-permute-start(bf16[112,768]{1,0:T(8,128)(2,1)S(1)} %get-tuple-element.45), channel_id=1, source_target_pairs={{0,2},{1,3},{2,0},{3,1},{4,6},{5,7},{6,4},{7,5},{8,10},{9,11},{10,... | collective-permute-start | bytes 516104 | tf_op jit(solution)/shard_map/ppermute | solution.py:608
  44.3 16.6 %collective-permute-start.6 = (bf16[112,768]{1,0:T(8,128)(2,1)S(1)}, bf16[112,768]{1,0:T(8,128)(2,1)S(1)}, u32[]{:S(2)}, u32[]{:S(2)}) collective-permute-start(bf16[112,768]{1,0:T(8,128)(2,1)S(1)} %get-tuple-element.46), channel_id=1, source_target_pairs={{0,3},{1,2},{2,1},{3,0},{4,7},{5,6},{6,5},{7,4},{8,11},{9,10},{10,... | collective-permute-start | bytes 516104 | tf_op jit(solution)/shard_map/ppermute | solution.py:608
  63.5 1.2 %collective-permute-start.11 = (f32[64,128]{1,0:T(8,128)S(1)}, f32[64,128]{1,0:T(8,128)S(1)}, u32[]{:S(2)}, u32[]{:S(2)}) collective-permute-start(f32[64,128]{1,0:T(8,128)S(1)} %get-tuple-element.59), channel_id=1, source_target_pairs={{0,4},{4,0},{8,12},{12,8},{16,20},{20,16},{24,28},{28,24},{1,5},{5... | collective-permute-start | bytes 98312 | tf_op jit(solution)/shard_map/ppermute | solution.py:648
  64.8 7.9 %copy-start.8 = (f32[64,128]{1,0:T(8,128)}, f32[64,128]{1,0:T(8,128)S(1)}, u32[]{:S(2)}) copy-start(f32[64,128]{1,0:T(8,128)S(1)} %add.3.refs_0_) | copy-start | bytes 98308
  64.8 4.0 %collective-permute-start.12 = (f32[64,128]{1,0:T(8,128)S(1)}, f32[64,128]{1,0:T(8,128)S(1)}, u32[]{:S(2)}, u32[]{:S(2)}) collective-permute-start(f32[64,128]{1,0:T(8,128)S(1)} %add.3.refs_0_), channel_id=1, source_target_pairs={{0,8},{4,12},{8,0},{12,4},{16,24},{20,28},{24,16},{28,20},{1,9},{5... | collective-permute-start | bytes 98312 | tf_op jit(solution)/shard_map/ppermute | solution.py:648
  66.3 3.9 %collective-permute-start.13 = (f32[64,128]{1,0:T(8,128)S(1)}, f32[64,128]{1,0:T(8,128)S(1)}, u32[]{:S(2)}, u32[]{:S(2)}) collective-permute-start(f32[64,128]{1,0:T(8,128)S(1)} %add.3.refs_0_), channel_id=1, source_target_pairs={{0,16},{4,20},{8,24},{12,28},{16,0},{20,4},{24,8},{28,12},{1,17},{... | collective-permute-start | bytes 98312 | tf_op jit(solution)/shard_map/ppermute | solution.py:648
  67.8 4.8 %collective-permute-start.14 = (f32[64,128]{1,0:T(8,128)S(1)}, f32[64,128]{1,0:T(8,128)S(1)}, u32[]{:S(2)}, u32[]{:S(2)}) collective-permute-start(f32[64,128]{1,0:T(8,128)S(1)} %add.3.refs_0_), channel_id=1, source_target_pairs={{0,24},{4,28},{8,16},{12,20},{16,8},{20,12},{24,0},{28,4},{1,25},{... | collective-permute-start | bytes 98312 | tf_op jit(solution)/shard_map/ppermute | solution.py:648
  68.7 3.9 %copy-start.9 = (f32[64,128]{1,0:T(8,128)}, f32[64,128]{1,0:T(8,128)S(1)}, u32[]{:S(2)}) copy-start(f32[64,128]{1,0:T(8,128)S(1)} %collective-permute-done.12.refs_1_) | copy-start | bytes 98308
  70.2 2.4 %copy-start.10 = (f32[64,128]{1,0:T(8,128)}, f32[64,128]{1,0:T(8,128)S(1)}, u32[]{:S(2)}) copy-start(f32[64,128]{1,0:T(8,128)S(1)} %collective-permute-done.13.refs_2_) | copy-start | bytes 98308
  72.7 0.6 copy-start.11

commit v4 on v3

--- a/solution.py
+++ b/solution.py
@@ -313,6 +313,7 @@
 WIDE = 12
 FAR = 9
 SHARED = 2
+REACH = 144
 
 
 def pick(values, me):
@@ -374,43 +375,86 @@
         direct3.append(rows[12:])
     direct_ref[...] = jnp.concatenate(own + near + direct2 + direct3, axis=0).astype(jnp.bfloat16)
     far = [rows_ref[far_block(me, s) - lo] for s in range(FAR)]
-    inner = ((me == 1) | (me == 2)).astype(jnp.float32)
-    shared = [rows_ref[pick([0, s, 10 - s, 0], me)] * inner for s in range(SHARED)]
     pieces = own + near
-    pieces += [r[4:] for r in shared] + [r[:4] for r in shared]
     pieces += [r[:4] for r in far[:-1]] + [r[4:] for r in far[:-1]]
     pieces += [far[-1], jnp.zeros((8, span), jnp.float32)]
     a_ref[...] = jnp.concatenate(pieces, axis=0).astype(jnp.bfloat16)
 
 
+def rotate(turning, cosine, sine, x, y):
+    width = x.shape[1]
+    cosine = jnp.concatenate([cosine] * (width // LANES), axis=1)
+    sine = jnp.concatenate([sine] * (width // LANES), axis=1)
+    x, y = x.astype(jnp.float32), y.astype(jnp.float32)
+    new_x = jnp.where(turning, cosine * x - sine * y, x)
+    new_y = jnp.where(turning, sine * x + cosine * y, y)
+    return new_x.astype(jnp.bfloat16), new_y.astype(jnp.bfloat16)
+
+
+def shared_rows(begin, me, starts_ref, freqs_ref):
+    rid = lax.broadcasted_iota(jnp.int32, (16, 1), 0)
+    f_of = jnp.where(rid < 8, me ^ 3, me ^ 2) * 2 + (rid // 2) % 2
+    freq = jnp.zeros((16, 1), jnp.float32)
+    for f in range(8):
+        freq = jnp.where(f_of == f, freqs_ref[f].astype(jnp.float32), freq)
+    first, second = (starts_ref[pick([0, 6 + s, 25 - s, 0], me)] for s in range(SHARED))
+    start = jnp.where((rid // 4) % 2 == 0, first, second)
+    ni = lax.broadcasted_iota(jnp.int32, (1, REACH), 1) + begin - start
+    nf = ni.astype(jnp.float32)
+    w = half_turn_sine(jnp.minimum(nf, NFFT - nf) * (1.0 / NFFT))
+    inner = (me == 1) | (me == 2)
+    w = jnp.where((ni >= 0) & (ni < NFFT) & inner, w * w * SCALE, 0.0)
+    turns = nf * (freq * (1.0 / NFFT)) + (rid % 2).astype(jnp.float32) * 0.25
+    return (cosine_of(turns) * w).astype(jnp.bfloat16)
+
+
 def line_dft_body(span, blocks, first, *refs):
     if first:
-        pos_ref, starts_ref, freqs_ref, angle_ref, mask_ref, vel_ref = refs[:6]
-        out_refs = refs[6:10]
-        shared_refs = refs[10:13]
-        rot_ref, a_ref, rows_ref = refs[13:]
+        pos_ref, starts_ref, freqs_ref, angle_ref, mask_ref, vel_ref, all_mask_ref, all_hbm = refs[:8]
+        out_refs = refs[8:12]
+        part_ref = refs[12]
+        shared_refs = refs[13:16]
+        rot_ref, a_ref, rows_ref, ends_ref, ends_rot_ref, ends_sem = refs[16:]
         _, cos_ref, sin_ref = shared_refs
 
         @pl.when(pl.program_id(0) == 0)
         def _():
-            build_line(span, blocks, pos_ref[0], starts_ref, freqs_ref, a_ref, shared_refs[0], rows_ref)
+            me = pos_ref[0]
+            begin = pl.multiple_of(jnp.where(me == 2, span - REACH, 0), 16)
+            load = pltpu.make_async_copy(all_hbm.at[:, pl.ds(begin, REACH), :], ends_ref, ends_sem)
+            load.start()
+            build_line(span, blocks, me, starts_ref, freqs_ref, a_ref, shared_refs[0], rows_ref)
             spread_column(jnp.cos(angle_ref[...].reshape(1, span)), span, cos_ref)
             spread_column(jnp.sin(angle_ref[...].reshape(1, span)), span, sin_ref)
+            rows = shared_rows(begin + me * span, me, starts_ref, freqs_ref)
+            load.wait()
+            for lane in range(0, part_ref.shape[1], TILE):
+                here = slice(lane, lane + TILE)
+                turning = all_mask_ref[:, here] == 1
+                for at in range(0, REACH, 16):
+                    row = slice(at, at + 16)
+                    t = pl.ds(pl.multiple_of(begin + at, 16), 16)
+                    new_x, new_y = rotate(
+                        turning, cos_ref[t, :], sin_ref[t, :], ends_ref[0, row, here], ends_ref[1, row, here]
+                    )
+                    ends_rot_ref[0, row, here] = new_x
+                    ends_rot_ref[1, row, here] = new_y
+                for c in range(COMPS):
+                    samples = ends_rot_ref[c, :, here] if c < 2 else ends_ref[2, :, here]
+                    sums = jnp.dot(rows, samples, preferred_element_type=jnp.float32)
+                    part_ref[16 * c:16 * c + 16, here] = sums.astype(jnp.bfloat16)
     else:
-        mask_ref, vel_ref, a_ref, cos_ref, sin_ref = refs[:5]
-        own_ref, near_ref, shared_ref, far2_ref, far3_ref, rot_ref = refs[6:]
+        part_ref, mask_ref, vel_ref, a_ref, cos_ref, sin_ref = refs[:6]
+        own_ref, near_ref, far2_ref, far3_ref, rot_ref = refs[7:]
     width = vel_ref.shape[2]
     turning = mask_ref[...] == 1
     for at in range(0, span, 16):
-        rows = min(16, span - at)
-        here = pl.ds(at, rows)
-        cosine = jnp.concatenate([cos_ref[here, :]] * (width // LANES), axis=1)
-        sine = jnp.concatenate([sin_ref[here, :]] * (width // LANES), axis=1)
-        x = vel_ref[0, here, :].astype(jnp.float32)
-        y = vel_ref[1, here, :].astype(jnp.float32)
-        rot_ref[0, here, :] = jnp.where(turning, cosine * x - sine * y, x).astype(jnp.bfloat16)
-        rot_ref[1, here, :] = jnp.where(turning, sine * x + cosine * y, y).astype(jnp.bfloat16)
+        here = pl.ds(at, min(16, span - at))
+        new_x, new_y = rotate(turning, cos_ref[here, :], sin_ref[here, :], vel_ref[0, here, :], vel_ref[1, here, :])
+        rot_ref[0, here, :] = new_x
+        rot_ref[1, here, :] = new_y
     tails = []
+    none = jnp.zeros((24, width), jnp.float32)
     for c in range(COMPS):
         samples = rot_ref[c] if c < 2 else vel_ref[2]
         sums = jnp.dot(a_ref[...], samples, preferred_element_type=jnp.float32)
@@ -420,19 +464,20 @@
             continue
         own_ref[48 * c:48 * c + 48, :] = sums[:48].astype(jnp.bfloat16)
         near_ref[48 * c:48 * c + 48, :] = sums[48:96].astype(jnp.bfloat16)
-        shared_ref[16 * c:16 * c + 16, :] = sums[96:112].astype(jnp.bfloat16)
-        far2_ref[32 * c:32 * c + 32, :] = sums[112:144].astype(jnp.bfloat16)
-        far3_ref[32 * c:32 * c + 32, :] = sums[144:176].astype(jnp.bfloat16)
-        tails.append(sums[176:184])
+        part = part_ref[16 * c:16 * c + 16, :].astype(jnp.float32)
+        far2 = sums[96:128] + jnp.concatenate([none, part[:8]], axis=0)
+        far3 = sums[128:160] + jnp.concatenate([none, part[8:]], axis=0)
+        far2_ref[32 * c:32 * c + 32, :] = far2.astype(jnp.bfloat16)
+        far3_ref[32 * c:32 * c + 32, :] = far3.astype(jnp.bfloat16)
+        tails.append(sums[160:168])
     if not first:
-        none = jnp.zeros((4, width), jnp.float32)
-        far2_ref[96:112, :] = jnp.concatenate([t[:4] for t in tails] + [none], axis=0).astype(jnp.bfloat16)
-        far3_ref[96:112, :] = jnp.concatenate([t[4:] for t in tails] + [none], axis=0).astype(jnp.bfloat16)
-
-
-def line_dft(blocks, offset, points, position, starts, freqs, angles, mask, velocity, shared, after):
+        far2_ref[96:112, :] = jnp.concatenate([t[:4] for t in tails] + [none[:4]], axis=0).astype(jnp.bfloat16)
+        far3_ref[96:112, :] = jnp.concatenate([t[4:] for t in tails] + [none[:4]], axis=0).astype(jnp.bfloat16)
+
+
+def line_dft(blocks, offset, points, position, starts, freqs, angles, mask, velocity, shared, part, after):
     first = shared is None
-    span = velocity.shape[1]
+    span, all_points = velocity.shape[1:]
     shift = offset // TILE
     whole = lambda shape: pl.BlockSpec(shape, lambda i: (0,) * len(shape))
     smem = pl.BlockSpec(memory_space=pltpu.SMEM)
@@ -441,24 +486,32 @@
         pl.BlockSpec((COMPS, span, TILE), lambda i: (0, 0, i + shift)),
     ]
     shared_types = [
-        jax.ShapeDtypeStruct((192, span), jnp.bfloat16),
+        jax.ShapeDtypeStruct((176, span), jnp.bfloat16),
         jax.ShapeDtypeStruct((span, LANES), jnp.float32),
         jax.ShapeDtypeStruct((span, LANES), jnp.float32),
     ]
     shared_specs = [whole(t.shape) for t in shared_types]
-    heights = [144] * 4 if first else [144, 144, 48, 112, 112]
+    heights = [144] * 4 if first else [144, 144, 112, 112]
     out_types = [jax.ShapeDtypeStruct((h, points), jnp.bfloat16) for h in heights]
     out_specs = [pl.BlockSpec((h, TILE), lambda i: (0, i)) for h in heights]
     scratch = [pltpu.VMEM((2, span, TILE), jnp.bfloat16)]
     if first:
-        args = (position, starts, freqs, angles, mask, velocity)
+        args = (position, starts, freqs, angles, mask, velocity, mask, velocity)
         in_specs = [smem] * 3 + [whole((span,))] + data_specs
-        out_types = out_types + shared_types
-        out_specs = out_specs + shared_specs
-        scratch += [pltpu.VMEM((192, span), jnp.bfloat16), pltpu.VMEM((WIDE, 8, span), jnp.float32)]
+        in_specs += [whole((1, all_points)), pl.BlockSpec(memory_space=pl.ANY)]
+        out_types += [jax.ShapeDtypeStruct((48, all_points), jnp.bfloat16)] + shared_types
+        out_specs += [whole((48, all_points))] + shared_specs
+        scratch += [
+            pltpu.VMEM((192, span), jnp.bfloat16),
+            pltpu.VMEM((WIDE, 8, span), jnp.float32),
+            pltpu.VMEM((COMPS, REACH, all_points), jnp.bfloat16),
+            pltpu.VMEM((2, REACH, all_points), jnp.bfloat16),
+            pltpu.SemaphoreType.DMA,
+        ]
     else:
-        args = (mask, velocity) + tuple(shared) + (after,)
-        in_specs = data_specs + shared_specs + [pl.BlockSpec(memory_space=pl.ANY)]
+        args = (part, mask, velocity) + tuple(shared) + (after,)
+        in_specs = [pl.BlockSpec((48, TILE), lambda i: (0, i + shift))] + data_specs + shared_specs
+        in_specs.append(pl.BlockSpec(memory_space=pl.ANY))
     out = pl.pallas_call(
         functools.partial(line_dft_body, span, blocks, first),
         grid=(points // TILE,),
@@ -467,32 +520,12 @@
         out_specs=out_specs,
         scratch_shapes=scratch,
         compiler_params=pltpu.CompilerParams(vmem_limit_bytes=(60 if first else 40) * 2**20),
-        cost_estimate=SHORT,
+        cost_estimate=pl.CostEstimate(
+            flops=2 * 192 * span * COMPS * points, bytes_accessed=2 * COMPS * span * points, transcendentals=0
+        ),
         name="rotate_dft",
     )(*args)
-    return (out[:4], out[4:]) if first else (out, shared)
-
-
-def combine_body(far2_ref, far3_ref, shared_ref, near_ref, out2_ref, out3_ref, near_out_ref):
-    for c in range(COMPS):
-        here = slice(32 * c, 32 * c + 32)
-        add = shared_ref[16 * c:16 * c + 16, :].astype(jnp.float32)
-        none = jnp.zeros((24, add.shape[1]), jnp.float32)
-        for src, dst, part in ((far2_ref, out2_ref, add[:8]), (far3_ref, out3_ref, add[8:])):
-            dst[here, :] = (src[here, :].astype(jnp.float32) + jnp.concatenate([none, part], axis=0)).astype(jnp.bfloat16)
-    near_out_ref[...] = near_ref[...]
-    out2_ref[96:112, :] = far2_ref[96:112, :]
-    out3_ref[96:112, :] = far3_ref[96:112, :]
-
-
-def combine(far2, far3, shared, near):
-    return pl.pallas_call(
-        combine_body,
-        out_shape=[jax.ShapeDtypeStruct(x.shape, x.dtype) for x in (far2, far3, near)],
-        compiler_params=pltpu.CompilerParams(vmem_limit_bytes=40 * 2**20),
-        cost_estimate=pl.CostEstimate(flops=far2.size, bytes_accessed=8 * far2.size, transcendentals=0),
-        name="add_shared",
-    )(far2, far3, shared, near)
+    return (out[:4], out[4], out[5:]) if first else (out, part, shared)
 
 
 def line_selection(blocks, me, direct, sel_ref):
@@ -598,7 +631,7 @@
 
 
 def line_chunks(points):
-    cuts = [0, points // 4, points * 5 // 8, points]
+    cuts = [0, points // 4, points * 5 // 8, points * 7 // 8, points]
     return [(a, b - a) for a, b in zip(cuts[:-1], cuts[1:])]
 
 
@@ -607,8 +640,9 @@
     blocks = block_starts.shape[0]
     move = lambda x, pairs: lax.ppermute(x, "tm", pairs)
     across = lambda x, k: move(x, [(i, i ^ k) for i in range(4)])
-    chunks = line_chunks(points)
-    spectra, gram, shared, sent = None, None, None, []
+    shared, part = None, None
+    spectra, gram = None, None
+    sent = []
 
     def assemble():
         at, count, own, near, fars = sent.pop(0)
@@ -616,18 +650,15 @@
             blocks, total, at, count, points, position, own, near, fars, spectra, gram, at + count == points
         )
 
-    for i, (at, count) in enumerate(chunks):
+    for i, (at, count) in enumerate(line_chunks(points)):
         if i >= 2:
             spectra, gram = assemble()
-        after = gram if i >= 2 else mask
-        sums, shared = line_dft(
-            blocks, at, count, position, block_starts, frequencies, angles, mask, samples, shared, after
+        (own, near, far2, far3), part, shared = line_dft(
+            blocks, at, count, position, block_starts, frequencies, angles, mask, samples, shared, part,
+            gram if i >= 2 else mask,
         )
         if i == 0:
-            own, near, far2, far3 = sums
-        else:
-            own, near, part, far2, far3 = sums
-            far2, far3, near = combine(far2, far3, move(part, [(1, 0), (2, 3)]), near)
+            part = move(part, [(1, 0), (2, 3)])
         sent.append((at, count, own, across(near, 1), [across(far2, 2), across(far3, 3)]))
     while sent:
         spectra, gram = assemble()
@@ -647,7 +678,8 @@
         return [lax.psum(gram, "space")]
     swap = lambda x, k: lax.ppermute(x, "space", [(i, i ^ k) for i in range(groups)])
     gram = gram + swap(gram, 1)
-    return [gram] + [swap(gram, k) for k in (2, 4, 6)]
+    gram = gram + swap(gram, 2)
+    return [gram, swap(gram, 4)]
 
 
 def chunks_of(points):

time: 77.5 us -> 78 us (level)
  waiting for transfers between devices: 25.6 us -> 17.5 us
  starting transfers between devices: 22 us -> 27.8 us
  Pallas kernels: 25 us -> 27.9 us
    ppermute x11 -> x13, waiting for transfers between devices: 20.1 us -> 11.8 us  [line_spectra(): move = lambda x, pairs: lax.ppermute(x, 'tm', pairs)]
    ppermute x11 -> x13, starting transfers between devices: 18.4 us -> 24.3 us  [line_spectra(): move = lambda x, pairs: lax.ppermute(x, 'tm', pairs)]
    pallas_call x3 -> x4, Pallas kernels: 14 us -> 16.8 us  [line_dft(): pl.pallas_call(functools.partial(line_dft_body, span, blocks, first), gri...]
    pallas_call x3 -> x4, Pallas kernels: 7.1 us -> 7.36 us  [line_assemble(): pl.pallas_call(functools.partial(line_assemble_body, blocks, total, has_s...]
    ppermute x4 -> x3, waiting for transfers between devices: 5.54 us -> 5.67 us  [sum_over_space(): lax.ppermute(x, 'space', [(i, i ^ k) for i in range(groups)])]
    ppermute x4 -> x3, starting transfers between devices: 3.56 us -> 3.43 us  [sum_over_space(): lax.ppermute(x, 'space', [(i, i ^ k) for i in range(groups)])]
    unnamed x24 -> x20, local copies, waits for them, and re-layouts: 3.74 us -> 3.72 us
  transfers between devices with their start and end apart: 15 -> 16, of which waited for: 8 -> 6; matrix products, arithmetic and copies ran while one was open for 0% -> 0% of each run, Pallas kernels for 18% -> 21%
where the time goes in v4:
time: 78 us; the launch traced here: 77.6 us
  Pallas kernels  27.9 us (36%)
  starting transfers between devices  27.8 us (36%)
  waiting for transfers between devices  17.5 us (22%)
  local copies, waits for them, and re-layouts  3.72 us (5%)
    ppermute x13, starting transfers between devices, line_spectra(): move = lambda x, pairs: lax.ppermute(x, 'tm', pairs)  24.3 us
    pallas_call x4, Pallas kernels, line_dft(): pl.pallas_call(functools.partial(line_dft_body, span, blocks, first), gri...  16.8 us
    ppermute x13, waiting for transfers between devices, line_spectra(): move = lambda x, pairs: lax.ppermute(x, 'tm', pairs)  11.8 us
    pallas_call x4, Pallas kernels, line_assemble(): pl.pallas_call(functools.partial(line_assemble_body, blocks, total, has_s...  7.36 us
    ppermute x3, waiting for transfers between devices, sum_over_space(): lax.ppermute(x, 'space', [(i, i ^ k) for i in range(groups)])  5.67 us
    pallas_call x1, Pallas kernels, factor_call(): pl.pallas_call(functools.partial(factor_body, owned, order, len(parts)),...  3.73 us
    unnamed x20, local copies, waits for them, and re-layouts  3.72 us
    ppermute x3, starting transfers between devices, sum_over_space(): lax.ppermute(x, 'space', [(i, i ^ k) for i in range(groups)])  3.43 us
  transfers between devices with their start and end apart: 16, of which 6 were waited for; matrix products, arithmetic and copies ran while one was open for 0% of the time, Pallas kernels for 21%

profile of v4, /device:TPU:0, one launch (start us, length us, event | category | flops | bytes accessed | tf_op | source)
XLA Modules:
  0.0 77.6 jit_solution(15957092174175262824)
XLA Ops:
  0.6 6.6 %rotate_dft.4 = (bf16[144,512]{1,0:T(8,128)(2,1)}, bf16[144,512]{1,0:T(8,128)(2,1)}, bf16[144,512]{1,0:T(8,128)(2,1)}, bf16[144,512]{1,0:T(8,128)(2,1)}, bf16[48...) custom-call(s32[1]{0:T(128)} %bitcast.refs_0_, s32[32]{0:T(128)} %refs_1_.1, ...), custom_call_target="tpu_custom_call" | custom-call | flops 632291328 | bytes 3293184 | tf_op jit(solution)/shard_map/rotate_dft/pallas_call | solution.py:515
  7.3 1.3 %collective-permute-start = (bf16[48,2048]{1,0:T(8,128)(2,1)}, bf16[48,2048]{1,0:T(8,128)(2,1)S(1)}, u32[]{:S(2)}, u32[]{:S(2)}) collective-permute-start(bf16[48,2048]{1,0:T(8,128)(2,1)} %get-tuple-element.30), channel_id=1, source_target_pairs={{1,0},{2,3},{5,4},{6,7},{9,8},{10,11},{13,12},{14,15},{17,16},{18,... | collective-permute-start | bytes 589832 | tf_op jit(solution)/shard_map/ppermute | solution.py:641
  8.6 3.1 %collective-permute-start.4 = (bf16[144,512]{1,0:T(8,128)(2,1)}, bf16[144,512]{1,0:T(8,128)(2,1)S(1)}, u32[]{:S(2)}, u32[]{:S(2)}) collective-permute-start(bf16[144,512]{1,0:T(8,128)(2,1)} %get-tuple-element.39), channel_id=1, source_target_pairs={{0,1},{1,0},{2,3},{3,2},{4,5},{5,4},{6,7},{7,6},{8,9},{9,8},{10,11... | collective-permute-start | bytes 442376 | tf_op jit(solution)/shard_map/ppermute | solution.py:641
  11.7 3.3 %collective-permute-start.5 = (bf16[144,512]{1,0:T(8,128)(2,1)}, bf16[144,512]{1,0:T(8,128)(2,1)S(1)}, u32[]{:S(2)}, u32[]{:S(2)}) collective-permute-start(bf16[144,512]{1,0:T(8,128)(2,1)} %get-tuple-element.40), channel_id=1, source_target_pairs={{0,2},{1,3},{2,0},{3,1},{4,6},{5,7},{6,4},{7,5},{8,10},{9,11},{10,... | collective-permute-start | bytes 442376 | tf_op jit(solution)/shard_map/ppermute | solution.py:641
  14.9 1.4 %collective-permute-start.6 = (bf16[144,512]{1,0:T(8,128)(2,1)}, bf16[144,512]{1,0:T(8,128)(2,1)S(1)}, u32[]{:S(2)}, u32[]{:S(2)}) collective-permute-start(bf16[144,512]{1,0:T(8,128)(2,1)} %get-tuple-element.41), channel_id=1, source_target_pairs={{0,3},{1,2},{2,1},{3,0},{4,7},{5,6},{6,5},{7,4},{8,11},{9,10},{10,... | collective-permute-start | bytes 442376 | tf_op jit(solution)/shard_map/ppermute | solution.py:641
  16.3 4.3 %collective-permute-done.refs_0_ = bf16[48,2048]{1,0:T(8,128)(2,1)S(1)} collective-permute-done((bf16[48,2048]{1,0:T(8,128)(2,1)}, bf16[48,2048]{1,0:T(8,128)(2,1)S(1)}, u32[]{:S(2)}, u32[]{:S(2)}) %collective-permute-start) | collective-permute-done | bytes 196640 | tf_op jit(solution)/shard_map/ppermute | solution.py:641
  20.7 1.0 %copy-done = f32[1072,128]{1,0:T(8,128)S(1)} copy-done((f32[1072,128]{1,0:T(8,128)S(1)}, f32[1072,128]{1,0:T(8,128)}, u32[]{:S(2)}) %copy-start) | copy-done | bytes 548888
  21.7 1.0 %copy-done.2 = f32[1072,128]{1,0:T(8,128)S(1)} copy-done((f32[1072,128]{1,0:T(8,128)S(1)}, f32[1072,128]{1,0:T(8,128)}, u32[]{:S(2)}) %copy-start.2) | copy-done | bytes 548888
  22.8 1.0 %copy-done.4 = bf16[176,1072]{1,0:T(8,128)(2,1)S(1)} copy-done((bf16[176,1072]{1,0:T(8,128)(2,1)S(1)}, bf16[176,1072]{1,0:T(8,128)(2,1)}, u32[]{:S(2)}) %copy-start.4) | copy-done | bytes 377368
  23.8 4.7 %rotate_dft.5 = (bf16[144,768]{1,0:T(8,128)(2,1)S(1)}, bf16[144,768]{1,0:T(8,128)(2,1)S(1)}, bf16[112,768]{1,0:T(8,128)(2,1)S(1)}, bf16[112,768]{1,0:T(8,128)(2,1)S(1)}) custom-call(bf16[48,2048]{1,0:T(8,128)(2,1)S(1)} %collective-permute-done.refs_0_, s32[1,2048]{1,0:T(1,128)S(1)} %bitcast.6, bf16[3,1072,2048]{2,1,0:T(8,128)(2,1)} %bitcast.12, ...), custom_call_target="tpu_custom_call" | custom-call | flops 948436992 | bytes 4939776 | tf_op jit(solution)/shard_map/rotate_dft/pallas_call | solution.py:515
  28.6 3.3 %collective-permute-start.2 = (bf16[112,768]{1,0:T(8,128)(2,1)S(1)}, bf16[112,768]{1,0:T(8,128)(2,1)S(1)}, u32[]{:S(2)}, u32[]{:S(2)}) collective-permute-start(bf16[112,768]{1,0:T(8,128)(2,1)S(1)} %get-tuple-element.36), channel_id=1, source_target_pairs={{0,2},{1,3},{2,0},{3,1},{4,6},{5,7},{6,4},{7,5},{8,10},{9,11},{10,... | collective-permute-start | bytes 516104 | tf_op jit(solution)/shard_map/ppermute | solution.py:641
  31.9 1.1 %collective-permute-start.3 = (bf16[112,768]{1,0:T(8,128)(2,1)S(1)}, bf16[112,768]{1,0:T(8,128)(2,1)S(1)}, u32[]{:S(2)}, u32[]{:S(2)}) collective-permute-start(bf16[112,768]{1,0:T(8,128)(2,1)S(1)} %get-tuple-element.37), channel_id=1, source_target_pairs={{0,3},{1,2},{2,1},{3,0},{4,7},{5,6},{6,5},{7,4},{8,11},{9,10},{10,... | collective-permute-start | bytes 516104 | tf_op jit(solution)/shard_map/ppermute | solution.py:641
  33.0 1.9 %assemble.4 = (f32[2,2,3,32,2048]{4,3,2,1,0:T(8,128)}, f32[256,256]{1,0:T(8,128)S(1)}) custom-call(s32[1]{0:T(128)} %bitcast.refs_0_, bf16[144,512]{1,0:T(8,128)(2,1)S(1)} %copy-done.7, bf16[144,512]{1,0:T(8,128)(2,1)S(1)} %collective-permute-done.4.refs_2_, bf16[144,512]{1,0:T(8,128)(2,1)S(1)} %collective-permute-done.5.refs_3_, ...), custom_call_target="tpu_custom_call" | custom-call | flops 1000 | bytes 1000 | tf_op jit(solution)/shard_map/assemble/pallas_call | solution.py:610
  34.8 3.2 %rotate_dft.7 = (bf16[144,512]{1,0:T(8,128)(2,1)S(1)}, bf16[144,512]{1,0:T(8,128)(2,1)S(1)}, bf16[112,512]{1,0:T(8,128)(2,1)S(1)}, bf16[112,512]{1,0:T(8,128)(2,1)S(1)}) custom-call(bf16[48,2048]{1,0:T(8,128)(2,1)S(1)} %collective-permute-done.refs_0_, s32[1,2048]{1,0:T(1,128)S(1)} %bitcast.8, bf16[3,1072,2048]{2,1,0:T(8,128)(2,1)} %bitcast.13, ...), custom_call_target="tpu_custom_call" | custom-call | flops 632291328 | bytes 3293184 | tf_op jit(solution)/shard_map/rotate_dft/pallas_call | solution.py:515
  38.6 2.8 %collective-permute-start.10 = (bf16[144,512]{1,0:T(8,128)(2,1)S(1)}, bf16[144,512]{1,0:T(8,128)(2,1)S(1)}, u32[]{:S(2)}, u32[]{:S(2)}) collective-permute-start(bf16[144,512]{1,0:T(8,128)(2,1)S(1)} %get-tuple-element.50), channel_id=1, source_target_pairs={{0,1},{1,0},{2,3},{3,2},{4,5},{5,4},{6,7},{7,6},{8,9},{9,8},{10,11... | collective-permute-start | bytes 442376 | tf_op jit(solution)/shard_map/ppermute | solution.py:641
  41.4 5.0 %collective-permute-done.2.refs_3_ = bf16[112,768]{1,0:T(8,128)(2,1)S(1)} collective-permute-done((bf16[112,768]{1,0:T(8,128)(2,1)S(1)}, bf16[112,768]{1,0:T(8,128)(2,1)S(1)}, u32[]{:S(2)}, u32[]{:S(2)}) %collective-permute-start.2) | collective-permute-done | bytes 172064 | tf_op jit(solution)/shard_map/ppermute | solution.py:641
  46.4 3.0 %collective-permute-start.12 = (bf16[112,512]{1,0:T(8,128)(2,1)S(1)}, bf16[112,512]{1,0:T(8,128)(2,1)S(1)}, u32[]{:S(2)}, u32[]{:S(2)}) collective-permute-start(bf16[112,512]{1,0:T(8,128)(2,1)S(1)} %get-tuple-element.52), channel_id=1, source_target_pairs={{0,3},{1,2},{2,1},{3,0},{4,7},{5,6},{6,5},{7,4},{8,11},{9,10},{10,... | collective-permute-start | bytes 344072 | tf_op jit(solution)/shard_map/ppermute | solution.py:641
  49.4 2.6 %assemble.5 = (f32[2,2,3,32,2048]{4,3,2,1,0:T(8,128)}, f32[256,256]{1,0:T(8,128)S(1)}) custom-call(s32[1]{0:T(128)} %bitcast.refs_0_, bf16[144,768]{1,0:T(8,128)(2,1)S(1)} %get-tuple-element.34.refs_1_, bf16[144,768]{1,0:T(8,128)(2,1)S(1)} %collective-permute-done.1.refs_2_, ...), custom_call_target="tpu_custom_call", output_to_operand_aliasing={{0}: (6, {})} | custom-call | flops 1000 | bytes 1000 | tf_op jit(solution)/shard_map/assemble/pallas_call | solution.py:610
  52.0 2.3 %rotate_dft.6 = (bf16[144,256]{1,0:T(8,128)(2,1)S(1)}, bf16[144,256]{1,0:T(8,128)(2,1)S(1)}, bf16[112,256]{1,0:T(8,128)(2,1)S(1)}, bf16[112,256]{1,0:T(8,128)(2,1)S(1)}) custom-call(bf16[48,2048]{1,0:T(8,128)(2,1)S(1)} %collective-permute-done.refs_0_, s32[1,2048]{1,0:T(1,128)S(1)} %bitcast.9, bf16[3,1072,2048]{2,1,0:T(8,128)(2,1)} %bitcast.14, ...), custom_call_target="tpu_custom_call" | custom-call | flops 316145664 | bytes 1646592 | tf_op jit(solution)/shard_map/rotate_dft/pallas_call | solution.py:515
  54.3 1.3 %collective-permute-start.7 = (bf16[144,256]{1,0:T(8,128)(2,1)S(1)}, bf16[144,256]{1,0:T(8,128)(2,1)S(1)}, u32[]{:S(2)}, u32[]{:S(2)}) collective-permute-start(bf16[144,256]{1,0:T(8,128)(2,1)S(1)} %get-tuple-element.46), channel_id=1, source_target_pairs={{0,1},{1,0},{2,3},{3,2},{4,5},{5,4},{6,7},{7,6},{8,9},{9,8},{10,11... | collective-permute-start | bytes 221192 | tf_op jit(solution)/shard_map/ppermute | solution.py:641
  55.6 1.4 %collective-permute-start.8 = (bf16[112,256]{1,0:T(8,128)(2,1)S(1)}, bf16[112,256]{1,0:T(8,128)(2,1)S(1)}, u32[]{:S(2)}, u32[]{:S(2)}) collective-permute-start(bf16[112,256]{1,0:T(8,128)(2,1)S(1)} %get-tuple-element.47), channel_id=1, source_target_pairs={{0,2},{1,3},{2,0},{3,1},{4,6},{5,7},{6,4},{7,5},{8,10},{9,11},{10,... | collective-permute-start | bytes 172040 | tf_op jit(solution)/shard_map/ppermute | solution.py:641
  57.0 1.8 %collective-permute-start.9 = (bf16[112,256]{1,0:T(8,128)(2,1)S(1)}, bf16[112,256]{1,0:T(8,128)(2,1)S(1)}, u32[]{:S(2)}, u32[]{:S(2)}) collective-permute-start(bf16[112,256]{1,0:T(8,128)(2,1)S(1)} %get-tuple-element.48), channel_id=1, source_target_pairs={{0,3},{1,2},{2,1},{3,0},{4,7},{5,6},{6,5},{7,4},{8,11},{9,10},{10,... | collective-permute-start | bytes 172040 | tf_op jit(solution)/shard_map/ppermute | solution.py:641
  58.8 1.9 %assemble.6 = (f32[2,2,3,32,2048]{4,3,2,1,0:T(8,128)}, f32[256,256]{1,0:T(8,128)S(1)}) custom-call(s32[1]{0:T(128)} %bitcast.refs_0_, bf16[144,512]{1,0:T(8,128)(2,1)S(1)} %get-tuple-element.49.refs_1_, bf16[144,512]{1,0:T(8,128)(2,1)S(1)} %collective-permute-done.10.refs_2_, ...), custom_call_target="tpu_custom_call", output_to_operand_aliasing={{0}: (6, {})} | custom-call | flops 1000 | bytes 1000 | tf_op jit(solution)/shard_map/assemble/pallas_call | solution.py:610
  60.7 2.4 %collective-permute-done.9.refs_4_ = bf16[112,256]{1,0:T(8,128)(2,1)S(1)} collective-permute-done((bf16[112,256]{1,0:T(8,128)(2,1)S(1)}, bf16[112,256]{1,0:T(8,128)(2,1)S(1)}, u32[]{:S(2)}, u32[]{:S(2)}) %collective-permute-start.9) | collective-permute-done | bytes 57376 | tf_op jit(solution)/shard_map/ppermute | solution.py:641
  63.1 1.0 %assemble.7 = (f32[2,2,3,32,2048]{4,3,2,1,0:T(8,128)}, f32[64,128]{1,0:T(8,128)S(1)}) custom-call(s32[1]{0:T(128)} %bitcast.refs_0_, bf16[144,256]{1,0:T(8,128)(2,1)S(1)} %get-tuple-element.45.refs_1_, bf16[144,256]{1,0:T(8,128)(2,1)S(1)} %collective-permute-done.7.refs_2_, ...), custom_call_target="tpu_custom_call", output_to_operand_aliasing={{0}: (6, {})} | custom-call | flops 1000 | bytes 1000 | tf_op jit(solution)/shard_map/assemble/pallas_call | solution.py:610
  64.1 1.2 %collective-permute-done.13 = f32[64,128]{1,0:T(8,128)S(1)} collective-permute-done((f32[64,128]{1,0:T(8,128)S(1)}, f32[64,128]{1,0:T(8,128)S(1)}, u32[]{:S(2)}, u32[]{:S(2)}) %collective-permute-start.13) | collective-permute-done | bytes 32800 | tf_op jit(solution)/shard_map/ppermute | solution.py:679
  65.3 1.7 %collective-permute-start.14 = (f32[64,128]{1,0:T(8,128)S(1)}, f32[64,128]{1,0:T(8,128)S(1)}, u32[]{:S(2)}, u32[]{:S(2)}) collective-permute-start(f32[64,128]{1,0:T(8,128)S(1)} %add.6), channel_id=1, source_target_pairs={{0,8},{4,12},{8,0},{12,4},{16,24},{20,28},{24,16},{28,20},{1,9},{5... | collective-permute-start | bytes 98312 | tf_op jit(solution)/shard_map/ppermute | solution.py:679
  67.0 2.2 %collective-permute-done.14 = f32[64,128]{1,0:T(8,128)S(1)} collective-permute-done((f32[64,128]{1,0:T(8,128)S(1)}, f32[64,128]{1,0:T(8,128)S(1)}, u32[]{:S(2)}, u32[]{:S(2)}) %collective-permute-start.14) | collective-permute-done | bytes 32800 | tf_op jit(solution)/shard_map/ppermute | solution.py:679
  69.2 1.8 %collective-permute-start.15 = (f32[64,128]{1,0:T(8,128)S(1)}, f32[64,128]{1,0:T(8,128)S(1)}, u32[]{:S(2)}, u32[]{:S(2)}) collective-permute-start(f32[64,128]{1,0:T(8,128)S(1)} %add.7.refs_0_), channel_id=1, source_target_pairs={{0,16},{4,20},{8,24},{12,28},{16,0},{20,4},{24,8},{28,12},{1,17},{... | collective-permute-start | bytes 98312 | tf_op jit(solution)/shard_map/ppermute | solution.py:679
  71.0 2.2 %collective-permute-done.15.refs_1_ = f32[64,128]{1,0:T(8,128)S(1)} collective-permute-done((f32[64,128]{1,0:T(8,128)S(1)}, f32[64,128]{1,0:T(8,128)S(1)}, u32[]{:S(2)}, u32[]{:S(2)}) %collective-permute-start.15) | collective-permute-done | bytes 32800 | tf_op jit(solution)/shard_map/ppermute | solution.py:679
  73.2 0.6 copy-done.9
  73.8 3.7 %factor.1 = f32[2,64,64]{2,1,0:T(8,128)} custom-call(f32[64,128]{1,0:T(8,128)} %copy-done.8, f32[64,128]{1,0:T(8,128)} %copy-done.9), custom_call_target="tpu_custom_call" | custom-call | tf_op jit(solution)/shard_map/factor/pallas_call | solution.py:303
  (31 shorter events, 0.7 us)
Async XLA Ops:
  0.6 20.0 %copy-start.6 = (s32[2048]{0:T(1024)S(1)}, s32[2048]{0:T(1024)}, u32[]{:S(2)}) copy-start(s32[2048]{0:T(1024)} %param.6) | copy-start | bytes 24580
  7.3 13.4 %collective-permute-start = (bf16[48,2048]{1,0:T(8,128)(2,1)}, bf16[48,2048]{1,0:T(8,128)(2,1)S(1)}, u32[]{:S(2)}, u32[]{:S(2)}) collective-permute-start(bf16[48,2048]{1,0:T(8,128)(2,1)} %get-tuple-element.30), channel_id=1, source_target_pairs={{1,0},{2,3},{5,4},{6,7},{9,8},{10,11},{13,12},{14,15},{17,16},{18,... | collective-permute-start | bytes 589832 | tf_op jit(solution)/shard_map/ppermute | solution.py:641
  8.6 23.3 %collective-permute-start.4 = (bf16[144,512]{1,0:T(8,128)(2,1)}, bf16[144,512]{1,0:T(8,128)(2,1)S(1)}, u32[]{:S(2)}, u32[]{:S(2)}) collective-permute-start(bf16[144,512]{1,0:T(8,128)(2,1)} %get-tuple-element.39), channel_id=1, source_target_pairs={{0,1},{1,0},{2,3},{3,2},{4,5},{5,4},{6,7},{7,6},{8,9},{9,8},{10,11... | collective-permute-start | bytes 442376 | tf_op jit(solution)/shard_map/ppermute | solution.py:641
  11.7 21.3 %collective-permute-start.5 = (bf16[144,512]{1,0:T(8,128)(2,1)}, bf16[144,512]{1,0:T(8,128)(2,1)S(1)}, u32[]{:S(2)}, u32[]{:S(2)}) collective-permute-start(bf16[144,512]{1,0:T(8,128)(2,1)} %get-tuple-element.40), channel_id=1, source_target_pairs={{0,2},{1,3},{2,0},{3,1},{4,6},{5,7},{6,4},{7,5},{8,10},{9,11},{10,... | collective-permute-start | bytes 442376 | tf_op jit(solution)/shard_map/ppermute | solution.py:641
  14.9 18.0 %collective-permute-start.6 = (bf16[144,512]{1,0:T(8,128)(2,1)}, bf16[144,512]{1,0:T(8,128)(2,1)S(1)}, u32[]{:S(2)}, u32[]{:S(2)}) collective-permute-start(bf16[144,512]{1,0:T(8,128)(2,1)} %get-tuple-element.41), channel_id=1, source_target_pairs={{0,3},{1,2},{2,1},{3,0},{4,7},{5,6},{6,5},{7,4},{8,11},{9,10},{10,... | collective-permute-start | bytes 442376 | tf_op jit(solution)/shard_map/ppermute | solution.py:641
  20.7 1.1 %copy-start = (f32[1072,128]{1,0:T(8,128)S(1)}, f32[1072,128]{1,0:T(8,128)}, u32[]{:S(2)}) copy-start(f32[1072,128]{1,0:T(8,128)} %get-tuple-element.32.refs_4_) | copy-start | bytes 1646596
  21.7 1.1 %copy-start.2 = (f32[1072,128]{1,0:T(8,128)S(1)}, f32[1072,128]{1,0:T(8,128)}, u32[]{:S(2)}) copy-start(f32[1072,128]{1,0:T(8,128)} %get-tuple-element.33.refs_5_) | copy-start | bytes 1646596
  22.8 1.0 %copy-start.4 = (bf16[176,1072]{1,0:T(8,128)(2,1)S(1)}, bf16[176,1072]{1,0:T(8,128)(2,1)}, u32[]{:S(2)}) copy-start(bf16[176,1072]{1,0:T(8,128)(2,1)} %get-tuple-element.31.refs_3_) | copy-start | bytes 1132036
  23.8 9.2 %copy-start.7 = (bf16[144,512]{1,0:T(8,128)(2,1)S(1)}, bf16[144,512]{1,0:T(8,128)(2,1)}, u32[]{:S(2)}) copy-start(bf16[144,512]{1,0:T(8,128)(2,1)} %get-tuple-element.38.refs_1_) | copy-start | bytes 442372
  23.8 11.1 %copy-start.1 = (f32[1072,128]{1,0:T(8,128)S(1)}, f32[1072,128]{1,0:T(8,128)}, u32[]{:S(2)}) copy-start(f32[1072,128]{1,0:T(8,128)} %get-tuple-element.32.refs_4_) | copy-start | bytes 1646596
  23.8 11.1 %copy-start.5 = (bf16[176,1072]{1,0:T(8,128)(2,1)S(1)}, bf16[176,1072]{1,0:T(8,128)(2,1)}, u32[]{:S(2)}) copy-start(bf16[176,1072]{1,0:T(8,128)(2,1)} %get-tuple-element.31.refs_3_) | copy-start | bytes 1132036
  28.5 20.9 %collective-permute-start.1 = (bf16[144,768]{1,0:T(8,128)(2,1)S(1)}, bf16[144,768]{1,0:T(8,128)(2,1)S(1)}, u32[]{:S(2)}, u32[]{:S(2)}) collective-permute-start(bf16[144,768]{1,0:T(8,128)(2,1)S(1)} %get-tuple-element.35), channel_id=1, source_target_pairs={{0,1},{1,0},{2,3},{3,2},{4,5},{5,4},{6,7},{7,6},{8,9},{9,8},{10,11... | collective-permute-start | bytes 663560 | tf_op jit(solution)/shard_map/ppermute | solution.py:641
  28.6 17.8 %collective-permute-start.2 = (bf16[112,768]{1,0:T(8,128)(2,1)S(1)}, bf16[112,768]{1,0:T(8,128)(2,1)S(1)}, u32[]{:S(2)}, u32[]{:S(2)}) collective-permute-start(bf16[112,768]{1,0:T(8,128)(2,1)S(1)} %get-tuple-element.36), channel_id=1, source_target_pairs={{0,2},{1,3},{2,0},{3,1},{4,6},{5,7},{6,4},{7,5},{8,10},{9,11},{10,... | collective-permute-start | bytes 516104 | tf_op jit(solution)/shard_map/ppermute | solution.py:641
  31.9 17.6 %collective-permute-start.3 = (bf16[112,768]{1,0:T(8,128)(2,1)S(1)}, bf16[112,768]{1,0:T(8,128)(2,1)S(1)}, u32[]{:S(2)}, u32[]{:S(2)}) collective-permute-start(bf16[112,768]{1,0:T(8,128)(2,1)S(1)} %get-tuple-element.37), channel_id=1, source_target_pairs={{0,3},{1,2},{2,1},{3,0},{4,7},{5,6},{6,5},{7,4},{8,11},{9,10},{10,... | collective-permute-start | bytes 516104 | tf_op jit(solution)/shard_map/ppermute | solution.py:641
  38.0 14.0 %copy-start.3 = (f32[1072,128]{1,0:T(8,128)S(1)}, f32[1072,128]{1,0:T(8,128)}, u32[]{:S(2)}) copy-start(f32[1072,128]{1,0:T(8,128)} %get-tuple-element.33.refs_5_) | copy-start | bytes 1646596
  38.0 19.0 %collective-permute-start.11 = (bf16[112,512]{1,0:T(8,128)(2,1)S(1)}, bf16[112,512]{1,0:T(8,128)(2,1)S(1)}, u32[]{:S(2)}, u32[]{:S(2)}) collective-permute-start(bf16[112,512]{1,0:T(8,128)(2,1)S(1)} %get-tuple-element.51), channel_id=1, source_target_pairs={{0,2},{1,3},{2,0},{3,1},{4,6},{5,7},{6,4},{7,5},{8,10},{9,11},{10,... | collective-permute-start | bytes 344072 | tf_op jit(solution)/shard_map/ppermute | solution.py:641
  38.6 20.2 %collective-permute-start.10 = (bf16[144,512]{1,0:T(8,128)(2,1)S(1)}, bf16[144,512]{1,0:T(8,128)(2,1)S(1)}, u32[]{:S(2)}, u32[]{:S(2)}) collective-permute-start(bf16[144,512]{1,0:T(8,128)(2,1)S(1)} %get-tuple-element.50), channel_id=1, source_target_pairs={{0,1},{1,0},{2,3},{3,2},{4,5},{5,4},{6,7},{7,6},{8,9},{9,8},{10,11... | collective-permute-start | bytes 442376 | tf_op jit(solution)/shard_map/ppermute | solution.py:641
  46.4 12.4 %collective-permute-start.12 = (bf16[112,512]{1,0:T(8,128)(2,1)S(1)}, bf16[112,512]{1,0:T(8,128)(2,1)S(1)}, u32[]{:S(2)}, u32[]{:S(2)}) collective-permute-start(bf16[112,512]{1,0:T(8,128)(2,1)S(1)} %get-tuple-element.52), channel_id=1, source_target_pairs={{0,3},{1,2},{2,1},{3,0},{4,7},{5,6},{6,5},{7,4},{8,11},{9,10},{10,... | collective-permute-start | bytes 344072 | tf_op jit(solution)/shard_map/ppermute | solution.py:641
  54.3 8.8 %collective-permute-start.7 = (bf16[144,256]{1,0:T(8,128)(2,1)S(1)}, bf16[144,256]{1,0:T(8,128)(2,1)S(1)}, u32[]{:S(2)}, u32[]{:S(2)}) collective-permute-start(bf16[144,256]{1,0:T(8,128)(2,1)S(1)} %get-tuple-element.46), channel_id=1, source_target_pairs={{0,1},{1,0},{2,3},{3,2},{4,5},{5,4},{6,7},{7,6},{8,9},{9,8},{10,11... | collective-permute-start | bytes 221192 | tf_op jit(solution)/shard_map/ppermute | solution.py:641
  55.6 5.1 %collective-permute-start.8 = (bf16[112,256]{1,0:T(8,128)(2,1)S(1)}, bf16[112,256]{1,0:T(8,128)(2,1)S(1)}, u32[]{:S(2)}, u32[]{:S(2)}) collective-permute-start(bf16[112,256]{1,0:T(8,128)(2,1)S(1)} %get-tuple-element.47), channel_id=1, source_target_pairs={{0,2},{1,3},{2,0},{3,1},{4,6},{5,7},{6,4},{7,5},{8,10},{9,11},{10,... | collective-permute-start | bytes 172040 | tf_op jit(solution)/shard_map/ppermute | solution.py:641
  57.0 6.1 %collective-permute-start.9 = (bf16[112,256]{1,0:T(8,128)(2,1)S(1)}, bf16[112,256]{1,0:T(8,128)(2,1)S(1)}, u32[]{:S(2)}, u32[]{:S(2)}) collective-permute-start(bf16[112,256]{1,0:T(8,128)(2,1)S(1)} %get-tuple-element.48), channel_id=1, source_target_pairs={{0,3},{1,2},{2,1},{3,0},{4,7},{5,6},{6,5},{7,4},{8,11},{9,10},{10,... | collective-permute-start | bytes 172040 | tf_op jit(solution)/shard_map/ppermute | solution.py:641
  64.1 1.2 %collective-permute-start.13 = (f32[64,128]{1,0:T(8,128)S(1)}, f32[64,128]{1,0:T(8,128)S(1)}, u32[]{:S(2)}, u32[]{:S(2)}) collective-permute-start(f32[64,128]{1,0:T(8,128)S(1)} %get-tuple-element.57), channel_id=1, source_target_pairs={{0,4},{4,0},{8,12},{12,8},{16,20},{20,16},{24,28},{28,24},{1,5},{5... | collective-permute-start | bytes 98312 | tf_op jit(solution)/shard_map/ppermute | solution.py:679
  65.3 3.9 %collective-permute-start.14 = (f32[64,128]{1,0:T(8,128)S(1)}, f32[64,128]{1,0:T(8,128)S(1)}, u32[]{:S(2)}, u32[]{:S(2)}) collective-permute-start(f32[64,128]{1,0:T(8,128)S(1)} %add.6), channel_id=1, source_target_pairs={{0,8},{4,12},{8,0},{12,4},{16,24},{20,28},{24,16},{28,20},{1,9},{5... | collective-permute-start | bytes 98312 | tf_op jit(solution)/shard_map/ppermute | solution.py:679
  69.2 4.0 %copy-start.8 = (f32[64,128]{1,0:T(8,128)}, f32[64,128]{1,0:T(8,128)S(1)}, u32[]{:S(2)}) copy-start(f32[64,128]{1,0:T(8,128)S(1)} %add.7.refs_0_) | copy-start | bytes 98308
  69.2 4.0 %collective-permute-start.15 = (f32[64,128]{1,0:T(8,128)S(1)}, f32[64,128]{1,0:T(8,128)S(1)}, u32[]{:S(2)}, u32[]{:S(2)}) collective-permute-start(f32[64,128]{1,0:T(8,128)S(1)} %add.7.refs_0_), channel_id=1, source_target_pairs={{0,16},{4,20},{8,24},{12,28},{16,0},{20,4},{24,8},{28,12},{1,17},{... | collective-permute-start | bytes 98312 | tf_op jit(solution)/shard_map/ppermute | solution.py:679
  73.2 0.6 copy-start.9

commit v5 on v4

--- a/solution.py
+++ b/solution.py
@@ -15,6 +15,7 @@
 LANES = 128
 TILE = 256
 PIVOT = 4
+LIMIT_A, LIMIT_B, LIMIT_C = 60, 60, 40
 SCALE = (8.0 / (3.0 * NFFT)) ** 0.5
 HIGHEST = lax.Precision.HIGHEST
 SHORT = pl.CostEstimate(flops=1000, bytes_accessed=1000, transcendentals=0)
@@ -408,124 +409,130 @@
     return (cosine_of(turns) * w).astype(jnp.bfloat16)
 
 
-def line_dft_body(span, blocks, first, *refs):
-    if first:
-        pos_ref, starts_ref, freqs_ref, angle_ref, mask_ref, vel_ref, all_mask_ref, all_hbm = refs[:8]
-        out_refs = refs[8:12]
-        part_ref = refs[12]
-        shared_refs = refs[13:16]
-        rot_ref, a_ref, rows_ref, ends_ref, ends_rot_ref, ends_sem = refs[16:]
-        _, cos_ref, sin_ref = shared_refs
-
-        @pl.when(pl.program_id(0) == 0)
-        def _():
-            me = pos_ref[0]
-            begin = pl.multiple_of(jnp.where(me == 2, span - REACH, 0), 16)
-            load = pltpu.make_async_copy(all_hbm.at[:, pl.ds(begin, REACH), :], ends_ref, ends_sem)
-            load.start()
-            build_line(span, blocks, me, starts_ref, freqs_ref, a_ref, shared_refs[0], rows_ref)
-            spread_column(jnp.cos(angle_ref[...].reshape(1, span)), span, cos_ref)
-            spread_column(jnp.sin(angle_ref[...].reshape(1, span)), span, sin_ref)
-            rows = shared_rows(begin + me * span, me, starts_ref, freqs_ref)
-            load.wait()
-            for lane in range(0, part_ref.shape[1], TILE):
-                here = slice(lane, lane + TILE)
-                turning = all_mask_ref[:, here] == 1
-                for at in range(0, REACH, 16):
-                    row = slice(at, at + 16)
-                    t = pl.ds(pl.multiple_of(begin + at, 16), 16)
-                    new_x, new_y = rotate(
-                        turning, cos_ref[t, :], sin_ref[t, :], ends_ref[0, row, here], ends_ref[1, row, here]
-                    )
-                    ends_rot_ref[0, row, here] = new_x
-                    ends_rot_ref[1, row, here] = new_y
-                for c in range(COMPS):
-                    samples = ends_rot_ref[c, :, here] if c < 2 else ends_ref[2, :, here]
-                    sums = jnp.dot(rows, samples, preferred_element_type=jnp.float32)
-                    part_ref[16 * c:16 * c + 16, here] = sums.astype(jnp.bfloat16)
-    else:
-        part_ref, mask_ref, vel_ref, a_ref, cos_ref, sin_ref = refs[:6]
-        own_ref, near_ref, far2_ref, far3_ref, rot_ref = refs[7:]
+def prepare_body(span, blocks, pos_ref, starts_ref, freqs_ref, angle_ref, mask_ref, all_hbm,
+                 part_ref, direct_ref, a_ref, cos_ref, sin_ref, rows_ref, ends_ref, ends_rot_ref, ends_sem):
+    me = pos_ref[0]
+    begin = pl.multiple_of(jnp.where(me == 2, span - REACH, 0), 16)
+    load = pltpu.make_async_copy(all_hbm.at[:, pl.ds(begin, REACH), :], ends_ref, ends_sem)
+    load.start()
+    build_line(span, blocks, me, starts_ref, freqs_ref, direct_ref, a_ref, rows_ref)
+    spread_column(jnp.cos(angle_ref[...].reshape(1, span)), span, cos_ref)
+    spread_column(jnp.sin(angle_ref[...].reshape(1, span)), span, sin_ref)
+    rows = shared_rows(begin + me * span, me, starts_ref, freqs_ref)
+    load.wait()
+    for lane in range(0, part_ref.shape[1], TILE):
+        here = slice(lane, lane + TILE)
+        turning = mask_ref[:, here] == 1
+        for at in range(0, REACH, 16):
+            row = slice(at, at + 16)
+            t = pl.ds(pl.multiple_of(begin + at, 16), 16)
+            new_x, new_y = rotate(
+                turning, cos_ref[t, :], sin_ref[t, :], ends_ref[0, row, here], ends_ref[1, row, here]
+            )
+            ends_rot_ref[0, row, here] = new_x
+            ends_rot_ref[1, row, here] = new_y
+        for c in range(COMPS):
+            samples = ends_rot_ref[c, :, here] if c < 2 else ends_ref[2, :, here]
+            sums = jnp.dot(rows, samples, preferred_element_type=jnp.float32)
+            part_ref[16 * c:16 * c + 16, here] = sums.astype(jnp.bfloat16)
+
+
+def prepare(blocks, position, starts, freqs, angles, mask, velocity):
+    span, points = velocity.shape[1:]
+    smem, vmem, anywhere = (pl.BlockSpec(memory_space=m) for m in (pltpu.SMEM, pltpu.VMEM, pl.ANY))
+    whole = lambda shape: pl.BlockSpec(shape, lambda i: (0,) * len(shape))
+    types = [
+        jax.ShapeDtypeStruct((48, points), jnp.bfloat16),
+        jax.ShapeDtypeStruct((192, span), jnp.bfloat16),
+        jax.ShapeDtypeStruct((176, span), jnp.bfloat16),
+        jax.ShapeDtypeStruct((span, LANES), jnp.float32),
+        jax.ShapeDtypeStruct((span, LANES), jnp.float32),
+    ]
+    return pl.pallas_call(
+        functools.partial(prepare_body, span, blocks),
+        grid=(1,),
+        out_shape=types,
+        in_specs=[smem] * 3 + [whole((span,)), whole((1, points)), anywhere],
+        out_specs=[whole(t.shape) for t in types],
+        scratch_shapes=[
+            pltpu.VMEM((WIDE, 8, span), jnp.float32),
+            pltpu.VMEM((COMPS, REACH, points), jnp.bfloat16),
+            pltpu.VMEM((2, REACH, points), jnp.bfloat16),
+            pltpu.SemaphoreType.DMA,
+        ],
+        compiler_params=pltpu.CompilerParams(vmem_limit_bytes=LIMIT_A * 2**20),
+        cost_estimate=pl.CostEstimate(flops=10**9, bytes_accessed=4 * 10**6, transcendentals=0),
+        name="prepare",
+    )(position, starts, freqs, angles, mask, velocity)
+
+
+def line_dft_body(span, direct, *refs):
+    mask_ref, vel_ref, a_ref, cos_ref, sin_ref = refs[:5]
+    own_ref, near_ref, far2_ref, far3_ref, rot_ref = refs[-5:]
+    part_ref = None if direct else refs[5]
     width = vel_ref.shape[2]
+    none = jnp.zeros((24, width), jnp.float32)
+    tails = [None] * COMPS
+
+    def send(c, samples):
+        sums = jnp.dot(a_ref[...], samples, preferred_element_type=jnp.float32)
+        own_ref[48 * c:48 * c + 48, :] = sums[:48].astype(jnp.bfloat16)
+        near_ref[48 * c:48 * c + 48, :] = sums[48:96].astype(jnp.bfloat16)
+        if direct:
+            far2_ref[48 * c:48 * c + 48, :] = sums[96:144].astype(jnp.bfloat16)
+            far3_ref[48 * c:48 * c + 48, :] = sums[144:].astype(jnp.bfloat16)
+        else:
+            part = part_ref[16 * c:16 * c + 16, :].astype(jnp.float32)
+            far2 = sums[96:128] + jnp.concatenate([none, part[:8]], axis=0)
+            far3 = sums[128:160] + jnp.concatenate([none, part[8:]], axis=0)
+            far2_ref[32 * c:32 * c + 32, :] = far2.astype(jnp.bfloat16)
+            far3_ref[32 * c:32 * c + 32, :] = far3.astype(jnp.bfloat16)
+            tails[c] = sums[160:168]
+
+    send(2, vel_ref[2])
     turning = mask_ref[...] == 1
     for at in range(0, span, 16):
         here = pl.ds(at, min(16, span - at))
         new_x, new_y = rotate(turning, cos_ref[here, :], sin_ref[here, :], vel_ref[0, here, :], vel_ref[1, here, :])
         rot_ref[0, here, :] = new_x
         rot_ref[1, here, :] = new_y
-    tails = []
-    none = jnp.zeros((24, width), jnp.float32)
-    for c in range(COMPS):
-        samples = rot_ref[c] if c < 2 else vel_ref[2]
-        sums = jnp.dot(a_ref[...], samples, preferred_element_type=jnp.float32)
-        if first:
-            for k, ref in enumerate(out_refs):
-                ref[48 * c:48 * c + 48, :] = sums[48 * k:48 * k + 48].astype(jnp.bfloat16)
-            continue
-        own_ref[48 * c:48 * c + 48, :] = sums[:48].astype(jnp.bfloat16)
-        near_ref[48 * c:48 * c + 48, :] = sums[48:96].astype(jnp.bfloat16)
-        part = part_ref[16 * c:16 * c + 16, :].astype(jnp.float32)
-        far2 = sums[96:128] + jnp.concatenate([none, part[:8]], axis=0)
-        far3 = sums[128:160] + jnp.concatenate([none, part[8:]], axis=0)
-        far2_ref[32 * c:32 * c + 32, :] = far2.astype(jnp.bfloat16)
-        far3_ref[32 * c:32 * c + 32, :] = far3.astype(jnp.bfloat16)
-        tails.append(sums[160:168])
-    if not first:
+    send(0, rot_ref[0])
+    send(1, rot_ref[1])
+    if not direct:
         far2_ref[96:112, :] = jnp.concatenate([t[:4] for t in tails] + [none[:4]], axis=0).astype(jnp.bfloat16)
         far3_ref[96:112, :] = jnp.concatenate([t[4:] for t in tails] + [none[:4]], axis=0).astype(jnp.bfloat16)
 
 
-def line_dft(blocks, offset, points, position, starts, freqs, angles, mask, velocity, shared, part, after):
-    first = shared is None
-    span, all_points = velocity.shape[1:]
+def line_dft(offset, points, mask, velocity, rows, cosine, sine, part, after):
+    span = velocity.shape[1]
     shift = offset // TILE
+    direct = part is None
     whole = lambda shape: pl.BlockSpec(shape, lambda i: (0,) * len(shape))
-    smem = pl.BlockSpec(memory_space=pltpu.SMEM)
-    data_specs = [
+    args = [mask, velocity, rows, cosine, sine]
+    in_specs = [
         pl.BlockSpec((1, TILE), lambda i: (0, i + shift)),
         pl.BlockSpec((COMPS, span, TILE), lambda i: (0, 0, i + shift)),
-    ]
-    shared_types = [
-        jax.ShapeDtypeStruct((176, span), jnp.bfloat16),
-        jax.ShapeDtypeStruct((span, LANES), jnp.float32),
-        jax.ShapeDtypeStruct((span, LANES), jnp.float32),
-    ]
-    shared_specs = [whole(t.shape) for t in shared_types]
-    heights = [144] * 4 if first else [144, 144, 112, 112]
-    out_types = [jax.ShapeDtypeStruct((h, points), jnp.bfloat16) for h in heights]
-    out_specs = [pl.BlockSpec((h, TILE), lambda i: (0, i)) for h in heights]
-    scratch = [pltpu.VMEM((2, span, TILE), jnp.bfloat16)]
-    if first:
-        args = (position, starts, freqs, angles, mask, velocity, mask, velocity)
-        in_specs = [smem] * 3 + [whole((span,))] + data_specs
-        in_specs += [whole((1, all_points)), pl.BlockSpec(memory_space=pl.ANY)]
-        out_types += [jax.ShapeDtypeStruct((48, all_points), jnp.bfloat16)] + shared_types
-        out_specs += [whole((48, all_points))] + shared_specs
-        scratch += [
-            pltpu.VMEM((192, span), jnp.bfloat16),
-            pltpu.VMEM((WIDE, 8, span), jnp.float32),
-            pltpu.VMEM((COMPS, REACH, all_points), jnp.bfloat16),
-            pltpu.VMEM((2, REACH, all_points), jnp.bfloat16),
-            pltpu.SemaphoreType.DMA,
-        ]
-    else:
-        args = (part, mask, velocity) + tuple(shared) + (after,)
-        in_specs = [pl.BlockSpec((48, TILE), lambda i: (0, i + shift))] + data_specs + shared_specs
+    ] + [whole(x.shape) for x in args[2:]]
+    if not direct:
+        args.append(part)
+        in_specs.append(pl.BlockSpec((48, TILE), lambda i: (0, i + shift)))
+    if after is not None:
+        args.append(after)
         in_specs.append(pl.BlockSpec(memory_space=pl.ANY))
-    out = pl.pallas_call(
-        functools.partial(line_dft_body, span, blocks, first),
+    heights = [144] * 4 if direct else [144, 144, 112, 112]
+    return pl.pallas_call(
+        functools.partial(line_dft_body, span, direct),
         grid=(points // TILE,),
-        out_shape=out_types,
+        out_shape=[jax.ShapeDtypeStruct((h, points), jnp.bfloat16) for h in heights],
         in_specs=in_specs,
-        out_specs=out_specs,
-        scratch_shapes=scratch,
-        compiler_params=pltpu.CompilerParams(vmem_limit_bytes=(60 if first else 40) * 2**20),
+        out_specs=[pl.BlockSpec((h, TILE), lambda i: (0, i)) for h in heights],
+        scratch_shapes=[pltpu.VMEM((2, span, TILE), jnp.bfloat16)],
+        compiler_params=pltpu.CompilerParams(vmem_limit_bytes=LIMIT_B * 2**20),
         cost_estimate=pl.CostEstimate(
             flops=2 * 192 * span * COMPS * points, bytes_accessed=2 * COMPS * span * points, transcendentals=0
         ),
         name="rotate_dft",
     )(*args)
-    return (out[:4], out[4], out[5:]) if first else (out, part, shared)
 
 
 def line_selection(blocks, me, direct, sel_ref):
@@ -553,7 +560,7 @@
     rest = refs[5:]
     if has_sum:
         sum_in, rest = rest[0], rest[2:]
-    spectra_ref, gram_ref, sel_ref, acc_ref = rest
+    spectra_ref, gram_ref, sel_ref, acc_ref = rest[-4:]
     step = pl.program_id(0)
     me = pos_ref[0]
 
@@ -593,7 +600,7 @@
             gram_ref[...] = jnp.concatenate([gram[:order, :order], gram[order:, order:]], axis=1)
 
 
-def line_assemble(blocks, total, offset, points, all_points, position, own, near, fars, spectra, gram, last):
+def line_assemble(blocks, total, offset, points, all_points, position, own, near, fars, spectra, gram, last, after):
     shift = offset // TILE
     order = 2 * blocks
     has_sum = gram is not None
@@ -607,6 +614,9 @@
         args += [gram, spectra]
         in_specs += [whole((4 * order, 4 * order)), pl.BlockSpec(memory_space=pl.ANY)]
         aliases = {len(args) - 1: 0}
+    if after is not None:
+        args.append(after)
+        in_specs.append(pl.BlockSpec(memory_space=pl.ANY))
     return pl.pallas_call(
         functools.partial(line_assemble_body, blocks, total, has_sum, last, fars[0].shape[0] == 144),
         grid=(points // TILE,),
@@ -624,14 +634,14 @@
             pltpu.VMEM((4 * order, 4 * order), jnp.float32),
         ],
         input_output_aliases=aliases,
-        compiler_params=pltpu.CompilerParams(vmem_limit_bytes=40 * 2**20),
+        compiler_params=pltpu.CompilerParams(vmem_limit_bytes=LIMIT_C * 2**20),
         cost_estimate=SHORT,
         name="assemble",
     )(*args)
 
 
 def line_chunks(points):
-    cuts = [0, points // 4, points * 5 // 8, points * 7 // 8, points]
+    cuts = [points * k // 8 for k in (0, 1, 3, 6, 8)]
     return [(a, b - a) for a, b in zip(cuts[:-1], cuts[1:])]
 
 
@@ -640,28 +650,28 @@
     blocks = block_starts.shape[0]
     move = lambda x, pairs: lax.ppermute(x, "tm", pairs)
     across = lambda x, k: move(x, [(i, i ^ k) for i in range(4)])
-    shared, part = None, None
+    part, direct_rows, rows, cosine, sine = prepare(
+        blocks, position, block_starts, frequencies, angles, mask, samples
+    )
+    part = move(part, [(1, 0), (2, 3)])
     spectra, gram = None, None
     sent = []
 
-    def assemble():
+    def assemble(after):
         at, count, own, near, fars = sent.pop(0)
         return line_assemble(
-            blocks, total, at, count, points, position, own, near, fars, spectra, gram, at + count == points
+            blocks, total, at, count, points, position, own, near, fars, spectra, gram, at + count == points, after
         )
 
     for i, (at, count) in enumerate(line_chunks(points)):
         if i >= 2:
-            spectra, gram = assemble()
-        (own, near, far2, far3), part, shared = line_dft(
-            blocks, at, count, position, block_starts, frequencies, angles, mask, samples, shared, part,
-            gram if i >= 2 else mask,
+            spectra, gram = assemble(own)
+        own, near, far2, far3 = line_dft(
+            at, count, mask, samples, rows if i else direct_rows, cosine, sine, part if i else None, gram
         )
-        if i == 0:
-            part = move(part, [(1, 0), (2, 3)])
         sent.append((at, count, own, across(near, 1), [across(far2, 2), across(far3, 3)]))
     while sent:
-        spectra, gram = assemble()
+        spectra, gram = assemble(None)
     return spectra, gram
 
 

time: 78 us -> 75.3 us (0.965)
  waiting for transfers between devices: 17.5 us -> 11.2 us
  Pallas kernels: 27.9 us -> 33.9 us
  starting transfers between devices: 27.8 us -> 24.5 us
  local copies, waits for them, and re-layouts: 3.72 us -> 4.58 us
    ppermute x13, waiting for transfers between devices: 11.8 us -> 5.22 us  [line_spectra(): move = lambda x, pairs: lax.ppermute(x, 'tm', pairs)]
    pallas_call x4 -> x5, Pallas kernels: 16.8 us -> 22.7 us  [the longest x4 18.9 us: line_dft(): pl.pallas_call(functools.partial(line_dft_body, span, direct), grid=(poin...]
    ppermute x13, starting transfers between devices: 24.3 us -> 21.5 us  [line_spectra(): move = lambda x, pairs: lax.ppermute(x, 'tm', pairs)]
    unnamed x20 -> x26, local copies, waits for them, and re-layouts: 3.72 us -> 4.58 us
  transfers between devices with their start and end apart: 16 -> 16, of which waited for: 6 -> 4; matrix products, arithmetic and copies ran while one was open for 0% -> 0% of each run, Pallas kernels for 21% -> 33%
where the time goes in v5:
time: 75.3 us; the launch traced here: 74.9 us
  Pallas kernels  33.9 us (45%)
  starting transfers between devices  24.5 us (33%)
  waiting for transfers between devices  11.2 us (15%)
  local copies, waits for them, and re-layouts  4.58 us (6%)
    ppermute x13, starting transfers between devices, line_spectra(): move = lambda x, pairs: lax.ppermute(x, 'tm', pairs)  21.5 us
    pallas_call x4, Pallas kernels, line_dft(): pl.pallas_call(functools.partial(line_dft_body, span, direct), grid=(poin...  18.9 us
    pallas_call x4, Pallas kernels, line_assemble(): pl.pallas_call(functools.partial(line_assemble_body, blocks, total, has_s...  7.43 us
    ppermute x3, waiting for transfers between devices, sum_over_space(): lax.ppermute(x, 'space', [(i, i ^ k) for i in range(groups)])  6.02 us
    ppermute x13, waiting for transfers between devices, line_spectra(): move = lambda x, pairs: lax.ppermute(x, 'tm', pairs)  5.22 us
    unnamed x26, local copies, waits for them, and re-layouts  4.58 us
    pallas_call x1, Pallas kernels, prepare(): pl.pallas_call(functools.partial(prepare_body, span, blocks), grid=(1,),...  3.83 us
    pallas_call x1, Pallas kernels, factor_call(): pl.pallas_call(functools.partial(factor_body, owned, order, len(parts)),...  3.73 us
  transfers between devices with their start and end apart: 16, of which 4 were waited for; matrix products, arithmetic and copies ran while one was open for 0% of the time, Pallas kernels for 33%

profile of v5, /device:TPU:0, one launch (start us, length us, event | category | flops | bytes accessed | tf_op | source)
XLA Modules:
  0.0 74.9 jit_solution(16242670529659498034)
XLA Ops:
  0.6 3.8 %prepare.1 = (bf16[48,2048]{1,0:T(8,128)(2,1)}, bf16[192,1072]{1,0:T(8,128)(2,1)}, bf16[176,1072]{1,0:T(8,128)(2,1)}, f32[1072,128]{1,0:T(8,128)}, f32[1072,128]{1,0:T(8,128)}) custom-call(s32[1]{0:T(128)} %bitcast.pos_ref.refs_0_, s32[32]{0:T(128)} %starts_ref.1, s32[8]{0:T(128)} %freqs_ref.1, f32[1072]{0:T(1024)} %angle_ref.1, s32[1,2048]{1,0:T(1,128)} %bitcast.10, ...), custom_call_target="tpu_custom_call" | custom-call | flops 1000000000 | bytes 4000000 | tf_op jit(solution)/shard_map/prepare/pallas_call | solution.py:451
  4.5 1.3 %collective-permute-start = (bf16[48,2048]{1,0:T(8,128)(2,1)}, bf16[48,2048]{1,0:T(8,128)(2,1)S(1)}, u32[]{:S(2)}, u32[]{:S(2)}) collective-permute-start(bf16[48,2048]{1,0:T(8,128)(2,1)} %get-tuple-element.34), channel_id=1, source_target_pairs={{1,0},{2,3},{5,4},{6,7},{9,8},{10,11},{13,12},{14,15},{17,16},{18,... | collective-permute-start | bytes 589832 | tf_op jit(solution)/shard_map/ppermute | solution.py:651
  5.8 3.3 %rotate_dft.5 = (bf16[144,256]{1,0:T(8,128)(2,1)}, bf16[144,256]{1,0:T(8,128)(2,1)}, bf16[144,256]{1,0:T(8,128)(2,1)}, bf16[144,256]{1,0:T(8,128)(2,1)}) custom-call(s32[1,2048]{1,0:T(1,128)} %bitcast.11, bf16[3,1072,2048]{2,1,0:T(8,128)(2,1)} %bitcast.5, bf16[192,1072]{1,0:T(8,128)(2,1)} %get-tuple-element.39.refs_2_, ...), custom_call_target="tpu_custom_call" | custom-call | flops 316145664 | bytes 1646592 | tf_op jit(solution)/shard_map/rotate_dft/pallas_call | solution.py:523
  9.1 3.0 %collective-permute-start.4 = (bf16[144,256]{1,0:T(8,128)(2,1)}, bf16[144,256]{1,0:T(8,128)(2,1)S(1)}, u32[]{:S(2)}, u32[]{:S(2)}) collective-permute-start(bf16[144,256]{1,0:T(8,128)(2,1)} %get-tuple-element.41), channel_id=1, source_target_pairs={{0,1},{1,0},{2,3},{3,2},{4,5},{5,4},{6,7},{7,6},{8,9},{9,8},{10,11... | collective-permute-start | bytes 221192 | tf_op jit(solution)/shard_map/ppermute | solution.py:651
  12.1 3.2 %collective-permute-start.5 = (bf16[144,256]{1,0:T(8,128)(2,1)}, bf16[144,256]{1,0:T(8,128)(2,1)S(1)}, u32[]{:S(2)}, u32[]{:S(2)}) collective-permute-start(bf16[144,256]{1,0:T(8,128)(2,1)} %get-tuple-element.42), channel_id=1, source_target_pairs={{0,2},{1,3},{2,0},{3,1},{4,6},{5,7},{6,4},{7,5},{8,10},{9,11},{10,... | collective-permute-start | bytes 221192 | tf_op jit(solution)/shard_map/ppermute | solution.py:651
  15.3 1.4 %collective-permute-start.6 = (bf16[144,256]{1,0:T(8,128)(2,1)}, bf16[144,256]{1,0:T(8,128)(2,1)S(1)}, u32[]{:S(2)}, u32[]{:S(2)}) collective-permute-start(bf16[144,256]{1,0:T(8,128)(2,1)} %get-tuple-element.43), channel_id=1, source_target_pairs={{0,3},{1,2},{2,1},{3,0},{4,7},{5,6},{6,5},{7,4},{8,11},{9,10},{10,... | collective-permute-start | bytes 221192 | tf_op jit(solution)/shard_map/ppermute | solution.py:651
  16.8 0.7 copy-done.10
  17.5 4.7 %rotate_dft.4 = (bf16[144,512]{1,0:T(8,128)(2,1)}, bf16[144,512]{1,0:T(8,128)(2,1)}, bf16[112,512]{1,0:T(8,128)(2,1)}, bf16[112,512]{1,0:T(8,128)(2,1)}) custom-call(s32[1,2048]{1,0:T(1,128)} %bitcast.12, bf16[3,1072,2048]{2,1,0:T(8,128)(2,1)} %bitcast.6, bf16[176,1072]{1,0:T(8,128)(2,1)} %get-tuple-element.31.refs_2_, ...), custom_call_target="tpu_custom_call" | custom-call | flops 632291328 | bytes 3293184 | tf_op jit(solution)/shard_map/rotate_dft/pallas_call | solution.py:523
  22.2 2.0 %collective-permute-start.2 = (bf16[112,512]{1,0:T(8,128)(2,1)}, bf16[112,512]{1,0:T(8,128)(2,1)S(1)}, u32[]{:S(2)}, u32[]{:S(2)}) collective-permute-start(bf16[112,512]{1,0:T(8,128)(2,1)} %get-tuple-element.37), channel_id=1, source_target_pairs={{0,2},{1,3},{2,0},{3,1},{4,6},{5,7},{6,4},{7,5},{8,10},{9,11},{10,... | collective-permute-start | bytes 344072 | tf_op jit(solution)/shard_map/ppermute | solution.py:651
  24.2 0.9 %collective-permute-start.3 = (bf16[112,512]{1,0:T(8,128)(2,1)}, bf16[112,512]{1,0:T(8,128)(2,1)S(1)}, u32[]{:S(2)}, u32[]{:S(2)}) collective-permute-start(bf16[112,512]{1,0:T(8,128)(2,1)} %get-tuple-element.38), channel_id=1, source_target_pairs={{0,3},{1,2},{2,1},{3,0},{4,7},{5,6},{6,5},{7,4},{8,11},{9,10},{10,... | collective-permute-start | bytes 344072 | tf_op jit(solution)/shard_map/ppermute | solution.py:651
  25.7 0.9 %copy-done.6 = bf16[144,512]{1,0:T(8,128)(2,1)S(1)} copy-done((bf16[144,512]{1,0:T(8,128)(2,1)S(1)}, bf16[144,512]{1,0:T(8,128)(2,1)}, u32[]{:S(2)}) %copy-start.6) | copy-done | bytes 147480
  26.6 1.0 %assemble.4 = (f32[2,2,3,32,2048]{4,3,2,1,0:T(8,128)}, f32[256,256]{1,0:T(8,128)S(1)}) custom-call(s32[1]{0:T(128)} %bitcast.pos_ref.refs_0_, bf16[144,256]{1,0:T(8,128)(2,1)S(1)} %copy-done.9, bf16[144,256]{1,0:T(8,128)(2,1)S(1)} %collective-permute-done.4.refs_2_, bf16[144,256]{1,0:T(8,128)(2,1)S(1)} %collective-permute-done.5.refs_3_, ...), custom_call_target="tpu_custom_call" | custom-call | flops 1000 | bytes 1000 | tf_op jit(solution)/shard_map/assemble/pallas_call | solution.py:620
  27.6 0.7 copy-done.2
  28.3 6.2 %rotate_dft.6 = (bf16[144,768]{1,0:T(8,128)(2,1)}, bf16[144,768]{1,0:T(8,128)(2,1)}, bf16[112,768]{1,0:T(8,128)(2,1)}, bf16[112,768]{1,0:T(8,128)(2,1)}) custom-call(s32[1,2048]{1,0:T(1,128)} %bitcast.13, bf16[3,1072,2048]{2,1,0:T(8,128)(2,1)} %bitcast.7, bf16[176,1072]{1,0:T(8,128)(2,1)} %get-tuple-element.31.refs_2_, ...), custom_call_target="tpu_custom_call" | custom-call | flops 948436992 | bytes 4939776 | tf_op jit(solution)/shard_map/rotate_dft/pallas_call | solution.py:523
  34.5 3.0 %collective-permute-start.11 = (bf16[112,768]{1,0:T(8,128)(2,1)}, bf16[112,768]{1,0:T(8,128)(2,1)S(1)}, u32[]{:S(2)}, u32[]{:S(2)}) collective-permute-start(bf16[112,768]{1,0:T(8,128)(2,1)} %get-tuple-element.53), channel_id=1, source_target_pairs={{0,2},{1,3},{2,0},{3,1},{4,6},{5,7},{6,4},{7,5},{8,10},{9,11},{10,... | collective-permute-start | bytes 516104 | tf_op jit(solution)/shard_map/ppermute | solution.py:651
  37.5 1.5 %collective-permute-start.12 = (bf16[112,768]{1,0:T(8,128)(2,1)}, bf16[112,768]{1,0:T(8,128)(2,1)S(1)}, u32[]{:S(2)}, u32[]{:S(2)}) collective-permute-start(bf16[112,768]{1,0:T(8,128)(2,1)} %get-tuple-element.54), channel_id=1, source_target_pairs={{0,3},{1,2},{2,1},{3,0},{4,7},{5,6},{6,5},{7,4},{8,11},{9,10},{10,... | collective-permute-start | bytes 516104 | tf_op jit(solution)/shard_map/ppermute | solution.py:651
  39.0 0.9 %copy-done.4 = bf16[144,768]{1,0:T(8,128)(2,1)S(1)} copy-done((bf16[144,768]{1,0:T(8,128)(2,1)S(1)}, bf16[144,768]{1,0:T(8,128)(2,1)}, u32[]{:S(2)}) %copy-start.4) | copy-done | bytes 221208
  39.9 1.9 %assemble.5 = (f32[2,2,3,32,2048]{4,3,2,1,0:T(8,128)}, f32[256,256]{1,0:T(8,128)S(1)}) custom-call(s32[1]{0:T(128)} %bitcast.pos_ref.refs_0_, bf16[144,512]{1,0:T(8,128)(2,1)S(1)} %copy-done.7, bf16[144,512]{1,0:T(8,128)(2,1)S(1)} %collective-permute-done.1.refs_2_, ...), custom_call_target="tpu_custom_call", output_to_operand_aliasing={{0}: (6, {})} | custom-call | flops 1000 | bytes 1000 | tf_op jit(solution)/shard_map/assemble/pallas_call | solution.py:620
  41.8 0.7 copy-done
  42.6 4.7 %rotate_dft.7 = (bf16[144,512]{1,0:T(8,128)(2,1)}, bf16[144,512]{1,0:T(8,128)(2,1)}, bf16[112,512]{1,0:T(8,128)(2,1)}, bf16[112,512]{1,0:T(8,128)(2,1)}) custom-call(s32[1,2048]{1,0:T(1,128)} %bitcast.14, bf16[3,1072,2048]{2,1,0:T(8,128)(2,1)} %bitcast.8, bf16[176,1072]{1,0:T(8,128)(2,1)} %get-tuple-element.31.refs_2_, ...), custom_call_target="tpu_custom_call" | custom-call | flops 632291328 | bytes 3293184 | tf_op jit(solution)/shard_map/rotate_dft/pallas_call | solution.py:523
  47.8 2.4 %collective-permute-start.8 = (bf16[112,512]{1,0:T(8,128)(2,1)}, bf16[112,512]{1,0:T(8,128)(2,1)S(1)}, u32[]{:S(2)}, u32[]{:S(2)}) collective-permute-start(bf16[112,512]{1,0:T(8,128)(2,1)} %get-tuple-element.50), channel_id=1, source_target_pairs={{0,2},{1,3},{2,0},{3,1},{4,6},{5,7},{6,4},{7,5},{8,10},{9,11},{10,... | collective-permute-start | bytes 344072 | tf_op jit(solution)/shard_map/ppermute | solution.py:651
  50.2 1.5 %collective-permute-start.9 = (bf16[112,512]{1,0:T(8,128)(2,1)}, bf16[112,512]{1,0:T(8,128)(2,1)S(1)}, u32[]{:S(2)}, u32[]{:S(2)}) collective-permute-start(bf16[112,512]{1,0:T(8,128)(2,1)} %get-tuple-element.51), channel_id=1, source_target_pairs={{0,3},{1,2},{2,1},{3,0},{4,7},{5,6},{6,5},{7,4},{8,11},{9,10},{10,... | collective-permute-start | bytes 344072 | tf_op jit(solution)/shard_map/ppermute | solution.py:651
  51.7 2.6 %assemble.6 = (f32[2,2,3,32,2048]{4,3,2,1,0:T(8,128)}, f32[256,256]{1,0:T(8,128)S(1)}) custom-call(s32[1]{0:T(128)} %bitcast.pos_ref.refs_0_, bf16[144,768]{1,0:T(8,128)(2,1)S(1)} %copy-done.5, bf16[144,768]{1,0:T(8,128)(2,1)S(1)} %collective-permute-done.10.refs_2_, ...), custom_call_target="tpu_custom_call", output_to_operand_aliasing={{0}: (6, {})} | custom-call | flops 1000 | bytes 1000 | tf_op jit(solution)/shard_map/assemble/pallas_call | solution.py:620
  54.4 5.2 %collective-permute-done.8.refs_3_ = bf16[112,512]{1,0:T(8,128)(2,1)S(1)} collective-permute-done((bf16[112,512]{1,0:T(8,128)(2,1)}, bf16[112,512]{1,0:T(8,128)(2,1)S(1)}, u32[]{:S(2)}, u32[]{:S(2)}) %collective-permute-start.8) | collective-permute-done | bytes 114720 | tf_op jit(solution)/shard_map/ppermute | solution.py:651
  59.6 1.9 %assemble.7 = (f32[2,2,3,32,2048]{4,3,2,1,0:T(8,128)}, f32[64,128]{1,0:T(8,128)S(1)}) custom-call(s32[1]{0:T(128)} %bitcast.pos_ref.refs_0_, bf16[144,512]{1,0:T(8,128)(2,1)S(1)} %copy-done.8, bf16[144,512]{1,0:T(8,128)(2,1)S(1)} %collective-permute-done.7.refs_2_, ...), custom_call_target="tpu_custom_call", output_to_operand_aliasing={{0}: (6, {})} | custom-call | flops 1000 | bytes 1000 | tf_op jit(solution)/shard_map/assemble/pallas_call | solution.py:620
  61.5 1.2 %collective-permute-done.13 = f32[64,128]{1,0:T(8,128)S(1)} collective-permute-done((f32[64,128]{1,0:T(8,128)S(1)}, f32[64,128]{1,0:T(8,128)S(1)}, u32[]{:S(2)}, u32[]{:S(2)}) %collective-permute-start.13) | collective-permute-done | bytes 32800 | tf_op jit(solution)/shard_map/ppermute | solution.py:689
  62.7 1.5 %collective-permute-start.14 = (f32[64,128]{1,0:T(8,128)S(1)}, f32[64,128]{1,0:T(8,128)S(1)}, u32[]{:S(2)}, u32[]{:S(2)}) collective-permute-start(f32[64,128]{1,0:T(8,128)S(1)} %add.6), channel_id=1, source_target_pairs={{0,8},{4,12},{8,0},{12,4},{16,24},{20,28},{24,16},{28,20},{1,9},{5... | collective-permute-start | bytes 98312 | tf_op jit(solution)/shard_map/ppermute | solution.py:689
  64.2 2.4 %collective-permute-done.14 = f32[64,128]{1,0:T(8,128)S(1)} collective-permute-done((f32[64,128]{1,0:T(8,128)S(1)}, f32[64,128]{1,0:T(8,128)S(1)}, u32[]{:S(2)}, u32[]{:S(2)}) %collective-permute-start.14) | collective-permute-done | bytes 32800 | tf_op jit(solution)/shard_map/ppermute | solution.py:689
  66.6 1.6 %collective-permute-start.15 = (f32[64,128]{1,0:T(8,128)S(1)}, f32[64,128]{1,0:T(8,128)S(1)}, u32[]{:S(2)}, u32[]{:S(2)}) collective-permute-start(f32[64,128]{1,0:T(8,128)S(1)} %add.7.refs_0_), channel_id=1, source_target_pairs={{0,16},{4,20},{8,24},{12,28},{16,0},{20,4},{24,8},{28,12},{1,17},{... | collective-permute-start | bytes 98312 | tf_op jit(solution)/shard_map/ppermute | solution.py:689
  68.2 2.4 %collective-permute-done.15.refs_1_ = f32[64,128]{1,0:T(8,128)S(1)} collective-permute-done((f32[64,128]{1,0:T(8,128)S(1)}, f32[64,128]{1,0:T(8,128)S(1)}, u32[]{:S(2)}, u32[]{:S(2)}) %collective-permute-start.15) | collective-permute-done | bytes 32800 | tf_op jit(solution)/shard_map/ppermute | solution.py:689
  70.6 0.6 copy-done.12
  71.2 3.7 %factor.1 = f32[2,64,64]{2,1,0:T(8,128)} custom-call(f32[64,128]{1,0:T(8,128)} %copy-done.11, f32[64,128]{1,0:T(8,128)} %copy-done.12), custom_call_target="tpu_custom_call" | custom-call | tf_op jit(solution)/shard_map/factor/pallas_call | solution.py:304
  (38 shorter events, 1.2 us)
Async XLA Ops:
  4.5 12.3 %collective-permute-start = (bf16[48,2048]{1,0:T(8,128)(2,1)}, bf16[48,2048]{1,0:T(8,128)(2,1)S(1)}, u32[]{:S(2)}, u32[]{:S(2)}) collective-permute-start(bf16[48,2048]{1,0:T(8,128)(2,1)} %get-tuple-element.34), channel_id=1, source_target_pairs={{1,0},{2,3},{5,4},{6,7},{9,8},{10,11},{13,12},{14,15},{17,16},{18,... | collective-permute-start | bytes 589832 | tf_op jit(solution)/shard_map/ppermute | solution.py:651
  9.1 16.0 %collective-permute-start.4 = (bf16[144,256]{1,0:T(8,128)(2,1)}, bf16[144,256]{1,0:T(8,128)(2,1)S(1)}, u32[]{:S(2)}, u32[]{:S(2)}) collective-permute-start(bf16[144,256]{1,0:T(8,128)(2,1)} %get-tuple-element.41), channel_id=1, source_target_pairs={{0,1},{1,0},{2,3},{3,2},{4,5},{5,4},{6,7},{7,6},{8,9},{9,8},{10,11... | collective-permute-start | bytes 221192 | tf_op jit(solution)/shard_map/ppermute | solution.py:651
  12.1 13.6 %collective-permute-start.5 = (bf16[144,256]{1,0:T(8,128)(2,1)}, bf16[144,256]{1,0:T(8,128)(2,1)S(1)}, u32[]{:S(2)}, u32[]{:S(2)}) collective-permute-start(bf16[144,256]{1,0:T(8,128)(2,1)} %get-tuple-element.42), channel_id=1, source_target_pairs={{0,2},{1,3},{2,0},{3,1},{4,6},{5,7},{6,4},{7,5},{8,10},{9,11},{10,... | collective-permute-start | bytes 221192 | tf_op jit(solution)/shard_map/ppermute | solution.py:651
  15.3 10.3 %collective-permute-start.6 = (bf16[144,256]{1,0:T(8,128)(2,1)}, bf16[144,256]{1,0:T(8,128)(2,1)S(1)}, u32[]{:S(2)}, u32[]{:S(2)}) collective-permute-start(bf16[144,256]{1,0:T(8,128)(2,1)} %get-tuple-element.43), channel_id=1, source_target_pairs={{0,3},{1,2},{2,1},{3,0},{4,7},{5,6},{6,5},{7,4},{8,11},{9,10},{10,... | collective-permute-start | bytes 221192 | tf_op jit(solution)/shard_map/ppermute | solution.py:651
  16.8 0.7 copy-start.10
  17.5 8.2 %copy-start.9 = (bf16[144,256]{1,0:T(8,128)(2,1)S(1)}, bf16[144,256]{1,0:T(8,128)(2,1)}, u32[]{:S(2)}) copy-start(bf16[144,256]{1,0:T(8,128)(2,1)} %get-tuple-element.40.refs_1_) | copy-start | bytes 221188
  22.2 15.3 %collective-permute-start.2 = (bf16[112,512]{1,0:T(8,128)(2,1)}, bf16[112,512]{1,0:T(8,128)(2,1)S(1)}, u32[]{:S(2)}, u32[]{:S(2)}) collective-permute-start(bf16[112,512]{1,0:T(8,128)(2,1)} %get-tuple-element.37), channel_id=1, source_target_pairs={{0,2},{1,3},{2,0},{3,1},{4,6},{5,7},{6,4},{7,5},{8,10},{9,11},{10,... | collective-permute-start | bytes 344072 | tf_op jit(solution)/shard_map/ppermute | solution.py:651
  24.2 14.8 %collective-permute-start.3 = (bf16[112,512]{1,0:T(8,128)(2,1)}, bf16[112,512]{1,0:T(8,128)(2,1)S(1)}, u32[]{:S(2)}, u32[]{:S(2)}) collective-permute-start(bf16[112,512]{1,0:T(8,128)(2,1)} %get-tuple-element.38), channel_id=1, source_target_pairs={{0,3},{1,2},{2,1},{3,0},{4,7},{5,6},{6,5},{7,4},{8,11},{9,10},{10,... | collective-permute-start | bytes 344072 | tf_op jit(solution)/shard_map/ppermute | solution.py:651
  25.1 13.9 %collective-permute-start.1 = (bf16[144,512]{1,0:T(8,128)(2,1)}, bf16[144,512]{1,0:T(8,128)(2,1)S(1)}, u32[]{:S(2)}, u32[]{:S(2)}) collective-permute-start(bf16[144,512]{1,0:T(8,128)(2,1)} %get-tuple-element.36), channel_id=1, source_target_pairs={{0,1},{1,0},{2,3},{3,2},{4,5},{5,4},{6,7},{7,6},{8,9},{9,8},{10,11... | collective-permute-start | bytes 442376 | tf_op jit(solution)/shard_map/ppermute | solution.py:651
  25.7 0.9 %copy-start.6 = (bf16[144,512]{1,0:T(8,128)(2,1)S(1)}, bf16[144,512]{1,0:T(8,128)(2,1)}, u32[]{:S(2)}) copy-start(bf16[144,512]{1,0:T(8,128)(2,1)} %get-tuple-element.35.refs_5_.refs_1_) | copy-start | bytes 442372
  27.6 0.7 copy-start.2
  28.3 10.7 %copy-start.3 = (f32[256,256]{1,0:T(8,128)S(1)}, f32[256,256]{1,0:T(8,128)}, u32[]{:S(2)}) copy-start(f32[256,256]{1,0:T(8,128)} %copy-done.2) | copy-start | bytes 786436
  28.3 10.7 %copy-start.7 = (bf16[144,512]{1,0:T(8,128)(2,1)S(1)}, bf16[144,512]{1,0:T(8,128)(2,1)}, u32[]{:S(2)}) copy-start(bf16[144,512]{1,0:T(8,128)(2,1)} %get-tuple-element.35.refs_5_.refs_1_) | copy-start | bytes 442372
  34.5 15.7 %collective-permute-start.11 = (bf16[112,768]{1,0:T(8,128)(2,1)}, bf16[112,768]{1,0:T(8,128)(2,1)S(1)}, u32[]{:S(2)}, u32[]{:S(2)}) collective-permute-start(bf16[112,768]{1,0:T(8,128)(2,1)} %get-tuple-element.53), channel_id=1, source_target_pairs={{0,2},{1,3},{2,0},{3,1},{4,6},{5,7},{6,4},{7,5},{8,10},{9,11},{10,... | collective-permute-start | bytes 516104 | tf_op jit(solution)/shard_map/ppermute | solution.py:651
  37.4 14.3 %collective-permute-start.10 = (bf16[144,768]{1,0:T(8,128)(2,1)}, bf16[144,768]{1,0:T(8,128)(2,1)S(1)}, u32[]{:S(2)}, u32[]{:S(2)}) collective-permute-start(bf16[144,768]{1,0:T(8,128)(2,1)} %get-tuple-element.52), channel_id=1, source_target_pairs={{0,1},{1,0},{2,3},{3,2},{4,5},{5,4},{6,7},{7,6},{8,9},{9,8},{10,11... | collective-permute-start | bytes 663560 | tf_op jit(solution)/shard_map/ppermute | solution.py:651
  37.5 14.3 %collective-permute-start.12 = (bf16[112,768]{1,0:T(8,128)(2,1)}, bf16[112,768]{1,0:T(8,128)(2,1)S(1)}, u32[]{:S(2)}, u32[]{:S(2)}) collective-permute-start(bf16[112,768]{1,0:T(8,128)(2,1)} %get-tuple-element.54), channel_id=1, source_target_pairs={{0,3},{1,2},{2,1},{3,0},{4,7},{5,6},{6,5},{7,4},{8,11},{9,10},{10,... | collective-permute-start | bytes 516104 | tf_op jit(solution)/shard_map/ppermute | solution.py:651
  39.0 0.9 %copy-start.4 = (bf16[144,768]{1,0:T(8,128)(2,1)S(1)}, bf16[144,768]{1,0:T(8,128)(2,1)}, u32[]{:S(2)}) copy-start(bf16[144,768]{1,0:T(8,128)(2,1)} %get-tuple-element.46.refs_7_.refs_1_) | copy-start | bytes 663556
  41.8 0.7 copy-start
  42.5 9.2 %copy-start.1 = (f32[256,256]{1,0:T(8,128)S(1)}, f32[256,256]{1,0:T(8,128)}, u32[]{:S(2)}) copy-start(f32[256,256]{1,0:T(8,128)} %copy-done) | copy-start | bytes 786436
  42.5 9.2 %copy-start.5 = (bf16[144,768]{1,0:T(8,128)(2,1)S(1)}, bf16[144,768]{1,0:T(8,128)(2,1)}, u32[]{:S(2)}) copy-start(bf16[144,768]{1,0:T(8,128)(2,1)} %get-tuple-element.46.refs_7_.refs_1_) | copy-start | bytes 663556
  47.3 12.3 %copy-start.8 = (bf16[144,512]{1,0:T(8,128)(2,1)S(1)}, bf16[144,512]{1,0:T(8,128)(2,1)}, u32[]{:S(2)}) copy-start(bf16[144,512]{1,0:T(8,128)(2,1)} %get-tuple-element.48.refs_1_) | copy-start | bytes 442372
  47.3 12.3 %collective-permute-start.7 = (bf16[144,512]{1,0:T(8,128)(2,1)}, bf16[144,512]{1,0:T(8,128)(2,1)S(1)}, u32[]{:S(2)}, u32[]{:S(2)}) collective-permute-start(bf16[144,512]{1,0:T(8,128)(2,1)} %get-tuple-element.49), channel_id=1, source_target_pairs={{0,1},{1,0},{2,3},{3,2},{4,5},{5,4},{6,7},{7,6},{8,9},{9,8},{10,11... | collective-permute-start | bytes 442376 | tf_op jit(solution)/shard_map/ppermute | solution.py:651
  47.8 11.7 %collective-permute-start.8 = (bf16[112,512]{1,0:T(8,128)(2,1)}, bf16[112,512]{1,0:T(8,128)(2,1)S(1)}, u32[]{:S(2)}, u32[]{:S(2)}) collective-permute-start(bf16[112,512]{1,0:T(8,128)(2,1)} %get-tuple-element.50), channel_id=1, source_target_pairs={{0,2},{1,3},{2,0},{3,1},{4,6},{5,7},{6,4},{7,5},{8,10},{9,11},{10,... | collective-permute-start | bytes 344072 | tf_op jit(solution)/shard_map/ppermute | solution.py:651
  50.2 9.4 %collective-permute-start.9 = (bf16[112,512]{1,0:T(8,128)(2,1)}, bf16[112,512]{1,0:T(8,128)(2,1)S(1)}, u32[]{:S(2)}, u32[]{:S(2)}) collective-permute-start(bf16[112,512]{1,0:T(8,128)(2,1)} %get-tuple-element.51), channel_id=1, source_target_pairs={{0,3},{1,2},{2,1},{3,0},{4,7},{5,6},{6,5},{7,4},{8,11},{9,10},{10,... | collective-permute-start | bytes 344072 | tf_op jit(solution)/shard_map/ppermute | solution.py:651
  61.5 1.2 %collective-permute-start.13 = (f32[64,128]{1,0:T(8,128)S(1)}, f32[64,128]{1,0:T(8,128)S(1)}, u32[]{:S(2)}, u32[]{:S(2)}) collective-permute-start(f32[64,128]{1,0:T(8,128)S(1)} %get-tuple-element.59), channel_id=1, source_target_pairs={{0,4},{4,0},{8,12},{12,8},{16,20},{20,16},{24,28},{28,24},{1,5},{5... | collective-permute-start | bytes 98312 | tf_op jit(solution)/shard_map/ppermute | solution.py:689
  62.7 3.9 %collective-permute-start.14 = (f32[64,128]{1,0:T(8,128)S(1)}, f32[64,128]{1,0:T(8,128)S(1)}, u32[]{:S(2)}, u32[]{:S(2)}) collective-permute-start(f32[64,128]{1,0:T(8,128)S(1)} %add.6), channel_id=1, source_target_pairs={{0,8},{4,12},{8,0},{12,4},{16,24},{20,28},{24,16},{28,20},{1,9},{5... | collective-permute-start | bytes 98312 | tf_op jit(solution)/shard_map/ppermute | solution.py:689
  66.6 4.0 %copy-start.11 = (f32[64,128]{1,0:T(8,128)}, f32[64,128]{1,0:T(8,128)S(1)}, u32[]{:S(2)}) copy-start(f32[64,128]{1,0:T(8,128)S(1)} %add.7.refs_0_) | copy-start | bytes 98308
  66.6 4.0 %collective-permute-start.15 = (f32[64,128]{1,0:T(8,128)S(1)}, f32[64,128]{1,0:T(8,128)S(1)}, u32[]{:S(2)}, u32[]{:S(2)}) collective-permute-start(f32[64,128]{1,0:T(8,128)S(1)} %add.7.refs_0_), channel_id=1, source_target_pairs={{0,16},{4,20},{8,24},{12,28},{16,0},{20,4},{24,8},{28,12},{1,17},{... | collective-permute-start | bytes 98312 | tf_op jit(solution)/shard_map/ppermute | solution.py:689
  70.6 0.6 copy-start.12

commit v6 on v5

--- a/solution.py
+++ b/solution.py
@@ -270,7 +270,7 @@
 def factor_body(owned, order, count, *refs):
     parts = refs[:count]
     out_ref, row_ref = refs[count:]
-    s = [p[...] for p in parts]
+    s = [p[...] for p in parts] if len(parts[0].shape) == 2 else [parts[0][i] for i in range(parts[0].shape[0])]
     while len(s) > 1:
         s = [a + b for a, b in zip(s[::2], s[1::2])]
     s = s[0]
@@ -641,7 +641,7 @@
 
 
 def line_chunks(points):
-    cuts = [points * k // 8 for k in (0, 1, 3, 6, 8)]
+    cuts = [points * k // 8 for k in (0, 2, 6, 8)]
     return [(a, b - a) for a, b in zip(cuts[:-1], cuts[1:])]
 
 
@@ -688,8 +688,10 @@
         return [lax.psum(gram, "space")]
     swap = lambda x, k: lax.ppermute(x, "space", [(i, i ^ k) for i in range(groups)])
     gram = gram + swap(gram, 1)
-    gram = gram + swap(gram, 2)
-    return [gram, swap(gram, 4)]
+    copies = jnp.broadcast_to(gram, (4,) + gram.shape)
+    chips = [[0, 2, 4, 6], [1, 3, 5, 7]]
+    copies = lax.all_to_all(copies, "space", 0, 0, axis_index_groups=chips, tiled=True)
+    return [copies]
 
 
 def chunks_of(points):

time: 75.3 us -> 73.8 us (0.980)
  blocking collectives: 0 us -> 9.17 us
  waiting for transfers between devices: 11.2 us -> 7.15 us
  Pallas kernels: 33.9 us -> 30.7 us
  local copies, waits for them, and re-layouts: 4.58 us -> 2.35 us
  starting transfers between devices: 24.5 us -> 23.4 us
    all_to_all x0 -> x1, blocking collectives: none -> 9.17 us  [sum_over_space(): lax.all_to_all(copies, 'space', 0, 0, axis_index_groups=chips, tiled=True)]
    ppermute x3 -> x1, waiting for transfers between devices: 6.02 us -> 1.2 us  [sum_over_space(): lax.ppermute(x, 'space', [(i, i ^ k) for i in range(groups)])]
    ppermute x3 -> x1, starting transfers between devices: 3.08 us -> 0.01 us  [sum_over_space(): lax.ppermute(x, 'space', [(i, i ^ k) for i in range(groups)])]
    pallas_call x4 -> x3, Pallas kernels: 18.9 us -> 16 us  [line_dft(): pl.pallas_call(functools.partial(line_dft_body, span, direct), grid=(poin...]
    unnamed x26 -> x14, local copies, waits for them, and re-layouts: 4.58 us -> 2.34 us
    ppermute x13 -> x10, starting transfers between devices: 21.5 us -> 23.4 us  [line_spectra(): move = lambda x, pairs: lax.ppermute(x, 'tm', pairs)]
    ppermute x13 -> x10, waiting for transfers between devices: 5.22 us -> 5.95 us  [line_spectra(): move = lambda x, pairs: lax.ppermute(x, 'tm', pairs)]
    pallas_call x4 -> x3, Pallas kernels: 7.43 us -> 6.99 us  [line_assemble(): pl.pallas_call(functools.partial(line_assemble_body, blocks, total, has_s...]
  transfers between devices with their start and end apart: 16 -> 11, of which waited for: 4 -> 2; matrix products, arithmetic and copies ran while one was open for 0% -> 0% of each run, Pallas kernels for 33% -> 29%
where the time goes in v6:
time: 73.8 us; the launch traced here: 73.4 us
  Pallas kernels  30.7 us (42%)
  starting transfers between devices  23.4 us (32%)
  blocking collectives  9.17 us (12%)
  waiting for transfers between devices  7.15 us (10%)
  local copies, waits for them, and re-layouts  2.35 us (3%)
    ppermute x10, starting transfers between devices, line_spectra(): move = lambda x, pairs: lax.ppermute(x, 'tm', pairs)  23.4 us
    pallas_call x3, Pallas kernels, line_dft(): pl.pallas_call(functools.partial(line_dft_body, span, direct), grid=(poin...  16 us
    all_to_all x1, blocking collectives, sum_over_space(): lax.all_to_all(copies, 'space', 0, 0, axis_index_groups=chips, tiled=True)  9.17 us
    pallas_call x3, Pallas kernels, line_assemble(): pl.pallas_call(functools.partial(line_assemble_body, blocks, total, has_s...  6.99 us
    ppermute x10, waiting for transfers between devices, line_spectra(): move = lambda x, pairs: lax.ppermute(x, 'tm', pairs)  5.95 us
    pallas_call x1, Pallas kernels, factor_call(): pl.pallas_call(functools.partial(factor_body, owned, order, len(parts)),...  3.86 us
    pallas_call x1, Pallas kernels, prepare(): pl.pallas_call(functools.partial(prepare_body, span, blocks), grid=(1,),...  3.82 us
    unnamed x14, local copies, waits for them, and re-layouts  2.34 us
  transfers between devices with their start and end apart: 11, of which 2 were waited for; matrix products, arithmetic and copies ran while one was open for 0% of the time, Pallas kernels for 29%

profile of v6, /device:TPU:0, one launch (start us, length us, event | category | flops | bytes accessed | tf_op | source)
XLA Modules:
  0.0 73.4 jit_solution(9505647153049090423)
XLA Ops:
  0.6 3.8 %prepare.1 = (bf16[48,2048]{1,0:T(8,128)(2,1)}, bf16[192,1072]{1,0:T(8,128)(2,1)}, bf16[176,1072]{1,0:T(8,128)(2,1)}, f32[1072,128]{1,0:T(8,128)}, f32[1072,128]{1,0:T(8,128)}) custom-call(s32[1]{0:T(128)} %bitcast.pos_ref.refs_0_, s32[32]{0:T(128)} %starts_ref.1, s32[8]{0:T(128)} %freqs_ref.1, f32[1072]{0:T(1024)} %angle_ref.1, s32[1,2048]{1,0:T(1,128)} %bitcast.9, ...), custom_call_target="tpu_custom_call" | custom-call | flops 1000000000 | bytes 4000000 | tf_op jit(solution)/shard_map/prepare/pallas_call | solution.py:451
  4.5 1.3 %collective-permute-start = (bf16[48,2048]{1,0:T(8,128)(2,1)}, bf16[48,2048]{1,0:T(8,128)(2,1)S(1)}, u32[]{:S(2)}, u32[]{:S(2)}) collective-permute-start(bf16[48,2048]{1,0:T(8,128)(2,1)} %get-tuple-element.28), channel_id=1, source_target_pairs={{1,0},{2,3},{5,4},{6,7},{9,8},{10,11},{13,12},{14,15},{17,16},{18,... | collective-permute-start | bytes 589832 | tf_op jit(solution)/shard_map/ppermute | solution.py:651
  5.8 4.2 %rotate_dft.3 = (bf16[144,512]{1,0:T(8,128)(2,1)}, bf16[144,512]{1,0:T(8,128)(2,1)}, bf16[144,512]{1,0:T(8,128)(2,1)}, bf16[144,512]{1,0:T(8,128)(2,1)}) custom-call(s32[1,2048]{1,0:T(1,128)} %bitcast.10, bf16[3,1072,2048]{2,1,0:T(8,128)(2,1)} %bitcast.5, bf16[192,1072]{1,0:T(8,128)(2,1)} %get-tuple-element.29.refs_2_, ...), custom_call_target="tpu_custom_call" | custom-call | flops 632291328 | bytes 3293184 | tf_op jit(solution)/shard_map/rotate_dft/pallas_call | solution.py:523
  9.9 3.1 %collective-permute-start.1 = (bf16[144,512]{1,0:T(8,128)(2,1)}, bf16[144,512]{1,0:T(8,128)(2,1)S(1)}, u32[]{:S(2)}, u32[]{:S(2)}) collective-permute-start(bf16[144,512]{1,0:T(8,128)(2,1)} %get-tuple-element.31), channel_id=1, source_target_pairs={{0,1},{1,0},{2,3},{3,2},{4,5},{5,4},{6,7},{7,6},{8,9},{9,8},{10,11... | collective-permute-start | bytes 442376 | tf_op jit(solution)/shard_map/ppermute | solution.py:651
  13.0 3.3 %collective-permute-start.2 = (bf16[144,512]{1,0:T(8,128)(2,1)}, bf16[144,512]{1,0:T(8,128)(2,1)S(1)}, u32[]{:S(2)}, u32[]{:S(2)}) collective-permute-start(bf16[144,512]{1,0:T(8,128)(2,1)} %get-tuple-element.32), channel_id=1, source_target_pairs={{0,2},{1,3},{2,0},{3,1},{4,6},{5,7},{6,4},{7,5},{8,10},{9,11},{10,... | collective-permute-start | bytes 442376 | tf_op jit(solution)/shard_map/ppermute | solution.py:651
  16.3 1.4 %collective-permute-start.3 = (bf16[144,512]{1,0:T(8,128)(2,1)}, bf16[144,512]{1,0:T(8,128)(2,1)S(1)}, u32[]{:S(2)}, u32[]{:S(2)}) collective-permute-start(bf16[144,512]{1,0:T(8,128)(2,1)} %get-tuple-element.33), channel_id=1, source_target_pairs={{0,3},{1,2},{2,1},{3,0},{4,7},{5,6},{6,5},{7,4},{8,11},{9,10},{10,... | collective-permute-start | bytes 442376 | tf_op jit(solution)/shard_map/ppermute | solution.py:651
  17.7 0.0 collective-permute-done.refs_5_
  17.7 0.7 copy-done.6
  18.3 7.1 %rotate_dft.4 = (bf16[144,1024]{1,0:T(8,128)(2,1)}, bf16[144,1024]{1,0:T(8,128)(2,1)}, bf16[112,1024]{1,0:T(8,128)(2,1)}, bf16[112,1024]{1,0:T(8,128)(2,1)}) custom-call(s32[1,2048]{1,0:T(1,128)} %bitcast.11, bf16[3,1072,2048]{2,1,0:T(8,128)(2,1)} %bitcast.6, bf16[176,1072]{1,0:T(8,128)(2,1)} %get-tuple-element.25.refs_2_, ...), custom_call_target="tpu_custom_call" | custom-call | flops 1264582656 | bytes 6586368 | tf_op jit(solution)/shard_map/rotate_dft/pallas_call | solution.py:523
  25.4 2.0 %collective-permute-start.8 = (bf16[112,1024]{1,0:T(8,128)(2,1)}, bf16[112,1024]{1,0:T(8,128)(2,1)S(1)}, u32[]{:S(2)}, u32[]{:S(2)}) collective-permute-start(bf16[112,1024]{1,0:T(8,128)(2,1)} %get-tuple-element.41), channel_id=1, source_target_pairs={{0,2},{1,3},{2,0},{3,1},{4,6},{5,7},{6,4},{7,5},{8,10},{9,11},{10,... | collective-permute-start | bytes 688136 | tf_op jit(solution)/shard_map/ppermute | solution.py:651
  27.5 1.0 %collective-permute-start.7 = (bf16[144,1024]{1,0:T(8,128)(2,1)}, bf16[144,1024]{1,0:T(8,128)(2,1)S(1)}, u32[]{:S(2)}, u32[]{:S(2)}) collective-permute-start(bf16[144,1024]{1,0:T(8,128)(2,1)} %get-tuple-element.40), channel_id=1, source_target_pairs={{0,1},{1,0},{2,3},{3,2},{4,5},{5,4},{6,7},{7,6},{8,9},{9,8},{10,11... | collective-permute-start | bytes 884744 | tf_op jit(solution)/shard_map/ppermute | solution.py:651
  28.5 0.0 collective-permute-done.1.refs_2_
  28.5 1.4 %collective-permute-start.9 = (bf16[112,1024]{1,0:T(8,128)(2,1)}, bf16[112,1024]{1,0:T(8,128)(2,1)S(1)}, u32[]{:S(2)}, u32[]{:S(2)}) collective-permute-start(bf16[112,1024]{1,0:T(8,128)(2,1)} %get-tuple-element.42), channel_id=1, source_target_pairs={{0,3},{1,2},{2,1},{3,0},{4,7},{5,6},{6,5},{7,4},{8,11},{9,10},{10,... | collective-permute-start | bytes 688136 | tf_op jit(solution)/shard_map/ppermute | solution.py:651
  29.9 0.0 collective-permute-done.2.refs_3_
  29.9 0.0 collective-permute-done.3.refs_4_
  29.9 1.0 %copy-done = bf16[144,1024]{1,0:T(8,128)(2,1)S(1)} copy-done((bf16[144,1024]{1,0:T(8,128)(2,1)S(1)}, bf16[144,1024]{1,0:T(8,128)(2,1)}, u32[]{:S(2)}) %copy-start) | copy-done | bytes 294936
  30.8 1.8 %assemble.3 = (f32[2,2,3,32,2048]{4,3,2,1,0:T(8,128)}, f32[256,256]{1,0:T(8,128)S(1)}) custom-call(s32[1]{0:T(128)} %bitcast.pos_ref.refs_0_, bf16[144,512]{1,0:T(8,128)(2,1)S(1)} %copy-done.5, bf16[144,512]{1,0:T(8,128)(2,1)S(1)} %collective-permute-done.1.refs_2_, bf16[144,512]{1,0:T(8,128)(2,1)S(1)} %collective-permute-done.2.refs_3_, ...), custom_call_target="tpu_custom_call" | custom-call | flops 1000 | bytes 1000 | tf_op jit(solution)/shard_map/assemble/pallas_call | solution.py:620
  32.7 0.7 copy-done.2
  33.4 4.7 %rotate_dft.5 = (bf16[144,512]{1,0:T(8,128)(2,1)}, bf16[144,512]{1,0:T(8,128)(2,1)}, bf16[112,512]{1,0:T(8,128)(2,1)}, bf16[112,512]{1,0:T(8,128)(2,1)}) custom-call(s32[1,2048]{1,0:T(1,128)} %bitcast.12, bf16[3,1072,2048]{2,1,0:T(8,128)(2,1)} %bitcast.7, bf16[176,1072]{1,0:T(8,128)(2,1)} %get-tuple-element.25.refs_2_, ...), custom_call_target="tpu_custom_call" | custom-call | flops 632291328 | bytes 3293184 | tf_op jit(solution)/shard_map/rotate_dft/pallas_call | solution.py:523
  38.1 5.8 %collective-permute-start.4 = (bf16[144,512]{1,0:T(8,128)(2,1)}, bf16[144,512]{1,0:T(8,128)(2,1)S(1)}, u32[]{:S(2)}, u32[]{:S(2)}) collective-permute-start(bf16[144,512]{1,0:T(8,128)(2,1)} %get-tuple-element.37), channel_id=1, source_target_pairs={{0,1},{1,0},{2,3},{3,2},{4,5},{5,4},{6,7},{7,6},{8,9},{9,8},{10,11... | collective-permute-start | bytes 442376 | tf_op jit(solution)/shard_map/ppermute | solution.py:651
  43.9 1.8 %collective-permute-start.5 = (bf16[112,512]{1,0:T(8,128)(2,1)}, bf16[112,512]{1,0:T(8,128)(2,1)S(1)}, u32[]{:S(2)}, u32[]{:S(2)}) collective-permute-start(bf16[112,512]{1,0:T(8,128)(2,1)} %get-tuple-element.38), channel_id=1, source_target_pairs={{0,2},{1,3},{2,0},{3,1},{4,6},{5,7},{6,4},{7,5},{8,10},{9,11},{10,... | collective-permute-start | bytes 344072 | tf_op jit(solution)/shard_map/ppermute | solution.py:651
  45.7 0.0 collective-permute-done.8.refs_3_
  45.7 2.4 %collective-permute-start.6 = (bf16[112,512]{1,0:T(8,128)(2,1)}, bf16[112,512]{1,0:T(8,128)(2,1)S(1)}, u32[]{:S(2)}, u32[]{:S(2)}) collective-permute-start(bf16[112,512]{1,0:T(8,128)(2,1)} %get-tuple-element.39), channel_id=1, source_target_pairs={{0,3},{1,2},{2,1},{3,0},{4,7},{5,6},{6,5},{7,4},{8,11},{9,10},{10,... | collective-permute-start | bytes 344072 | tf_op jit(solution)/shard_map/ppermute | solution.py:651
  48.1 0.0 collective-permute-done.9.refs_4_
  48.1 0.0 collective-permute-done.7.refs_2_
  48.1 3.2 %assemble.4 = (f32[2,2,3,32,2048]{4,3,2,1,0:T(8,128)}, f32[256,256]{1,0:T(8,128)S(1)}) custom-call(s32[1]{0:T(128)} %bitcast.pos_ref.refs_0_, bf16[144,1024]{1,0:T(8,128)(2,1)S(1)} %copy-done.1, bf16[144,1024]{1,0:T(8,128)(2,1)S(1)} %collective-permute-done.7.refs_2_, ...), custom_call_target="tpu_custom_call", output_to_operand_aliasing={{0}: (6, {})} | custom-call | flops 1000 | bytes 1000 | tf_op jit(solution)/shard_map/assemble/pallas_call | solution.py:620
  51.3 5.9 %collective-permute-done.5.refs_3_ = bf16[112,512]{1,0:T(8,128)(2,1)S(1)} collective-permute-done((bf16[112,512]{1,0:T(8,128)(2,1)}, bf16[112,512]{1,0:T(8,128)(2,1)S(1)}, u32[]{:S(2)}, u32[]{:S(2)}) %collective-permute-start.5) | collective-permute-done | bytes 114720 | tf_op jit(solution)/shard_map/ppermute | solution.py:651
  57.3 1.9 %assemble.5 = (f32[2,2,3,32,2048]{4,3,2,1,0:T(8,128)}, f32[64,128]{1,0:T(8,128)S(1)}) custom-call(s32[1]{0:T(128)} %bitcast.pos_ref.refs_0_, bf16[144,512]{1,0:T(8,128)(2,1)S(1)} %copy-done.4, bf16[144,512]{1,0:T(8,128)(2,1)S(1)} %collective-permute-done.4.refs_2_, ...), custom_call_target="tpu_custom_call", output_to_operand_aliasing={{0}: (6, {})} | custom-call | flops 1000 | bytes 1000 | tf_op jit(solution)/shard_map/assemble/pallas_call | solution.py:620
  59.2 0.0 collective-permute-start.10
  59.2 1.2 %collective-permute-done.10 = f32[64,128]{1,0:T(8,128)S(1)} collective-permute-done((f32[64,128]{1,0:T(8,128)S(1)}, f32[64,128]{1,0:T(8,128)S(1)}, u32[]{:S(2)}, u32[]{:S(2)}) %collective-permute-start.10) | collective-permute-done | bytes 32800 | tf_op jit(solution)/shard_map/ppermute | solution.py:689
  60.4 9.2 %all_to_all.5.refs_0_ = f32[4,64,128]{2,1,0:T(8,128)} all-to-all(f32[4,64,128]{2,1,0:T(8,128)S(1)} %broadcast_in_dim.3), channel_id=1, replica_groups={{0,8,16,24},{4,12,20,28},{1,9,17,25},{5,13,21,29},{2,10,18,26},{6,14,22..., dimensions={0} | all-to-all | bytes 262144 | tf_op jit(solution)/shard_map/all_to_all | solution.py:693
  69.6 3.9 %factor.1 = f32[2,64,64]{2,1,0:T(8,128)} custom-call(f32[4,64,128]{2,1,0:T(8,128)} %all_to_all.5.refs_0_), custom_call_target="tpu_custom_call" | custom-call | tf_op jit(solution)/shard_map/factor/pallas_call | solution.py:304
  (15 shorter events, 0.0 us)
Async XLA Ops:
  4.5 13.2 %collective-permute-start = (bf16[48,2048]{1,0:T(8,128)(2,1)}, bf16[48,2048]{1,0:T(8,128)(2,1)S(1)}, u32[]{:S(2)}, u32[]{:S(2)}) collective-permute-start(bf16[48,2048]{1,0:T(8,128)(2,1)} %get-tuple-element.28), channel_id=1, source_target_pairs={{1,0},{2,3},{5,4},{6,7},{9,8},{10,11},{13,12},{14,15},{17,16},{18,... | collective-permute-start | bytes 589832 | tf_op jit(solution)/shard_map/ppermute | solution.py:651
  9.9 18.5 %collective-permute-start.1 = (bf16[144,512]{1,0:T(8,128)(2,1)}, bf16[144,512]{1,0:T(8,128)(2,1)S(1)}, u32[]{:S(2)}, u32[]{:S(2)}) collective-permute-start(bf16[144,512]{1,0:T(8,128)(2,1)} %get-tuple-element.31), channel_id=1, source_target_pairs={{0,1},{1,0},{2,3},{3,2},{4,5},{5,4},{6,7},{7,6},{8,9},{9,8},{10,11... | collective-permute-start | bytes 442376 | tf_op jit(solution)/shard_map/ppermute | solution.py:651
  13.0 16.9 %collective-permute-start.2 = (bf16[144,512]{1,0:T(8,128)(2,1)}, bf16[144,512]{1,0:T(8,128)(2,1)S(1)}, u32[]{:S(2)}, u32[]{:S(2)}) collective-permute-start(bf16[144,512]{1,0:T(8,128)(2,1)} %get-tuple-element.32), channel_id=1, source_target_pairs={{0,2},{1,3},{2,0},{3,1},{4,6},{5,7},{6,4},{7,5},{8,10},{9,11},{10,... | collective-permute-start | bytes 442376 | tf_op jit(solution)/shard_map/ppermute | solution.py:651
  16.3 13.6 %collective-permute-start.3 = (bf16[144,512]{1,0:T(8,128)(2,1)}, bf16[144,512]{1,0:T(8,128)(2,1)S(1)}, u32[]{:S(2)}, u32[]{:S(2)}) collective-permute-start(bf16[144,512]{1,0:T(8,128)(2,1)} %get-tuple-element.33), channel_id=1, source_target_pairs={{0,3},{1,2},{2,1},{3,0},{4,7},{5,6},{6,5},{7,4},{8,11},{9,10},{10,... | collective-permute-start | bytes 442376 | tf_op jit(solution)/shard_map/ppermute | solution.py:651
  17.7 0.7 copy-start.6
  18.3 11.5 %copy-start.5 = (bf16[144,512]{1,0:T(8,128)(2,1)S(1)}, bf16[144,512]{1,0:T(8,128)(2,1)}, u32[]{:S(2)}) copy-start(bf16[144,512]{1,0:T(8,128)(2,1)} %get-tuple-element.30.refs_1_) | copy-start | bytes 442372
  25.4 20.3 %collective-permute-start.8 = (bf16[112,1024]{1,0:T(8,128)(2,1)}, bf16[112,1024]{1,0:T(8,128)(2,1)S(1)}, u32[]{:S(2)}, u32[]{:S(2)}) collective-permute-start(bf16[112,1024]{1,0:T(8,128)(2,1)} %get-tuple-element.41), channel_id=1, source_target_pairs={{0,2},{1,3},{2,0},{3,1},{4,6},{5,7},{6,4},{7,5},{8,10},{9,11},{10,... | collective-permute-start | bytes 688136 | tf_op jit(solution)/shard_map/ppermute | solution.py:651
  27.5 20.6 %collective-permute-start.7 = (bf16[144,1024]{1,0:T(8,128)(2,1)}, bf16[144,1024]{1,0:T(8,128)(2,1)S(1)}, u32[]{:S(2)}, u32[]{:S(2)}) collective-permute-start(bf16[144,1024]{1,0:T(8,128)(2,1)} %get-tuple-element.40), channel_id=1, source_target_pairs={{0,1},{1,0},{2,3},{3,2},{4,5},{5,4},{6,7},{7,6},{8,9},{9,8},{10,11... | collective-permute-start | bytes 884744 | tf_op jit(solution)/shard_map/ppermute | solution.py:651
  28.5 19.6 %collective-permute-start.9 = (bf16[112,1024]{1,0:T(8,128)(2,1)}, bf16[112,1024]{1,0:T(8,128)(2,1)S(1)}, u32[]{:S(2)}, u32[]{:S(2)}) collective-permute-start(bf16[112,1024]{1,0:T(8,128)(2,1)} %get-tuple-element.42), channel_id=1, source_target_pairs={{0,3},{1,2},{2,1},{3,0},{4,7},{5,6},{6,5},{7,4},{8,11},{9,10},{10,... | collective-permute-start | bytes 688136 | tf_op jit(solution)/shard_map/ppermute | solution.py:651
  29.9 1.0 %copy-start = (bf16[144,1024]{1,0:T(8,128)(2,1)S(1)}, bf16[144,1024]{1,0:T(8,128)(2,1)}, u32[]{:S(2)}) copy-start(bf16[144,1024]{1,0:T(8,128)(2,1)} %get-tuple-element.34.refs_5_.refs_1_) | copy-start | bytes 884740
  32.7 0.7 copy-start.2
  33.4 14.7 %copy-start.1 = (bf16[144,1024]{1,0:T(8,128)(2,1)S(1)}, bf16[144,1024]{1,0:T(8,128)(2,1)}, u32[]{:S(2)}) copy-start(bf16[144,1024]{1,0:T(8,128)(2,1)} %get-tuple-element.34.refs_5_.refs_1_) | copy-start | bytes 884740
  33.4 14.7 %copy-start.3 = (f32[256,256]{1,0:T(8,128)S(1)}, f32[256,256]{1,0:T(8,128)}, u32[]{:S(2)}) copy-start(f32[256,256]{1,0:T(8,128)} %copy-done.2) | copy-start | bytes 786436
  38.1 19.2 %copy-start.4 = (bf16[144,512]{1,0:T(8,128)(2,1)S(1)}, bf16[144,512]{1,0:T(8,128)(2,1)}, u32[]{:S(2)}) copy-start(bf16[144,512]{1,0:T(8,128)(2,1)} %get-tuple-element.36.refs_1_) | copy-start | bytes 442372
  38.1 19.1 %collective-permute-start.4 = (bf16[144,512]{1,0:T(8,128)(2,1)}, bf16[144,512]{1,0:T(8,128)(2,1)S(1)}, u32[]{:S(2)}, u32[]{:S(2)}) collective-permute-start(bf16[144,512]{1,0:T(8,128)(2,1)} %get-tuple-element.37), channel_id=1, source_target_pairs={{0,1},{1,0},{2,3},{3,2},{4,5},{5,4},{6,7},{7,6},{8,9},{9,8},{10,11... | collective-permute-start | bytes 442376 | tf_op jit(solution)/shard_map/ppermute | solution.py:651
  43.9 13.4 %collective-permute-start.5 = (bf16[112,512]{1,0:T(8,128)(2,1)}, bf16[112,512]{1,0:T(8,128)(2,1)S(1)}, u32[]{:S(2)}, u32[]{:S(2)}) collective-permute-start(bf16[112,512]{1,0:T(8,128)(2,1)} %get-tuple-element.38), channel_id=1, source_target_pairs={{0,2},{1,3},{2,0},{3,1},{4,6},{5,7},{6,4},{7,5},{8,10},{9,11},{10,... | collective-permute-start | bytes 344072 | tf_op jit(solution)/shard_map/ppermute | solution.py:651
  45.7 11.5 %collective-permute-start.6 = (bf16[112,512]{1,0:T(8,128)(2,1)}, bf16[112,512]{1,0:T(8,128)(2,1)S(1)}, u32[]{:S(2)}, u32[]{:S(2)}) collective-permute-start(bf16[112,512]{1,0:T(8,128)(2,1)} %get-tuple-element.39), channel_id=1, source_target_pairs={{0,3},{1,2},{2,1},{3,0},{4,7},{5,6},{6,5},{7,4},{8,11},{9,10},{10,... | collective-permute-start | bytes 344072 | tf_op jit(solution)/shard_map/ppermute | solution.py:651
  59.2 1.2 %collective-permute-start.10 = (f32[64,128]{1,0:T(8,128)S(1)}, f32[64,128]{1,0:T(8,128)S(1)}, u32[]{:S(2)}, u32[]{:S(2)}) collective-permute-start(f32[64,128]{1,0:T(8,128)S(1)} %get-tuple-element.47), channel_id=1, source_target_pairs={{0,4},{4,0},{8,12},{12,8},{16,20},{20,16},{24,28},{28,24},{1,5},{5... | collective-permute-start | bytes 98312 | tf_op jit(solution)/shard_map/ppermute | solution.py:689

commit v7 on v5

--- a/solution.py
+++ b/solution.py
@@ -14,7 +14,7 @@
 HOP = 128
 LANES = 128
 TILE = 256
-PIVOT = 4
+PIVOT = 8
 LIMIT_A, LIMIT_B, LIMIT_C = 60, 60, 40
 SCALE = (8.0 / (3.0 * NFFT)) ** 0.5
 HIGHEST = lax.Precision.HIGHEST
@@ -333,7 +333,7 @@
     return 1.0 - 2.0 * s * s
 
 
-def build_line(span, blocks, me, starts_ref, freqs_ref, direct_ref, a_ref, rows_ref):
+def build_line(span, blocks, me, starts_ref, freqs_ref, a_ref, rows_ref):
     lo = pick(LINE_LO, me)
     starts = [starts_ref[jnp.minimum(lo + s, blocks - 1)] for s in range(WIDE)]
 
@@ -366,15 +366,12 @@
     w = half_turn_sine(jnp.minimum(nf, NFFT - nf) * (1.0 / NFFT))
     w = jnp.where((ni >= 0) & (ni < NFFT) & (slot + lo < blocks), w * w * SCALE, 0.0)
 
-    own, near, direct2, direct3 = [], [], [], []
+    own, near = [], []
     for s in range(WIDE):
         rows = (cos_t * cos_b[:, s:s + 1] + sin_t * sin_b[:, s:s + 1]) * w[s:s + 1]
         rows_ref[s] = rows[8:]
         own.append(rows[:4])
         near.append(rows[4:8])
-        direct2.append(rows[8:12])
-        direct3.append(rows[12:])
-    direct_ref[...] = jnp.concatenate(own + near + direct2 + direct3, axis=0).astype(jnp.bfloat16)
     far = [rows_ref[far_block(me, s) - lo] for s in range(FAR)]
     pieces = own + near
     pieces += [r[:4] for r in far[:-1]] + [r[4:] for r in far[:-1]]
@@ -410,12 +407,12 @@
 
 
 def prepare_body(span, blocks, pos_ref, starts_ref, freqs_ref, angle_ref, mask_ref, all_hbm,
-                 part_ref, direct_ref, a_ref, cos_ref, sin_ref, rows_ref, ends_ref, ends_rot_ref, ends_sem):
+                 part_ref, a_ref, cos_ref, sin_ref, rows_ref, ends_ref, ends_rot_ref, ends_sem):
     me = pos_ref[0]
     begin = pl.multiple_of(jnp.where(me == 2, span - REACH, 0), 16)
     load = pltpu.make_async_copy(all_hbm.at[:, pl.ds(begin, REACH), :], ends_ref, ends_sem)
     load.start()
-    build_line(span, blocks, me, starts_ref, freqs_ref, direct_ref, a_ref, rows_ref)
+    build_line(span, blocks, me, starts_ref, freqs_ref, a_ref, rows_ref)
     spread_column(jnp.cos(angle_ref[...].reshape(1, span)), span, cos_ref)
     spread_column(jnp.sin(angle_ref[...].reshape(1, span)), span, sin_ref)
     rows = shared_rows(begin + me * span, me, starts_ref, freqs_ref)
@@ -443,7 +440,6 @@
     whole = lambda shape: pl.BlockSpec(shape, lambda i: (0,) * len(shape))
     types = [
         jax.ShapeDtypeStruct((48, points), jnp.bfloat16),
-        jax.ShapeDtypeStruct((192, span), jnp.bfloat16),
         jax.ShapeDtypeStruct((176, span), jnp.bfloat16),
         jax.ShapeDtypeStruct((span, LANES), jnp.float32),
         jax.ShapeDtypeStruct((span, LANES), jnp.float32),
@@ -466,10 +462,10 @@
     )(position, starts, freqs, angles, mask, velocity)
 
 
-def line_dft_body(span, direct, *refs):
+def line_dft_body(span, has_part, *refs):
     mask_ref, vel_ref, a_ref, cos_ref, sin_ref = refs[:5]
     own_ref, near_ref, far2_ref, far3_ref, rot_ref = refs[-5:]
-    part_ref = None if direct else refs[5]
+    part_ref = refs[5] if has_part else None
     width = vel_ref.shape[2]
     none = jnp.zeros((24, width), jnp.float32)
     tails = [None] * COMPS
@@ -478,16 +474,14 @@
         sums = jnp.dot(a_ref[...], samples, preferred_element_type=jnp.float32)
         own_ref[48 * c:48 * c + 48, :] = sums[:48].astype(jnp.bfloat16)
         near_ref[48 * c:48 * c + 48, :] = sums[48:96].astype(jnp.bfloat16)
-        if direct:
-            far2_ref[48 * c:48 * c + 48, :] = sums[96:144].astype(jnp.bfloat16)
-            far3_ref[48 * c:48 * c + 48, :] = sums[144:].astype(jnp.bfloat16)
-        else:
+        far2, far3 = sums[96:128], sums[128:160]
+        if has_part:
             part = part_ref[16 * c:16 * c + 16, :].astype(jnp.float32)
-            far2 = sums[96:128] + jnp.concatenate([none, part[:8]], axis=0)
-            far3 = sums[128:160] + jnp.concatenate([none, part[8:]], axis=0)
-            far2_ref[32 * c:32 * c + 32, :] = far2.astype(jnp.bfloat16)
-            far3_ref[32 * c:32 * c + 32, :] = far3.astype(jnp.bfloat16)
-            tails[c] = sums[160:168]
+            far2 = far2 + jnp.concatenate([none, part[:8]], axis=0)
+            far3 = far3 + jnp.concatenate([none, part[8:]], axis=0)
+        far2_ref[32 * c:32 * c + 32, :] = far2.astype(jnp.bfloat16)
+        far3_ref[32 * c:32 * c + 32, :] = far3.astype(jnp.bfloat16)
+        tails[c] = sums[160:168]
 
     send(2, vel_ref[2])
     turning = mask_ref[...] == 1
@@ -498,30 +492,28 @@
         rot_ref[1, here, :] = new_y
     send(0, rot_ref[0])
     send(1, rot_ref[1])
-    if not direct:
-        far2_ref[96:112, :] = jnp.concatenate([t[:4] for t in tails] + [none[:4]], axis=0).astype(jnp.bfloat16)
-        far3_ref[96:112, :] = jnp.concatenate([t[4:] for t in tails] + [none[:4]], axis=0).astype(jnp.bfloat16)
+    far2_ref[96:112, :] = jnp.concatenate([t[:4] for t in tails] + [none[:4]], axis=0).astype(jnp.bfloat16)
+    far3_ref[96:112, :] = jnp.concatenate([t[4:] for t in tails] + [none[:4]], axis=0).astype(jnp.bfloat16)
 
 
 def line_dft(offset, points, mask, velocity, rows, cosine, sine, part, after):
     span = velocity.shape[1]
     shift = offset // TILE
-    direct = part is None
     whole = lambda shape: pl.BlockSpec(shape, lambda i: (0,) * len(shape))
     args = [mask, velocity, rows, cosine, sine]
     in_specs = [
         pl.BlockSpec((1, TILE), lambda i: (0, i + shift)),
         pl.BlockSpec((COMPS, span, TILE), lambda i: (0, 0, i + shift)),
     ] + [whole(x.shape) for x in args[2:]]
-    if not direct:
+    if part is not None:
         args.append(part)
         in_specs.append(pl.BlockSpec((48, TILE), lambda i: (0, i + shift)))
     if after is not None:
         args.append(after)
         in_specs.append(pl.BlockSpec(memory_space=pl.ANY))
-    heights = [144] * 4 if direct else [144, 144, 112, 112]
+    heights = [144, 144, 112, 112]
     return pl.pallas_call(
-        functools.partial(line_dft_body, span, direct),
+        functools.partial(line_dft_body, span, part is not None),
         grid=(points // TILE,),
         out_shape=[jax.ShapeDtypeStruct((h, points), jnp.bfloat16) for h in heights],
         in_specs=in_specs,
@@ -535,48 +527,76 @@
     )(*args)
 
 
-def line_selection(blocks, me, direct, sel_ref):
+def combine_body(far2_ref, far3_ref, part_ref, out2_ref, out3_ref):
+    for c in range(COMPS):
+        here = slice(32 * c, 32 * c + 32)
+        add = part_ref[16 * c:16 * c + 16, :].astype(jnp.float32)
+        none = jnp.zeros((24, add.shape[1]), jnp.float32)
+        for src, dst, part in ((far2_ref, out2_ref, add[:8]), (far3_ref, out3_ref, add[8:])):
+            dst[here, :] = (src[here, :].astype(jnp.float32) + jnp.concatenate([none, part], axis=0)).astype(jnp.bfloat16)
+    out2_ref[96:112, :] = far2_ref[96:112, :]
+    out3_ref[96:112, :] = far3_ref[96:112, :]
+
+
+def combine(far2, far3, part):
+    spec = pl.BlockSpec(far2.shape, lambda i: (0, 0))
+    return pl.pallas_call(
+        combine_body,
+        grid=(1,),
+        out_shape=[jax.ShapeDtypeStruct(far2.shape, far2.dtype)] * 2,
+        in_specs=[spec, spec, pl.BlockSpec((48, far2.shape[1]), lambda i: (0, 0))],
+        out_specs=[spec, spec],
+        compiler_params=pltpu.CompilerParams(vmem_limit_bytes=LIMIT_B * 2**20),
+        cost_estimate=pl.CostEstimate(flops=far2.size, bytes_accessed=8 * far2.size, transcendentals=0),
+        name="add_shared",
+    )(far2, far3, part)
+
+
+def line_selection(blocks, me, sel_ref):
     shape = (4 * blocks, 192)
     out = lax.broadcasted_iota(jnp.int32, shape, 0)
     col = lax.broadcasted_iota(jnp.int32, shape, 1)
     two, three = me ^ 2, me ^ 3
     block = jnp.where(col < 48, pick(LINE_LO, me) + col // 4, pick(LINE_LO, me ^ 1) + (col - 48) // 4)
-    if direct:
-        block = jnp.where(col >= 96, pick(LINE_LO, two) + (col - 96) // 4, block)
-        block = jnp.where(col >= 144, pick(LINE_LO, three) + (col - 144) // 4, block)
-    else:
-        block = jnp.where(col >= 96, far_block(two, (col - 96) // 4), block)
-        block = jnp.where(col >= 128, far_block(three, (col - 128) // 4), block)
-        block = jnp.where(col >= 160, far_block(two, FAR - 1), block)
-        block = jnp.where(col >= 176, far_block(three, FAR - 1), block)
+    block = jnp.where(col >= 96, far_block(two, (col - 96) // 4), block)
+    block = jnp.where(col >= 128, far_block(three, (col - 128) // 4), block)
+    block = jnp.where(col >= 160, far_block(two, FAR - 1), block)
+    block = jnp.where(col >= 176, far_block(three, FAR - 1), block)
     same = (out // blocks == col % 4) & (out % blocks == block)
     for c in range(COMPS):
-        mine = same if direct else same & ((col < 160) | ((col % 16) // 4 == c))
+        mine = same & ((col < 160) | ((col % 16) // 4 == c))
         sel_ref[c] = jnp.where(mine, 1.0, 0.0).astype(jnp.bfloat16)
 
 
-def line_assemble_body(blocks, total, has_sum, last, direct, *refs):
+def line_assemble_body(blocks, total, has_sum, last, has_carry, *refs):
     pos_ref, own_ref, near_ref, far2_ref, far3_ref = refs[:5]
-    rest = refs[5:]
+    *refs, acc_ref = refs
+    if has_carry:
+        *refs, carry_out_ref = refs
     if has_sum:
-        sum_in, rest = rest[0], rest[2:]
-    spectra_ref, gram_ref, sel_ref, acc_ref = rest[-4:]
+        sum_in, sel_ref = refs[5:7]
+        spectra_ref, gram_ref = refs[-2:]
+    else:
+        spectra_ref, gram_ref, sel_ref = refs[-3:]
+    if has_carry:
+        carry_ref = refs[8 if has_sum else 5]
     step = pl.program_id(0)
-    me = pos_ref[0]
 
     @pl.when(step == 0)
     def _():
-        line_selection(blocks, me, direct, sel_ref)
+        if not has_sum:
+            line_selection(blocks, pos_ref[0], sel_ref)
         acc_ref[...] = sum_in[...] if has_sum else jnp.zeros_like(acc_ref)
+        if has_carry:
+            carry_out_ref[...] = carry_ref[...]
 
     for c in range(COMPS):
         wide = slice(48 * c, 48 * c + 48)
-        parts = [own_ref[wide, :], near_ref[wide, :]]
-        if direct:
-            parts += [far2_ref[wide, :], far3_ref[wide, :]]
-        else:
-            here = slice(32 * c, 32 * c + 32)
-            parts += [far2_ref[here, :], far3_ref[here, :], far2_ref[96:112, :], far3_ref[96:112, :]]
+        here = slice(32 * c, 32 * c + 32)
+        parts = [
+            own_ref[wide, :], near_ref[wide, :],
+            far2_ref[here, :], far3_ref[here, :], far2_ref[96:112, :], far3_ref[96:112, :],
+        ]
         stack = jnp.concatenate(parts, axis=0)
         full = jnp.dot(sel_ref[c], stack, preferred_element_type=jnp.float32)
         for jr in range(4):
@@ -600,7 +620,7 @@
             gram_ref[...] = jnp.concatenate([gram[:order, :order], gram[order:, order:]], axis=1)
 
 
-def line_assemble(blocks, total, offset, points, all_points, position, own, near, fars, spectra, gram, last, after):
+def line_assemble(blocks, total, offset, points, all_points, position, own, near, fars, spectra, gram, sel, last, carry):
     shift = offset // TILE
     order = 2 * blocks
     has_sum = gram is not None
@@ -611,37 +631,45 @@
     in_specs += [pl.BlockSpec((a.shape[0], TILE), lambda i: (0, i)) for a in args[1:]]
     aliases = {}
     if has_sum:
-        args += [gram, spectra]
-        in_specs += [whole((4 * order, 4 * order)), pl.BlockSpec(memory_space=pl.ANY)]
+        args += [gram, sel, spectra]
+        in_specs += [whole(gram.shape), whole(sel.shape), pl.BlockSpec(memory_space=pl.ANY)]
         aliases = {len(args) - 1: 0}
-    if after is not None:
-        args.append(after)
-        in_specs.append(pl.BlockSpec(memory_space=pl.ANY))
-    return pl.pallas_call(
-        functools.partial(line_assemble_body, blocks, total, has_sum, last, fars[0].shape[0] == 144),
+    if carry is not None:
+        args.append(carry)
+        in_specs.append(whole(carry.shape))
+    out_shape = [
+        jax.ShapeDtypeStruct((2, 2, COMPS, blocks, all_points), jnp.float32),
+        jax.ShapeDtypeStruct(gram_shape, jnp.float32),
+    ]
+    out_specs = [
+        pl.BlockSpec((2, 2, COMPS, blocks, TILE), lambda i: (0, 0, 0, 0, i + shift)),
+        whole(gram_shape),
+    ]
+    if not has_sum:
+        out_shape.append(jax.ShapeDtypeStruct((COMPS, 4 * blocks, 192), jnp.bfloat16))
+        out_specs.append(whole((COMPS, 4 * blocks, 192)))
+    if carry is not None:
+        out_shape.append(jax.ShapeDtypeStruct(carry.shape, carry.dtype))
+        out_specs.append(whole(carry.shape))
+    out = pl.pallas_call(
+        functools.partial(line_assemble_body, blocks, total, has_sum, last, carry is not None),
         grid=(points // TILE,),
-        out_shape=[
-            jax.ShapeDtypeStruct((2, 2, COMPS, blocks, all_points), jnp.float32),
-            jax.ShapeDtypeStruct(gram_shape, jnp.float32),
-        ],
+        out_shape=out_shape,
         in_specs=in_specs,
-        out_specs=[
-            pl.BlockSpec((2, 2, COMPS, blocks, TILE), lambda i: (0, 0, 0, 0, i + shift)),
-            whole(gram_shape),
-        ],
-        scratch_shapes=[
-            pltpu.VMEM((COMPS, 4 * blocks, 192), jnp.bfloat16),
-            pltpu.VMEM((4 * order, 4 * order), jnp.float32),
-        ],
+        out_specs=out_specs,
+        scratch_shapes=[pltpu.VMEM((4 * order, 4 * order), jnp.float32)],
         input_output_aliases=aliases,
         compiler_params=pltpu.CompilerParams(vmem_limit_bytes=LIMIT_C * 2**20),
-        cost_estimate=SHORT,
+        cost_estimate=pl.CostEstimate(
+            flops=4 * 256 * 256 * COMPS * points, bytes_accessed=8 * order * COMPS * points, transcendentals=0
+        ),
         name="assemble",
     )(*args)
+    return list(out[:2]) + [sel if has_sum else out[2], out[-1]]
 
 
 def line_chunks(points):
-    cuts = [points * k // 8 for k in (0, 1, 3, 6, 8)]
+    cuts = [points * k // 8 for k in (0, 3, 6, 8)]
     return [(a, b - a) for a, b in zip(cuts[:-1], cuts[1:])]
 
 
@@ -650,28 +678,30 @@
     blocks = block_starts.shape[0]
     move = lambda x, pairs: lax.ppermute(x, "tm", pairs)
     across = lambda x, k: move(x, [(i, i ^ k) for i in range(4)])
-    part, direct_rows, rows, cosine, sine = prepare(
-        blocks, position, block_starts, frequencies, angles, mask, samples
-    )
+    part, rows, cosine, sine = prepare(blocks, position, block_starts, frequencies, angles, mask, samples)
     part = move(part, [(1, 0), (2, 3)])
-    spectra, gram = None, None
+    spectra, gram, sel, added = None, None, None, None
     sent = []
 
-    def assemble(after):
+    def assemble(carry):
         at, count, own, near, fars = sent.pop(0)
         return line_assemble(
-            blocks, total, at, count, points, position, own, near, fars, spectra, gram, at + count == points, after
+            blocks, total, at, count, points, position, own, across(near, 1), fars,
+            spectra, gram, sel, at + count == points, carry,
         )
 
     for i, (at, count) in enumerate(line_chunks(points)):
         if i >= 2:
-            spectra, gram = assemble(own)
-        own, near, far2, far3 = line_dft(
-            at, count, mask, samples, rows if i else direct_rows, cosine, sine, part if i else None, gram
-        )
-        sent.append((at, count, own, across(near, 1), [across(far2, 2), across(far3, 3)]))
+            spectra, gram, sel, _ = assemble(None)
+
+        wait = gram if i >= 2 else added
+        own, near, far2, far3 = line_dft(at, count, mask, samples, rows, cosine, sine, part if i else None, wait)
+        if i == 0:
+            far2, far3 = combine(far2, far3, part)
+            added = far2
+        sent.append([at, count, own, near, [across(far2, 2), across(far3, 3)]])
     while sent:
-        spectra, gram = assemble(None)
+        spectra, gram, sel, _ = assemble(None)
     return spectra, gram
 
 
@@ -688,8 +718,11 @@
         return [lax.psum(gram, "space")]
     swap = lambda x, k: lax.ppermute(x, "space", [(i, i ^ k) for i in range(groups)])
     gram = gram + swap(gram, 1)
-    gram = gram + swap(gram, 2)
-    return [gram, swap(gram, 4)]
+    side = [(i, i ^ (4 if i % 2 else 2)) for i in range(groups)]
+    corner = [(i, i ^ 6) for i in range(1, groups, 2)]
+    beside, across = lax.ppermute(gram, "space", side), lax.ppermute(gram, "space", corner)
+    half = beside + jnp.where(lax.axis_index("space") % 2 == 0, gram, across)
+    return [half, swap(half, 1)]
 
 
 def chunks_of(points):

time: 75.3 us -> 79.9 us (1.061)
  starting transfers between devices: 24.5 us -> 29.4 us
  waiting for transfers between devices: 11.2 us -> 15.1 us
  local copies, waits for them, and re-layouts: 4.58 us -> 2.02 us
  Pallas kernels: 33.9 us -> 32.3 us
    ppermute x13 -> x10, waiting for transfers between devices: 5.22 us -> 11.4 us  [line_spectra(): move = lambda x, pairs: lax.ppermute(x, 'tm', pairs)]
    ppermute x3 -> x2, waiting for transfers between devices: 6.02 us -> 2.06 us  [sum_over_space(): lax.ppermute(x, 'space', [(i, i ^ k) for i in range(groups)])]
    unnamed x26 -> x16, local copies, waits for them, and re-layouts: 4.58 us -> 2.02 us
    ppermute x13 -> x10, starting transfers between devices: 21.5 us -> 24 us  [line_spectra(): move = lambda x, pairs: lax.ppermute(x, 'tm', pairs)]
    ppermute x0 -> x2, starting transfers between devices: none -> 2.24 us  [the longest x1 1.59 us: sum_over_space(): lax.ppermute(gram, 'space', side)]
    ppermute x0 -> x2, waiting for transfers between devices: none -> 1.66 us  [the longest x1 1.65 us: sum_over_space(): lax.ppermute(gram, 'space', side)]
    pallas_call x4 -> x3, Pallas kernels: 7.43 us -> 7.04 us  [line_assemble(): pl.pallas_call(functools.partial(line_assemble_body, blocks, total, has_s...]
    ppermute x3 -> x2, starting transfers between devices: 3.08 us -> 3.18 us  [sum_over_space(): lax.ppermute(x, 'space', [(i, i ^ k) for i in range(groups)])]
  transfers between devices with their start and end apart: 16 -> 14, of which waited for: 4 -> 5; matrix products, arithmetic and copies ran while one was open for 0% -> 0% of each run, Pallas kernels for 33% -> 29%
where the time goes in v7:
time: 79.9 us; the launch traced here: 79.5 us
  Pallas kernels  32.3 us (40%)
  starting transfers between devices  29.4 us (37%)
  waiting for transfers between devices  15.1 us (19%)
  local copies, waits for them, and re-layouts  2.02 us (3%)
    ppermute x10, starting transfers between devices, line_spectra(): move = lambda x, pairs: lax.ppermute(x, 'tm', pairs)  24 us
    pallas_call x3, Pallas kernels, line_dft(): pl.pallas_call(functools.partial(line_dft_body, span, part is not None),...  16.4 us
    ppermute x10, waiting for transfers between devices, line_spectra(): move = lambda x, pairs: lax.ppermute(x, 'tm', pairs)  11.4 us
    pallas_call x3, Pallas kernels, line_assemble(): pl.pallas_call(functools.partial(line_assemble_body, blocks, total, has_s...  7.04 us
    pallas_call x1, Pallas kernels, prepare(): pl.pallas_call(functools.partial(prepare_body, span, blocks), grid=(1,),...  3.78 us
    pallas_call x1, Pallas kernels, factor_call(): pl.pallas_call(functools.partial(factor_body, owned, order, len(parts)),...  3.21 us
    ppermute x2, starting transfers between devices, sum_over_space(): lax.ppermute(x, 'space', [(i, i ^ k) for i in range(groups)])  3.18 us
    ppermute x2, waiting for transfers between devices, sum_over_space(): lax.ppermute(x, 'space', [(i, i ^ k) for i in range(groups)])  2.06 us
  transfers between devices with their start and end apart: 14, of which 5 were waited for; matrix products, arithmetic and copies ran while one was open for 0% of the time, Pallas kernels for 29%

profile of v7, /device:TPU:0, one launch (start us, length us, event | category | flops | bytes accessed | tf_op | source)
XLA Modules:
  0.0 79.5 jit_solution(11626838816378633209)
XLA Ops:
  0.6 3.8 %prepare.1 = (bf16[48,2048]{1,0:T(8,128)(2,1)}, bf16[176,1072]{1,0:T(8,128)(2,1)}, f32[1072,128]{1,0:T(8,128)}, f32[1072,128]{1,0:T(8,128)}) custom-call(s32[1]{0:T(128)} %bitcast.pos_ref.refs_0_, s32[32]{0:T(128)} %starts_ref.1, s32[8]{0:T(128)} %freqs_ref.1, f32[1072]{0:T(1024)} %angle_ref.1, s32[1,2048]{1,0:T(1,128)} %bitcast.9, ...), custom_call_target="tpu_custom_call" | custom-call | flops 1000000000 | bytes 4000000 | tf_op jit(solution)/shard_map/prepare/pallas_call | solution.py:447
  4.4 1.3 %collective-permute-start = (bf16[48,2048]{1,0:T(8,128)(2,1)}, bf16[48,2048]{1,0:T(8,128)(2,1)S(1)}, u32[]{:S(2)}, u32[]{:S(2)}) collective-permute-start(bf16[48,2048]{1,0:T(8,128)(2,1)} %get-tuple-element.30), channel_id=1, source_target_pairs={{1,0},{2,3},{5,4},{6,7},{9,8},{10,11},{13,12},{14,15},{17,16},{18,... | collective-permute-start | bytes 589832 | tf_op jit(solution)/shard_map/ppermute | solution.py:679
  5.7 5.6 %rotate_dft.3 = (bf16[144,768]{1,0:T(8,128)(2,1)}, bf16[144,768]{1,0:T(8,128)(2,1)}, bf16[112,768]{1,0:T(8,128)(2,1)}, bf16[112,768]{1,0:T(8,128)(2,1)}) custom-call(s32[1,2048]{1,0:T(1,128)} %bitcast.10, bf16[3,1072,2048]{2,1,0:T(8,128)(2,1)} %bitcast.5, bf16[176,1072]{1,0:T(8,128)(2,1)} %get-tuple-element.27.refs_2_, ...), custom_call_target="tpu_custom_call" | custom-call | flops 948436992 | bytes 4939776 | tf_op jit(solution)/shard_map/rotate_dft/pallas_call | solution.py:515
  11.3 3.1 %collective-permute-start.1 = (bf16[144,768]{1,0:T(8,128)(2,1)}, bf16[144,768]{1,0:T(8,128)(2,1)S(1)}, u32[]{:S(2)}, u32[]{:S(2)}) collective-permute-start(bf16[144,768]{1,0:T(8,128)(2,1)} %get-tuple-element.32), channel_id=1, source_target_pairs={{0,1},{1,0},{2,3},{3,2},{4,5},{5,4},{6,7},{7,6},{8,9},{9,8},{10,11... | collective-permute-start | bytes 663560 | tf_op jit(solution)/shard_map/ppermute | solution.py:679
  14.4 0.0 collective-permute-done.part_ref.refs_5_
  14.4 0.7 copy-done.5
  15.1 1.8 %add_shared.1 = (bf16[112,768]{1,0:T(8,128)(2,1)}, bf16[112,768]{1,0:T(8,128)(2,1)}) custom-call(bf16[112,768]{1,0:T(8,128)(2,1)} %get-tuple-element.33.far2_ref, bf16[112,768]{1,0:T(8,128)(2,1)} %get-tuple-element.34.far3_ref, bf16[48,2048]{1,0:T(8,128)(2,1)} %copy-done.5), custom_call_target="tpu_custom_call" | custom-call | flops 86016 | bytes 688128 | tf_op jit(solution)/shard_map/add_shared/pallas_call | solution.py:543
  16.9 3.2 %collective-permute-start.2 = (bf16[112,768]{1,0:T(8,128)(2,1)}, bf16[112,768]{1,0:T(8,128)(2,1)S(1)}, u32[]{:S(2)}, u32[]{:S(2)}) collective-permute-start(bf16[112,768]{1,0:T(8,128)(2,1)} %get-tuple-element.35.refs_6_), channel_id=1, source_target_pairs={{0,2},{1,3},{2,0},{3,1},{4,6},{5,7},{6,4},{7,5},{8,10},{9,11},{10,... | collective-permute-start | bytes 516104 | tf_op jit(solution)/shard_map/ppermute | solution.py:679
  20.1 1.5 %collective-permute-start.3 = (bf16[112,768]{1,0:T(8,128)(2,1)}, bf16[112,768]{1,0:T(8,128)(2,1)S(1)}, u32[]{:S(2)}, u32[]{:S(2)}) collective-permute-start(bf16[112,768]{1,0:T(8,128)(2,1)} %get-tuple-element.36), channel_id=1, source_target_pairs={{0,3},{1,2},{2,1},{3,0},{4,7},{5,6},{6,5},{7,4},{8,11},{9,10},{10,... | collective-permute-start | bytes 516104 | tf_op jit(solution)/shard_map/ppermute | solution.py:679
  21.6 6.2 %rotate_dft.5 = (bf16[144,768]{1,0:T(8,128)(2,1)}, bf16[144,768]{1,0:T(8,128)(2,1)}, bf16[112,768]{1,0:T(8,128)(2,1)}, bf16[112,768]{1,0:T(8,128)(2,1)}) custom-call(s32[1,2048]{1,0:T(1,128)} %bitcast.11, bf16[3,1072,2048]{2,1,0:T(8,128)(2,1)} %bitcast.6, bf16[176,1072]{1,0:T(8,128)(2,1)} %get-tuple-element.27.refs_2_, ...), custom_call_target="tpu_custom_call" | custom-call | flops 948436992 | bytes 4939776 | tf_op jit(solution)/shard_map/rotate_dft/pallas_call | solution.py:515
  27.7 2.0 %collective-permute-start.8 = (bf16[112,768]{1,0:T(8,128)(2,1)}, bf16[112,768]{1,0:T(8,128)(2,1)S(1)}, u32[]{:S(2)}, u32[]{:S(2)}) collective-permute-start(bf16[112,768]{1,0:T(8,128)(2,1)} %get-tuple-element.44), channel_id=1, source_target_pairs={{0,2},{1,3},{2,0},{3,1},{4,6},{5,7},{6,4},{7,5},{8,10},{9,11},{10,... | collective-permute-start | bytes 516104 | tf_op jit(solution)/shard_map/ppermute | solution.py:679
  29.8 0.9 %collective-permute-start.7 = (bf16[144,768]{1,0:T(8,128)(2,1)}, bf16[144,768]{1,0:T(8,128)(2,1)S(1)}, u32[]{:S(2)}, u32[]{:S(2)}) collective-permute-start(bf16[144,768]{1,0:T(8,128)(2,1)} %get-tuple-element.43), channel_id=1, source_target_pairs={{0,1},{1,0},{2,3},{3,2},{4,5},{5,4},{6,7},{7,6},{8,9},{9,8},{10,11... | collective-permute-start | bytes 663560 | tf_op jit(solution)/shard_map/ppermute | solution.py:679
  30.7 0.0 collective-permute-done.1.refs_2_
  30.7 1.5 %collective-permute-start.9 = (bf16[112,768]{1,0:T(8,128)(2,1)}, bf16[112,768]{1,0:T(8,128)(2,1)S(1)}, u32[]{:S(2)}, u32[]{:S(2)}) collective-permute-start(bf16[112,768]{1,0:T(8,128)(2,1)} %get-tuple-element.45), channel_id=1, source_target_pairs={{0,3},{1,2},{2,1},{3,0},{4,7},{5,6},{6,5},{7,4},{8,11},{9,10},{10,... | collective-permute-start | bytes 516104 | tf_op jit(solution)/shard_map/ppermute | solution.py:679
  32.1 4.5 %collective-permute-done.2.refs_3_ = bf16[112,768]{1,0:T(8,128)(2,1)S(1)} collective-permute-done((bf16[112,768]{1,0:T(8,128)(2,1)}, bf16[112,768]{1,0:T(8,128)(2,1)S(1)}, u32[]{:S(2)}, u32[]{:S(2)}) %collective-permute-start.2) | collective-permute-done | bytes 172064 | tf_op jit(solution)/shard_map/ppermute | solution.py:679
  36.6 2.6 %assemble.3 = (f32[2,2,3,32,2048]{4,3,2,1,0:T(8,128)}, f32[256,256]{1,0:T(8,128)S(1)}, bf16[3,128,192]{2,1,0:T(8,128)(2,1)S(1)}) custom-call(s32[1]{0:T(128)} %bitcast.pos_ref.refs_0_, bf16[144,768]{1,0:T(8,128)(2,1)S(1)} %copy-done.4, bf16[144,768]{1,0:T(8,128)(2,1)S(1)} %collective-permute-done.1.refs_2_, ...), custom_call_target="tpu_custom_call" | custom-call | flops 603979776 | bytes 1179648 | tf_op jit(solution)/shard_map/assemble/pallas_call | solution.py:654
  39.2 0.7 copy-done
  39.9 4.7 %rotate_dft.4 = (bf16[144,512]{1,0:T(8,128)(2,1)}, bf16[144,512]{1,0:T(8,128)(2,1)}, bf16[112,512]{1,0:T(8,128)(2,1)}, bf16[112,512]{1,0:T(8,128)(2,1)}) custom-call(s32[1,2048]{1,0:T(1,128)} %bitcast.12, bf16[3,1072,2048]{2,1,0:T(8,128)(2,1)} %bitcast.7, bf16[176,1072]{1,0:T(8,128)(2,1)} %get-tuple-element.27.refs_2_, ...), custom_call_target="tpu_custom_call" | custom-call | flops 632291328 | bytes 3293184 | tf_op jit(solution)/shard_map/rotate_dft/pallas_call | solution.py:515
  44.6 8.0 %collective-permute-start.4 = (bf16[144,512]{1,0:T(8,128)(2,1)}, bf16[144,512]{1,0:T(8,128)(2,1)S(1)}, u32[]{:S(2)}, u32[]{:S(2)}) collective-permute-start(bf16[144,512]{1,0:T(8,128)(2,1)} %get-tuple-element.39), channel_id=1, source_target_pairs={{0,1},{1,0},{2,3},{3,2},{4,5},{5,4},{6,7},{7,6},{8,9},{9,8},{10,11... | collective-permute-start | bytes 442376 | tf_op jit(solution)/shard_map/ppermute | solution.py:679
  52.6 1.1 %collective-permute-start.5 = (bf16[112,512]{1,0:T(8,128)(2,1)}, bf16[112,512]{1,0:T(8,128)(2,1)S(1)}, u32[]{:S(2)}, u32[]{:S(2)}) collective-permute-start(bf16[112,512]{1,0:T(8,128)(2,1)} %get-tuple-element.40), channel_id=1, source_target_pairs={{0,2},{1,3},{2,0},{3,1},{4,6},{5,7},{6,4},{7,5},{8,10},{9,11},{10,... | collective-permute-start | bytes 344072 | tf_op jit(solution)/shard_map/ppermute | solution.py:679
  53.7 1.4 %collective-permute-start.6 = (bf16[112,512]{1,0:T(8,128)(2,1)}, bf16[112,512]{1,0:T(8,128)(2,1)S(1)}, u32[]{:S(2)}, u32[]{:S(2)}) collective-permute-start(bf16[112,512]{1,0:T(8,128)(2,1)} %get-tuple-element.41), channel_id=1, source_target_pairs={{0,3},{1,2},{2,1},{3,0},{4,7},{5,6},{6,5},{7,4},{8,11},{9,10},{10,... | collective-permute-start | bytes 344072 | tf_op jit(solution)/shard_map/ppermute | solution.py:679
  55.1 2.6 %assemble.4 = (f32[2,2,3,32,2048]{4,3,2,1,0:T(8,128)}, f32[256,256]{1,0:T(8,128)S(1)}) custom-call(s32[1]{0:T(128)} %bitcast.pos_ref.refs_0_, bf16[144,768]{1,0:T(8,128)(2,1)S(1)} %copy-done.2, bf16[144,768]{1,0:T(8,128)(2,1)S(1)} %collective-permute-done.7.refs_2_, ...), custom_call_target="tpu_custom_call", output_to_operand_aliasing={{0}: (7, {})} | custom-call | flops 603979776 | bytes 1179648 | tf_op jit(solution)/shard_map/assemble/pallas_call | solution.py:654
  57.7 6.9 %collective-permute-done.5.refs_3_ = bf16[112,512]{1,0:T(8,128)(2,1)S(1)} collective-permute-done((bf16[112,512]{1,0:T(8,128)(2,1)}, bf16[112,512]{1,0:T(8,128)(2,1)S(1)}, u32[]{:S(2)}, u32[]{:S(2)}) %collective-permute-start.5) | collective-permute-done | bytes 114720 | tf_op jit(solution)/shard_map/ppermute | solution.py:679
  64.7 1.9 %assemble.5 = (f32[2,2,3,32,2048]{4,3,2,1,0:T(8,128)}, f32[64,128]{1,0:T(8,128)S(1)}) custom-call(s32[1]{0:T(128)} %bitcast.pos_ref.refs_0_, bf16[144,512]{1,0:T(8,128)(2,1)S(1)} %copy-done.3, bf16[144,512]{1,0:T(8,128)(2,1)S(1)} %collective-permute-done.4.refs_2_, ...), custom_call_target="tpu_custom_call", output_to_operand_aliasing={{0}: (7, {})} | custom-call | flops 402653184 | bytes 786432 | tf_op jit(solution)/shard_map/assemble/pallas_call | solution.py:654
  66.5 1.2 %collective-permute-done.10 = f32[64,128]{1,0:T(8,128)S(1)} collective-permute-done((f32[64,128]{1,0:T(8,128)S(1)}, f32[64,128]{1,0:T(8,128)S(1)}, u32[]{:S(2)}, u32[]{:S(2)}) %collective-permute-start.10) | collective-permute-done | bytes 32800 | tf_op jit(solution)/shard_map/ppermute | solution.py:719
  67.7 1.6 %collective-permute-start.11 = (f32[64,128]{1,0:T(8,128)S(1)}, f32[64,128]{1,0:T(8,128)S(1)}, u32[]{:S(2)}, u32[]{:S(2)}) collective-permute-start(f32[64,128]{1,0:T(8,128)S(1)} %add.10), channel_id=1, source_target_pairs={{0,8},{4,20},{8,0},{12,28},{16,24},{20,4},{24,16},{28,12},{1,9},{5... | collective-permute-start | bytes 98312 | tf_op jit(solution)/shard_map/ppermute | solution.py:723
  69.3 0.7 collective-permute-start.12
  70.0 1.7 %collective-permute-done.11 = f32[64,128]{1,0:T(8,128)S(1)} collective-permute-done((f32[64,128]{1,0:T(8,128)S(1)}, f32[64,128]{1,0:T(8,128)S(1)}, u32[]{:S(2)}, u32[]{:S(2)}) %collective-permute-start.11) | collective-permute-done | bytes 32800 | tf_op jit(solution)/shard_map/ppermute | solution.py:723
  71.7 3.2 %collective-permute-start.13 = (f32[64,128]{1,0:T(8,128)S(1)}, f32[64,128]{1,0:T(8,128)S(1)}, u32[]{:S(2)}, u32[]{:S(2)}) collective-permute-start(f32[64,128]{1,0:T(8,128)S(1)} %select_add_fusion.refs_0_), channel_id=1, source_target_pairs={{0,4},{4,0},{8,12},{12,8},{16,20},{20,16},{24,28},{28,24},{1,5},{5... | collective-permute-start | bytes 98312 | tf_op jit(solution)/shard_map/ppermute | solution.py:719
  74.9 0.9 %collective-permute-done.13.refs_1_ = f32[64,128]{1,0:T(8,128)S(1)} collective-permute-done((f32[64,128]{1,0:T(8,128)S(1)}, f32[64,128]{1,0:T(8,128)S(1)}, u32[]{:S(2)}, u32[]{:S(2)}) %collective-permute-start.13) | collective-permute-done | bytes 32800 | tf_op jit(solution)/shard_map/ppermute | solution.py:719
  75.7 0.6 copy-done.7
  76.3 3.2 %factor.1 = f32[2,64,64]{2,1,0:T(8,128)} custom-call(f32[64,128]{1,0:T(8,128)} %copy-done.6, f32[64,128]{1,0:T(8,128)} %copy-done.7), custom_call_target="tpu_custom_call" | custom-call | tf_op jit(solution)/shard_map/factor/pallas_call | solution.py:304
  (23 shorter events, 0.1 us)
Async XLA Ops:
  4.4 10.0 %collective-permute-start = (bf16[48,2048]{1,0:T(8,128)(2,1)}, bf16[48,2048]{1,0:T(8,128)(2,1)S(1)}, u32[]{:S(2)}, u32[]{:S(2)}) collective-permute-start(bf16[48,2048]{1,0:T(8,128)(2,1)} %get-tuple-element.30), channel_id=1, source_target_pairs={{1,0},{2,3},{5,4},{6,7},{9,8},{10,11},{13,12},{14,15},{17,16},{18,... | collective-permute-start | bytes 589832 | tf_op jit(solution)/shard_map/ppermute | solution.py:679
  11.3 19.4 %collective-permute-start.1 = (bf16[144,768]{1,0:T(8,128)(2,1)}, bf16[144,768]{1,0:T(8,128)(2,1)S(1)}, u32[]{:S(2)}, u32[]{:S(2)}) collective-permute-start(bf16[144,768]{1,0:T(8,128)(2,1)} %get-tuple-element.32), channel_id=1, source_target_pairs={{0,1},{1,0},{2,3},{3,2},{4,5},{5,4},{6,7},{7,6},{8,9},{9,8},{10,11... | collective-permute-start | bytes 663560 | tf_op jit(solution)/shard_map/ppermute | solution.py:679
  14.4 0.7 copy-start.5
  16.9 19.7 %collective-permute-start.2 = (bf16[112,768]{1,0:T(8,128)(2,1)}, bf16[112,768]{1,0:T(8,128)(2,1)S(1)}, u32[]{:S(2)}, u32[]{:S(2)}) collective-permute-start(bf16[112,768]{1,0:T(8,128)(2,1)} %get-tuple-element.35.refs_6_), channel_id=1, source_target_pairs={{0,2},{1,3},{2,0},{3,1},{4,6},{5,7},{6,4},{7,5},{8,10},{9,11},{10,... | collective-permute-start | bytes 516104 | tf_op jit(solution)/shard_map/ppermute | solution.py:679
  20.1 16.5 %copy-start.4 = (bf16[144,768]{1,0:T(8,128)(2,1)S(1)}, bf16[144,768]{1,0:T(8,128)(2,1)}, u32[]{:S(2)}) copy-start(bf16[144,768]{1,0:T(8,128)(2,1)} %get-tuple-element.31.refs_1_) | copy-start | bytes 663556
  20.1 16.5 %collective-permute-start.3 = (bf16[112,768]{1,0:T(8,128)(2,1)}, bf16[112,768]{1,0:T(8,128)(2,1)S(1)}, u32[]{:S(2)}, u32[]{:S(2)}) collective-permute-start(bf16[112,768]{1,0:T(8,128)(2,1)} %get-tuple-element.36), channel_id=1, source_target_pairs={{0,3},{1,2},{2,1},{3,0},{4,7},{5,6},{6,5},{7,4},{8,11},{9,10},{10,... | collective-permute-start | bytes 516104 | tf_op jit(solution)/shard_map/ppermute | solution.py:679
  27.7 26.0 %collective-permute-start.8 = (bf16[112,768]{1,0:T(8,128)(2,1)}, bf16[112,768]{1,0:T(8,128)(2,1)S(1)}, u32[]{:S(2)}, u32[]{:S(2)}) collective-permute-start(bf16[112,768]{1,0:T(8,128)(2,1)} %get-tuple-element.44), channel_id=1, source_target_pairs={{0,2},{1,3},{2,0},{3,1},{4,6},{5,7},{6,4},{7,5},{8,10},{9,11},{10,... | collective-permute-start | bytes 516104 | tf_op jit(solution)/shard_map/ppermute | solution.py:679
  29.8 25.4 %collective-permute-start.7 = (bf16[144,768]{1,0:T(8,128)(2,1)}, bf16[144,768]{1,0:T(8,128)(2,1)S(1)}, u32[]{:S(2)}, u32[]{:S(2)}) collective-permute-start(bf16[144,768]{1,0:T(8,128)(2,1)} %get-tuple-element.43), channel_id=1, source_target_pairs={{0,1},{1,0},{2,3},{3,2},{4,5},{5,4},{6,7},{7,6},{8,9},{9,8},{10,11... | collective-permute-start | bytes 663560 | tf_op jit(solution)/shard_map/ppermute | solution.py:679
  30.7 24.4 %collective-permute-start.9 = (bf16[112,768]{1,0:T(8,128)(2,1)}, bf16[112,768]{1,0:T(8,128)(2,1)S(1)}, u32[]{:S(2)}, u32[]{:S(2)}) collective-permute-start(bf16[112,768]{1,0:T(8,128)(2,1)} %get-tuple-element.45), channel_id=1, source_target_pairs={{0,3},{1,2},{2,1},{3,0},{4,7},{5,6},{6,5},{7,4},{8,11},{9,10},{10,... | collective-permute-start | bytes 516104 | tf_op jit(solution)/shard_map/ppermute | solution.py:679
  39.2 0.7 copy-start
  39.9 15.2 %copy-start.1 = (f32[256,256]{1,0:T(8,128)S(1)}, f32[256,256]{1,0:T(8,128)}, u32[]{:S(2)}) copy-start(f32[256,256]{1,0:T(8,128)} %copy-done) | copy-start | bytes 786436
  39.9 15.2 %copy-start.2 = (bf16[144,768]{1,0:T(8,128)(2,1)S(1)}, bf16[144,768]{1,0:T(8,128)(2,1)}, u32[]{:S(2)}) copy-start(bf16[144,768]{1,0:T(8,128)(2,1)} %get-tuple-element.42.refs_1_) | copy-start | bytes 663556
  44.6 20.0 %copy-start.3 = (bf16[144,512]{1,0:T(8,128)(2,1)S(1)}, bf16[144,512]{1,0:T(8,128)(2,1)}, u32[]{:S(2)}) copy-start(bf16[144,512]{1,0:T(8,128)(2,1)} %get-tuple-element.38.refs_1_) | copy-start | bytes 442372
  44.6 20.0 %collective-permute-start.4 = (bf16[144,512]{1,0:T(8,128)(2,1)}, bf16[144,512]{1,0:T(8,128)(2,1)S(1)}, u32[]{:S(2)}, u32[]{:S(2)}) collective-permute-start(bf16[144,512]{1,0:T(8,128)(2,1)} %get-tuple-element.39), channel_id=1, source_target_pairs={{0,1},{1,0},{2,3},{3,2},{4,5},{5,4},{6,7},{7,6},{8,9},{9,8},{10,11... | collective-permute-start | bytes 442376 | tf_op jit(solution)/shard_map/ppermute | solution.py:679
  52.6 12.0 %collective-permute-start.5 = (bf16[112,512]{1,0:T(8,128)(2,1)}, bf16[112,512]{1,0:T(8,128)(2,1)S(1)}, u32[]{:S(2)}, u32[]{:S(2)}) collective-permute-start(bf16[112,512]{1,0:T(8,128)(2,1)} %get-tuple-element.40), channel_id=1, source_target_pairs={{0,2},{1,3},{2,0},{3,1},{4,6},{5,7},{6,4},{7,5},{8,10},{9,11},{10,... | collective-permute-start | bytes 344072 | tf_op jit(solution)/shard_map/ppermute | solution.py:679
  53.7 10.9 %collective-permute-start.6 = (bf16[112,512]{1,0:T(8,128)(2,1)}, bf16[112,512]{1,0:T(8,128)(2,1)S(1)}, u32[]{:S(2)}, u32[]{:S(2)}) collective-permute-start(bf16[112,512]{1,0:T(8,128)(2,1)} %get-tuple-element.41), channel_id=1, source_target_pairs={{0,3},{1,2},{2,1},{3,0},{4,7},{5,6},{6,5},{7,4},{8,11},{9,10},{10,... | collective-permute-start | bytes 344072 | tf_op jit(solution)/shard_map/ppermute | solution.py:679
  66.5 1.2 %collective-permute-start.10 = (f32[64,128]{1,0:T(8,128)S(1)}, f32[64,128]{1,0:T(8,128)S(1)}, u32[]{:S(2)}, u32[]{:S(2)}) collective-permute-start(f32[64,128]{1,0:T(8,128)S(1)} %get-tuple-element.51), channel_id=1, source_target_pairs={{0,4},{4,0},{8,12},{12,8},{16,20},{20,16},{24,28},{28,24},{1,5},{5... | collective-permute-start | bytes 98312 | tf_op jit(solution)/shard_map/ppermute | solution.py:719
  67.7 3.9 %collective-permute-start.11 = (f32[64,128]{1,0:T(8,128)S(1)}, f32[64,128]{1,0:T(8,128)S(1)}, u32[]{:S(2)}, u32[]{:S(2)}) collective-permute-start(f32[64,128]{1,0:T(8,128)S(1)} %add.10), channel_id=1, source_target_pairs={{0,8},{4,20},{8,0},{12,28},{16,24},{20,4},{24,16},{28,12},{1,9},{5... | collective-permute-start | bytes 98312 | tf_op jit(solution)/shard_map/ppermute | solution.py:723
  69.3 2.3 %collective-permute-start.12 = (f32[64,128]{1,0:T(8,128)S(1)}, f32[64,128]{1,0:T(8,128)S(1)}, u32[]{:S(2)}, u32[]{:S(2)}) collective-permute-start(f32[64,128]{1,0:T(8,128)S(1)} %add.10), channel_id=1, source_target_pairs={{4,28},{12,20},{20,12},{28,4},{5,29},{13,21},{21,13},{29,5},{6,30}... | collective-permute-start | bytes 98312 | tf_op jit(solution)/shard_map/ppermute | solution.py:723
  71.7 4.1 %copy-start.6 = (f32[64,128]{1,0:T(8,128)}, f32[64,128]{1,0:T(8,128)S(1)}, u32[]{:S(2)}) copy-start(f32[64,128]{1,0:T(8,128)S(1)} %select_add_fusion.refs_0_) | copy-start | bytes 98308
  71.7 4.0 %collective-permute-start.13 = (f32[64,128]{1,0:T(8,128)S(1)}, f32[64,128]{1,0:T(8,128)S(1)}, u32[]{:S(2)}, u32[]{:S(2)}) collective-permute-start(f32[64,128]{1,0:T(8,128)S(1)} %select_add_fusion.refs_0_), channel_id=1, source_target_pairs={{0,4},{4,0},{8,12},{12,8},{16,20},{20,16},{24,28},{28,24},{1,5},{5... | collective-permute-start | bytes 98312 | tf_op jit(solution)/shard_map/ppermute | solution.py:719
  75.7 0.6 copy-start.7

commit v8 on v2

--- a/solution.py
+++ b/solution.py
@@ -14,7 +14,7 @@
 HOP = 128
 LANES = 128
 TILE = 256
-PIVOT = 4
+PIVOT = 8
 SCALE = (8.0 / (3.0 * NFFT)) ** 0.5
 HIGHEST = lax.Precision.HIGHEST
 
@@ -23,14 +23,13 @@
     return jnp.maximum((shard * span - (NFFT + JIT - 1) + HOP) // HOP, 0)
 
 
-def slot_count(shards, span, blocks, rows_per_slot):
+def slot_count(shards, span, blocks):
     most = 0
     for s in range(shards):
         lo = max((s * span - (NFFT + JIT - 1) + HOP) // HOP, 0)
         hi = min((span * (s + 1) - 1) // HOP, blocks - 1)
         most = max(most, hi - lo + 1)
-    step = 16 // math.gcd(16, rows_per_slot)
-    return -(-most // step) * step
+    return most
 
 
 def half_turn_sine(x):
@@ -42,35 +41,59 @@
     return acc * x
 
 
+def layout(rows):
+    main = rows // 16 * 16
+    return main, rows - main, -(-COMPS * rows // 8) * 8
+
+
+def cosine_of(turns):
+    s = half_turn_sine(turns - jnp.floor(turns + 0.5))
+    return 1.0 - 2.0 * s * s
+
+
 def build_rows(n, owned, slots, span, blocks, me, starts_ref, freqs_ref, a_ref):
     group = owned * 2
+    lo = first_block(me, span)
+    starts = [starts_ref[jnp.minimum(lo + s, blocks - 1)] for s in range(slots)]
+
+    def by_slot(shape, axis):
+        at = lax.broadcasted_iota(jnp.int32, shape, axis)
+        out = jnp.full(shape, starts[0], jnp.int32)
+        for s in range(1, slots):
+            out = jnp.where(at == s, starts[s], out)
+        return out
+
     rid = lax.broadcasted_iota(jnp.int32, (n * group, 1), 0)
-    k_of, j_of, r_of = rid // group, (rid // 2) % owned, rid % 2
-    f_of = lax.rem(me + k_of, n) * owned + j_of
+    f_of = lax.rem(me + rid // group, n) * owned + (rid // 2) % owned
     freq = jnp.zeros((n * group, 1), jnp.float32)
     for f in range(n * owned):
         freq = jnp.where(f_of == f, freqs_ref[f].astype(jnp.float32), freq)
     step = freq * (1.0 / NFFT)
-    quarter = r_of.astype(jnp.float32) * 0.25
-    lo = first_block(me, span)
+    quarter = (rid % 2).astype(jnp.float32) * 0.25
+
     sample = lax.broadcasted_iota(jnp.int32, (1, span), 1) + me * span
+    turns = sample.astype(jnp.float32) * step
+    turns = turns - jnp.floor(turns) + quarter
+    cos_t, sin_t = cosine_of(turns), cosine_of(turns - 0.25)
+    begin = by_slot((1, LANES), 1).astype(jnp.float32) * step
+    begin = begin - jnp.floor(begin)
+    cos_b, sin_b = cosine_of(begin), cosine_of(begin - 0.25)
+
+    slot = lax.broadcasted_iota(jnp.int32, (16, 1), 0)
+    ni = sample - by_slot((16, 1), 0)
+    nf = ni.astype(jnp.float32)
+    w = half_turn_sine(jnp.minimum(nf, NFFT - nf) * (1.0 / NFFT))
+    w = jnp.where((ni >= 0) & (ni < NFFT) & (slot + lo < blocks), w * w * SCALE, 0.0)
+
     pieces = [[] for _ in range(n)]
     for s in range(slots):
-        b = lo + s
-        start = starts_ref[jnp.minimum(b, blocks - 1)]
-        ni = sample - start
-        inside = (ni >= 0) & (ni < NFFT) & (b < blocks)
-        nf = ni.astype(jnp.float32)
-        w = half_turn_sine(jnp.minimum(nf, NFFT - nf) * (1.0 / NFFT))
-        w = jnp.where(inside, w * w * SCALE, 0.0)
-        nf = jnp.where(inside, nf, 0.0)
-        turns = nf * step + quarter
-        turns = turns - jnp.floor(turns + 0.5)
-        h = half_turn_sine(turns)
-        rows = w * (1.0 - 2.0 * h * h)
+        rows = (cos_t * cos_b[:, s:s + 1] + sin_t * sin_b[:, s:s + 1]) * w[s:s + 1]
         for k in range(n):
             pieces[k].append(rows[k * group:(k + 1) * group])
+    padding = a_ref.shape[1] - slots * group
     for k in range(n):
+        if padding:
+            pieces[k].append(jnp.zeros((padding, span), jnp.float32))
         a_ref[k] = jnp.concatenate(pieces[k], axis=0).astype(jnp.bfloat16)
 
 
@@ -112,17 +135,30 @@
         rot_ref[0, here, :] = jnp.where(turning, cosine * x - sine * y, x).astype(jnp.bfloat16)
         rot_ref[1, here, :] = jnp.where(turning, sine * x + cosine * y, y).astype(jnp.bfloat16)
     rows = a_ref.shape[1]
+    main, tail, height = layout(slots * owned * 2)
     a = a_ref[...].reshape(n * rows, span)
+    tails = []
     for c in range(COMPS):
         samples = rot_ref[c] if c < 2 else vel_ref[2]
-        sums = jnp.dot(a, samples, preferred_element_type=jnp.float32).astype(jnp.bfloat16)
-        for k in range(n):
-            outs[k][c * rows:(c + 1) * rows, :] = sums[k * rows:(k + 1) * rows]
+        sums = jnp.dot(a, samples, preferred_element_type=jnp.float32)
+        outs[0][c * rows:(c + 1) * rows, :] = sums[:rows].astype(jnp.bfloat16)
+        if main:
+            for k in range(1, n):
+                outs[k][c * main:(c + 1) * main, :] = sums[k * rows:k * rows + main].astype(jnp.bfloat16)
+        tails.append(sums)
+    if height > COMPS * main:
+        for k in range(1, n):
+            parts = [t[k * rows + main:k * rows + main + tail] for t in tails] if tail else []
+            padding = height - COMPS * (main + tail)
+            if padding:
+                parts.append(jnp.zeros((padding, width), jnp.float32))
+            outs[k][COMPS * main:, :] = jnp.concatenate(parts, axis=0).astype(jnp.bfloat16)
 
 
 def dft_call(n, owned, slots, blocks, first, offset, points, position, starts, freqs, angles, mask, velocity, shared):
     span = velocity.shape[1]
-    rows = slots * owned * 2
+    rows = -(-slots * owned * 2 // 16) * 16
+    heights = [COMPS * rows] + [layout(slots * owned * 2)[2]] * (n - 1)
     shift = offset // TILE
     whole = lambda shape: pl.BlockSpec(shape, lambda i: (0,) * len(shape))
     smem = pl.BlockSpec(memory_space=pltpu.SMEM)
@@ -136,8 +172,8 @@
         jax.ShapeDtypeStruct((span, LANES), jnp.float32),
     ]
     shared_specs = [whole(t.shape) for t in shared_types]
-    out_types = [jax.ShapeDtypeStruct((COMPS * rows, points), jnp.bfloat16)] * n
-    out_specs = [pl.BlockSpec((COMPS * rows, TILE), lambda i: (0, i))] * n
+    out_types = [jax.ShapeDtypeStruct((h, points), jnp.bfloat16) for h in heights]
+    out_specs = [pl.BlockSpec((h, TILE), lambda i: (0, i)) for h in heights]
     if first:
         args = (position, starts, freqs, angles, mask, velocity)
         in_specs = [smem] * 3 + [whole((span,))] + data_specs
@@ -164,47 +200,74 @@
     return out[:n], out[n:] if first else shared
 
 
-def selection(n, owned, slots, span, blocks, me):
-    rows = slots * owned * 2
-    shape = (owned * 2 * blocks, n * rows)
+def stack_width(n, rows):
+    main, tail, height = layout(rows)
+    return -(-rows // 16) * 16 + (n - 1) * (height - (COMPS - 1) * main)
+
+
+def selection(n, owned, slots, span, blocks, me, sel_ref):
+    group = owned * 2
+    main, tail, height = layout(slots * group)
+    rest = height - COMPS * main
+    shape = sel_ref.shape[1:]
     out = lax.broadcasted_iota(jnp.int32, shape, 0)
     col = lax.broadcasted_iota(jnp.int32, shape, 1)
-    k_of = jnp.zeros(shape, jnp.int32)
+    at = -(-slots * group // 16) * 16
     lo = jnp.broadcast_to(first_block(me, span), shape)
-    for k in range(1, n):
-        past = col >= k * rows
-        k_of = jnp.where(past, k, k_of)
-        lo = jnp.where(past, first_block(lax.rem(me + n - k, n), span), lo)
-    rem = col - k_of * rows
-    slot = rem // (owned * 2)
-    same = (out // blocks == rem % (owned * 2)) & (out % blocks == lo + slot)
-    return jnp.where(same, 1.0, 0.0)
+    row = jnp.where(col < slots * group, col, -1)
+    comp = jnp.full(shape, -1, jnp.int32)
+    for size, base in ((main, 0), (rest, main)):
+        for k in range(1, n):
+            here = (col >= at) & (col < at + size)
+            lo = jnp.where(here, first_block(lax.rem(me + n - k, n), span), lo)
+            if base == 0:
+                row = jnp.where(here, col - at, row)
+            elif tail:
+                piece = (col - at) // tail
+                row = jnp.where(here, jnp.where(piece < COMPS, main + (col - at) % tail, -1), row)
+                comp = jnp.where(here, piece, comp)
+            at += size
+    same = (row >= 0) & (out // blocks == row % group) & (out % blocks == lo + row // group)
+    for c in range(COMPS):
+        sel_ref[c] = jnp.where(same & ((comp < 0) | (comp == c)), 1.0, 0.0).astype(jnp.bfloat16)
 
 
 def assemble_body(n, owned, slots, span, blocks, total, has_sum, last, *refs):
     pos_ref = refs[0]
     parts = refs[1:1 + n]
-    rest = refs[1 + n:]
+    *rest, acc_ref = refs[1 + n:]
     if has_sum:
-        sum_in, rest = rest[0], rest[2:]
-    spectra_ref, gram_ref, sel_ref, acc_ref = rest
+        sum_in, sel_ref, _, spectra_ref, gram_ref = rest
+    else:
+        spectra_ref, gram_ref, sel_ref = rest
     step = pl.program_id(0)
-    rows = slots * owned * 2
+    main, tail, height = layout(slots * owned * 2)
+    rows = parts[0].shape[0] // COMPS
+    order = 2 * blocks
 
     @pl.when(step == 0)
     def _():
-        sel_ref[...] = selection(n, owned, slots, span, blocks, pos_ref[0]).astype(jnp.bfloat16)
+        if not has_sum:
+            selection(n, owned, slots, span, blocks, pos_ref[0], sel_ref)
         acc_ref[...] = sum_in[...] if has_sum else jnp.zeros_like(acc_ref)
 
     for c in range(COMPS):
-        stack = jnp.concatenate([p[c * rows:(c + 1) * rows, :] for p in parts], axis=0)
-        full = jnp.dot(sel_ref[...], stack, preferred_element_type=jnp.float32)
+        pieces = [parts[0][c * rows:(c + 1) * rows, :]]
+        if main:
+            pieces += [p[c * main:(c + 1) * main, :] for p in parts[1:]]
+        if height > COMPS * main:
+            pieces += [p[COMPS * main:, :] for p in parts[1:]]
+        stack = jnp.concatenate(pieces, axis=0)
+        full = jnp.dot(sel_ref[c], stack, preferred_element_type=jnp.float32)
         for j in range(owned):
             for r in range(2):
                 at = (j * 2 + r) * blocks
                 spectra_ref[j, r, c] = full[at:at + blocks]
+        high = full.astype(jnp.bfloat16)
+        low = (full - high.astype(jnp.float32)).astype(jnp.bfloat16)
+        pair = jnp.concatenate([high, low], axis=0)
         acc_ref[...] += lax.dot_general(
-            stack, stack, (((1,), (1,)), ((), ())), preferred_element_type=jnp.float32
+            pair, pair, (((1,), (1,)), ((), ())), preferred_element_type=jnp.float32
         )
 
     @pl.when(step == pl.num_programs(0) - 1)
@@ -212,67 +275,68 @@
         if not last:
             gram_ref[...] = acc_ref[...]
         else:
-            sel = sel_ref[...].astype(jnp.float32)
-            half = jnp.dot(sel, acc_ref[...], precision=HIGHEST, preferred_element_type=jnp.float32)
-            order = 2 * blocks
-            gram = lax.dot_general(
-                half, sel, (((1,), (1,)), ((), ())), precision=HIGHEST, preferred_element_type=jnp.float32
-            ) * (1.0 / total)
-            gram = jnp.concatenate(
+            m = owned * order
+            acc = acc_ref[...]
+            gram = (acc[:m, :m] + (acc[:m, m:] + acc[m:, :m])) * (1.0 / total)
+            gram_ref[...] = jnp.concatenate(
                 [gram[j * order:(j + 1) * order, j * order:(j + 1) * order] for j in range(owned)], axis=1
             )
-            for at in range(0, gram_ref.shape[0], order):
-                gram_ref[at:at + order, :] = gram
-
-
-def assemble_call(n, owned, slots, span, blocks, total, offset, points, all_points, position, parts, spectra, gram, last, copies):
-    rows = slots * owned * 2
+
+
+def assemble_call(n, owned, slots, span, blocks, total, offset, points, all_points, position, parts, spectra, gram, sel, last):
     tile = min(points, 512)
     shift = offset // tile
     order = 2 * blocks
     has_sum = gram is not None
     whole = lambda shape: pl.BlockSpec(shape, lambda i: (0,) * len(shape))
-    gram_shape = (copies * order, owned * order) if last else (n * rows, n * rows)
+    acc_shape = (2 * owned * order, 2 * owned * order)
+    gram_shape = (order, owned * order) if last else acc_shape
+    sel_shape = (COMPS, owned * order, stack_width(n, slots * owned * 2))
     args = [position] + list(parts)
-    in_specs = [pl.BlockSpec(memory_space=pltpu.SMEM)] + [pl.BlockSpec((COMPS * rows, tile), lambda i: (0, i))] * n
+    in_specs = [pl.BlockSpec(memory_space=pltpu.SMEM)]
+    in_specs += [pl.BlockSpec((p.shape[0], tile), lambda i: (0, i)) for p in parts]
+    out_shape = [
+        jax.ShapeDtypeStruct((owned, 2, COMPS, blocks, all_points), jnp.float32),
+        jax.ShapeDtypeStruct(gram_shape, jnp.float32),
+    ]
+    out_specs = [
+        pl.BlockSpec((owned, 2, COMPS, blocks, tile), lambda i: (0, 0, 0, 0, i + shift)),
+        whole(gram_shape),
+    ]
     aliases = {}
     if has_sum:
-        args += [gram, spectra]
-        in_specs += [whole((n * rows, n * rows)), pl.BlockSpec(memory_space=pl.ANY)]
+        args += [gram, sel, spectra]
+        in_specs += [whole(acc_shape), whole(sel_shape), pl.BlockSpec(memory_space=pl.ANY)]
         aliases = {len(args) - 1: 0}
-    return pl.pallas_call(
+    else:
+        out_shape.append(jax.ShapeDtypeStruct(sel_shape, jnp.bfloat16))
+        out_specs.append(whole(sel_shape))
+    out = pl.pallas_call(
         functools.partial(assemble_body, n, owned, slots, span, blocks, total, has_sum, last),
         grid=(points // tile,),
-        out_shape=[
-            jax.ShapeDtypeStruct((owned, 2, COMPS, blocks, all_points), jnp.float32),
-            jax.ShapeDtypeStruct(gram_shape, jnp.float32),
-        ],
+        out_shape=out_shape,
         in_specs=in_specs,
-        out_specs=[
-            pl.BlockSpec((owned, 2, COMPS, blocks, tile), lambda i: (0, 0, 0, 0, i + shift)),
-            whole(gram_shape),
-        ],
-        scratch_shapes=[
-            pltpu.VMEM((owned * order, n * rows), jnp.bfloat16),
-            pltpu.VMEM((n * rows, n * rows), jnp.float32),
-        ],
+        out_specs=out_specs,
+        scratch_shapes=[pltpu.VMEM(acc_shape, jnp.float32)],
         input_output_aliases=aliases,
         compiler_params=pltpu.CompilerParams(vmem_limit_bytes=40 * 2**20),
         cost_estimate=pl.CostEstimate(
-            flops=4 * (n * rows) ** 2 * COMPS * points,
+            flops=4 * 192 * 192 * COMPS * points,
             bytes_accessed=4 * owned * order * COMPS * points,
             transcendentals=0,
         ),
         name="assemble",
     )(*args)
+    return list(out[:2]) + [sel if has_sum else out[2]]
 
 
 def factor_body(owned, order, count, *refs):
     parts = refs[:count]
     out_ref, row_ref = refs[count:]
-    s = parts[0][...]
-    if len(s.shape) == 3:
-        s = sum(s[i] for i in range(s.shape[0]))
+    s = [p[...] for p in parts]
+    while len(s) > 1:
+        s = [a + b for a, b in zip(s[::2], s[1::2])]
+    s = s[0]
     lane = lax.broadcasted_iota(jnp.int32, (1, owned * order), 1)
     for k in range(0, order, PIVOT):
         base = k // 8 * 8
@@ -308,6 +372,15 @@
     )(*parts)
 
 
+def sum_over_space(gram, groups):
+    if groups != 8:
+        return [lax.psum(gram, "space")]
+    swap = lambda x, k: lax.ppermute(x, "space", [(i, i ^ k) for i in range(groups)])
+    gram = gram + swap(gram, 1)
+    gram = gram + swap(gram, 2)
+    return [gram, swap(gram, 4)]
+
+
 def chunks_of(points):
     tile = 512
     return [(at, tile) for at in range(0, points, tile)]
@@ -320,7 +393,7 @@
     blocks = block_starts.shape[0]
     owned = frequencies.shape[0] // n
     order = 2 * blocks
-    slots = slot_count(n, span, blocks, owned * 2)
+    slots = slot_count(n, span, blocks)
     position = lax.axis_index("tm").astype(jnp.int32).reshape(1)
     samples = velocity.transpose(1, 0, 2)
     mask = rotor_mask.reshape(1, points)
@@ -338,18 +411,14 @@
         ]
         pieces.append((at, count, moved))
 
-    spectra, gram = None, None
+    spectra, gram, sel = None, None, None
     total = COMPS * points * groups
     for at, count, moved in pieces:
         last = at + count == points
-        spectra, gram = assemble_call(
-            n, owned, slots, span, blocks, total, at, count, points, position, moved, spectra, gram, last, groups if groups <= 8 else 1
+        spectra, gram, sel = assemble_call(
+            n, owned, slots, span, blocks, total, at, count, points, position, moved, spectra, gram, sel, last
         )
-    if groups <= 8:
-        gram = lax.all_to_all(gram, "space", 0, 0, tiled=True).reshape(groups, order, owned * order)
-    else:
-        gram = lax.psum(gram, "space")
-    factors = factor_call(owned, order, [gram])
+    factors = factor_call(owned, order, sum_over_space(gram, groups))
     return spectra.transpose(0, 1, 3, 2, 4), factors
 
 

time: 76.4 us -> 71.5 us (0.936)
  blocking collectives: 10.5 us -> 0 us
  waiting for transfers between devices: 11.1 us -> 14.1 us
  starting transfers between devices: 25.8 us -> 28.5 us
    all_to_all x1 -> x0, blocking collectives: 10.5 us -> none  [per_device(): lax.all_to_all(gram, 'space', 0, 0, tiled=True)]
    ppermute x0 -> x3, waiting for transfers between devices: none -> 6.03 us  [sum_over_space(): lax.ppermute(x, 'space', [(i, i ^ k) for i in range(groups)])]
    ppermute x0 -> x3, starting transfers between devices: none -> 3.08 us  [sum_over_space(): lax.ppermute(x, 'space', [(i, i ^ k) for i in range(groups)])]
    ppermute x12, waiting for transfers between devices: 11.1 us -> 8.05 us  [per_device(): lax.ppermute(sums[k], 'tm', [(i, (i + k) % n) for i in range(n)])]
    pallas_call x4, Pallas kernels: 5.46 us -> 6.53 us  [assemble_call(): pl.pallas_call(functools.partial(assemble_body, n, owned, slots, span, bl...]
    unnamed x10 -> x14, local copies, waits for them, and re-layouts: 3.12 us -> 3.73 us
  transfers between devices with their start and end apart: 12 -> 15, of which waited for: 3 -> 5; matrix products, arithmetic and copies ran while one was open for 0% -> 0% of each run, Pallas kernels for 18% -> 20%
where the time goes in v8:
time: 71.5 us; the launch traced here: 70.8 us
  starting transfers between devices  28.5 us (40%)
  Pallas kernels  23.8 us (33%)
  waiting for transfers between devices  14.1 us (20%)
  local copies, waits for them, and re-layouts  3.73 us (5%)
    ppermute x12, starting transfers between devices, per_device(): lax.ppermute(sums[k], 'tm', [(i, (i + k) % n) for i in range(n)])  25.4 us
    pallas_call x4, Pallas kernels, dft_call(): pl.pallas_call(functools.partial(dft_body, n, owned, slots, span, blocks,...  14 us
    ppermute x12, waiting for transfers between devices, per_device(): lax.ppermute(sums[k], 'tm', [(i, (i + k) % n) for i in range(n)])  8.05 us
    pallas_call x4, Pallas kernels, assemble_call(): pl.pallas_call(functools.partial(assemble_body, n, owned, slots, span, bl...  6.53 us
    ppermute x3, waiting for transfers between devices, sum_over_space(): lax.ppermute(x, 'space', [(i, i ^ k) for i in range(groups)])  6.03 us
    unnamed x14, local copies, waits for them, and re-layouts  3.73 us
    pallas_call x1, Pallas kernels, factor_call(): pl.pallas_call(functools.partial(factor_body, owned, order, len(parts)),...  3.21 us
    ppermute x3, starting transfers between devices, sum_over_space(): lax.ppermute(x, 'space', [(i, i ^ k) for i in range(groups)])  3.08 us
  transfers between devices with their start and end apart: 15, of which 5 were waited for; matrix products, arithmetic and copies ran while one was open for 0% of the time, Pallas kernels for 20%

profile of v8, /device:TPU:0, one launch (start us, length us, event | category | flops | bytes accessed | tf_op | source)
XLA Modules:
  0.0 70.8 jit_solution(17558466377350942202)
XLA Ops:
  0.6 4.7 %rotate_dft.4 = (bf16[144,512]{1,0:T(8,128)(2,1)}, bf16[136,512]{1,0:T(8,128)(2,1)}, bf16[136,512]{1,0:T(8,128)(2,1)}, bf16[136,512]{1,0:T(8,128)(2,1)}, bf16[4,...) custom-call(s32[1]{0:T(128)} %bitcast.refs_0_, s32[32]{0:T(128)} %refs_1_.1, s32[8]{0:T(128)} %refs_2_.1, ...), custom_call_target="tpu_custom_call" | custom-call | flops 632291328 | bytes 3293184 | tf_op jit(solution)/shard_map/rotate_dft/pallas_call | solution.py:185
  5.3 3.1 %collective-permute-start.9 = (bf16[136,512]{1,0:T(8,128)(2,1)}, bf16[136,512]{1,0:T(8,128)(2,1)S(1)}, u32[]{:S(2)}, u32[]{:S(2)}) collective-permute-start(bf16[136,512]{1,0:T(8,128)(2,1)} %get-tuple-element.46), channel_id=1, source_target_pairs={{0,1},{1,2},{2,3},{3,0},{4,5},{5,6},{6,7},{7,4},{8,9},{9,10},{10,1... | collective-permute-start | bytes 417800 | tf_op jit(solution)/shard_map/ppermute | solution.py:410
  8.4 2.6 %collective-permute-start.10 = (bf16[136,512]{1,0:T(8,128)(2,1)}, bf16[136,512]{1,0:T(8,128)(2,1)S(1)}, u32[]{:S(2)}, u32[]{:S(2)}) collective-permute-start(bf16[136,512]{1,0:T(8,128)(2,1)} %get-tuple-element.47), channel_id=1, source_target_pairs={{0,2},{1,3},{2,0},{3,1},{4,6},{5,7},{6,4},{7,5},{8,10},{9,11},{10,... | collective-permute-start | bytes 417800 | tf_op jit(solution)/shard_map/ppermute | solution.py:410
  11.0 1.3 %collective-permute-start.11 = (bf16[136,512]{1,0:T(8,128)(2,1)}, bf16[136,512]{1,0:T(8,128)(2,1)S(1)}, u32[]{:S(2)}, u32[]{:S(2)}) collective-permute-start(bf16[136,512]{1,0:T(8,128)(2,1)} %get-tuple-element.48), channel_id=1, source_target_pairs={{0,3},{1,0},{2,1},{3,2},{4,7},{5,4},{6,5},{7,6},{8,11},{9,8},{10,9... | collective-permute-start | bytes 417800 | tf_op jit(solution)/shard_map/ppermute | solution.py:410
  12.3 1.0 %copy-done = f32[1072,128]{1,0:T(8,128)S(1)} copy-done((f32[1072,128]{1,0:T(8,128)S(1)}, f32[1072,128]{1,0:T(8,128)}, u32[]{:S(2)}) %copy-start) | copy-done | bytes 548888
  13.4 1.0 %copy-done.1 = f32[1072,128]{1,0:T(8,128)S(1)} copy-done((f32[1072,128]{1,0:T(8,128)S(1)}, f32[1072,128]{1,0:T(8,128)}, u32[]{:S(2)}) %copy-start.1) | copy-done | bytes 548888
  14.4 1.0 %copy-done.2 = bf16[4,48,1072]{2,1,0:T(8,128)(2,1)S(1)} copy-done((bf16[4,48,1072]{2,1,0:T(8,128)(2,1)S(1)}, bf16[4,48,1072]{2,1,0:T(8,128)(2,1)}, u32[]{:S(2)}) %copy-start.2) | copy-done | bytes 411672
  15.4 3.1 %rotate_dft.7 = (bf16[144,512]{1,0:T(8,128)(2,1)S(1)}, bf16[136,512]{1,0:T(8,128)(2,1)S(1)}, bf16[136,512]{1,0:T(8,128)(2,1)S(1)}, bf16[136,512]{1,0:T(8,128)(2,1)S(1)}) custom-call(s32[1,2048]{1,0:T(1,128)S(1)} %bitcast.5, bf16[3,1072,2048]{2,1,0:T(8,128)(2,1)} %bitcast.9, bf16[4,48,1072]{2,1,0:T(8,128)(2,1)S(1)} %copy-done.2, f32[1072,128]{1,0:T(8,128)S(1)} %copy-done, ...), custom_call_target="tpu_custom_call" | custom-call | flops 632291328 | bytes 3293184 | tf_op jit(solution)/shard_map/rotate_dft/pallas_call | solution.py:185
  18.6 0.7 %collective-permute-start.6 = (bf16[136,512]{1,0:T(8,128)(2,1)S(1)}, bf16[136,512]{1,0:T(8,128)(2,1)S(1)}, u32[]{:S(2)}, u32[]{:S(2)}) collective-permute-start(bf16[136,512]{1,0:T(8,128)(2,1)S(1)} %get-tuple-element.42), channel_id=1, source_target_pairs={{0,1},{1,2},{2,3},{3,0},{4,5},{5,6},{6,7},{7,4},{8,9},{9,10},{10,1... | collective-permute-start | bytes 417800 | tf_op jit(solution)/shard_map/ppermute | solution.py:410
  19.3 0.3 collective-permute-start.7
  19.6 3.1 %rotate_dft.6 = (bf16[144,512]{1,0:T(8,128)(2,1)S(1)}, bf16[136,512]{1,0:T(8,128)(2,1)S(1)}, bf16[136,512]{1,0:T(8,128)(2,1)S(1)}, bf16[136,512]{1,0:T(8,128)(2,1)S(1)}) custom-call(s32[1,2048]{1,0:T(1,128)S(1)} %bitcast.6, bf16[3,1072,2048]{2,1,0:T(8,128)(2,1)} %bitcast.10, bf16[4,48,1072]{2,1,0:T(8,128)(2,1)S(1)} %copy-done.2, f32[1072,128]{1,0:T(8,128)S(1)} %copy-done, ...), custom_call_target="tpu_custom_call" | custom-call | flops 632291328 | bytes 3293184 | tf_op jit(solution)/shard_map/rotate_dft/pallas_call | solution.py:185
  22.8 2.9 %collective-permute-start.8 = (bf16[136,512]{1,0:T(8,128)(2,1)S(1)}, bf16[136,512]{1,0:T(8,128)(2,1)S(1)}, u32[]{:S(2)}, u32[]{:S(2)}) collective-permute-start(bf16[136,512]{1,0:T(8,128)(2,1)S(1)} %get-tuple-element.44), channel_id=1, source_target_pairs={{0,3},{1,0},{2,1},{3,2},{4,7},{5,4},{6,5},{7,6},{8,11},{9,8},{10,9... | collective-permute-start | bytes 417800 | tf_op jit(solution)/shard_map/ppermute | solution.py:410
  25.6 0.6 collective-permute-start.3
  26.3 4.8 %collective-permute-start.4 = (bf16[136,512]{1,0:T(8,128)(2,1)S(1)}, bf16[136,512]{1,0:T(8,128)(2,1)S(1)}, u32[]{:S(2)}, u32[]{:S(2)}) collective-permute-start(bf16[136,512]{1,0:T(8,128)(2,1)S(1)} %get-tuple-element.39), channel_id=1, source_target_pairs={{0,2},{1,3},{2,0},{3,1},{4,6},{5,7},{6,4},{7,5},{8,10},{9,11},{10,... | collective-permute-start | bytes 417800 | tf_op jit(solution)/shard_map/ppermute | solution.py:410
  31.1 0.4 collective-permute-start.5
  31.5 3.1 %rotate_dft.5 = (bf16[144,512]{1,0:T(8,128)(2,1)S(1)}, bf16[136,512]{1,0:T(8,128)(2,1)S(1)}, bf16[136,512]{1,0:T(8,128)(2,1)S(1)}, bf16[136,512]{1,0:T(8,128)(2,1)S(1)}) custom-call(s32[1,2048]{1,0:T(1,128)S(1)} %bitcast.7, bf16[3,1072,2048]{2,1,0:T(8,128)(2,1)} %bitcast.11, bf16[4,48,1072]{2,1,0:T(8,128)(2,1)S(1)} %copy-done.2, f32[1072,128]{1,0:T(8,128)S(1)} %copy-done, ...), custom_call_target="tpu_custom_call" | custom-call | flops 632291328 | bytes 3293184 | tf_op jit(solution)/shard_map/rotate_dft/pallas_call | solution.py:185
  34.7 3.0 %collective-permute-done.7.refs_3_ = bf16[136,512]{1,0:T(8,128)(2,1)S(1)} collective-permute-done((bf16[136,512]{1,0:T(8,128)(2,1)S(1)}, bf16[136,512]{1,0:T(8,128)(2,1)S(1)}, u32[]{:S(2)}, u32[]{:S(2)}) %collective-permute-start.7) | collective-permute-done | bytes 139296 | tf_op jit(solution)/shard_map/ppermute | solution.py:410
  37.7 3.5 %collective-permute-start = (bf16[136,512]{1,0:T(8,128)(2,1)S(1)}, bf16[136,512]{1,0:T(8,128)(2,1)S(1)}, u32[]{:S(2)}, u32[]{:S(2)}) collective-permute-start(bf16[136,512]{1,0:T(8,128)(2,1)S(1)} %get-tuple-element.34), channel_id=1, source_target_pairs={{0,1},{1,2},{2,3},{3,0},{4,5},{5,6},{6,7},{7,4},{8,9},{9,10},{10,1... | collective-permute-start | bytes 417800 | tf_op jit(solution)/shard_map/ppermute | solution.py:410
  41.2 4.2 %collective-permute-start.1 = (bf16[136,512]{1,0:T(8,128)(2,1)S(1)}, bf16[136,512]{1,0:T(8,128)(2,1)S(1)}, u32[]{:S(2)}, u32[]{:S(2)}) collective-permute-start(bf16[136,512]{1,0:T(8,128)(2,1)S(1)} %get-tuple-element.35), channel_id=1, source_target_pairs={{0,2},{1,3},{2,0},{3,1},{4,6},{5,7},{6,4},{7,5},{8,10},{9,11},{10,... | collective-permute-start | bytes 417800 | tf_op jit(solution)/shard_map/ppermute | solution.py:410
  45.3 0.9 %collective-permute-start.2 = (bf16[136,512]{1,0:T(8,128)(2,1)S(1)}, bf16[136,512]{1,0:T(8,128)(2,1)S(1)}, u32[]{:S(2)}, u32[]{:S(2)}) collective-permute-start(bf16[136,512]{1,0:T(8,128)(2,1)S(1)} %get-tuple-element.36), channel_id=1, source_target_pairs={{0,3},{1,0},{2,1},{3,2},{4,7},{5,4},{6,5},{7,6},{8,11},{9,8},{10,9... | collective-permute-start | bytes 417800 | tf_op jit(solution)/shard_map/ppermute | solution.py:410
  46.3 1.7 %assemble.4 = (f32[2,2,3,32,2048]{4,3,2,1,0:T(8,128)}, f32[256,256]{1,0:T(8,128)S(1)}, bf16[3,128,264]{2,1,0:T(8,128)(2,1)S(1)}) custom-call(s32[1]{0:T(128)} %bitcast.refs_0_, bf16[144,512]{1,0:T(8,128)(2,1)S(1)} %copy-done.4, bf16[136,512]{1,0:T(8,128)(2,1)S(1)} %collective-permute-done.9.refs_2_, bf16[136,512]{1,0:T(8,128)(2,1)S(1)} %collective-permute-done.10.refs_3_, ...), custom_call_target="tpu_custom_call" | custom-call | flops 226492416 | bytes 786432 | tf_op jit(solution)/shard_map/assemble/pallas_call | solution.py:314
  47.9 1.6 %assemble.5 = (f32[2,2,3,32,2048]{4,3,2,1,0:T(8,128)}, f32[256,256]{1,0:T(8,128)S(1)}) custom-call(s32[1]{0:T(128)} %bitcast.refs_0_, bf16[144,512]{1,0:T(8,128)(2,1)S(1)} %get-tuple-element.41.refs_1_, bf16[136,512]{1,0:T(8,128)(2,1)S(1)} %collective-permute-done.6.refs_2_, ...), custom_call_target="tpu_custom_call", output_to_operand_aliasing={{0}: (7, {})} | custom-call | flops 226492416 | bytes 786432 | tf_op jit(solution)/shard_map/assemble/pallas_call | solution.py:314
  49.6 1.6 %assemble.6 = (f32[2,2,3,32,2048]{4,3,2,1,0:T(8,128)}, f32[256,256]{1,0:T(8,128)S(1)}) custom-call(s32[1]{0:T(128)} %bitcast.refs_0_, bf16[144,512]{1,0:T(8,128)(2,1)S(1)} %get-tuple-element.37.refs_1_, bf16[136,512]{1,0:T(8,128)(2,1)S(1)} %collective-permute-done.3.refs_2_, ...), custom_call_target="tpu_custom_call", output_to_operand_aliasing={{0}: (7, {})} | custom-call | flops 226492416 | bytes 786432 | tf_op jit(solution)/shard_map/assemble/pallas_call | solution.py:314
  51.2 5.0 %collective-permute-done.1.refs_3_ = bf16[136,512]{1,0:T(8,128)(2,1)S(1)} collective-permute-done((bf16[136,512]{1,0:T(8,128)(2,1)S(1)}, bf16[136,512]{1,0:T(8,128)(2,1)S(1)}, u32[]{:S(2)}, u32[]{:S(2)}) %collective-permute-start.1) | collective-permute-done | bytes 139296 | tf_op jit(solution)/shard_map/ppermute | solution.py:410
  56.2 1.6 %assemble.7 = (f32[2,2,3,32,2048]{4,3,2,1,0:T(8,128)}, f32[64,128]{1,0:T(8,128)S(1)}) custom-call(s32[1]{0:T(128)} %bitcast.refs_0_, bf16[144,512]{1,0:T(8,128)(2,1)S(1)} %get-tuple-element.33.refs_1_, bf16[136,512]{1,0:T(8,128)(2,1)S(1)} %collective-permute-done.refs_2_, ...), custom_call_target="tpu_custom_call", output_to_operand_aliasing={{0}: (7, {})} | custom-call | flops 226492416 | bytes 786432 | tf_op jit(solution)/shard_map/assemble/pallas_call | solution.py:314
  57.8 1.2 %collective-permute-done.12 = f32[64,128]{1,0:T(8,128)S(1)} collective-permute-done((f32[64,128]{1,0:T(8,128)S(1)}, f32[64,128]{1,0:T(8,128)S(1)}, u32[]{:S(2)}, u32[]{:S(2)}) %collective-permute-start.12) | collective-permute-done | bytes 32800 | tf_op jit(solution)/shard_map/ppermute | solution.py:378
  59.1 1.5 %collective-permute-start.13 = (f32[64,128]{1,0:T(8,128)S(1)}, f32[64,128]{1,0:T(8,128)S(1)}, u32[]{:S(2)}, u32[]{:S(2)}) collective-permute-start(f32[64,128]{1,0:T(8,128)S(1)} %add.6), channel_id=1, source_target_pairs={{0,8},{4,12},{8,0},{12,4},{16,24},{20,28},{24,16},{28,20},{1,9},{5... | collective-permute-start | bytes 98312 | tf_op jit(solution)/shard_map/ppermute | solution.py:378
  60.5 2.4 %collective-permute-done.13 = f32[64,128]{1,0:T(8,128)S(1)} collective-permute-done((f32[64,128]{1,0:T(8,128)S(1)}, f32[64,128]{1,0:T(8,128)S(1)}, u32[]{:S(2)}, u32[]{:S(2)}) %collective-permute-start.13) | collective-permute-done | bytes 32800 | tf_op jit(solution)/shard_map/ppermute | solution.py:378
  63.0 1.6 %collective-permute-start.14 = (f32[64,128]{1,0:T(8,128)S(1)}, f32[64,128]{1,0:T(8,128)S(1)}, u32[]{:S(2)}, u32[]{:S(2)}) collective-permute-start(f32[64,128]{1,0:T(8,128)S(1)} %add.7.refs_0_), channel_id=1, source_target_pairs={{0,16},{4,20},{8,24},{12,28},{16,0},{20,4},{24,8},{28,12},{1,17},{... | collective-permute-start | bytes 98312 | tf_op jit(solution)/shard_map/ppermute | solution.py:378
  64.6 2.4 %collective-permute-done.14.refs_1_ = f32[64,128]{1,0:T(8,128)S(1)} collective-permute-done((f32[64,128]{1,0:T(8,128)S(1)}, f32[64,128]{1,0:T(8,128)S(1)}, u32[]{:S(2)}, u32[]{:S(2)}) %collective-permute-start.14) | collective-permute-done | bytes 32800 | tf_op jit(solution)/shard_map/ppermute | solution.py:378
  67.0 0.6 copy-done.6
  67.6 3.2 %factor.1 = f32[2,64,64]{2,1,0:T(8,128)} custom-call(f32[64,128]{1,0:T(8,128)} %copy-done.5, f32[64,128]{1,0:T(8,128)} %copy-done.6), custom_call_target="tpu_custom_call" | custom-call | tf_op jit(solution)/shard_map/factor/pallas_call | solution.py:367
  (23 shorter events, 0.1 us)
Async XLA Ops:
  0.6 11.7 %copy-start.3 = (s32[2048]{0:T(1024)S(1)}, s32[2048]{0:T(1024)}, u32[]{:S(2)}) copy-start(s32[2048]{0:T(1024)} %param.6) | copy-start | bytes 24580
  5.3 17.4 %collective-permute-start.9 = (bf16[136,512]{1,0:T(8,128)(2,1)}, bf16[136,512]{1,0:T(8,128)(2,1)S(1)}, u32[]{:S(2)}, u32[]{:S(2)}) collective-permute-start(bf16[136,512]{1,0:T(8,128)(2,1)} %get-tuple-element.46), channel_id=1, source_target_pairs={{0,1},{1,2},{2,3},{3,0},{4,5},{5,6},{6,7},{7,4},{8,9},{9,10},{10,1... | collective-permute-start | bytes 417800 | tf_op jit(solution)/shard_map/ppermute | solution.py:410
  8.4 17.2 %collective-permute-start.10 = (bf16[136,512]{1,0:T(8,128)(2,1)}, bf16[136,512]{1,0:T(8,128)(2,1)S(1)}, u32[]{:S(2)}, u32[]{:S(2)}) collective-permute-start(bf16[136,512]{1,0:T(8,128)(2,1)} %get-tuple-element.47), channel_id=1, source_target_pairs={{0,2},{1,3},{2,0},{3,1},{4,6},{5,7},{6,4},{7,5},{8,10},{9,11},{10,... | collective-permute-start | bytes 417800 | tf_op jit(solution)/shard_map/ppermute | solution.py:410
  11.0 15.3 %collective-permute-start.11 = (bf16[136,512]{1,0:T(8,128)(2,1)}, bf16[136,512]{1,0:T(8,128)(2,1)S(1)}, u32[]{:S(2)}, u32[]{:S(2)}) collective-permute-start(bf16[136,512]{1,0:T(8,128)(2,1)} %get-tuple-element.48), channel_id=1, source_target_pairs={{0,3},{1,0},{2,1},{3,2},{4,7},{5,4},{6,5},{7,6},{8,11},{9,8},{10,9... | collective-permute-start | bytes 417800 | tf_op jit(solution)/shard_map/ppermute | solution.py:410
  12.3 1.1 %copy-start = (f32[1072,128]{1,0:T(8,128)S(1)}, f32[1072,128]{1,0:T(8,128)}, u32[]{:S(2)}) copy-start(f32[1072,128]{1,0:T(8,128)} %get-tuple-element.31.refs_3_) | copy-start | bytes 1646596
  13.4 1.1 %copy-start.1 = (f32[1072,128]{1,0:T(8,128)S(1)}, f32[1072,128]{1,0:T(8,128)}, u32[]{:S(2)}) copy-start(f32[1072,128]{1,0:T(8,128)} %get-tuple-element.32.refs_4_) | copy-start | bytes 1646596
  14.4 1.0 %copy-start.2 = (bf16[4,48,1072]{2,1,0:T(8,128)(2,1)S(1)}, bf16[4,48,1072]{2,1,0:T(8,128)(2,1)}, u32[]{:S(2)}) copy-start(bf16[4,48,1072]{2,1,0:T(8,128)(2,1)} %get-tuple-element.30.refs_2_) | copy-start | bytes 1234948
  18.6 12.5 %collective-permute-start.6 = (bf16[136,512]{1,0:T(8,128)(2,1)S(1)}, bf16[136,512]{1,0:T(8,128)(2,1)S(1)}, u32[]{:S(2)}, u32[]{:S(2)}) collective-permute-start(bf16[136,512]{1,0:T(8,128)(2,1)S(1)} %get-tuple-element.42), channel_id=1, source_target_pairs={{0,1},{1,2},{2,3},{3,0},{4,5},{5,6},{6,7},{7,4},{8,9},{9,10},{10,1... | collective-permute-start | bytes 417800 | tf_op jit(solution)/shard_map/ppermute | solution.py:410
  19.3 18.4 %collective-permute-start.7 = (bf16[136,512]{1,0:T(8,128)(2,1)S(1)}, bf16[136,512]{1,0:T(8,128)(2,1)S(1)}, u32[]{:S(2)}, u32[]{:S(2)}) collective-permute-start(bf16[136,512]{1,0:T(8,128)(2,1)S(1)} %get-tuple-element.43), channel_id=1, source_target_pairs={{0,2},{1,3},{2,0},{3,1},{4,6},{5,7},{6,4},{7,5},{8,10},{9,11},{10,... | collective-permute-start | bytes 417800 | tf_op jit(solution)/shard_map/ppermute | solution.py:410
  22.8 18.4 %collective-permute-start.8 = (bf16[136,512]{1,0:T(8,128)(2,1)S(1)}, bf16[136,512]{1,0:T(8,128)(2,1)S(1)}, u32[]{:S(2)}, u32[]{:S(2)}) collective-permute-start(bf16[136,512]{1,0:T(8,128)(2,1)S(1)} %get-tuple-element.44), channel_id=1, source_target_pairs={{0,3},{1,0},{2,1},{3,2},{4,7},{5,4},{6,5},{7,6},{8,11},{9,8},{10,9... | collective-permute-start | bytes 417800 | tf_op jit(solution)/shard_map/ppermute | solution.py:410
  25.6 19.7 %collective-permute-start.3 = (bf16[136,512]{1,0:T(8,128)(2,1)S(1)}, bf16[136,512]{1,0:T(8,128)(2,1)S(1)}, u32[]{:S(2)}, u32[]{:S(2)}) collective-permute-start(bf16[136,512]{1,0:T(8,128)(2,1)S(1)} %get-tuple-element.38), channel_id=1, source_target_pairs={{0,1},{1,2},{2,3},{3,0},{4,5},{5,6},{6,7},{7,4},{8,9},{9,10},{10,1... | collective-permute-start | bytes 417800 | tf_op jit(solution)/shard_map/ppermute | solution.py:410
  26.3 23.3 %collective-permute-start.4 = (bf16[136,512]{1,0:T(8,128)(2,1)S(1)}, bf16[136,512]{1,0:T(8,128)(2,1)S(1)}, u32[]{:S(2)}, u32[]{:S(2)}) collective-permute-start(bf16[136,512]{1,0:T(8,128)(2,1)S(1)} %get-tuple-element.39), channel_id=1, source_target_pairs={{0,2},{1,3},{2,0},{3,1},{4,6},{5,7},{6,4},{7,5},{8,10},{9,11},{10,... | collective-permute-start | bytes 417800 | tf_op jit(solution)/shard_map/ppermute | solution.py:410
  31.1 15.1 %copy-start.4 = (bf16[144,512]{1,0:T(8,128)(2,1)S(1)}, bf16[144,512]{1,0:T(8,128)(2,1)}, u32[]{:S(2)}) copy-start(bf16[144,512]{1,0:T(8,128)(2,1)} %get-tuple-element.45.refs_1_) | copy-start | bytes 442372
  31.1 18.4 %collective-permute-start.5 = (bf16[136,512]{1,0:T(8,128)(2,1)S(1)}, bf16[136,512]{1,0:T(8,128)(2,1)S(1)}, u32[]{:S(2)}, u32[]{:S(2)}) collective-permute-start(bf16[136,512]{1,0:T(8,128)(2,1)S(1)} %get-tuple-element.40), channel_id=1, source_target_pairs={{0,3},{1,0},{2,1},{3,2},{4,7},{5,4},{6,5},{7,6},{8,11},{9,8},{10,9... | collective-permute-start | bytes 417800 | tf_op jit(solution)/shard_map/ppermute | solution.py:410
  37.7 13.5 %collective-permute-start = (bf16[136,512]{1,0:T(8,128)(2,1)S(1)}, bf16[136,512]{1,0:T(8,128)(2,1)S(1)}, u32[]{:S(2)}, u32[]{:S(2)}) collective-permute-start(bf16[136,512]{1,0:T(8,128)(2,1)S(1)} %get-tuple-element.34), channel_id=1, source_target_pairs={{0,1},{1,2},{2,3},{3,0},{4,5},{5,6},{6,7},{7,4},{8,9},{9,10},{10,1... | collective-permute-start | bytes 417800 | tf_op jit(solution)/shard_map/ppermute | solution.py:410
  41.2 15.1 %collective-permute-start.1 = (bf16[136,512]{1,0:T(8,128)(2,1)S(1)}, bf16[136,512]{1,0:T(8,128)(2,1)S(1)}, u32[]{:S(2)}, u32[]{:S(2)}) collective-permute-start(bf16[136,512]{1,0:T(8,128)(2,1)S(1)} %get-tuple-element.35), channel_id=1, source_target_pairs={{0,2},{1,3},{2,0},{3,1},{4,6},{5,7},{6,4},{7,5},{8,10},{9,11},{10,... | collective-permute-start | bytes 417800 | tf_op jit(solution)/shard_map/ppermute | solution.py:410
  45.3 10.9 %collective-permute-start.2 = (bf16[136,512]{1,0:T(8,128)(2,1)S(1)}, bf16[136,512]{1,0:T(8,128)(2,1)S(1)}, u32[]{:S(2)}, u32[]{:S(2)}) collective-permute-start(bf16[136,512]{1,0:T(8,128)(2,1)S(1)} %get-tuple-element.36), channel_id=1, source_target_pairs={{0,3},{1,0},{2,1},{3,2},{4,7},{5,4},{6,5},{7,6},{8,11},{9,8},{10,9... | collective-permute-start | bytes 417800 | tf_op jit(solution)/shard_map/ppermute | solution.py:410
  57.8 1.2 %collective-permute-start.12 = (f32[64,128]{1,0:T(8,128)S(1)}, f32[64,128]{1,0:T(8,128)S(1)}, u32[]{:S(2)}, u32[]{:S(2)}) collective-permute-start(f32[64,128]{1,0:T(8,128)S(1)} %get-tuple-element.57), channel_id=1, source_target_pairs={{0,4},{4,0},{8,12},{12,8},{16,20},{20,16},{24,28},{28,24},{1,5},{5... | collective-permute-start | bytes 98312 | tf_op jit(solution)/shard_map/ppermute | solution.py:378
  59.1 3.9 %collective-permute-start.13 = (f32[64,128]{1,0:T(8,128)S(1)}, f32[64,128]{1,0:T(8,128)S(1)}, u32[]{:S(2)}, u32[]{:S(2)}) collective-permute-start(f32[64,128]{1,0:T(8,128)S(1)} %add.6), channel_id=1, source_target_pairs={{0,8},{4,12},{8,0},{12,4},{16,24},{20,28},{24,16},{28,20},{1,9},{5... | collective-permute-start | bytes 98312 | tf_op jit(solution)/shard_map/ppermute | solution.py:378
  63.0 4.0 %copy-start.5 = (f32[64,128]{1,0:T(8,128)}, f32[64,128]{1,0:T(8,128)S(1)}, u32[]{:S(2)}) copy-start(f32[64,128]{1,0:T(8,128)S(1)} %add.7.refs_0_) | copy-start | bytes 98308
  63.0 4.0 %collective-permute-start.14 = (f32[64,128]{1,0:T(8,128)S(1)}, f32[64,128]{1,0:T(8,128)S(1)}, u32[]{:S(2)}, u32[]{:S(2)}) collective-permute-start(f32[64,128]{1,0:T(8,128)S(1)} %add.7.refs_0_), channel_id=1, source_target_pairs={{0,16},{4,20},{8,24},{12,28},{16,0},{20,4},{24,8},{28,12},{1,17},{... | collective-permute-start | bytes 98312 | tf_op jit(solution)/shard_map/ppermute | solution.py:378
  67.0 0.6 copy-start.6

commit v9 on v8

--- a/solution.py
+++ b/solution.py
@@ -14,7 +14,7 @@
 HOP = 128
 LANES = 128
 TILE = 256
-PIVOT = 8
+PIVOT = 16
 SCALE = (8.0 / (3.0 * NFFT)) ** 0.5
 HIGHEST = lax.Precision.HIGHEST
 
@@ -284,7 +284,7 @@
 
 
 def assemble_call(n, owned, slots, span, blocks, total, offset, points, all_points, position, parts, spectra, gram, sel, last):
-    tile = min(points, 512)
+    tile = TILE
     shift = offset // tile
     order = 2 * blocks
     has_sum = gram is not None
@@ -382,8 +382,8 @@
 
 
 def chunks_of(points):
-    tile = 512
-    return [(at, tile) for at in range(0, points, tile)]
+    cuts = [points * k // 8 for k in (0, 2, 4, 7, 8)]
+    return [(a, b - a) for a, b in zip(cuts[:-1], cuts[1:])]
 
 
 def per_device(velocity, rotor_mask, rotor_angle, block_starts, frequencies):

time: 71.5 us -> 77.7 us (1.087)
  waiting for transfers between devices: 14.1 us -> 22.8 us
  starting transfers between devices: 28.5 us -> 24.6 us
  Pallas kernels: 23.8 us -> 25.5 us
    ppermute x12, waiting for transfers between devices: 8.05 us -> 16.7 us  [per_device(): lax.ppermute(sums[k], 'tm', [(i, (i + k) % n) for i in range(n)])]
    ppermute x12, starting transfers between devices: 25.4 us -> 21.6 us  [per_device(): lax.ppermute(sums[k], 'tm', [(i, (i + k) % n) for i in range(n)])]
    pallas_call x4, Pallas kernels: 6.53 us -> 8 us  [assemble_call(): pl.pallas_call(functools.partial(assemble_body, n, owned, slots, span, bl...]
  transfers between devices with their start and end apart: 15 -> 15, of which waited for: 5 -> 4; matrix products, arithmetic and copies ran while one was open for 0% -> 0% of each run, Pallas kernels for 20% -> 22%
where the time goes in v9:
time: 77.7 us; the launch traced here: 77.3 us
  Pallas kernels  25.5 us (33%)
  starting transfers between devices  24.6 us (32%)
  waiting for transfers between devices  22.8 us (29%)
  local copies, waits for them, and re-layouts  3.73 us (5%)
    ppermute x12, starting transfers between devices, per_device(): lax.ppermute(sums[k], 'tm', [(i, (i + k) % n) for i in range(n)])  21.6 us
    ppermute x12, waiting for transfers between devices, per_device(): lax.ppermute(sums[k], 'tm', [(i, (i + k) % n) for i in range(n)])  16.7 us
    pallas_call x4, Pallas kernels, dft_call(): pl.pallas_call(functools.partial(dft_body, n, owned, slots, span, blocks,...  14.6 us
    pallas_call x4, Pallas kernels, assemble_call(): pl.pallas_call(functools.partial(assemble_body, n, owned, slots, span, bl...  8 us
    ppermute x3, waiting for transfers between devices, sum_over_space(): lax.ppermute(x, 'space', [(i, i ^ k) for i in range(groups)])  6.03 us
    unnamed x14, local copies, waits for them, and re-layouts  3.73 us
    ppermute x3, starting transfers between devices, sum_over_space(): lax.ppermute(x, 'space', [(i, i ^ k) for i in range(groups)])  3.07 us
    pallas_call x1, Pallas kernels, factor_call(): pl.pallas_call(functools.partial(factor_body, owned, order, len(parts)),...  2.9 us
  transfers between devices with their start and end apart: 15, of which 4 were waited for; matrix products, arithmetic and copies ran while one was open for 0% of the time, Pallas kernels for 22%

profile of v9, /device:TPU:0, one launch (start us, length us, event | category | flops | bytes accessed | tf_op | source)
XLA Modules:
  0.0 77.3 jit_solution(17130604637897907681)
XLA Ops:
  0.6 4.7 %rotate_dft.4 = (bf16[144,512]{1,0:T(8,128)(2,1)}, bf16[136,512]{1,0:T(8,128)(2,1)}, bf16[136,512]{1,0:T(8,128)(2,1)}, bf16[136,512]{1,0:T(8,128)(2,1)}, bf16[4,...) custom-call(s32[1]{0:T(128)} %bitcast.refs_0_, s32[32]{0:T(128)} %refs_1_.1, s32[8]{0:T(128)} %refs_2_.1, ...), custom_call_target="tpu_custom_call" | custom-call | flops 632291328 | bytes 3293184 | tf_op jit(solution)/shard_map/rotate_dft/pallas_call | solution.py:185
  5.3 3.1 %collective-permute-start.9 = (bf16[136,512]{1,0:T(8,128)(2,1)}, bf16[136,512]{1,0:T(8,128)(2,1)S(1)}, u32[]{:S(2)}, u32[]{:S(2)}) collective-permute-start(bf16[136,512]{1,0:T(8,128)(2,1)} %get-tuple-element.46), channel_id=1, source_target_pairs={{0,1},{1,2},{2,3},{3,0},{4,5},{5,6},{6,7},{7,4},{8,9},{9,10},{10,1... | collective-permute-start | bytes 417800 | tf_op jit(solution)/shard_map/ppermute | solution.py:410
  8.4 2.6 %collective-permute-start.10 = (bf16[136,512]{1,0:T(8,128)(2,1)}, bf16[136,512]{1,0:T(8,128)(2,1)S(1)}, u32[]{:S(2)}, u32[]{:S(2)}) collective-permute-start(bf16[136,512]{1,0:T(8,128)(2,1)} %get-tuple-element.47), channel_id=1, source_target_pairs={{0,2},{1,3},{2,0},{3,1},{4,6},{5,7},{6,4},{7,5},{8,10},{9,11},{10,... | collective-permute-start | bytes 417800 | tf_op jit(solution)/shard_map/ppermute | solution.py:410
  11.0 1.3 %collective-permute-start.11 = (bf16[136,512]{1,0:T(8,128)(2,1)}, bf16[136,512]{1,0:T(8,128)(2,1)S(1)}, u32[]{:S(2)}, u32[]{:S(2)}) collective-permute-start(bf16[136,512]{1,0:T(8,128)(2,1)} %get-tuple-element.48), channel_id=1, source_target_pairs={{0,3},{1,0},{2,1},{3,2},{4,7},{5,4},{6,5},{7,6},{8,11},{9,8},{10,9... | collective-permute-start | bytes 417800 | tf_op jit(solution)/shard_map/ppermute | solution.py:410
  12.3 1.0 %copy-done = f32[1072,128]{1,0:T(8,128)S(1)} copy-done((f32[1072,128]{1,0:T(8,128)S(1)}, f32[1072,128]{1,0:T(8,128)}, u32[]{:S(2)}) %copy-start) | copy-done | bytes 548888
  13.4 1.0 %copy-done.1 = f32[1072,128]{1,0:T(8,128)S(1)} copy-done((f32[1072,128]{1,0:T(8,128)S(1)}, f32[1072,128]{1,0:T(8,128)}, u32[]{:S(2)}) %copy-start.1) | copy-done | bytes 548888
  14.4 1.0 %copy-done.2 = bf16[4,48,1072]{2,1,0:T(8,128)(2,1)S(1)} copy-done((bf16[4,48,1072]{2,1,0:T(8,128)(2,1)S(1)}, bf16[4,48,1072]{2,1,0:T(8,128)(2,1)}, u32[]{:S(2)}) %copy-start.2) | copy-done | bytes 411672
  15.4 3.1 %rotate_dft.7 = (bf16[144,512]{1,0:T(8,128)(2,1)S(1)}, bf16[136,512]{1,0:T(8,128)(2,1)S(1)}, bf16[136,512]{1,0:T(8,128)(2,1)S(1)}, bf16[136,512]{1,0:T(8,128)(2,1)S(1)}) custom-call(s32[1,2048]{1,0:T(1,128)S(1)} %bitcast.5, bf16[3,1072,2048]{2,1,0:T(8,128)(2,1)} %bitcast.9, bf16[4,48,1072]{2,1,0:T(8,128)(2,1)S(1)} %copy-done.2, f32[1072,128]{1,0:T(8,128)S(1)} %copy-done, ...), custom_call_target="tpu_custom_call" | custom-call | flops 632291328 | bytes 3293184 | tf_op jit(solution)/shard_map/rotate_dft/pallas_call | solution.py:185
  18.6 0.7 collective-permute-start.6
  19.3 4.5 %rotate_dft.6 = (bf16[144,768]{1,0:T(8,128)(2,1)S(1)}, bf16[136,768]{1,0:T(8,128)(2,1)S(1)}, bf16[136,768]{1,0:T(8,128)(2,1)S(1)}, bf16[136,768]{1,0:T(8,128)(2,1)S(1)}) custom-call(s32[1,2048]{1,0:T(1,128)S(1)} %bitcast.6, bf16[3,1072,2048]{2,1,0:T(8,128)(2,1)} %bitcast.10, bf16[4,48,1072]{2,1,0:T(8,128)(2,1)S(1)} %copy-done.2, f32[1072,128]{1,0:T(8,128)S(1)} %copy-done, ...), custom_call_target="tpu_custom_call" | custom-call | flops 948436992 | bytes 4939776 | tf_op jit(solution)/shard_map/rotate_dft/pallas_call | solution.py:185
  23.8 0.1 collective-permute-start.3
  24.0 3.6 %collective-permute-start.4 = (bf16[136,768]{1,0:T(8,128)(2,1)S(1)}, bf16[136,768]{1,0:T(8,128)(2,1)S(1)}, u32[]{:S(2)}, u32[]{:S(2)}) collective-permute-start(bf16[136,768]{1,0:T(8,128)(2,1)S(1)} %get-tuple-element.39), channel_id=1, source_target_pairs={{0,2},{1,3},{2,0},{3,1},{4,6},{5,7},{6,4},{7,5},{8,10},{9,11},{10,... | collective-permute-start | bytes 626696 | tf_op jit(solution)/shard_map/ppermute | solution.py:410
  27.6 0.0 collective-permute-done.10.refs_3_
  27.6 0.2 collective-permute-start.5
  27.8 2.0 %collective-permute-start.7 = (bf16[136,512]{1,0:T(8,128)(2,1)S(1)}, bf16[136,512]{1,0:T(8,128)(2,1)S(1)}, u32[]{:S(2)}, u32[]{:S(2)}) collective-permute-start(bf16[136,512]{1,0:T(8,128)(2,1)S(1)} %get-tuple-element.43), channel_id=1, source_target_pairs={{0,2},{1,3},{2,0},{3,1},{4,6},{5,7},{6,4},{7,5},{8,10},{9,11},{10,... | collective-permute-start | bytes 417800 | tf_op jit(solution)/shard_map/ppermute | solution.py:410
  29.8 2.3 %collective-permute-start.8 = (bf16[136,512]{1,0:T(8,128)(2,1)S(1)}, bf16[136,512]{1,0:T(8,128)(2,1)S(1)}, u32[]{:S(2)}, u32[]{:S(2)}) collective-permute-start(bf16[136,512]{1,0:T(8,128)(2,1)S(1)} %get-tuple-element.44), channel_id=1, source_target_pairs={{0,3},{1,0},{2,1},{3,2},{4,7},{5,4},{6,5},{7,6},{8,11},{9,8},{10,9... | collective-permute-start | bytes 417800 | tf_op jit(solution)/shard_map/ppermute | solution.py:410
  32.0 2.3 %rotate_dft.5 = (bf16[144,256]{1,0:T(8,128)(2,1)S(1)}, bf16[136,256]{1,0:T(8,128)(2,1)S(1)}, bf16[136,256]{1,0:T(8,128)(2,1)S(1)}, bf16[136,256]{1,0:T(8,128)(2,1)S(1)}) custom-call(s32[1,2048]{1,0:T(1,128)S(1)} %bitcast.7, bf16[3,1072,2048]{2,1,0:T(8,128)(2,1)} %bitcast.11, bf16[4,48,1072]{2,1,0:T(8,128)(2,1)S(1)} %copy-done.2, f32[1072,128]{1,0:T(8,128)S(1)} %copy-done, ...), custom_call_target="tpu_custom_call" | custom-call | flops 316145664 | bytes 1646592 | tf_op jit(solution)/shard_map/rotate_dft/pallas_call | solution.py:185
  34.3 16.7 %collective-permute-done.7.refs_3_ = bf16[136,512]{1,0:T(8,128)(2,1)S(1)} collective-permute-done((bf16[136,512]{1,0:T(8,128)(2,1)S(1)}, bf16[136,512]{1,0:T(8,128)(2,1)S(1)}, u32[]{:S(2)}, u32[]{:S(2)}) %collective-permute-start.7) | collective-permute-done | bytes 139296 | tf_op jit(solution)/shard_map/ppermute | solution.py:410
  51.0 1.5 %collective-permute-start = (bf16[136,256]{1,0:T(8,128)(2,1)S(1)}, bf16[136,256]{1,0:T(8,128)(2,1)S(1)}, u32[]{:S(2)}, u32[]{:S(2)}) collective-permute-start(bf16[136,256]{1,0:T(8,128)(2,1)S(1)} %get-tuple-element.34), channel_id=1, source_target_pairs={{0,1},{1,2},{2,3},{3,0},{4,5},{5,6},{6,7},{7,4},{8,9},{9,10},{10,1... | collective-permute-start | bytes 208904 | tf_op jit(solution)/shard_map/ppermute | solution.py:410
  52.5 3.4 %collective-permute-start.1 = (bf16[136,256]{1,0:T(8,128)(2,1)S(1)}, bf16[136,256]{1,0:T(8,128)(2,1)S(1)}, u32[]{:S(2)}, u32[]{:S(2)}) collective-permute-start(bf16[136,256]{1,0:T(8,128)(2,1)S(1)} %get-tuple-element.35), channel_id=1, source_target_pairs={{0,2},{1,3},{2,0},{3,1},{4,6},{5,7},{6,4},{7,5},{8,10},{9,11},{10,... | collective-permute-start | bytes 208904 | tf_op jit(solution)/shard_map/ppermute | solution.py:410
  55.9 0.8 %collective-permute-start.2 = (bf16[136,256]{1,0:T(8,128)(2,1)S(1)}, bf16[136,256]{1,0:T(8,128)(2,1)S(1)}, u32[]{:S(2)}, u32[]{:S(2)}) collective-permute-start(bf16[136,256]{1,0:T(8,128)(2,1)S(1)} %get-tuple-element.36), channel_id=1, source_target_pairs={{0,3},{1,0},{2,1},{3,2},{4,7},{5,4},{6,5},{7,6},{8,11},{9,8},{10,9... | collective-permute-start | bytes 208904 | tf_op jit(solution)/shard_map/ppermute | solution.py:410
  56.7 2.1 %assemble.4 = (f32[2,2,3,32,2048]{4,3,2,1,0:T(8,128)}, f32[256,256]{1,0:T(8,128)S(1)}, bf16[3,128,264]{2,1,0:T(8,128)(2,1)S(1)}) custom-call(s32[1]{0:T(128)} %bitcast.refs_0_, bf16[144,512]{1,0:T(8,128)(2,1)S(1)} %copy-done.4, bf16[136,512]{1,0:T(8,128)(2,1)S(1)} %collective-permute-done.9.refs_2_, bf16[136,512]{1,0:T(8,128)(2,1)S(1)} %collective-permute-done.10.refs_3_, ...), custom_call_target="tpu_custom_call" | custom-call | flops 226492416 | bytes 786432 | tf_op jit(solution)/shard_map/assemble/pallas_call | solution.py:314
  58.8 2.0 %assemble.5 = (f32[2,2,3,32,2048]{4,3,2,1,0:T(8,128)}, f32[256,256]{1,0:T(8,128)S(1)}) custom-call(s32[1]{0:T(128)} %bitcast.refs_0_, bf16[144,512]{1,0:T(8,128)(2,1)S(1)} %get-tuple-element.41.refs_1_, bf16[136,512]{1,0:T(8,128)(2,1)S(1)} %collective-permute-done.6.refs_2_, ...), custom_call_target="tpu_custom_call", output_to_operand_aliasing={{0}: (7, {})} | custom-call | flops 226492416 | bytes 786432 | tf_op jit(solution)/shard_map/assemble/pallas_call | solution.py:314
  60.8 2.8 %assemble.6 = (f32[2,2,3,32,2048]{4,3,2,1,0:T(8,128)}, f32[256,256]{1,0:T(8,128)S(1)}) custom-call(s32[1]{0:T(128)} %bitcast.refs_0_, bf16[144,768]{1,0:T(8,128)(2,1)S(1)} %get-tuple-element.37.refs_1_, bf16[136,768]{1,0:T(8,128)(2,1)S(1)} %collective-permute-done.3.refs_2_, ...), custom_call_target="tpu_custom_call", output_to_operand_aliasing={{0}: (7, {})} | custom-call | flops 339738624 | bytes 1179648 | tf_op jit(solution)/shard_map/assemble/pallas_call | solution.py:314
  63.6 1.1 %assemble.7 = (f32[2,2,3,32,2048]{4,3,2,1,0:T(8,128)}, f32[64,128]{1,0:T(8,128)S(1)}) custom-call(s32[1]{0:T(128)} %bitcast.refs_0_, bf16[144,256]{1,0:T(8,128)(2,1)S(1)} %get-tuple-element.33.refs_1_, bf16[136,256]{1,0:T(8,128)(2,1)S(1)} %collective-permute-done.refs_2_, ...), custom_call_target="tpu_custom_call", output_to_operand_aliasing={{0}: (7, {})} | custom-call | flops 113246208 | bytes 393216 | tf_op jit(solution)/shard_map/assemble/pallas_call | solution.py:314
  64.7 1.2 %collective-permute-done.12 = f32[64,128]{1,0:T(8,128)S(1)} collective-permute-done((f32[64,128]{1,0:T(8,128)S(1)}, f32[64,128]{1,0:T(8,128)S(1)}, u32[]{:S(2)}, u32[]{:S(2)}) %collective-permute-start.12) | collective-permute-done | bytes 32800 | tf_op jit(solution)/shard_map/ppermute | solution.py:378
  65.9 1.5 %collective-permute-start.13 = (f32[64,128]{1,0:T(8,128)S(1)}, f32[64,128]{1,0:T(8,128)S(1)}, u32[]{:S(2)}, u32[]{:S(2)}) collective-permute-start(f32[64,128]{1,0:T(8,128)S(1)} %add.6), channel_id=1, source_target_pairs={{0,8},{4,12},{8,0},{12,4},{16,24},{20,28},{24,16},{28,20},{1,9},{5... | collective-permute-start | bytes 98312 | tf_op jit(solution)/shard_map/ppermute | solution.py:378
  67.4 2.4 %collective-permute-done.13 = f32[64,128]{1,0:T(8,128)S(1)} collective-permute-done((f32[64,128]{1,0:T(8,128)S(1)}, f32[64,128]{1,0:T(8,128)S(1)}, u32[]{:S(2)}, u32[]{:S(2)}) %collective-permute-start.13) | collective-permute-done | bytes 32800 | tf_op jit(solution)/shard_map/ppermute | solution.py:378
  69.9 1.6 %collective-permute-start.14 = (f32[64,128]{1,0:T(8,128)S(1)}, f32[64,128]{1,0:T(8,128)S(1)}, u32[]{:S(2)}, u32[]{:S(2)}) collective-permute-start(f32[64,128]{1,0:T(8,128)S(1)} %add.7.refs_0_), channel_id=1, source_target_pairs={{0,16},{4,20},{8,24},{12,28},{16,0},{20,4},{24,8},{28,12},{1,17},{... | collective-permute-start | bytes 98312 | tf_op jit(solution)/shard_map/ppermute | solution.py:378
  71.4 2.4 %collective-permute-done.14.refs_1_ = f32[64,128]{1,0:T(8,128)S(1)} collective-permute-done((f32[64,128]{1,0:T(8,128)S(1)}, f32[64,128]{1,0:T(8,128)S(1)}, u32[]{:S(2)}, u32[]{:S(2)}) %collective-permute-start.14) | collective-permute-done | bytes 32800 | tf_op jit(solution)/shard_map/ppermute | solution.py:378
  73.8 0.6 copy-done.6
  74.4 2.9 %factor.1 = f32[2,64,64]{2,1,0:T(8,128)} custom-call(f32[64,128]{1,0:T(8,128)} %copy-done.5, f32[64,128]{1,0:T(8,128)} %copy-done.6), custom_call_target="tpu_custom_call" | custom-call | tf_op jit(solution)/shard_map/factor/pallas_call | solution.py:367
  (23 shorter events, 0.1 us)
Async XLA Ops:
  0.6 11.7 %copy-start.3 = (s32[2048]{0:T(1024)S(1)}, s32[2048]{0:T(1024)}, u32[]{:S(2)}) copy-start(s32[2048]{0:T(1024)} %param.6) | copy-start | bytes 24580
  5.3 18.7 %collective-permute-start.9 = (bf16[136,512]{1,0:T(8,128)(2,1)}, bf16[136,512]{1,0:T(8,128)(2,1)S(1)}, u32[]{:S(2)}, u32[]{:S(2)}) collective-permute-start(bf16[136,512]{1,0:T(8,128)(2,1)} %get-tuple-element.46), channel_id=1, source_target_pairs={{0,1},{1,2},{2,3},{3,0},{4,5},{5,6},{6,7},{7,4},{8,9},{9,10},{10,1... | collective-permute-start | bytes 417800 | tf_op jit(solution)/shard_map/ppermute | solution.py:410
  8.4 19.2 %collective-permute-start.10 = (bf16[136,512]{1,0:T(8,128)(2,1)}, bf16[136,512]{1,0:T(8,128)(2,1)S(1)}, u32[]{:S(2)}, u32[]{:S(2)}) collective-permute-start(bf16[136,512]{1,0:T(8,128)(2,1)} %get-tuple-element.47), channel_id=1, source_target_pairs={{0,2},{1,3},{2,0},{3,1},{4,6},{5,7},{6,4},{7,5},{8,10},{9,11},{10,... | collective-permute-start | bytes 417800 | tf_op jit(solution)/shard_map/ppermute | solution.py:410
  11.0 16.8 %collective-permute-start.11 = (bf16[136,512]{1,0:T(8,128)(2,1)}, bf16[136,512]{1,0:T(8,128)(2,1)S(1)}, u32[]{:S(2)}, u32[]{:S(2)}) collective-permute-start(bf16[136,512]{1,0:T(8,128)(2,1)} %get-tuple-element.48), channel_id=1, source_target_pairs={{0,3},{1,0},{2,1},{3,2},{4,7},{5,4},{6,5},{7,6},{8,11},{9,8},{10,9... | collective-permute-start | bytes 417800 | tf_op jit(solution)/shard_map/ppermute | solution.py:410
  12.3 1.1 %copy-start = (f32[1072,128]{1,0:T(8,128)S(1)}, f32[1072,128]{1,0:T(8,128)}, u32[]{:S(2)}) copy-start(f32[1072,128]{1,0:T(8,128)} %get-tuple-element.31.refs_3_) | copy-start | bytes 1646596
  13.4 1.1 %copy-start.1 = (f32[1072,128]{1,0:T(8,128)S(1)}, f32[1072,128]{1,0:T(8,128)}, u32[]{:S(2)}) copy-start(f32[1072,128]{1,0:T(8,128)} %get-tuple-element.32.refs_4_) | copy-start | bytes 1646596
  14.4 1.0 %copy-start.2 = (bf16[4,48,1072]{2,1,0:T(8,128)(2,1)S(1)}, bf16[4,48,1072]{2,1,0:T(8,128)(2,1)}, u32[]{:S(2)}) copy-start(bf16[4,48,1072]{2,1,0:T(8,128)(2,1)} %get-tuple-element.30.refs_2_) | copy-start | bytes 1234948
  18.6 11.2 %collective-permute-start.6 = (bf16[136,512]{1,0:T(8,128)(2,1)S(1)}, bf16[136,512]{1,0:T(8,128)(2,1)S(1)}, u32[]{:S(2)}, u32[]{:S(2)}) collective-permute-start(bf16[136,512]{1,0:T(8,128)(2,1)S(1)} %get-tuple-element.42), channel_id=1, source_target_pairs={{0,1},{1,2},{2,3},{3,0},{4,5},{5,6},{6,7},{7,4},{8,9},{9,10},{10,1... | collective-permute-start | bytes 417800 | tf_op jit(solution)/shard_map/ppermute | solution.py:410
  23.8 32.0 %collective-permute-start.3 = (bf16[136,768]{1,0:T(8,128)(2,1)S(1)}, bf16[136,768]{1,0:T(8,128)(2,1)S(1)}, u32[]{:S(2)}, u32[]{:S(2)}) collective-permute-start(bf16[136,768]{1,0:T(8,128)(2,1)S(1)} %get-tuple-element.38), channel_id=1, source_target_pairs={{0,1},{1,2},{2,3},{3,0},{4,5},{5,6},{6,7},{7,4},{8,9},{9,10},{10,1... | collective-permute-start | bytes 626696 | tf_op jit(solution)/shard_map/ppermute | solution.py:410
  24.0 36.8 %collective-permute-start.4 = (bf16[136,768]{1,0:T(8,128)(2,1)S(1)}, bf16[136,768]{1,0:T(8,128)(2,1)S(1)}, u32[]{:S(2)}, u32[]{:S(2)}) collective-permute-start(bf16[136,768]{1,0:T(8,128)(2,1)S(1)} %get-tuple-element.39), channel_id=1, source_target_pairs={{0,2},{1,3},{2,0},{3,1},{4,6},{5,7},{6,4},{7,5},{8,10},{9,11},{10,... | collective-permute-start | bytes 626696 | tf_op jit(solution)/shard_map/ppermute | solution.py:410
  27.6 33.2 %collective-permute-start.5 = (bf16[136,768]{1,0:T(8,128)(2,1)S(1)}, bf16[136,768]{1,0:T(8,128)(2,1)S(1)}, u32[]{:S(2)}, u32[]{:S(2)}) collective-permute-start(bf16[136,768]{1,0:T(8,128)(2,1)S(1)} %get-tuple-element.40), channel_id=1, source_target_pairs={{0,3},{1,0},{2,1},{3,2},{4,7},{5,4},{6,5},{7,6},{8,11},{9,8},{10,9... | collective-permute-start | bytes 626696 | tf_op jit(solution)/shard_map/ppermute | solution.py:410
  27.8 23.2 %collective-permute-start.7 = (bf16[136,512]{1,0:T(8,128)(2,1)S(1)}, bf16[136,512]{1,0:T(8,128)(2,1)S(1)}, u32[]{:S(2)}, u32[]{:S(2)}) collective-permute-start(bf16[136,512]{1,0:T(8,128)(2,1)S(1)} %get-tuple-element.43), channel_id=1, source_target_pairs={{0,2},{1,3},{2,0},{3,1},{4,6},{5,7},{6,4},{7,5},{8,10},{9,11},{10,... | collective-permute-start | bytes 417800 | tf_op jit(solution)/shard_map/ppermute | solution.py:410
  29.8 26.9 %copy-start.4 = (bf16[144,512]{1,0:T(8,128)(2,1)S(1)}, bf16[144,512]{1,0:T(8,128)(2,1)}, u32[]{:S(2)}) copy-start(bf16[144,512]{1,0:T(8,128)(2,1)} %get-tuple-element.45.refs_1_) | copy-start | bytes 442372
  29.8 22.7 %collective-permute-start.8 = (bf16[136,512]{1,0:T(8,128)(2,1)S(1)}, bf16[136,512]{1,0:T(8,128)(2,1)S(1)}, u32[]{:S(2)}, u32[]{:S(2)}) collective-permute-start(bf16[136,512]{1,0:T(8,128)(2,1)S(1)} %get-tuple-element.44), channel_id=1, source_target_pairs={{0,3},{1,0},{2,1},{3,2},{4,7},{5,4},{6,5},{7,6},{8,11},{9,8},{10,9... | collective-permute-start | bytes 417800 | tf_op jit(solution)/shard_map/ppermute | solution.py:410
  51.0 12.6 %collective-permute-start = (bf16[136,256]{1,0:T(8,128)(2,1)S(1)}, bf16[136,256]{1,0:T(8,128)(2,1)S(1)}, u32[]{:S(2)}, u32[]{:S(2)}) collective-permute-start(bf16[136,256]{1,0:T(8,128)(2,1)S(1)} %get-tuple-element.34), channel_id=1, source_target_pairs={{0,1},{1,2},{2,3},{3,0},{4,5},{5,6},{6,7},{7,4},{8,9},{9,10},{10,1... | collective-permute-start | bytes 208904 | tf_op jit(solution)/shard_map/ppermute | solution.py:410
  52.5 11.1 %collective-permute-start.1 = (bf16[136,256]{1,0:T(8,128)(2,1)S(1)}, bf16[136,256]{1,0:T(8,128)(2,1)S(1)}, u32[]{:S(2)}, u32[]{:S(2)}) collective-permute-start(bf16[136,256]{1,0:T(8,128)(2,1)S(1)} %get-tuple-element.35), channel_id=1, source_target_pairs={{0,2},{1,3},{2,0},{3,1},{4,6},{5,7},{6,4},{7,5},{8,10},{9,11},{10,... | collective-permute-start | bytes 208904 | tf_op jit(solution)/shard_map/ppermute | solution.py:410
  55.9 7.7 %collective-permute-start.2 = (bf16[136,256]{1,0:T(8,128)(2,1)S(1)}, bf16[136,256]{1,0:T(8,128)(2,1)S(1)}, u32[]{:S(2)}, u32[]{:S(2)}) collective-permute-start(bf16[136,256]{1,0:T(8,128)(2,1)S(1)} %get-tuple-element.36), channel_id=1, source_target_pairs={{0,3},{1,0},{2,1},{3,2},{4,7},{5,4},{6,5},{7,6},{8,11},{9,8},{10,9... | collective-permute-start | bytes 208904 | tf_op jit(solution)/shard_map/ppermute | solution.py:410
  64.7 1.2 %collective-permute-start.12 = (f32[64,128]{1,0:T(8,128)S(1)}, f32[64,128]{1,0:T(8,128)S(1)}, u32[]{:S(2)}, u32[]{:S(2)}) collective-permute-start(f32[64,128]{1,0:T(8,128)S(1)} %get-tuple-element.57), channel_id=1, source_target_pairs={{0,4},{4,0},{8,12},{12,8},{16,20},{20,16},{24,28},{28,24},{1,5},{5... | collective-permute-start | bytes 98312 | tf_op jit(solution)/shard_map/ppermute | solution.py:378
  65.9 3.9 %collective-permute-start.13 = (f32[64,128]{1,0:T(8,128)S(1)}, f32[64,128]{1,0:T(8,128)S(1)}, u32[]{:S(2)}, u32[]{:S(2)}) collective-permute-start(f32[64,128]{1,0:T(8,128)S(1)} %add.6), channel_id=1, source_target_pairs={{0,8},{4,12},{8,0},{12,4},{16,24},{20,28},{24,16},{28,20},{1,9},{5... | collective-permute-start | bytes 98312 | tf_op jit(solution)/shard_map/ppermute | solution.py:378
  69.9 4.0 %copy-start.5 = (f32[64,128]{1,0:T(8,128)}, f32[64,128]{1,0:T(8,128)S(1)}, u32[]{:S(2)}) copy-start(f32[64,128]{1,0:T(8,128)S(1)} %add.7.refs_0_) | copy-start | bytes 98308
  69.9 4.0 %collective-permute-start.14 = (f32[64,128]{1,0:T(8,128)S(1)}, f32[64,128]{1,0:T(8,128)S(1)}, u32[]{:S(2)}, u32[]{:S(2)}) collective-permute-start(f32[64,128]{1,0:T(8,128)S(1)} %add.7.refs_0_), channel_id=1, source_target_pairs={{0,16},{4,20},{8,24},{12,28},{16,0},{20,4},{24,8},{28,12},{1,17},{... | collective-permute-start | bytes 98312 | tf_op jit(solution)/shard_map/ppermute | solution.py:378
  73.8 0.6 copy-start.6

commit v10 on v8

--- a/solution.py
+++ b/solution.py
@@ -14,7 +14,7 @@
 HOP = 128
 LANES = 128
 TILE = 256
-PIVOT = 8
+PIVOT = 16
 SCALE = (8.0 / (3.0 * NFFT)) ** 0.5
 HIGHEST = lax.Precision.HIGHEST
 
@@ -107,22 +107,39 @@
         out_ref[at:at + width, :] = turned[:width]
 
 
-def dft_body(n, owned, slots, span, blocks, first, *refs):
-    if first:
+def dft_body(n, owned, slots, span, blocks, offset, mode, *refs):
+    *refs, rot_ref = refs
+    step = pl.program_id(0)
+    if mode == "use":
+        mask_ref, vel_ref, a_ref, cos_ref, sin_ref = refs[:5]
+        outs = refs[5:]
+    else:
         pos_ref, starts_ref, freqs_ref, angle_ref, mask_ref, vel_ref = refs[:6]
         outs = refs[6:6 + n]
         a_ref, cos_ref, sin_ref = refs[6 + n:9 + n]
-        rot_ref = refs[9 + n]
-
-        @pl.when(pl.program_id(0) == 0)
+    if mode == "lead":
+        vel_hbm, (held_ref, sem) = vel_ref, refs[9 + n:]
+
+        def load(i):
+            columns = pl.ds(pl.multiple_of(offset + i * TILE, TILE), TILE)
+            return pltpu.make_async_copy(vel_hbm.at[:, :, columns], held_ref.at[i], sem.at[i])
+
+        @pl.when(step == 0)
+        def _():
+            for i in range(held_ref.shape[0]):
+                load(i).start()
+
+    if mode != "use":
+
+        @pl.when(step == 0)
         def _():
             build_rows(n, owned, slots, span, blocks, pos_ref[0], starts_ref, freqs_ref, a_ref)
             spread_column(jnp.cos(angle_ref[...].reshape(1, span)), span, cos_ref)
             spread_column(jnp.sin(angle_ref[...].reshape(1, span)), span, sin_ref)
-    else:
-        mask_ref, vel_ref, a_ref, cos_ref, sin_ref = refs[:5]
-        outs = refs[5:5 + n]
-        rot_ref = refs[5 + n]
+
+    if mode == "lead":
+        load(step).wait()
+        vel_ref = held_ref.at[step]
     width = vel_ref.shape[2]
     turning = mask_ref[...] == 1
     for at in range(0, span, 16):
@@ -155,7 +172,7 @@
             outs[k][COMPS * main:, :] = jnp.concatenate(parts, axis=0).astype(jnp.bfloat16)
 
 
-def dft_call(n, owned, slots, blocks, first, offset, points, position, starts, freqs, angles, mask, velocity, shared):
+def dft_call(n, owned, slots, blocks, mode, offset, points, position, starts, freqs, angles, mask, velocity, shared):
     span = velocity.shape[1]
     rows = -(-slots * owned * 2 // 16) * 16
     heights = [COMPS * rows] + [layout(slots * owned * 2)[2]] * (n - 1)
@@ -174,22 +191,29 @@
     shared_specs = [whole(t.shape) for t in shared_types]
     out_types = [jax.ShapeDtypeStruct((h, points), jnp.bfloat16) for h in heights]
     out_specs = [pl.BlockSpec((h, TILE), lambda i: (0, i)) for h in heights]
-    if first:
+    scratch = []
+    if mode != "use":
         args = (position, starts, freqs, angles, mask, velocity)
         in_specs = [smem] * 3 + [whole((span,))] + data_specs
+    if mode == "lead":
+        in_specs[-1] = pl.BlockSpec(memory_space=pl.ANY)
+        scratch += [pltpu.VMEM(t.shape, t.dtype) for t in shared_types]
+        scratch.append(pltpu.VMEM((points // TILE, COMPS, span, TILE), jnp.bfloat16))
+        scratch.append(pltpu.SemaphoreType.DMA((points // TILE,)))
+    elif mode == "build":
         out_types = out_types + shared_types
         out_specs = out_specs + shared_specs
     else:
         args = (mask, velocity) + tuple(shared)
         in_specs = data_specs + shared_specs
     out = pl.pallas_call(
-        functools.partial(dft_body, n, owned, slots, span, blocks, first),
+        functools.partial(dft_body, n, owned, slots, span, blocks, offset, mode),
         grid=(points // TILE,),
         out_shape=out_types,
         in_specs=in_specs,
         out_specs=out_specs,
-        scratch_shapes=[pltpu.VMEM((2, span, TILE), jnp.bfloat16)],
-        compiler_params=pltpu.CompilerParams(vmem_limit_bytes=(60 if first else 40) * 2**20),
+        scratch_shapes=scratch + [pltpu.VMEM((2, span, TILE), jnp.bfloat16)],
+        compiler_params=pltpu.CompilerParams(vmem_limit_bytes=(60 if mode == "lead" else 40) * 2**20),
         cost_estimate=pl.CostEstimate(
             flops=2 * n * rows * span * COMPS * points,
             bytes_accessed=2 * COMPS * span * points,
@@ -197,7 +221,7 @@
         ),
         name="rotate_dft",
     )(*args)
-    return out[:n], out[n:] if first else shared
+    return out[:n], out[n:] if mode == "build" else shared
 
 
 def stack_width(n, rows):
@@ -401,13 +425,13 @@
 
     pieces = []
     shared = None
-    for at, count in chunks_of(points):
+    for i, (at, count) in enumerate(chunks_of(points)):
         sums, shared = dft_call(
-            n, owned, slots, blocks, shared is None, at, count,
+            n, owned, slots, blocks, ("lead", "build")[i] if i < 2 else "use", at, count,
             position, block_starts, frequencies, angles, mask, samples, shared,
         )
         moved = [sums[0]] + [
-            lax.ppermute(sums[k], "tm", [(i, (i + k) % n) for i in range(n)]) for k in range(1, n)
+            lax.ppermute(sums[k], "tm", [(j, (j + k) % n) for j in range(n)]) for k in range(1, n)
         ]
         pieces.append((at, count, moved))
 

time: 71.5 us -> 71.4 us (level)
  starting transfers between devices: 28.5 us -> 32.5 us
  local copies, waits for them, and re-layouts: 3.73 us -> 0.63 us
  waiting for transfers between devices: 14.1 us -> 12 us
  Pallas kernels: 23.8 us -> 24.8 us
    ppermute x12, starting transfers between devices: 25.4 us -> 29.4 us  [per_device(): lax.ppermute(sums[k], 'tm', [(j, (j + k) % n) for j in range(n)])]
    unnamed x14, local copies, waits for them, and re-layouts: 3.73 us -> 0.63 us
    ppermute x12, waiting for transfers between devices: 8.05 us -> 6 us  [per_device(): lax.ppermute(sums[k], 'tm', [(j, (j + k) % n) for j in range(n)])]
    pallas_call x4, Pallas kernels: 14 us -> 15.4 us  [dft_call(): pl.pallas_call(functools.partial(dft_body, n, owned, slots, span, blocks,...]
  transfers between devices with their start and end apart: 15 -> 15, of which waited for: 5 -> 5; matrix products, arithmetic and copies ran while one was open for 0% -> 0% of each run, Pallas kernels for 20% -> 22%
where the time goes in v10:
time: 71.4 us; the launch traced here: 70.7 us
  starting transfers between devices  32.5 us (46%)
  Pallas kernels  24.8 us (35%)
  waiting for transfers between devices  12 us (17%)
  between operations  0.74 us (1%)
    ppermute x12, starting transfers between devices, per_device(): lax.ppermute(sums[k], 'tm', [(j, (j + k) % n) for j in range(n)])  29.4 us
    pallas_call x4, Pallas kernels, dft_call(): pl.pallas_call(functools.partial(dft_body, n, owned, slots, span, blocks,...  15.4 us
    pallas_call x4, Pallas kernels, assemble_call(): pl.pallas_call(functools.partial(assemble_body, n, owned, slots, span, bl...  6.55 us
    ppermute x3, waiting for transfers between devices, sum_over_space(): lax.ppermute(x, 'space', [(i, i ^ k) for i in range(groups)])  6.02 us
    ppermute x12, waiting for transfers between devices, per_device(): lax.ppermute(sums[k], 'tm', [(j, (j + k) % n) for j in range(n)])  6 us
    ppermute x3, starting transfers between devices, sum_over_space(): lax.ppermute(x, 'space', [(i, i ^ k) for i in range(groups)])  3.08 us
    pallas_call x1, Pallas kernels, factor_call(): pl.pallas_call(functools.partial(factor_body, owned, order, len(parts)),...  2.9 us
  transfers between devices with their start and end apart: 15, of which 5 were waited for; matrix products, arithmetic and copies ran while one was open for 0% of the time, Pallas kernels for 22%

profile of v10, /device:TPU:0, one launch (start us, length us, event | category | flops | bytes accessed | tf_op | source)
XLA Modules:
  0.0 70.7 jit_solution(18006879909111845444)
XLA Ops:
  0.7 4.9 %rotate_dft.7 = (bf16[144,512]{1,0:T(8,128)(2,1)}, bf16[136,512]{1,0:T(8,128)(2,1)}, bf16[136,512]{1,0:T(8,128)(2,1)}, bf16[136,512]{1,0:T(8,128)(2,1)}) custom-call(s32[1]{0:T(128)} %bitcast.refs_0_, s32[32]{0:T(128)} %refs_1_.3, s32[8]{0:T(128)} %refs_2_.3, f32[1072]{0:T(1024)} %refs_3_.3, s32[1,2048]{1,0:T(1,128)} %bitcast.4, bf16[3,1072,2048]{2,1,0:T(8,128)(2,1)} %bitcast.8), custom_call_target="tpu_custom_call" | custom-call | flops 632291328 | bytes 3293184 | tf_op jit(solution)/shard_map/rotate_dft/pallas_call | solution.py:209
  5.5 3.1 %collective-permute-start.9 = (bf16[136,512]{1,0:T(8,128)(2,1)}, bf16[136,512]{1,0:T(8,128)(2,1)S(1)}, u32[]{:S(2)}, u32[]{:S(2)}) collective-permute-start(bf16[136,512]{1,0:T(8,128)(2,1)} %get-tuple-element.46), channel_id=1, source_target_pairs={{0,1},{1,2},{2,3},{3,0},{4,5},{5,6},{6,7},{7,4},{8,9},{9,10},{10,1... | collective-permute-start | bytes 417800 | tf_op jit(solution)/shard_map/ppermute | solution.py:434
  8.6 2.6 %collective-permute-start.10 = (bf16[136,512]{1,0:T(8,128)(2,1)}, bf16[136,512]{1,0:T(8,128)(2,1)S(1)}, u32[]{:S(2)}, u32[]{:S(2)}) collective-permute-start(bf16[136,512]{1,0:T(8,128)(2,1)} %get-tuple-element.47), channel_id=1, source_target_pairs={{0,2},{1,3},{2,0},{3,1},{4,6},{5,7},{6,4},{7,5},{8,10},{9,11},{10,... | collective-permute-start | bytes 417800 | tf_op jit(solution)/shard_map/ppermute | solution.py:434
  11.2 1.3 %collective-permute-start.11 = (bf16[136,512]{1,0:T(8,128)(2,1)}, bf16[136,512]{1,0:T(8,128)(2,1)S(1)}, u32[]{:S(2)}, u32[]{:S(2)}) collective-permute-start(bf16[136,512]{1,0:T(8,128)(2,1)} %get-tuple-element.48), channel_id=1, source_target_pairs={{0,3},{1,0},{2,1},{3,2},{4,7},{5,4},{6,5},{7,6},{8,11},{9,8},{10,9... | collective-permute-start | bytes 417800 | tf_op jit(solution)/shard_map/ppermute | solution.py:434
  12.6 4.1 %rotate_dft.4 = (bf16[144,512]{1,0:T(8,128)(2,1)S(1)}, bf16[136,512]{1,0:T(8,128)(2,1)S(1)}, bf16[136,512]{1,0:T(8,128)(2,1)S(1)}, bf16[136,512]{1,0:T(8,128)(2,...) custom-call(s32[1]{0:T(128)} %bitcast.refs_0_, s32[32]{0:T(128)S(1)} %copy-done.2, ...), custom_call_target="tpu_custom_call" | custom-call | flops 632291328 | bytes 3293184 | tf_op jit(solution)/shard_map/rotate_dft/pallas_call | solution.py:209
  16.6 0.7 %collective-permute-start.6 = (bf16[136,512]{1,0:T(8,128)(2,1)S(1)}, bf16[136,512]{1,0:T(8,128)(2,1)S(1)}, u32[]{:S(2)}, u32[]{:S(2)}) collective-permute-start(bf16[136,512]{1,0:T(8,128)(2,1)S(1)} %get-tuple-element.42), channel_id=1, source_target_pairs={{0,1},{1,2},{2,3},{3,0},{4,5},{5,6},{6,7},{7,4},{8,9},{9,10},{10,1... | collective-permute-start | bytes 417800 | tf_op jit(solution)/shard_map/ppermute | solution.py:434
  17.4 0.3 collective-permute-start.7
  17.7 3.2 %rotate_dft.6 = (bf16[144,512]{1,0:T(8,128)(2,1)S(1)}, bf16[136,512]{1,0:T(8,128)(2,1)S(1)}, bf16[136,512]{1,0:T(8,128)(2,1)S(1)}, bf16[136,512]{1,0:T(8,128)(2,1)S(1)}) custom-call(s32[1,2048]{1,0:T(1,128)S(1)} %bitcast.6, bf16[3,1072,2048]{2,1,0:T(8,128)(2,1)} %bitcast.10, bf16[4,48,1072]{2,1,0:T(8,128)(2,1)S(1)} %get-tuple-element.30.refs_2_, ...), custom_call_target="tpu_custom_call" | custom-call | flops 632291328 | bytes 3293184 | tf_op jit(solution)/shard_map/rotate_dft/pallas_call | solution.py:209
  21.0 2.9 %collective-permute-start.8 = (bf16[136,512]{1,0:T(8,128)(2,1)S(1)}, bf16[136,512]{1,0:T(8,128)(2,1)S(1)}, u32[]{:S(2)}, u32[]{:S(2)}) collective-permute-start(bf16[136,512]{1,0:T(8,128)(2,1)S(1)} %get-tuple-element.44), channel_id=1, source_target_pairs={{0,3},{1,0},{2,1},{3,2},{4,7},{5,4},{6,5},{7,6},{8,11},{9,8},{10,9... | collective-permute-start | bytes 417800 | tf_op jit(solution)/shard_map/ppermute | solution.py:434
  23.8 5.3 %collective-permute-start.3 = (bf16[136,512]{1,0:T(8,128)(2,1)S(1)}, bf16[136,512]{1,0:T(8,128)(2,1)S(1)}, u32[]{:S(2)}, u32[]{:S(2)}) collective-permute-start(bf16[136,512]{1,0:T(8,128)(2,1)S(1)} %get-tuple-element.38), channel_id=1, source_target_pairs={{0,1},{1,2},{2,3},{3,0},{4,5},{5,6},{6,7},{7,4},{8,9},{9,10},{10,1... | collective-permute-start | bytes 417800 | tf_op jit(solution)/shard_map/ppermute | solution.py:434
  29.1 3.7 %collective-permute-start.4 = (bf16[136,512]{1,0:T(8,128)(2,1)S(1)}, bf16[136,512]{1,0:T(8,128)(2,1)S(1)}, u32[]{:S(2)}, u32[]{:S(2)}) collective-permute-start(bf16[136,512]{1,0:T(8,128)(2,1)S(1)} %get-tuple-element.39), channel_id=1, source_target_pairs={{0,2},{1,3},{2,0},{3,1},{4,6},{5,7},{6,4},{7,5},{8,10},{9,11},{10,... | collective-permute-start | bytes 417800 | tf_op jit(solution)/shard_map/ppermute | solution.py:434
  32.9 0.0 collective-permute-done.6.refs_2_
  32.9 1.1 %collective-permute-start.5 = (bf16[136,512]{1,0:T(8,128)(2,1)S(1)}, bf16[136,512]{1,0:T(8,128)(2,1)S(1)}, u32[]{:S(2)}, u32[]{:S(2)}) collective-permute-start(bf16[136,512]{1,0:T(8,128)(2,1)S(1)} %get-tuple-element.40), channel_id=1, source_target_pairs={{0,3},{1,0},{2,1},{3,2},{4,7},{5,4},{6,5},{7,6},{8,11},{9,8},{10,9... | collective-permute-start | bytes 417800 | tf_op jit(solution)/shard_map/ppermute | solution.py:434
  34.0 3.2 %rotate_dft.5 = (bf16[144,512]{1,0:T(8,128)(2,1)S(1)}, bf16[136,512]{1,0:T(8,128)(2,1)S(1)}, bf16[136,512]{1,0:T(8,128)(2,1)S(1)}, bf16[136,512]{1,0:T(8,128)(2,1)S(1)}) custom-call(s32[1,2048]{1,0:T(1,128)S(1)} %bitcast.7, bf16[3,1072,2048]{2,1,0:T(8,128)(2,1)} %bitcast.11, bf16[4,48,1072]{2,1,0:T(8,128)(2,1)S(1)} %get-tuple-element.30.refs_2_, ...), custom_call_target="tpu_custom_call" | custom-call | flops 632291328 | bytes 3293184 | tf_op jit(solution)/shard_map/rotate_dft/pallas_call | solution.py:209
  37.2 0.4 collective-permute-done.7.refs_3_
  37.6 3.7 %collective-permute-start = (bf16[136,512]{1,0:T(8,128)(2,1)S(1)}, bf16[136,512]{1,0:T(8,128)(2,1)S(1)}, u32[]{:S(2)}, u32[]{:S(2)}) collective-permute-start(bf16[136,512]{1,0:T(8,128)(2,1)S(1)} %get-tuple-element.34), channel_id=1, source_target_pairs={{0,1},{1,2},{2,3},{3,0},{4,5},{5,6},{6,7},{7,4},{8,9},{9,10},{10,1... | collective-permute-start | bytes 417800 | tf_op jit(solution)/shard_map/ppermute | solution.py:434
  41.3 0.0 collective-permute-done.8.refs_4_
  41.3 3.5 %collective-permute-start.1 = (bf16[136,512]{1,0:T(8,128)(2,1)S(1)}, bf16[136,512]{1,0:T(8,128)(2,1)S(1)}, u32[]{:S(2)}, u32[]{:S(2)}) collective-permute-start(bf16[136,512]{1,0:T(8,128)(2,1)S(1)} %get-tuple-element.35), channel_id=1, source_target_pairs={{0,2},{1,3},{2,0},{3,1},{4,6},{5,7},{6,4},{7,5},{8,10},{9,11},{10,... | collective-permute-start | bytes 417800 | tf_op jit(solution)/shard_map/ppermute | solution.py:434
  44.8 1.1 %collective-permute-start.2 = (bf16[136,512]{1,0:T(8,128)(2,1)S(1)}, bf16[136,512]{1,0:T(8,128)(2,1)S(1)}, u32[]{:S(2)}, u32[]{:S(2)}) collective-permute-start(bf16[136,512]{1,0:T(8,128)(2,1)S(1)} %get-tuple-element.36), channel_id=1, source_target_pairs={{0,3},{1,0},{2,1},{3,2},{4,7},{5,4},{6,5},{7,6},{8,11},{9,8},{10,9... | collective-permute-start | bytes 417800 | tf_op jit(solution)/shard_map/ppermute | solution.py:434
  45.9 1.7 %assemble.4 = (f32[2,2,3,32,2048]{4,3,2,1,0:T(8,128)}, f32[256,256]{1,0:T(8,128)S(1)}, bf16[3,128,264]{2,1,0:T(8,128)(2,1)S(1)}) custom-call(s32[1]{0:T(128)} %bitcast.refs_0_, bf16[144,512]{1,0:T(8,128)(2,1)S(1)} %copy-done.4, bf16[136,512]{1,0:T(8,128)(2,1)S(1)} %collective-permute-done.9.refs_2_, bf16[136,512]{1,0:T(8,128)(2,1)S(1)} %collective-permute-done.10.refs_3_, ...), custom_call_target="tpu_custom_call" | custom-call | flops 226492416 | bytes 786432 | tf_op jit(solution)/shard_map/assemble/pallas_call | solution.py:338
  47.6 1.6 %assemble.5 = (f32[2,2,3,32,2048]{4,3,2,1,0:T(8,128)}, f32[256,256]{1,0:T(8,128)S(1)}) custom-call(s32[1]{0:T(128)} %bitcast.refs_0_, bf16[144,512]{1,0:T(8,128)(2,1)S(1)} %get-tuple-element.41.refs_1_, bf16[136,512]{1,0:T(8,128)(2,1)S(1)} %collective-permute-done.6.refs_2_, ...), custom_call_target="tpu_custom_call", output_to_operand_aliasing={{0}: (7, {})} | custom-call | flops 226492416 | bytes 786432 | tf_op jit(solution)/shard_map/assemble/pallas_call | solution.py:338
  49.2 0.0 collective-permute-done.4.refs_3_
  49.3 1.6 %assemble.6 = (f32[2,2,3,32,2048]{4,3,2,1,0:T(8,128)}, f32[256,256]{1,0:T(8,128)S(1)}) custom-call(s32[1]{0:T(128)} %bitcast.refs_0_, bf16[144,512]{1,0:T(8,128)(2,1)S(1)} %get-tuple-element.37.refs_1_, bf16[136,512]{1,0:T(8,128)(2,1)S(1)} %collective-permute-done.3.refs_2_, ...), custom_call_target="tpu_custom_call", output_to_operand_aliasing={{0}: (7, {})} | custom-call | flops 226492416 | bytes 786432 | tf_op jit(solution)/shard_map/assemble/pallas_call | solution.py:338
  50.9 5.6 %collective-permute-done.1.refs_3_ = bf16[136,512]{1,0:T(8,128)(2,1)S(1)} collective-permute-done((bf16[136,512]{1,0:T(8,128)(2,1)S(1)}, bf16[136,512]{1,0:T(8,128)(2,1)S(1)}, u32[]{:S(2)}, u32[]{:S(2)}) %collective-permute-start.1) | collective-permute-done | bytes 139296 | tf_op jit(solution)/shard_map/ppermute | solution.py:434
  56.5 1.6 %assemble.7 = (f32[2,2,3,32,2048]{4,3,2,1,0:T(8,128)}, f32[64,128]{1,0:T(8,128)S(1)}) custom-call(s32[1]{0:T(128)} %bitcast.refs_0_, bf16[144,512]{1,0:T(8,128)(2,1)S(1)} %get-tuple-element.33.refs_1_, bf16[136,512]{1,0:T(8,128)(2,1)S(1)} %collective-permute-done.refs_2_, ...), custom_call_target="tpu_custom_call", output_to_operand_aliasing={{0}: (7, {})} | custom-call | flops 226492416 | bytes 786432 | tf_op jit(solution)/shard_map/assemble/pallas_call | solution.py:338
  58.1 1.2 %collective-permute-done.12 = f32[64,128]{1,0:T(8,128)S(1)} collective-permute-done((f32[64,128]{1,0:T(8,128)S(1)}, f32[64,128]{1,0:T(8,128)S(1)}, u32[]{:S(2)}, u32[]{:S(2)}) %collective-permute-start.12) | collective-permute-done | bytes 32800 | tf_op jit(solution)/shard_map/ppermute | solution.py:402
  59.3 1.5 %collective-permute-start.13 = (f32[64,128]{1,0:T(8,128)S(1)}, f32[64,128]{1,0:T(8,128)S(1)}, u32[]{:S(2)}, u32[]{:S(2)}) collective-permute-start(f32[64,128]{1,0:T(8,128)S(1)} %add.6), channel_id=1, source_target_pairs={{0,8},{4,12},{8,0},{12,4},{16,24},{20,28},{24,16},{28,20},{1,9},{5... | collective-permute-start | bytes 98312 | tf_op jit(solution)/shard_map/ppermute | solution.py:402
  60.8 2.4 %collective-permute-done.13 = f32[64,128]{1,0:T(8,128)S(1)} collective-permute-done((f32[64,128]{1,0:T(8,128)S(1)}, f32[64,128]{1,0:T(8,128)S(1)}, u32[]{:S(2)}, u32[]{:S(2)}) %collective-permute-start.13) | collective-permute-done | bytes 32800 | tf_op jit(solution)/shard_map/ppermute | solution.py:402
  63.2 1.6 %collective-permute-start.14 = (f32[64,128]{1,0:T(8,128)S(1)}, f32[64,128]{1,0:T(8,128)S(1)}, u32[]{:S(2)}, u32[]{:S(2)}) collective-permute-start(f32[64,128]{1,0:T(8,128)S(1)} %add.7.refs_0_), channel_id=1, source_target_pairs={{0,16},{4,20},{8,24},{12,28},{16,0},{20,4},{24,8},{28,12},{1,17},{... | collective-permute-start | bytes 98312 | tf_op jit(solution)/shard_map/ppermute | solution.py:402
  64.8 2.4 %collective-permute-done.14.refs_1_ = f32[64,128]{1,0:T(8,128)S(1)} collective-permute-done((f32[64,128]{1,0:T(8,128)S(1)}, f32[64,128]{1,0:T(8,128)S(1)}, u32[]{:S(2)}, u32[]{:S(2)}) %collective-permute-start.14) | collective-permute-done | bytes 32800 | tf_op jit(solution)/shard_map/ppermute | solution.py:402
  67.2 0.6 copy-done.6
  67.8 2.9 %factor.1 = f32[2,64,64]{2,1,0:T(8,128)} custom-call(f32[64,128]{1,0:T(8,128)} %copy-done.5, f32[64,128]{1,0:T(8,128)} %copy-done.6), custom_call_target="tpu_custom_call" | custom-call | tf_op jit(solution)/shard_map/factor/pallas_call | solution.py:391
  (23 shorter events, 0.1 us)
Async XLA Ops:
  0.6 11.9 %copy-start = (s32[2048]{0:T(1024)S(1)}, s32[2048]{0:T(1024)}, u32[]{:S(2)}) copy-start(s32[2048]{0:T(1024)} %param.6) | copy-start | bytes 24580
  0.6 11.9 %copy-start.1 = (f32[1072]{0:T(1024)S(1)}, f32[1072]{0:T(1024)}, u32[]{:S(2)}) copy-start(f32[1072]{0:T(1024)} %refs_3_.3) | copy-start | bytes 12868
  0.7 11.9 %copy-start.2 = (s32[32]{0:T(128)S(1)}, s32[32]{0:T(128)}, u32[]{:S(2)}) copy-start(s32[32]{0:T(128)} %refs_1_.3) | copy-start | bytes 388
  0.7 11.9 %copy-start.3 = (s32[8]{0:T(128)S(1)}, s32[8]{0:T(128)}, u32[]{:S(2)}) copy-start(s32[8]{0:T(128)} %refs_2_.3) | copy-start | bytes 100
  5.5 15.4 %collective-permute-start.9 = (bf16[136,512]{1,0:T(8,128)(2,1)}, bf16[136,512]{1,0:T(8,128)(2,1)S(1)}, u32[]{:S(2)}, u32[]{:S(2)}) collective-permute-start(bf16[136,512]{1,0:T(8,128)(2,1)} %get-tuple-element.46), channel_id=1, source_target_pairs={{0,1},{1,2},{2,3},{3,0},{4,5},{5,6},{6,7},{7,4},{8,9},{9,10},{10,1... | collective-permute-start | bytes 417800 | tf_op jit(solution)/shard_map/ppermute | solution.py:434
  8.6 15.2 %collective-permute-start.10 = (bf16[136,512]{1,0:T(8,128)(2,1)}, bf16[136,512]{1,0:T(8,128)(2,1)S(1)}, u32[]{:S(2)}, u32[]{:S(2)}) collective-permute-start(bf16[136,512]{1,0:T(8,128)(2,1)} %get-tuple-element.47), channel_id=1, source_target_pairs={{0,2},{1,3},{2,0},{3,1},{4,6},{5,7},{6,4},{7,5},{8,10},{9,11},{10,... | collective-permute-start | bytes 417800 | tf_op jit(solution)/shard_map/ppermute | solution.py:434
  11.2 17.9 %collective-permute-start.11 = (bf16[136,512]{1,0:T(8,128)(2,1)}, bf16[136,512]{1,0:T(8,128)(2,1)S(1)}, u32[]{:S(2)}, u32[]{:S(2)}) collective-permute-start(bf16[136,512]{1,0:T(8,128)(2,1)} %get-tuple-element.48), channel_id=1, source_target_pairs={{0,3},{1,0},{2,1},{3,2},{4,7},{5,4},{6,5},{7,6},{8,11},{9,8},{10,9... | collective-permute-start | bytes 417800 | tf_op jit(solution)/shard_map/ppermute | solution.py:434
  16.6 16.2 %collective-permute-start.6 = (bf16[136,512]{1,0:T(8,128)(2,1)S(1)}, bf16[136,512]{1,0:T(8,128)(2,1)S(1)}, u32[]{:S(2)}, u32[]{:S(2)}) collective-permute-start(bf16[136,512]{1,0:T(8,128)(2,1)S(1)} %get-tuple-element.42), channel_id=1, source_target_pairs={{0,1},{1,2},{2,3},{3,0},{4,5},{5,6},{6,7},{7,4},{8,9},{9,10},{10,1... | collective-permute-start | bytes 417800 | tf_op jit(solution)/shard_map/ppermute | solution.py:434
  17.4 20.2 %collective-permute-start.7 = (bf16[136,512]{1,0:T(8,128)(2,1)S(1)}, bf16[136,512]{1,0:T(8,128)(2,1)S(1)}, u32[]{:S(2)}, u32[]{:S(2)}) collective-permute-start(bf16[136,512]{1,0:T(8,128)(2,1)S(1)} %get-tuple-element.43), channel_id=1, source_target_pairs={{0,2},{1,3},{2,0},{3,1},{4,6},{5,7},{6,4},{7,5},{8,10},{9,11},{10,... | collective-permute-start | bytes 417800 | tf_op jit(solution)/shard_map/ppermute | solution.py:434
  21.0 20.3 %collective-permute-start.8 = (bf16[136,512]{1,0:T(8,128)(2,1)S(1)}, bf16[136,512]{1,0:T(8,128)(2,1)S(1)}, u32[]{:S(2)}, u32[]{:S(2)}) collective-permute-start(bf16[136,512]{1,0:T(8,128)(2,1)S(1)} %get-tuple-element.44), channel_id=1, source_target_pairs={{0,3},{1,0},{2,1},{3,2},{4,7},{5,4},{6,5},{7,6},{8,11},{9,8},{10,9... | collective-permute-start | bytes 417800 | tf_op jit(solution)/shard_map/ppermute | solution.py:434
  23.8 21.0 %collective-permute-start.3 = (bf16[136,512]{1,0:T(8,128)(2,1)S(1)}, bf16[136,512]{1,0:T(8,128)(2,1)S(1)}, u32[]{:S(2)}, u32[]{:S(2)}) collective-permute-start(bf16[136,512]{1,0:T(8,128)(2,1)S(1)} %get-tuple-element.38), channel_id=1, source_target_pairs={{0,1},{1,2},{2,3},{3,0},{4,5},{5,6},{6,7},{7,4},{8,9},{9,10},{10,1... | collective-permute-start | bytes 417800 | tf_op jit(solution)/shard_map/ppermute | solution.py:434
  29.1 20.1 %collective-permute-start.4 = (bf16[136,512]{1,0:T(8,128)(2,1)S(1)}, bf16[136,512]{1,0:T(8,128)(2,1)S(1)}, u32[]{:S(2)}, u32[]{:S(2)}) collective-permute-start(bf16[136,512]{1,0:T(8,128)(2,1)S(1)} %get-tuple-element.39), channel_id=1, source_target_pairs={{0,2},{1,3},{2,0},{3,1},{4,6},{5,7},{6,4},{7,5},{8,10},{9,11},{10,... | collective-permute-start | bytes 417800 | tf_op jit(solution)/shard_map/ppermute | solution.py:434
  32.9 13.1 %copy-start.4 = (bf16[144,512]{1,0:T(8,128)(2,1)S(1)}, bf16[144,512]{1,0:T(8,128)(2,1)}, u32[]{:S(2)}) copy-start(bf16[144,512]{1,0:T(8,128)(2,1)} %get-tuple-element.45.refs_1_) | copy-start | bytes 442372
  32.9 16.4 %collective-permute-start.5 = (bf16[136,512]{1,0:T(8,128)(2,1)S(1)}, bf16[136,512]{1,0:T(8,128)(2,1)S(1)}, u32[]{:S(2)}, u32[]{:S(2)}) collective-permute-start(bf16[136,512]{1,0:T(8,128)(2,1)S(1)} %get-tuple-element.40), channel_id=1, source_target_pairs={{0,3},{1,0},{2,1},{3,2},{4,7},{5,4},{6,5},{7,6},{8,11},{9,8},{10,9... | collective-permute-start | bytes 417800 | tf_op jit(solution)/shard_map/ppermute | solution.py:434
  37.6 13.3 %collective-permute-start = (bf16[136,512]{1,0:T(8,128)(2,1)S(1)}, bf16[136,512]{1,0:T(8,128)(2,1)S(1)}, u32[]{:S(2)}, u32[]{:S(2)}) collective-permute-start(bf16[136,512]{1,0:T(8,128)(2,1)S(1)} %get-tuple-element.34), channel_id=1, source_target_pairs={{0,1},{1,2},{2,3},{3,0},{4,5},{5,6},{6,7},{7,4},{8,9},{9,10},{10,1... | collective-permute-start | bytes 417800 | tf_op jit(solution)/shard_map/ppermute | solution.py:434
  41.3 15.2 %collective-permute-start.1 = (bf16[136,512]{1,0:T(8,128)(2,1)S(1)}, bf16[136,512]{1,0:T(8,128)(2,1)S(1)}, u32[]{:S(2)}, u32[]{:S(2)}) collective-permute-start(bf16[136,512]{1,0:T(8,128)(2,1)S(1)} %get-tuple-element.35), channel_id=1, source_target_pairs={{0,2},{1,3},{2,0},{3,1},{4,6},{5,7},{6,4},{7,5},{8,10},{9,11},{10,... | collective-permute-start | bytes 417800 | tf_op jit(solution)/shard_map/ppermute | solution.py:434
  44.8 11.7 %collective-permute-start.2 = (bf16[136,512]{1,0:T(8,128)(2,1)S(1)}, bf16[136,512]{1,0:T(8,128)(2,1)S(1)}, u32[]{:S(2)}, u32[]{:S(2)}) collective-permute-start(bf16[136,512]{1,0:T(8,128)(2,1)S(1)} %get-tuple-element.36), channel_id=1, source_target_pairs={{0,3},{1,0},{2,1},{3,2},{4,7},{5,4},{6,5},{7,6},{8,11},{9,8},{10,9... | collective-permute-start | bytes 417800 | tf_op jit(solution)/shard_map/ppermute | solution.py:434
  58.1 1.2 %collective-permute-start.12 = (f32[64,128]{1,0:T(8,128)S(1)}, f32[64,128]{1,0:T(8,128)S(1)}, u32[]{:S(2)}, u32[]{:S(2)}) collective-permute-start(f32[64,128]{1,0:T(8,128)S(1)} %get-tuple-element.57), channel_id=1, source_target_pairs={{0,4},{4,0},{8,12},{12,8},{16,20},{20,16},{24,28},{28,24},{1,5},{5... | collective-permute-start | bytes 98312 | tf_op jit(solution)/shard_map/ppermute | solution.py:402
  59.3 3.9 %collective-permute-start.13 = (f32[64,128]{1,0:T(8,128)S(1)}, f32[64,128]{1,0:T(8,128)S(1)}, u32[]{:S(2)}, u32[]{:S(2)}) collective-permute-start(f32[64,128]{1,0:T(8,128)S(1)} %add.6), channel_id=1, source_target_pairs={{0,8},{4,12},{8,0},{12,4},{16,24},{20,28},{24,16},{28,20},{1,9},{5... | collective-permute-start | bytes 98312 | tf_op jit(solution)/shard_map/ppermute | solution.py:402
  63.2 4.0 %copy-start.5 = (f32[64,128]{1,0:T(8,128)}, f32[64,128]{1,0:T(8,128)S(1)}, u32[]{:S(2)}) copy-start(f32[64,128]{1,0:T(8,128)S(1)} %add.7.refs_0_) | copy-start | bytes 98308
  63.2 4.0 %collective-permute-start.14 = (f32[64,128]{1,0:T(8,128)S(1)}, f32[64,128]{1,0:T(8,128)S(1)}, u32[]{:S(2)}, u32[]{:S(2)}) collective-permute-start(f32[64,128]{1,0:T(8,128)S(1)} %add.7.refs_0_), channel_id=1, source_target_pairs={{0,16},{4,20},{8,24},{12,28},{16,0},{20,4},{24,8},{28,12},{1,17},{... | collective-permute-start | bytes 98312 | tf_op jit(solution)/shard_map/ppermute | solution.py:402
  67.2 0.6 copy-start.6

commit v11 on v10

--- a/solution.py
+++ b/solution.py
@@ -51,9 +51,9 @@
     return 1.0 - 2.0 * s * s
 
 
-def build_rows(n, owned, slots, span, blocks, me, starts_ref, freqs_ref, a_ref):
+def build_rows(n, owned, slots, blocks, me, lo, sample, known, starts_ref, freqs_ref, a_ref):
     group = owned * 2
-    lo = first_block(me, span)
+    width = a_ref.shape[2]
     starts = [starts_ref[jnp.minimum(lo + s, blocks - 1)] for s in range(slots)]
 
     def by_slot(shape, axis):
@@ -71,7 +71,6 @@
     step = freq * (1.0 / NFFT)
     quarter = (rid % 2).astype(jnp.float32) * 0.25
 
-    sample = lax.broadcasted_iota(jnp.int32, (1, span), 1) + me * span
     turns = sample.astype(jnp.float32) * step
     turns = turns - jnp.floor(turns) + quarter
     cos_t, sin_t = cosine_of(turns), cosine_of(turns - 0.25)
@@ -83,7 +82,7 @@
     ni = sample - by_slot((16, 1), 0)
     nf = ni.astype(jnp.float32)
     w = half_turn_sine(jnp.minimum(nf, NFFT - nf) * (1.0 / NFFT))
-    w = jnp.where((ni >= 0) & (ni < NFFT) & (slot + lo < blocks), w * w * SCALE, 0.0)
+    w = jnp.where((ni >= 0) & (ni < NFFT) & (slot + lo < blocks) & known, w * w * SCALE, 0.0)
 
     pieces = [[] for _ in range(n)]
     for s in range(slots):
@@ -93,8 +92,27 @@
     padding = a_ref.shape[1] - slots * group
     for k in range(n):
         if padding:
-            pieces[k].append(jnp.zeros((padding, span), jnp.float32))
+            pieces[k].append(jnp.zeros((padding, width), jnp.float32))
         a_ref[k] = jnp.concatenate(pieces[k], axis=0).astype(jnp.bfloat16)
+
+
+LINE_LO = [0, 6, 15, 23]
+LINE_HI = [8, 16, 25, 31]
+SHORT = 10
+EDGE = 16
+
+
+def skipped(shard):
+    return jnp.where(shard == 1, 1, 0)
+
+
+def fits_line(n, span, blocks, owned):
+    if n != 4 or owned != 2 or blocks != 32 or span < 1072:
+        return False
+    lo = [max((s * span - (NFFT + JIT - 1) + HOP) // HOP, 0) for s in range(n)]
+    hi = [min((span * (s + 1) - 1) // HOP, blocks - 1) for s in range(n)]
+    reach = max(HOP * LINE_LO[1] + JIT - 1 + NFFT - span, 3 * span - HOP * LINE_HI[2])
+    return lo == LINE_LO and hi == LINE_HI and reach <= EDGE
 
 
 def spread_column(row, span, out_ref):
@@ -107,35 +125,75 @@
         out_ref[at:at + width, :] = turned[:width]
 
 
-def dft_body(n, owned, slots, span, blocks, offset, mode, *refs):
+def dft_body(n, owned, slots, span, blocks, offset, mode, line, *refs):
     *refs, rot_ref = refs
     step = pl.program_id(0)
     if mode == "use":
         mask_ref, vel_ref, a_ref, cos_ref, sin_ref = refs[:5]
-        outs = refs[5:]
+        if line:
+            near_ref, edge_ref = refs[5:7]
+            slots = SHORT
+        outs = refs[-n:]
     else:
         pos_ref, starts_ref, freqs_ref, angle_ref, mask_ref, vel_ref = refs[:6]
         outs = refs[6:6 + n]
         a_ref, cos_ref, sin_ref = refs[6 + n:9 + n]
+        if mode == "build" and line:
+            short_ref, cos_ref, sin_ref, near_ref, a_ref = refs[6 + n:]
     if mode == "lead":
-        vel_hbm, (held_ref, sem) = vel_ref, refs[9 + n:]
+        if line:
+            edge_mask_ref, edge_out_ref = refs[6], refs[7 + n]
+            outs = refs[7:7 + n]
+            a_ref, cos_ref, sin_ref, held_ref, sem, edge_ref, edge_sem = refs[8 + n:]
+        else:
+            held_ref, sem = refs[9 + n:]
+        vel_hbm = vel_ref
 
         def load(i):
             columns = pl.ds(pl.multiple_of(offset + i * TILE, TILE), TILE)
             return pltpu.make_async_copy(vel_hbm.at[:, :, columns], held_ref.at[i], sem.at[i])
+
+        if line:
+            begin = pl.multiple_of(jnp.where(pos_ref[0] == 2, span - EDGE, 0), EDGE)
+            count = edge_ref.shape[2]
+            half = vel_hbm.shape[2] - count
+
+            def load_edge():
+                return pltpu.make_async_copy(vel_hbm.at[:, pl.ds(begin, EDGE), pl.ds(half, count)], edge_ref, edge_sem)
 
         @pl.when(step == 0)
         def _():
             for i in range(held_ref.shape[0]):
                 load(i).start()
+            if line:
+                load_edge().start()
 
     if mode != "use":
 
         @pl.when(step == 0)
         def _():
-            build_rows(n, owned, slots, span, blocks, pos_ref[0], starts_ref, freqs_ref, a_ref)
+            me = pos_ref[0]
+            lo = first_block(me, span)
+            sample = lax.broadcasted_iota(jnp.int32, (1, span), 1) + me * span
+            build_rows(n, owned, slots, blocks, me, lo, sample, True, starts_ref, freqs_ref, a_ref)
+            if line and mode == "build":
+                lo = lo + skipped(me)
+                build_rows(n, owned, SHORT, blocks, me, lo, sample, True, starts_ref, freqs_ref, short_ref)
+                edge = lax.broadcasted_iota(jnp.int32, (1, EDGE), 1) + jnp.where(me == 3, me * span - EDGE, span)
+                left = jnp.where(me == 0, LINE_LO[1], LINE_HI[2])
+                mine = (lax.broadcasted_iota(jnp.int32, (16, 1), 0) + lo == left) & ((me == 0) | (me == 3))
+                build_rows(n, owned, SHORT, blocks, me, lo, edge, mine, starts_ref, freqs_ref, near_ref)
             spread_column(jnp.cos(angle_ref[...].reshape(1, span)), span, cos_ref)
             spread_column(jnp.sin(angle_ref[...].reshape(1, span)), span, sin_ref)
+            if line and mode == "lead":
+                load_edge().wait()
+                cosine = jnp.concatenate([cos_ref[pl.ds(begin, EDGE), :]] * (count // LANES), axis=1)
+                sine = jnp.concatenate([sin_ref[pl.ds(begin, EDGE), :]] * (count // LANES), axis=1)
+                x, y = edge_ref[0].astype(jnp.float32), edge_ref[1].astype(jnp.float32)
+                there = edge_mask_ref[...] == 1
+                edge_out_ref[:EDGE, :] = jnp.where(there, cosine * x - sine * y, x).astype(jnp.bfloat16)
+                edge_out_ref[EDGE:2 * EDGE, :] = jnp.where(there, sine * x + cosine * y, y).astype(jnp.bfloat16)
+                edge_out_ref[2 * EDGE:, :] = edge_ref[2]
 
     if mode == "lead":
         load(step).wait()
@@ -158,6 +216,11 @@
     for c in range(COMPS):
         samples = rot_ref[c] if c < 2 else vel_ref[2]
         sums = jnp.dot(a, samples, preferred_element_type=jnp.float32)
+        if mode == "use" and line:
+            sums += jnp.dot(
+                near_ref[...].reshape(n * rows, EDGE), edge_ref[c * EDGE:(c + 1) * EDGE, :],
+                preferred_element_type=jnp.float32,
+            )
         outs[0][c * rows:(c + 1) * rows, :] = sums[:rows].astype(jnp.bfloat16)
         if main:
             for k in range(1, n):
@@ -172,8 +235,10 @@
             outs[k][COMPS * main:, :] = jnp.concatenate(parts, axis=0).astype(jnp.bfloat16)
 
 
-def dft_call(n, owned, slots, blocks, mode, offset, points, position, starts, freqs, angles, mask, velocity, shared):
-    span = velocity.shape[1]
+def dft_call(n, owned, slots, blocks, mode, offset, points, position, starts, freqs, angles, mask, velocity, shared, line=False, edge=None):
+    span, all_points = velocity.shape[1:]
+    if line and mode == "use":
+        slots = SHORT
     rows = -(-slots * owned * 2 // 16) * 16
     heights = [COMPS * rows] + [layout(slots * owned * 2)[2]] * (n - 1)
     shift = offset // TILE
@@ -200,14 +265,30 @@
         scratch += [pltpu.VMEM(t.shape, t.dtype) for t in shared_types]
         scratch.append(pltpu.VMEM((points // TILE, COMPS, span, TILE), jnp.bfloat16))
         scratch.append(pltpu.SemaphoreType.DMA((points // TILE,)))
+        if line:
+            half = all_points // 2
+            args += (mask,)
+            in_specs.append(pl.BlockSpec((1, half), lambda i: (0, 1)))
+            out_types = out_types + [jax.ShapeDtypeStruct((COMPS * EDGE, half), jnp.bfloat16)]
+            out_specs = out_specs + [whole((COMPS * EDGE, half))]
+            scratch += [pltpu.VMEM((COMPS, EDGE, half), jnp.bfloat16), pltpu.SemaphoreType.DMA]
     elif mode == "build":
+        if line:
+            shared_types.append(jax.ShapeDtypeStruct((n, rows, EDGE), jnp.bfloat16))
+            shared_specs.append(whole((n, rows, EDGE)))
+            scratch.append(pltpu.VMEM((n, rows, span), jnp.bfloat16))
         out_types = out_types + shared_types
         out_specs = out_specs + shared_specs
     else:
         args = (mask, velocity) + tuple(shared)
         in_specs = data_specs + shared_specs
+        if line:
+            first_edge = (all_points - edge.shape[1]) // TILE
+            args += (edge,)
+            in_specs.append(whole(shared[3].shape))
+            in_specs.append(pl.BlockSpec((edge.shape[0], TILE), lambda i: (0, i + shift - first_edge)))
     out = pl.pallas_call(
-        functools.partial(dft_body, n, owned, slots, span, blocks, offset, mode),
+        functools.partial(dft_body, n, owned, slots, span, blocks, offset, mode, line),
         grid=(points // TILE,),
         out_shape=out_types,
         in_specs=in_specs,
@@ -221,7 +302,7 @@
         ),
         name="rotate_dft",
     )(*args)
-    return out[:n], out[n:] if mode == "build" else shared
+    return out[:n], out[n:] if mode != "use" else shared
 
 
 def stack_width(n, rows):
@@ -229,7 +310,7 @@
     return -(-rows // 16) * 16 + (n - 1) * (height - (COMPS - 1) * main)
 
 
-def selection(n, owned, slots, span, blocks, me, sel_ref):
+def selection(n, owned, slots, span, blocks, short, me, sel_ref):
     group = owned * 2
     main, tail, height = layout(slots * group)
     rest = height - COMPS * main
@@ -237,13 +318,14 @@
     out = lax.broadcasted_iota(jnp.int32, shape, 0)
     col = lax.broadcasted_iota(jnp.int32, shape, 1)
     at = -(-slots * group // 16) * 16
-    lo = jnp.broadcast_to(first_block(me, span), shape)
+    begin = lambda shard: first_block(shard, span) + (skipped(shard) if short else 0)
+    lo = jnp.broadcast_to(begin(me), shape)
     row = jnp.where(col < slots * group, col, -1)
     comp = jnp.full(shape, -1, jnp.int32)
     for size, base in ((main, 0), (rest, main)):
         for k in range(1, n):
             here = (col >= at) & (col < at + size)
-            lo = jnp.where(here, first_block(lax.rem(me + n - k, n), span), lo)
+            lo = jnp.where(here, begin(lax.rem(me + n - k, n)), lo)
             if base == 0:
                 row = jnp.where(here, col - at, row)
             elif tail:
@@ -256,14 +338,17 @@
         sel_ref[c] = jnp.where(same & ((comp < 0) | (comp == c)), 1.0, 0.0).astype(jnp.bfloat16)
 
 
-def assemble_body(n, owned, slots, span, blocks, total, has_sum, last, *refs):
+def assemble_body(n, owned, slots, span, blocks, total, short, has_sum, has_sel, last, *refs):
     pos_ref = refs[0]
     parts = refs[1:1 + n]
     *rest, acc_ref = refs[1 + n:]
     if has_sum:
-        sum_in, sel_ref, _, spectra_ref, gram_ref = rest
+        sum_in, *rest = rest
+    if has_sel:
+        sel_ref, *rest = rest
     else:
-        spectra_ref, gram_ref, sel_ref = rest
+        *rest, sel_ref = rest
+    spectra_ref, gram_ref = rest[-2:]
     step = pl.program_id(0)
     main, tail, height = layout(slots * owned * 2)
     rows = parts[0].shape[0] // COMPS
@@ -271,8 +356,8 @@
 
     @pl.when(step == 0)
     def _():
-        if not has_sum:
-            selection(n, owned, slots, span, blocks, pos_ref[0], sel_ref)
+        if not has_sel:
+            selection(n, owned, slots, span, blocks, short, pos_ref[0], sel_ref)
         acc_ref[...] = sum_in[...] if has_sum else jnp.zeros_like(acc_ref)
 
     for c in range(COMPS):
@@ -307,11 +392,12 @@
             )
 
 
-def assemble_call(n, owned, slots, span, blocks, total, offset, points, all_points, position, parts, spectra, gram, sel, last):
+def assemble_call(n, owned, slots, span, blocks, total, offset, points, all_points, position, parts, spectra, gram, sel, last, short):
     tile = min(points, 512)
     shift = offset // tile
     order = 2 * blocks
     has_sum = gram is not None
+    has_sel = sel is not None
     whole = lambda shape: pl.BlockSpec(shape, lambda i: (0,) * len(shape))
     acc_shape = (2 * owned * order, 2 * owned * order)
     gram_shape = (order, owned * order) if last else acc_shape
@@ -329,14 +415,20 @@
     ]
     aliases = {}
     if has_sum:
-        args += [gram, sel, spectra]
-        in_specs += [whole(acc_shape), whole(sel_shape), pl.BlockSpec(memory_space=pl.ANY)]
+        args.append(gram)
+        in_specs.append(whole(acc_shape))
+    if has_sel:
+        args.append(sel)
+        in_specs.append(whole(sel_shape))
+    if has_sum:
+        args.append(spectra)
+        in_specs.append(pl.BlockSpec(memory_space=pl.ANY))
         aliases = {len(args) - 1: 0}
-    else:
+    if not has_sel:
         out_shape.append(jax.ShapeDtypeStruct(sel_shape, jnp.bfloat16))
         out_specs.append(whole(sel_shape))
     out = pl.pallas_call(
-        functools.partial(assemble_body, n, owned, slots, span, blocks, total, has_sum, last),
+        functools.partial(assemble_body, n, owned, slots, span, blocks, total, short, has_sum, has_sel, last),
         grid=(points // tile,),
         out_shape=out_shape,
         in_specs=in_specs,
@@ -351,7 +443,7 @@
         ),
         name="assemble",
     )(*args)
-    return list(out[:2]) + [sel if has_sum else out[2]]
+    return list(out[:2]) + [sel if has_sel else out[2]]
 
 
 def factor_body(owned, order, count, *refs):
@@ -424,12 +516,16 @@
     angles = rotor_angle
 
     pieces = []
-    shared = None
+    shared, edge = None, None
+    line = fits_line(n, span, blocks, owned)
+    half = points // 2
     for i, (at, count) in enumerate(chunks_of(points)):
         sums, shared = dft_call(
             n, owned, slots, blocks, ("lead", "build")[i] if i < 2 else "use", at, count,
-            position, block_starts, frequencies, angles, mask, samples, shared,
+            position, block_starts, frequencies, angles, mask, samples, shared, line, edge,
         )
+        if line and i == 0:
+            edge = lax.ppermute(shared[0], "tm", [(1, 0), (2, 3)])
         moved = [sums[0]] + [
             lax.ppermute(sums[k], "tm", [(j, (j + k) % n) for j in range(n)]) for k in range(1, n)
         ]
@@ -438,9 +534,12 @@
     spectra, gram, sel = None, None, None
     total = COMPS * points * groups
     for at, count, moved in pieces:
-        last = at + count == points
+        short = line and at >= half
+        if short and at == half:
+            sel = None
         spectra, gram, sel = assemble_call(
-            n, owned, slots, span, blocks, total, at, count, points, position, moved, spectra, gram, sel, last
+            n, owned, SHORT if short else slots, span, blocks, total, at, count, points, position, moved,
+            spectra, gram, sel, at + count == points, short,
         )
     factors = factor_call(owned, order, sum_over_space(gram, groups))
     return spectra.transpose(0, 1, 3, 2, 4), factors

time: 71.4 us -> 69 us (0.966)
  starting transfers between devices: 32.5 us -> 27.9 us
  waiting for transfers between devices: 12 us -> 14.3 us
    ppermute x12, starting transfers between devices: 29.4 us -> 23.4 us  [per_device(): lax.ppermute(sums[k], 'tm', [(j, (j + k) % n) for j in range(n)])]
    ppermute x12, waiting for transfers between devices: 6 us -> 8.49 us  [per_device(): lax.ppermute(sums[k], 'tm', [(j, (j + k) % n) for j in range(n)])]
    ppermute x0 -> x1, starting transfers between devices: none -> 1.28 us  [per_device(): edge = lax.ppermute(shared[0], 'tm', [(1, 0), (2, 3)])]
  transfers between devices with their start and end apart: 15 -> 16, of which waited for: 5 -> 6; matrix products, arithmetic and copies ran while one was open for 0% -> 0% of each run, Pallas kernels for 22% -> 23%
where the time goes in v11:
time: 69 us; the launch traced here: 68.7 us
  starting transfers between devices  27.9 us (40%)
  Pallas kernels  25.1 us (36%)
  waiting for transfers between devices  14.3 us (21%)
  between operations  0.74 us (1%)
    ppermute x12, starting transfers between devices, per_device(): lax.ppermute(sums[k], 'tm', [(j, (j + k) % n) for j in range(n)])  23.4 us
    pallas_call x4, Pallas kernels, dft_call(): pl.pallas_call(functools.partial(dft_body, n, owned, slots, span, blocks,...  15.8 us
    ppermute x12, waiting for transfers between devices, per_device(): lax.ppermute(sums[k], 'tm', [(j, (j + k) % n) for j in range(n)])  8.49 us
    pallas_call x4, Pallas kernels, assemble_call(): pl.pallas_call(functools.partial(assemble_body, n, owned, slots, span, bl...  6.37 us
    ppermute x3, waiting for transfers between devices, sum_over_space(): lax.ppermute(x, 'space', [(i, i ^ k) for i in range(groups)])  5.84 us
    ppermute x3, starting transfers between devices, sum_over_space(): lax.ppermute(x, 'space', [(i, i ^ k) for i in range(groups)])  3.27 us
    pallas_call x1, Pallas kernels, factor_call(): pl.pallas_call(functools.partial(factor_body, owned, order, len(parts)),...  2.9 us
  transfers between devices with their start and end apart: 16, of which 6 were waited for; matrix products, arithmetic and copies ran while one was open for 0% of the time, Pallas kernels for 23%

profile of v11, /device:TPU:0, one launch (start us, length us, event | category | flops | bytes accessed | tf_op | source)
XLA Modules:
  0.0 68.7 jit_solution(8157146805123146967)
XLA Ops:
  0.7 5.1 %rotate_dft.5 = (bf16[144,512]{1,0:T(8,128)(2,1)}, bf16[136,512]{1,0:T(8,128)(2,1)}, bf16[136,512]{1,0:T(8,128)(2,1)}, bf16[136,512]{1,0:T(8,128)(2,1)}, bf16[48,1024]{1,0:T(8,128)(2,1)}) custom-call(s32[1]{0:T(128)} %bitcast.refs_0_, s32[32]{0:T(128)} %refs_1_.3, s32[8]{0:T(128)} %refs_2_.3, f32[1072]{0:T(1024)} %refs_3_.3, s32[1,2048]{1,0:T(1,128)} %bitcast.4, ...), custom_call_target="tpu_custom_call" | custom-call | flops 632291328 | bytes 3293184 | tf_op jit(solution)/shard_map/rotate_dft/pallas_call | solution.py:290
  5.8 3.1 %collective-permute-start.10 = (bf16[136,512]{1,0:T(8,128)(2,1)}, bf16[136,512]{1,0:T(8,128)(2,1)S(1)}, u32[]{:S(2)}, u32[]{:S(2)}) collective-permute-start(bf16[136,512]{1,0:T(8,128)(2,1)} %get-tuple-element.51), channel_id=1, source_target_pairs={{0,1},{1,2},{2,3},{3,0},{4,5},{5,6},{6,7},{7,4},{8,9},{9,10},{10,1... | collective-permute-start | bytes 417800 | tf_op jit(solution)/shard_map/ppermute | solution.py:530
  8.9 1.3 %collective-permute-start = (bf16[48,1024]{1,0:T(8,128)(2,1)}, bf16[48,1024]{1,0:T(8,128)(2,1)S(1)}, u32[]{:S(2)}, u32[]{:S(2)}) collective-permute-start(bf16[48,1024]{1,0:T(8,128)(2,1)} %get-tuple-element.37), channel_id=1, source_target_pairs={{1,0},{2,3},{5,4},{6,7},{9,8},{10,11},{13,12},{14,15},{17,16},{18,... | collective-permute-start | bytes 294920 | tf_op jit(solution)/shard_map/ppermute | solution.py:528
  10.2 3.3 %collective-permute-start.11 = (bf16[136,512]{1,0:T(8,128)(2,1)}, bf16[136,512]{1,0:T(8,128)(2,1)S(1)}, u32[]{:S(2)}, u32[]{:S(2)}) collective-permute-start(bf16[136,512]{1,0:T(8,128)(2,1)} %get-tuple-element.52), channel_id=1, source_target_pairs={{0,2},{1,3},{2,0},{3,1},{4,6},{5,7},{6,4},{7,5},{8,10},{9,11},{10,... | collective-permute-start | bytes 417800 | tf_op jit(solution)/shard_map/ppermute | solution.py:530
  13.5 1.8 %collective-permute-start.12 = (bf16[136,512]{1,0:T(8,128)(2,1)}, bf16[136,512]{1,0:T(8,128)(2,1)S(1)}, u32[]{:S(2)}, u32[]{:S(2)}) collective-permute-start(bf16[136,512]{1,0:T(8,128)(2,1)} %get-tuple-element.53), channel_id=1, source_target_pairs={{0,3},{1,0},{2,1},{3,2},{4,7},{5,4},{6,5},{7,6},{8,11},{9,8},{10,9... | collective-permute-start | bytes 417800 | tf_op jit(solution)/shard_map/ppermute | solution.py:530
  15.3 4.4 %rotate_dft.4 = (bf16[144,512]{1,0:T(8,128)(2,1)S(1)}, bf16[136,512]{1,0:T(8,128)(2,1)S(1)}, bf16[136,512]{1,0:T(8,128)(2,1)S(1)}, bf16[136,512]{1,0:T(8,128)(2,...) custom-call(s32[1]{0:T(128)} %bitcast.refs_0_, ...), custom_call_target="tpu_custom_call" | custom-call | flops 632291328 | bytes 3293184 | tf_op jit(solution)/shard_map/rotate_dft/pallas_call | solution.py:290
  19.7 0.3 collective-permute-start.7
  20.0 0.3 collective-permute-start.8
  20.3 3.3 %collective-permute-start.9 = (bf16[136,512]{1,0:T(8,128)(2,1)S(1)}, bf16[136,512]{1,0:T(8,128)(2,1)S(1)}, u32[]{:S(2)}, u32[]{:S(2)}) collective-permute-start(bf16[136,512]{1,0:T(8,128)(2,1)S(1)} %get-tuple-element.49), channel_id=1, source_target_pairs={{0,3},{1,0},{2,1},{3,2},{4,7},{5,4},{6,5},{7,6},{8,11},{9,8},{10,9... | collective-permute-start | bytes 417800 | tf_op jit(solution)/shard_map/ppermute | solution.py:530
  23.6 3.2 %rotate_dft.7 = (bf16[144,512]{1,0:T(8,128)(2,1)S(1)}, bf16[120,512]{1,0:T(8,128)(2,1)S(1)}, bf16[120,512]{1,0:T(8,128)(2,1)S(1)}, bf16[120,512]{1,0:T(8,128)(2,1)S(1)}) custom-call(s32[1,2048]{1,0:T(1,128)S(1)} %bitcast.7, bf16[3,1072,2048]{2,1,0:T(8,128)(2,1)} %bitcast.11, bf16[4,48,1072]{2,1,0:T(8,128)(2,1)S(1)} %get-tuple-element.33.refs_2_, ...), custom_call_target="tpu_custom_call" | custom-call | flops 632291328 | bytes 3293184 | tf_op jit(solution)/shard_map/rotate_dft/pallas_call | solution.py:290
  26.8 0.0 collective-permute-done.11.refs_3_
  26.8 0.6 collective-permute-start.4
  27.3 1.5 %collective-permute-start.5 = (bf16[120,512]{1,0:T(8,128)(2,1)S(1)}, bf16[120,512]{1,0:T(8,128)(2,1)S(1)}, u32[]{:S(2)}, u32[]{:S(2)}) collective-permute-start(bf16[120,512]{1,0:T(8,128)(2,1)S(1)} %get-tuple-element.44), channel_id=1, source_target_pairs={{0,2},{1,3},{2,0},{3,1},{4,6},{5,7},{6,4},{7,5},{8,10},{9,11},{10,... | collective-permute-start | bytes 368648 | tf_op jit(solution)/shard_map/ppermute | solution.py:530
  28.9 3.3 %collective-permute-start.6 = (bf16[120,512]{1,0:T(8,128)(2,1)S(1)}, bf16[120,512]{1,0:T(8,128)(2,1)S(1)}, u32[]{:S(2)}, u32[]{:S(2)}) collective-permute-start(bf16[120,512]{1,0:T(8,128)(2,1)S(1)} %get-tuple-element.45), channel_id=1, source_target_pairs={{0,3},{1,0},{2,1},{3,2},{4,7},{5,4},{6,5},{7,6},{8,11},{9,8},{10,9... | collective-permute-start | bytes 368648 | tf_op jit(solution)/shard_map/ppermute | solution.py:530
  32.2 3.2 %rotate_dft.6 = (bf16[144,512]{1,0:T(8,128)(2,1)S(1)}, bf16[120,512]{1,0:T(8,128)(2,1)S(1)}, bf16[120,512]{1,0:T(8,128)(2,1)S(1)}, bf16[120,512]{1,0:T(8,128)(2,1)S(1)}) custom-call(s32[1,2048]{1,0:T(1,128)S(1)} %bitcast.8, bf16[3,1072,2048]{2,1,0:T(8,128)(2,1)} %bitcast.12, bf16[4,48,1072]{2,1,0:T(8,128)(2,1)S(1)} %get-tuple-element.33.refs_2_, ...), custom_call_target="tpu_custom_call" | custom-call | flops 632291328 | bytes 3293184 | tf_op jit(solution)/shard_map/rotate_dft/pallas_call | solution.py:290
  35.3 3.1 %collective-permute-done.8.refs_3_ = bf16[136,512]{1,0:T(8,128)(2,1)S(1)} collective-permute-done((bf16[136,512]{1,0:T(8,128)(2,1)S(1)}, bf16[136,512]{1,0:T(8,128)(2,1)S(1)}, u32[]{:S(2)}, u32[]{:S(2)}) %collective-permute-start.8) | collective-permute-done | bytes 139296 | tf_op jit(solution)/shard_map/ppermute | solution.py:530
  38.4 2.0 %collective-permute-start.1 = (bf16[120,512]{1,0:T(8,128)(2,1)S(1)}, bf16[120,512]{1,0:T(8,128)(2,1)S(1)}, u32[]{:S(2)}, u32[]{:S(2)}) collective-permute-start(bf16[120,512]{1,0:T(8,128)(2,1)S(1)} %get-tuple-element.39), channel_id=1, source_target_pairs={{0,1},{1,2},{2,3},{3,0},{4,5},{5,6},{6,7},{7,4},{8,9},{9,10},{10,1... | collective-permute-start | bytes 368648 | tf_op jit(solution)/shard_map/ppermute | solution.py:530
  40.4 3.4 %collective-permute-start.2 = (bf16[120,512]{1,0:T(8,128)(2,1)S(1)}, bf16[120,512]{1,0:T(8,128)(2,1)S(1)}, u32[]{:S(2)}, u32[]{:S(2)}) collective-permute-start(bf16[120,512]{1,0:T(8,128)(2,1)S(1)} %get-tuple-element.40), channel_id=1, source_target_pairs={{0,2},{1,3},{2,0},{3,1},{4,6},{5,7},{6,4},{7,5},{8,10},{9,11},{10,... | collective-permute-start | bytes 368648 | tf_op jit(solution)/shard_map/ppermute | solution.py:530
  43.8 0.5 collective-permute-start.3
  44.3 1.7 %assemble.4 = (f32[2,2,3,32,2048]{4,3,2,1,0:T(8,128)}, f32[256,256]{1,0:T(8,128)S(1)}, bf16[3,128,264]{2,1,0:T(8,128)(2,1)S(1)}) custom-call(s32[1]{0:T(128)} %bitcast.refs_0_, bf16[144,512]{1,0:T(8,128)(2,1)S(1)} %copy-done.4, bf16[136,512]{1,0:T(8,128)(2,1)S(1)} %collective-permute-done.10.refs_2_, bf16[136,512]{1,0:T(8,128)(2,1)S(1)} %collective-permute-done.11.refs_3_, ...), custom_call_target="tpu_custom_call" | custom-call | flops 226492416 | bytes 786432 | tf_op jit(solution)/shard_map/assemble/pallas_call | solution.py:430
  46.0 1.6 %assemble.5 = (f32[2,2,3,32,2048]{4,3,2,1,0:T(8,128)}, f32[256,256]{1,0:T(8,128)S(1)}) custom-call(s32[1]{0:T(128)} %bitcast.refs_0_, bf16[144,512]{1,0:T(8,128)(2,1)S(1)} %get-tuple-element.46.refs_1_, bf16[136,512]{1,0:T(8,128)(2,1)S(1)} %collective-permute-done.7.refs_2_, ...), custom_call_target="tpu_custom_call", output_to_operand_aliasing={{0}: (7, {})} | custom-call | flops 226492416 | bytes 786432 | tf_op jit(solution)/shard_map/assemble/pallas_call | solution.py:430
  47.6 0.9 %collective-permute-done.5.refs_3_ = bf16[120,512]{1,0:T(8,128)(2,1)S(1)} collective-permute-done((bf16[120,512]{1,0:T(8,128)(2,1)S(1)}, bf16[120,512]{1,0:T(8,128)(2,1)S(1)}, u32[]{:S(2)}, u32[]{:S(2)}) %collective-permute-start.5) | collective-permute-done | bytes 122912 | tf_op jit(solution)/shard_map/ppermute | solution.py:530
  48.5 1.5 %assemble.6 = (f32[2,2,3,32,2048]{4,3,2,1,0:T(8,128)}, f32[256,256]{1,0:T(8,128)S(1)}, bf16[3,128,216]{2,1,0:T(8,128)(2,1)S(1)}) custom-call(s32[1]{0:T(128)} %bitcast.refs_0_, bf16[144,512]{1,0:T(8,128)(2,1)S(1)} %get-tuple-element.42.refs_1_, bf16[120,512]{1,0:T(8,128)(2,1)S(1)} %collective-permute-done.4.refs_2_, ...), custom_call_target="tpu_custom_call", output_to_operand_aliasing={{0}: (6, {})} | custom-call | flops 226492416 | bytes 786432 | tf_op jit(solution)/shard_map/assemble/pallas_call | solution.py:430
  50.1 4.5 %collective-permute-done.2.refs_3_ = bf16[120,512]{1,0:T(8,128)(2,1)S(1)} collective-permute-done((bf16[120,512]{1,0:T(8,128)(2,1)S(1)}, bf16[120,512]{1,0:T(8,128)(2,1)S(1)}, u32[]{:S(2)}, u32[]{:S(2)}) %collective-permute-start.2) | collective-permute-done | bytes 122912 | tf_op jit(solution)/shard_map/ppermute | solution.py:530
  54.6 1.5 %assemble.7 = (f32[2,2,3,32,2048]{4,3,2,1,0:T(8,128)}, f32[64,128]{1,0:T(8,128)S(1)}) custom-call(s32[1]{0:T(128)} %bitcast.refs_0_, bf16[144,512]{1,0:T(8,128)(2,1)S(1)} %get-tuple-element.38.refs_1_, bf16[120,512]{1,0:T(8,128)(2,1)S(1)} %collective-permute-done.1.refs_2_, ...), custom_call_target="tpu_custom_call", output_to_operand_aliasing={{0}: (7, {})} | custom-call | flops 226492416 | bytes 786432 | tf_op jit(solution)/shard_map/assemble/pallas_call | solution.py:430
  56.1 1.2 %collective-permute-done.13 = f32[64,128]{1,0:T(8,128)S(1)} collective-permute-done((f32[64,128]{1,0:T(8,128)S(1)}, f32[64,128]{1,0:T(8,128)S(1)}, u32[]{:S(2)}, u32[]{:S(2)}) %collective-permute-start.13) | collective-permute-done | bytes 32800 | tf_op jit(solution)/shard_map/ppermute | solution.py:494
  57.3 1.6 %collective-permute-start.14 = (f32[64,128]{1,0:T(8,128)S(1)}, f32[64,128]{1,0:T(8,128)S(1)}, u32[]{:S(2)}, u32[]{:S(2)}) collective-permute-start(f32[64,128]{1,0:T(8,128)S(1)} %add.6), channel_id=1, source_target_pairs={{0,8},{4,12},{8,0},{12,4},{16,24},{20,28},{24,16},{28,20},{1,9},{5... | collective-permute-start | bytes 98312 | tf_op jit(solution)/shard_map/ppermute | solution.py:494
  58.9 2.3 %collective-permute-done.14 = f32[64,128]{1,0:T(8,128)S(1)} collective-permute-done((f32[64,128]{1,0:T(8,128)S(1)}, f32[64,128]{1,0:T(8,128)S(1)}, u32[]{:S(2)}, u32[]{:S(2)}) %collective-permute-start.14) | collective-permute-done | bytes 32800 | tf_op jit(solution)/shard_map/ppermute | solution.py:494
  61.2 1.7 %collective-permute-start.15 = (f32[64,128]{1,0:T(8,128)S(1)}, f32[64,128]{1,0:T(8,128)S(1)}, u32[]{:S(2)}, u32[]{:S(2)}) collective-permute-start(f32[64,128]{1,0:T(8,128)S(1)} %add.7.refs_0_), channel_id=1, source_target_pairs={{0,16},{4,20},{8,24},{12,28},{16,0},{20,4},{24,8},{28,12},{1,17},{... | collective-permute-start | bytes 98312 | tf_op jit(solution)/shard_map/ppermute | solution.py:494
  62.9 2.3 %collective-permute-done.15.refs_1_ = f32[64,128]{1,0:T(8,128)S(1)} collective-permute-done((f32[64,128]{1,0:T(8,128)S(1)}, f32[64,128]{1,0:T(8,128)S(1)}, u32[]{:S(2)}, u32[]{:S(2)}) %collective-permute-start.15) | collective-permute-done | bytes 32800 | tf_op jit(solution)/shard_map/ppermute | solution.py:494
  65.2 0.6 copy-done.6
  65.8 2.9 %factor.1 = f32[2,64,64]{2,1,0:T(8,128)} custom-call(f32[64,128]{1,0:T(8,128)} %copy-done.5, f32[64,128]{1,0:T(8,128)} %copy-done.6), custom_call_target="tpu_custom_call" | custom-call | tf_op jit(solution)/shard_map/factor/pallas_call | solution.py:483
  (25 shorter events, 0.1 us)
Async XLA Ops:
  0.6 14.6 %copy-start = (s32[2048]{0:T(1024)S(1)}, s32[2048]{0:T(1024)}, u32[]{:S(2)}) copy-start(s32[2048]{0:T(1024)} %param.6) | copy-start | bytes 24580
  0.6 14.6 %copy-start.1 = (f32[1072]{0:T(1024)S(1)}, f32[1072]{0:T(1024)}, u32[]{:S(2)}) copy-start(f32[1072]{0:T(1024)} %refs_3_.3) | copy-start | bytes 12868
  0.7 14.6 %copy-start.2 = (s32[32]{0:T(128)S(1)}, s32[32]{0:T(128)}, u32[]{:S(2)}) copy-start(s32[32]{0:T(128)} %refs_1_.3) | copy-start | bytes 388
  0.7 14.6 %copy-start.3 = (s32[8]{0:T(128)S(1)}, s32[8]{0:T(128)}, u32[]{:S(2)}) copy-start(s32[8]{0:T(128)} %refs_2_.3) | copy-start | bytes 100
  5.8 14.5 %collective-permute-start.10 = (bf16[136,512]{1,0:T(8,128)(2,1)}, bf16[136,512]{1,0:T(8,128)(2,1)S(1)}, u32[]{:S(2)}, u32[]{:S(2)}) collective-permute-start(bf16[136,512]{1,0:T(8,128)(2,1)} %get-tuple-element.51), channel_id=1, source_target_pairs={{0,1},{1,2},{2,3},{3,0},{4,5},{5,6},{6,7},{7,4},{8,9},{9,10},{10,1... | collective-permute-start | bytes 417800 | tf_op jit(solution)/shard_map/ppermute | solution.py:530
  8.9 11.1 %collective-permute-start = (bf16[48,1024]{1,0:T(8,128)(2,1)}, bf16[48,1024]{1,0:T(8,128)(2,1)S(1)}, u32[]{:S(2)}, u32[]{:S(2)}) collective-permute-start(bf16[48,1024]{1,0:T(8,128)(2,1)} %get-tuple-element.37), channel_id=1, source_target_pairs={{1,0},{2,3},{5,4},{6,7},{9,8},{10,11},{13,12},{14,15},{17,16},{18,... | collective-permute-start | bytes 294920 | tf_op jit(solution)/shard_map/ppermute | solution.py:528
  10.2 16.6 %collective-permute-start.11 = (bf16[136,512]{1,0:T(8,128)(2,1)}, bf16[136,512]{1,0:T(8,128)(2,1)S(1)}, u32[]{:S(2)}, u32[]{:S(2)}) collective-permute-start(bf16[136,512]{1,0:T(8,128)(2,1)} %get-tuple-element.52), channel_id=1, source_target_pairs={{0,2},{1,3},{2,0},{3,1},{4,6},{5,7},{6,4},{7,5},{8,10},{9,11},{10,... | collective-permute-start | bytes 417800 | tf_op jit(solution)/shard_map/ppermute | solution.py:530
  13.5 13.9 %collective-permute-start.12 = (bf16[136,512]{1,0:T(8,128)(2,1)}, bf16[136,512]{1,0:T(8,128)(2,1)S(1)}, u32[]{:S(2)}, u32[]{:S(2)}) collective-permute-start(bf16[136,512]{1,0:T(8,128)(2,1)} %get-tuple-element.53), channel_id=1, source_target_pairs={{0,3},{1,0},{2,1},{3,2},{4,7},{5,4},{6,5},{7,6},{8,11},{9,8},{10,9... | collective-permute-start | bytes 417800 | tf_op jit(solution)/shard_map/ppermute | solution.py:530
  19.7 9.2 %collective-permute-start.7 = (bf16[136,512]{1,0:T(8,128)(2,1)S(1)}, bf16[136,512]{1,0:T(8,128)(2,1)S(1)}, u32[]{:S(2)}, u32[]{:S(2)}) collective-permute-start(bf16[136,512]{1,0:T(8,128)(2,1)S(1)} %get-tuple-element.47), channel_id=1, source_target_pairs={{0,1},{1,2},{2,3},{3,0},{4,5},{5,6},{6,7},{7,4},{8,9},{9,10},{10,1... | collective-permute-start | bytes 417800 | tf_op jit(solution)/shard_map/ppermute | solution.py:530
  20.0 18.4 %collective-permute-start.8 = (bf16[136,512]{1,0:T(8,128)(2,1)S(1)}, bf16[136,512]{1,0:T(8,128)(2,1)S(1)}, u32[]{:S(2)}, u32[]{:S(2)}) collective-permute-start(bf16[136,512]{1,0:T(8,128)(2,1)S(1)} %get-tuple-element.48), channel_id=1, source_target_pairs={{0,2},{1,3},{2,0},{3,1},{4,6},{5,7},{6,4},{7,5},{8,10},{9,11},{10,... | collective-permute-start | bytes 417800 | tf_op jit(solution)/shard_map/ppermute | solution.py:530
  20.3 20.1 %collective-permute-start.9 = (bf16[136,512]{1,0:T(8,128)(2,1)S(1)}, bf16[136,512]{1,0:T(8,128)(2,1)S(1)}, u32[]{:S(2)}, u32[]{:S(2)}) collective-permute-start(bf16[136,512]{1,0:T(8,128)(2,1)S(1)} %get-tuple-element.49), channel_id=1, source_target_pairs={{0,3},{1,0},{2,1},{3,2},{4,7},{5,4},{6,5},{7,6},{8,11},{9,8},{10,9... | collective-permute-start | bytes 417800 | tf_op jit(solution)/shard_map/ppermute | solution.py:530
  26.8 17.0 %collective-permute-start.4 = (bf16[120,512]{1,0:T(8,128)(2,1)S(1)}, bf16[120,512]{1,0:T(8,128)(2,1)S(1)}, u32[]{:S(2)}, u32[]{:S(2)}) collective-permute-start(bf16[120,512]{1,0:T(8,128)(2,1)S(1)} %get-tuple-element.43), channel_id=1, source_target_pairs={{0,1},{1,2},{2,3},{3,0},{4,5},{5,6},{6,7},{7,4},{8,9},{9,10},{10,1... | collective-permute-start | bytes 368648 | tf_op jit(solution)/shard_map/ppermute | solution.py:530
  27.3 21.2 %collective-permute-start.5 = (bf16[120,512]{1,0:T(8,128)(2,1)S(1)}, bf16[120,512]{1,0:T(8,128)(2,1)S(1)}, u32[]{:S(2)}, u32[]{:S(2)}) collective-permute-start(bf16[120,512]{1,0:T(8,128)(2,1)S(1)} %get-tuple-element.44), channel_id=1, source_target_pairs={{0,2},{1,3},{2,0},{3,1},{4,6},{5,7},{6,4},{7,5},{8,10},{9,11},{10,... | collective-permute-start | bytes 368648 | tf_op jit(solution)/shard_map/ppermute | solution.py:530
  28.9 15.4 %copy-start.4 = (bf16[144,512]{1,0:T(8,128)(2,1)S(1)}, bf16[144,512]{1,0:T(8,128)(2,1)}, u32[]{:S(2)}) copy-start(bf16[144,512]{1,0:T(8,128)(2,1)} %get-tuple-element.50.refs_1_) | copy-start | bytes 442372
  28.9 19.6 %collective-permute-start.6 = (bf16[120,512]{1,0:T(8,128)(2,1)S(1)}, bf16[120,512]{1,0:T(8,128)(2,1)S(1)}, u32[]{:S(2)}, u32[]{:S(2)}) collective-permute-start(bf16[120,512]{1,0:T(8,128)(2,1)S(1)} %get-tuple-element.45), channel_id=1, source_target_pairs={{0,3},{1,0},{2,1},{3,2},{4,7},{5,4},{6,5},{7,6},{8,11},{9,8},{10,9... | collective-permute-start | bytes 368648 | tf_op jit(solution)/shard_map/ppermute | solution.py:530
  38.4 11.6 %collective-permute-start.1 = (bf16[120,512]{1,0:T(8,128)(2,1)S(1)}, bf16[120,512]{1,0:T(8,128)(2,1)S(1)}, u32[]{:S(2)}, u32[]{:S(2)}) collective-permute-start(bf16[120,512]{1,0:T(8,128)(2,1)S(1)} %get-tuple-element.39), channel_id=1, source_target_pairs={{0,1},{1,2},{2,3},{3,0},{4,5},{5,6},{6,7},{7,4},{8,9},{9,10},{10,1... | collective-permute-start | bytes 368648 | tf_op jit(solution)/shard_map/ppermute | solution.py:530
  40.4 14.2 %collective-permute-start.2 = (bf16[120,512]{1,0:T(8,128)(2,1)S(1)}, bf16[120,512]{1,0:T(8,128)(2,1)S(1)}, u32[]{:S(2)}, u32[]{:S(2)}) collective-permute-start(bf16[120,512]{1,0:T(8,128)(2,1)S(1)} %get-tuple-element.40), channel_id=1, source_target_pairs={{0,2},{1,3},{2,0},{3,1},{4,6},{5,7},{6,4},{7,5},{8,10},{9,11},{10,... | collective-permute-start | bytes 368648 | tf_op jit(solution)/shard_map/ppermute | solution.py:530
  43.8 10.8 %collective-permute-start.3 = (bf16[120,512]{1,0:T(8,128)(2,1)S(1)}, bf16[120,512]{1,0:T(8,128)(2,1)S(1)}, u32[]{:S(2)}, u32[]{:S(2)}) collective-permute-start(bf16[120,512]{1,0:T(8,128)(2,1)S(1)} %get-tuple-element.41), channel_id=1, source_target_pairs={{0,3},{1,0},{2,1},{3,2},{4,7},{5,4},{6,5},{7,6},{8,11},{9,8},{10,9... | collective-permute-start | bytes 368648 | tf_op jit(solution)/shard_map/ppermute | solution.py:530
  56.1 1.2 %collective-permute-start.13 = (f32[64,128]{1,0:T(8,128)S(1)}, f32[64,128]{1,0:T(8,128)S(1)}, u32[]{:S(2)}, u32[]{:S(2)}) collective-permute-start(f32[64,128]{1,0:T(8,128)S(1)} %get-tuple-element.63), channel_id=1, source_target_pairs={{0,4},{4,0},{8,12},{12,8},{16,20},{20,16},{24,28},{28,24},{1,5},{5... | collective-permute-start | bytes 98312 | tf_op jit(solution)/shard_map/ppermute | solution.py:494
  57.3 3.9 %collective-permute-start.14 = (f32[64,128]{1,0:T(8,128)S(1)}, f32[64,128]{1,0:T(8,128)S(1)}, u32[]{:S(2)}, u32[]{:S(2)}) collective-permute-start(f32[64,128]{1,0:T(8,128)S(1)} %add.6), channel_id=1, source_target_pairs={{0,8},{4,12},{8,0},{12,4},{16,24},{20,28},{24,16},{28,20},{1,9},{5... | collective-permute-start | bytes 98312 | tf_op jit(solution)/shard_map/ppermute | solution.py:494
  61.2 4.0 %copy-start.5 = (f32[64,128]{1,0:T(8,128)}, f32[64,128]{1,0:T(8,128)S(1)}, u32[]{:S(2)}) copy-start(f32[64,128]{1,0:T(8,128)S(1)} %add.7.refs_0_) | copy-start | bytes 98308
  61.2 4.0 %collective-permute-start.15 = (f32[64,128]{1,0:T(8,128)S(1)}, f32[64,128]{1,0:T(8,128)S(1)}, u32[]{:S(2)}, u32[]{:S(2)}) collective-permute-start(f32[64,128]{1,0:T(8,128)S(1)} %add.7.refs_0_), channel_id=1, source_target_pairs={{0,16},{4,20},{8,24},{12,28},{16,0},{20,4},{24,8},{28,12},{1,17},{... | collective-permute-start | bytes 98312 | tf_op jit(solution)/shard_map/ppermute | solution.py:494
  65.2 0.6 copy-start.6
